TPU v7x, 32 devices: a whole 2x2x4 slice. The times are simulated.
32 devices in a mesh: groups: 2 (over y), row: 16 (over z, x, core).
Axes of the slice: x: 2, y: 2, z: 4, core: 2. Of those that a mesh axis runs over, the one named last changes fastest.
Arguments:
- sigma_blocks: bfloat16 [2, 16, 5, 512, 512], P('groups', 'row'), parts along dimension 0, may hold values from -6 to 6
- first_panel: bfloat16 [2, 16, 512, 512], P('groups', 'row'), parts along dimension 0, may hold values from -0.0625 to 0.0625
- second_panel: bfloat16 [2, 16, 512, 512], P('groups', 'row'), parts along dimension 0, may hold values from -0.0625 to 0.0625
- lower_panel: bfloat16 [1024, 512], P('groups'), parts along dimension 0, may hold values from -0.25 to 0.25
- first_diag: float32 [1024, 512], P('groups'), parts along dimension 0, may hold values from -6 to 6
- second_diag: float32 [1024, 512], P('groups'), parts along dimension 0, may hold values from -6 to 6
- task_list: int32 [2, 16, 5], P('groups', 'row'), parts along dimension 0, may hold values from -2 to 2, as said below
- task_count: int32 [2, 16], P('groups', 'row'), parts along dimension 0, may hold values from 1 to 5, as said below
Outputs:
- column_first: bfloat16 [2, 16, 512, 512], P('groups', 'row'), parts along dimension 0
- block_first: float32 [1024, 512], P('groups'), parts along dimension 0
- block_link: float32 [1024, 512], P('groups'), parts along dimension 0
- column_second: bfloat16 [2, 16, 512, 512], P('groups', 'row'), parts along dimension 0
- block_second: float32 [1024, 512], P('groups'), parts along dimension 0
There are 2 independent parts, one for each index of `groups`. A program takes and returns all parts, laid end to end along the dimension named above; each array names one. Nothing has to cross between parts.
Inputs may be any that keep to these rules, and one draw needn't show every extreme that they name: For slots s < task_count, block row i + task_list[i, s] lies in 0 to 15; the live offsets of a row are distinct, increasing, and include 0; slots from task_count on hold 0. `task_count`: some block row has all 5 couplings live and some has only its own.
All inputs are finite; a program needn't handle non-finite values.
Results may differ from a plain program's by a relative error of at most 0.0041.
Values may be sent and summed in bfloat16 or wider, within the bound.
No kernel may reach another device: no remote copies, remote signals or barrier semaphores. Data moves between devices by JAX's collectives and lax.ppermute only.
A program may use at most 64 MiB of HBM per device.

v0:
```python
import jax
import jax.numpy as jnp
from jax import lax
from jax.sharding import PartitionSpec as P


def shifted(block, axis, distance):
    devices = range(lax.axis_size(axis))
    route = [((i - distance) % len(devices), i) for i in devices]
    return lax.ppermute(block, axis, route)


def settle(received, offset, position, devices):
    empty = jnp.zeros_like(received)
    if offset > 0:
        moved = jnp.concatenate([received[1:], empty], axis=0)
        return jnp.where(position + offset >= devices, moved, received)
    moved = jnp.concatenate([empty, received[:-1]], axis=0)
    return jnp.where(position + offset < 0, moved, received)


def band_product(sigma_blocks, neighbours, task_list, task_count, reach_width):
    local_row = 0

    def add_slot(slot_index, running, local_row=local_row):
        offset = task_list[local_row, 0, slot_index] + reach_width
        panel_block = lax.dynamic_index_in_dim(neighbours[local_row, 0], offset, 0, keepdims=False)
        sigma_block = lax.dynamic_index_in_dim(
            sigma_blocks[local_row, 0], slot_index, 0, keepdims=False
        )
        return running + jnp.dot(sigma_block, panel_block, preferred_element_type=jnp.float32)

    start_value = jnp.zeros((sigma_blocks.shape[-2], neighbours.shape[-1]), jnp.float32)
    results = [lax.fori_loop(0, task_count[local_row, 0], add_slot, start_value)]
    return jnp.stack(results)[:, None]


def shards(
    sigma_blocks,
    first_panel,
    second_panel,
    lower_panel,
    first_diag,
    second_diag,
    task_list,
    task_count,
):
    reach_width = (task_list.shape[-1] - 1) // 2
    position = lax.axis_index("row")
    devices = lax.axis_size("row")
    offset_range = list(range(-reach_width, reach_width + 1))
    pieces = []
    for offset in offset_range:
        if offset == 0:
            pieces.append(first_panel)
        else:
            received = shifted(first_panel, "row", -offset)
            pieces.append(settle(received, offset, position, devices))
    first_band = band_product(
        sigma_blocks, jnp.stack(pieces, axis=2), task_list, task_count, reach_width
    )
    pieces = []
    for offset in offset_range:
        if offset == 0:
            pieces.append(second_panel)
        else:
            received = shifted(second_panel, "row", -offset)
            pieces.append(settle(received, offset, position, devices))
    second_band = band_product(
        sigma_blocks, jnp.stack(pieces, axis=2), task_list, task_count, reach_width
    )
    column_first = (-first_band).astype(jnp.bfloat16)
    part_diag = -jnp.einsum(
        "jnab,jnac->bc", first_panel, column_first, preferred_element_type=jnp.float32
    )
    part_cross = jnp.einsum(
        "jnab,jnac->bc", column_first, second_panel, preferred_element_type=jnp.float32
    )
    second_total = second_band + jnp.einsum(
        "jnab,bc->jnac", column_first, lower_panel, preferred_element_type=jnp.float32
    )
    column_second = (-second_total).astype(jnp.bfloat16)
    part_second = -jnp.einsum(
        "jnab,jnac->bc", second_panel, column_second, preferred_element_type=jnp.float32
    )
    sum_diag, sum_cross = lax.psum((part_diag, part_cross), "row")
    sum_second = lax.psum(part_second, "row")
    lower_wide = lower_panel.astype(jnp.float32)
    block_first = first_diag + sum_diag
    link = jnp.dot(block_first, lower_wide, precision=lax.Precision.HIGHEST) + sum_cross
    block_link = -link
    block_second = (
        second_diag + jnp.dot(lower_wide.T, link, precision=lax.Precision.HIGHEST) + sum_second
    )
    return (column_first, block_first, block_link, column_second, block_second)


def solution(mesh):
    return jax.shard_map(
        shards,
        mesh=mesh,
        in_specs=(
            P("groups", "row", None, None, None),
            P("groups", "row", None, None),
            P("groups", "row", None, None),
            P("groups", None),
            P("groups", None),
            P("groups", None),
            P("groups", "row", None),
            P("groups", "row"),
        ),
        out_specs=(
            P("groups", "row", None, None),
            P("groups", None),
            P("groups", None),
            P("groups", "row", None, None),
            P("groups", None),
        ),
        check_vma=False,
    )
```

profile of v0, /device:TPU:0, one launch (start us, length us, event | category | flops | bytes accessed | tf_op | source)
XLA Modules:
  0.0 255.4 jit_solution(16867468872295853440)
XLA Ops:
  7.2 3.0 %collective-permute-start.4 = (bf16[1,1,512,512]{3,2,1,0:T(8,128)(2,1)}, bf16[1,1,512,512]{3,2,1,0:T(8,128)(2,1)}, u32[]{:S(2)}, u32[]{:S(2)}) collective-permute-start(bf16[1,1,512,512]{3,2,1,0:T(8,128)(2,1)} %param.14), channel_id=1, source_target_pairs={{14,0},{15,1},{0,2},{1,3},{2,4},{3,5},{4,6},{5,7},{6,8},{7,9},{8,1... | collective-permute-start | bytes 1572872 | tf_op jit(solution)/shard_map/ppermute | solution.py:10
  10.2 4.4 %collective-permute-start.6 = (bf16[1,1,512,512]{3,2,1,0:T(8,128)(2,1)}, bf16[1,1,512,512]{3,2,1,0:T(8,128)(2,1)S(1)}, u32[]{:S(2)}, u32[]{:S(2)}) collective-permute-start(bf16[1,1,512,512]{3,2,1,0:T(8,128)(2,1)} %param.14), channel_id=1, source_target_pairs={{1,0},{2,1},{3,2},{4,3},{5,4},{6,5},{7,6},{8,7},{9,8},{10,9},{11,1... | collective-permute-start | bytes 1572872 | tf_op jit(solution)/shard_map/ppermute | solution.py:10
  14.7 13.8 %collective-permute-done.4 = bf16[1,1,512,512]{3,2,1,0:T(8,128)(2,1)} collective-permute-done((bf16[1,1,512,512]{3,2,1,0:T(8,128)(2,1)}, bf16[1,1,512,512]{3,2,1,0:T(8,128)(2,1)}, u32[]{:S(2)}, u32[]{:S(2)}) %collective-permute-start.4) | collective-permute-done | bytes 524320 | tf_op jit(solution)/shard_map/ppermute | solution.py:10
  28.5 2.9 %collective-permute-start.2 = (bf16[1,1,512,512]{3,2,1,0:T(8,128)(2,1)}, bf16[1,1,512,512]{3,2,1,0:T(8,128)(2,1)S(1)}, u32[]{:S(2)}, u32[]{:S(2)}) collective-permute-start(bf16[1,1,512,512]{3,2,1,0:T(8,128)(2,1)} %param.13), channel_id=1, source_target_pairs={{1,0},{2,1},{3,2},{4,3},{5,4},{6,5},{7,6},{8,7},{9,8},{10,9},{11,1... | collective-permute-start | bytes 1572872 | tf_op jit(solution)/shard_map/ppermute | solution.py:10
  31.5 4.5 %collective-permute-done.5 = bf16[1,1,512,512]{3,2,1,0:T(8,128)(2,1)} collective-permute-done((bf16[1,1,512,512]{3,2,1,0:T(8,128)(2,1)}, bf16[1,1,512,512]{3,2,1,0:T(8,128)(2,1)}, u32[]{:S(2)}, u32[]{:S(2)}) %collective-permute-start.5) | collective-permute-done | bytes 524320 | tf_op jit(solution)/shard_map/ppermute | solution.py:10
  36.0 12.6 %collective-permute-start.3 = (bf16[1,1,512,512]{3,2,1,0:T(8,128)(2,1)}, bf16[1,1,512,512]{3,2,1,0:T(8,128)(2,1)S(1)}, u32[]{:S(2)}, u32[]{:S(2)}) collective-permute-start(bf16[1,1,512,512]{3,2,1,0:T(8,128)(2,1)} %param.13), channel_id=1, source_target_pairs={{2,0},{3,1},{4,2},{5,3},{6,4},{7,5},{8,6},{9,7},{10,8},{11,9},{12,... | collective-permute-start | bytes 1572872 | tf_op jit(solution)/shard_map/ppermute | solution.py:10
  48.7 1.1 bitcast_dynamic-update-slice_fusion.2
  49.7 6.7 %collective-permute-done = bf16[1,1,512,512]{3,2,1,0:T(8,128)(2,1)S(1)} collective-permute-done((bf16[1,1,512,512]{3,2,1,0:T(8,128)(2,1)}, bf16[1,1,512,512]{3,2,1,0:T(8,128)(2,1)S(1)}, u32[]{:S(2)}, u32[]{:S(2)}) %collective-permute-start) | collective-permute-done | bytes 524320 | tf_op jit(solution)/shard_map/ppermute | solution.py:10
  56.4 5.6 %collective-permute-start.7 = (bf16[1,1,512,512]{3,2,1,0:T(8,128)(2,1)S(1)}, bf16[1,1,512,512]{3,2,1,0:T(8,128)(2,1)S(1)}, u32[]{:S(2)}, u32[]{:S(2)}) collective-permute-start(bf16[1,1,512,512]{3,2,1,0:T(8,128)(2,1)S(1)} %copy-done.1), channel_id=1, source_target_pairs={{2,0},{3,1},{4,2},{5,3},{6,4},{7,5},{8,6},{9,7},{10,8},{11,9},{12,... | collective-permute-start | bytes 1572872 | tf_op jit(solution)/shard_map/ppermute | solution.py:10
  62.5 13.5 %collective-permute-done.3 = bf16[1,1,512,512]{3,2,1,0:T(8,128)(2,1)S(1)} collective-permute-done((bf16[1,1,512,512]{3,2,1,0:T(8,128)(2,1)}, bf16[1,1,512,512]{3,2,1,0:T(8,128)(2,1)S(1)}, u32[]{:S(2)}, u32[]{:S(2)}) %collective-permute-start.3) | collective-permute-done | bytes 524320 | tf_op jit(solution)/shard_map/ppermute | solution.py:10
  76.0 5.6 %collective-permute-done.7 = bf16[1,1,512,512]{3,2,1,0:T(8,128)(2,1)S(1)} collective-permute-done((bf16[1,1,512,512]{3,2,1,0:T(8,128)(2,1)S(1)}, bf16[1,1,512,512]{3,2,1,0:T(8,128)(2,1)S(1)}, u32[]{:S(2)}, u32[]{:S(2)}) %collective-permute-start.7) | collective-permute-done | bytes 524320 | tf_op jit(solution)/shard_map/ppermute | solution.py:10
  81.8 1.5 copy-done.3
  83.4 0.7 copy-done.4
  84.1 5.5 %while.24 = (s32[]{:T(128)}, f32[512,512]{1,0:T(8,128)S(1)}, s32[]{:T(128)}, bf16[1,1,5,512,512]{4,3,2,1,0:T(8,128)(2,1)}, s32[1,1,5]{2,1,0:T(1,128)S(1)}, /*ind...) while((s32[]{:T(128)}, f32[512,512]{1,0:T(8,128)S(1)}, ...), condition=%wide.region_1.2_spmd, body=%wide.region_0.1_spmd.sunk | while | flops 268697600 | bytes 3145921 | solution.py:34
  84.8 0.6 fusion.41
  87.3 1.7 convolution_add_fusion.6
  89.6 1.4 fusion.12
  91.1 1.4 fusion.17
  92.7 5.5 %while.25 = (s32[]{:T(128)}, f32[512,512]{1,0:T(8,128)S(1)}, s32[]{:T(128)}, bf16[1,1,5,512,512]{4,3,2,1,0:T(8,128)(2,1)}, s32[1,1,5]{2,1,0:T(1,128)S(1)}, /*ind...) while((s32[]{:T(128)}, f32[512,512]{1,0:T(8,128)S(1)}, ...), condition=%wide.region_5.6_spmd, body=%wide.region_4.5_spmd.sunk | while | flops 268697600 | bytes 3145921 | solution.py:34
  93.3 0.6 fusion.44
  95.9 1.7 convolution_add_fusion.7
  98.7 0.8 copy-done.6
  99.4 1.4 fusion.10
  100.9 1.6 copy.13
  102.5 2.5 copy.14
  105.0 0.9 fusion.32
  105.9 135.5 %all-reduce.3.cloned.1.call-done = (f32[512,512]{0,1:T(8,128)}, f32[512,512]{1,0:T(8,128)}, f32[512,512]{0,1:T(8,128)}) async-done(((f32[512,512]{0,1:T(8,128)}, f32[512,512]{1,0:T(8,128)}, f32[512,512]{0,1:T(8,128)}), (f32[512,512]{0,1:T(8,128)}, f32[512,512]{1,0:T(8,128)}, f32[512,512]{0,1:T(8,128)})) %all-reduce.3.cloned.1.call-update) | async-done | bytes 3145744 | tf_op jit(solution)/shard_map/psum | solution.py:86
  241.4 1.4 add.126
  242.9 1.3 copy.15
  244.2 2.0 fusion.22
  246.2 1.0 fusion.14
  247.2 1.3 copy.16
  (36 shorter events, 1.6 us)
Async XLA Ops:
  7.2 91.0 %copy-start = (bf16[512,512]{1,0:T(8,128)(2,1)S(1)}, bf16[512,512]{1,0:T(8,128)(2,1)}, u32[]{:S(2)}) copy-start(bf16[512,512]{1,0:T(8,128)(2,1)} %param.15) | copy-start | bytes 1572868
  7.2 49.3 %copy-start.1 = (bf16[1,1,512,512]{3,2,1,0:T(8,128)(2,1)S(1)}, bf16[1,1,512,512]{3,2,1,0:T(8,128)(2,1)}, u32[]{:S(2)}) copy-start(bf16[1,1,512,512]{3,2,1,0:T(8,128)(2,1)} %param.14) | copy-start | bytes 1572868
  7.2 234.2 %all-reduce.3.cloned.1.call-start = ((), (), s32[]{:S(2)}) async-start(), calls=%async_computation | async-start | bytes 6291456 | tf_op jit(solution)/shard_map/psum | solution.py:86
  7.2 21.3 %collective-permute-start.4 = (bf16[1,1,512,512]{3,2,1,0:T(8,128)(2,1)}, bf16[1,1,512,512]{3,2,1,0:T(8,128)(2,1)}, u32[]{:S(2)}, u32[]{:S(2)}) collective-permute-start(bf16[1,1,512,512]{3,2,1,0:T(8,128)(2,1)} %param.14), channel_id=1, source_target_pairs={{14,0},{15,1},{0,2},{1,3},{2,4},{3,5},{4,6},{5,7},{6,8},{7,9},{8,1... | collective-permute-start | bytes 1572872 | tf_op jit(solution)/shard_map/ppermute | solution.py:10
  10.2 25.8 %collective-permute-start.5 = (bf16[1,1,512,512]{3,2,1,0:T(8,128)(2,1)}, bf16[1,1,512,512]{3,2,1,0:T(8,128)(2,1)}, u32[]{:S(2)}, u32[]{:S(2)}) collective-permute-start(bf16[1,1,512,512]{3,2,1,0:T(8,128)(2,1)} %param.14), channel_id=1, source_target_pairs={{15,0},{0,1},{1,2},{2,3},{3,4},{4,5},{5,6},{6,7},{7,8},{8,9},{9,10... | collective-permute-start | bytes 1572872 | tf_op jit(solution)/shard_map/ppermute | solution.py:10
  10.2 52.0 %collective-permute-start.6 = (bf16[1,1,512,512]{3,2,1,0:T(8,128)(2,1)}, bf16[1,1,512,512]{3,2,1,0:T(8,128)(2,1)S(1)}, u32[]{:S(2)}, u32[]{:S(2)}) collective-permute-start(bf16[1,1,512,512]{3,2,1,0:T(8,128)(2,1)} %param.14), channel_id=1, source_target_pairs={{1,0},{2,1},{3,2},{4,3},{5,4},{6,5},{7,6},{8,7},{9,8},{10,9},{11,1... | collective-permute-start | bytes 1572872 | tf_op jit(solution)/shard_map/ppermute | solution.py:10
  14.7 41.8 %collective-permute-start = (bf16[1,1,512,512]{3,2,1,0:T(8,128)(2,1)}, bf16[1,1,512,512]{3,2,1,0:T(8,128)(2,1)S(1)}, u32[]{:S(2)}, u32[]{:S(2)}) collective-permute-start(bf16[1,1,512,512]{3,2,1,0:T(8,128)(2,1)} %param.13), channel_id=1, source_target_pairs={{14,0},{15,1},{0,2},{1,3},{2,4},{3,5},{4,6},{5,7},{6,8},{7,9},{8,1... | collective-permute-start | bytes 1572872 | tf_op jit(solution)/shard_map/ppermute | solution.py:10
  14.7 47.4 %collective-permute-start.1 = (bf16[1,1,512,512]{3,2,1,0:T(8,128)(2,1)}, bf16[1,1,512,512]{3,2,1,0:T(8,128)(2,1)S(1)}, u32[]{:S(2)}, u32[]{:S(2)}) collective-permute-start(bf16[1,1,512,512]{3,2,1,0:T(8,128)(2,1)} %param.13), channel_id=1, source_target_pairs={{15,0},{0,1},{1,2},{2,3},{3,4},{4,5},{5,6},{6,7},{7,8},{8,9},{9,10... | collective-permute-start | bytes 1572872 | tf_op jit(solution)/shard_map/ppermute | solution.py:10
  14.7 47.5 %copy-start.5 = (bf16[1,1,512,512]{3,2,1,0:T(8,128)(2,1)S(1)}, bf16[1,1,512,512]{3,2,1,0:T(8,128)(2,1)}, u32[]{:S(2)}) copy-start(bf16[1,1,512,512]{3,2,1,0:T(8,128)(2,1)} %param.13) | copy-start | bytes 1572868
  28.5 33.9 %collective-permute-start.2 = (bf16[1,1,512,512]{3,2,1,0:T(8,128)(2,1)}, bf16[1,1,512,512]{3,2,1,0:T(8,128)(2,1)S(1)}, u32[]{:S(2)}, u32[]{:S(2)}) collective-permute-start(bf16[1,1,512,512]{3,2,1,0:T(8,128)(2,1)} %param.13), channel_id=1, source_target_pairs={{1,0},{2,1},{3,2},{4,3},{5,4},{6,5},{7,6},{8,7},{9,8},{10,9},{11,1... | collective-permute-start | bytes 1572872 | tf_op jit(solution)/shard_map/ppermute | solution.py:10
  36.0 40.0 %collective-permute-start.3 = (bf16[1,1,512,512]{3,2,1,0:T(8,128)(2,1)}, bf16[1,1,512,512]{3,2,1,0:T(8,128)(2,1)S(1)}, u32[]{:S(2)}, u32[]{:S(2)}) collective-permute-start(bf16[1,1,512,512]{3,2,1,0:T(8,128)(2,1)} %param.13), channel_id=1, source_target_pairs={{2,0},{3,1},{4,2},{5,3},{6,4},{7,5},{8,6},{9,7},{10,8},{11,9},{12,... | collective-permute-start | bytes 1572872 | tf_op jit(solution)/shard_map/ppermute | solution.py:10
  56.4 25.1 %collective-permute-start.7 = (bf16[1,1,512,512]{3,2,1,0:T(8,128)(2,1)S(1)}, bf16[1,1,512,512]{3,2,1,0:T(8,128)(2,1)S(1)}, u32[]{:S(2)}, u32[]{:S(2)}) collective-permute-start(bf16[1,1,512,512]{3,2,1,0:T(8,128)(2,1)S(1)} %copy-done.1), channel_id=1, source_target_pairs={{2,0},{3,1},{4,2},{5,3},{6,4},{7,5},{8,6},{9,7},{10,8},{11,9},{12,... | collective-permute-start | bytes 1572872 | tf_op jit(solution)/shard_map/ppermute | solution.py:10
  62.3 21.9 %copy-start.9 = (s32[1,1,5]{2,1,0:T(1,128)S(1)}, s32[1,1,5]{2,1,0:T(1,128)}, u32[]{:S(2)}) copy-start(s32[1,1,5]{2,1,0:T(1,128)} %param.18) | copy-start | bytes 64
  81.8 1.5 copy-start.3
  81.8 2.3 copy-start.4
  98.6 0.8 copy-start.6
  242.9 1.3 copy-start.8
  244.2 2.0 copy-start.2
  244.2 2.0 copy-start.7
Sparse Core Ops, SparseCore 0:
  101.0 140.3 all-reduce.2
where the time goes:
time: 256 us; the launch traced here: 255 us
  waiting for transfers between devices  180 us (70%)
  starting transfers between devices  28.5 us (11%)
  between operations  14.2 us (6%)
  local copies, waits for them, and re-layouts  11.1 us (4%)
  matrix products  11.1 us (4%)
  loops' own time  6.54 us (3%)
  other arithmetic  4.26 us (2%)
    psum x1, waiting for transfers between devices, shards(): sum_diag, sum_cross = lax.psum((part_diag, part_cross), 'row')  136 us
    ppermute x8, waiting for transfers between devices, shifted(): return lax.ppermute(block, axis, route)  44.1 us
    ppermute x8, starting transfers between devices, shifted(): return lax.ppermute(block, axis, route)  28.5 us
    unnamed x26, local copies, waits for them, and re-layouts  10.8 us
    another operation x2, loops' own time, band_product(): lax.fori_loop(0, task_count[local_row, 0], add_slot, start_value)  6.54 us
  transfers between devices with their start and end apart: 9, of which 6 were waited for; matrix products, arithmetic and copies ran while one was open for 3% of the time, Pallas kernels for 0%

commit v1 on v0

v1 whole, which is shorter than its diff:
```python
import functools

import jax
import jax.numpy as jnp
from jax import lax
from jax.experimental import pallas as pl
from jax.experimental.pallas import tpu as pltpu
from jax.sharding import PartitionSpec as P

VMEM_BYTES = 40 * 1024 * 1024


def vmem_spec():
    return pl.BlockSpec(memory_space=pltpu.VMEM)


def smem_spec():
    return pl.BlockSpec(memory_space=pltpu.SMEM)


def call(body, outs, args, scalars, scratch, flops):
    moved = sum(a.size * a.dtype.itemsize for a in args) + sum(o.size * o.dtype.itemsize for o in outs)
    return pl.pallas_call(
        body,
        out_shape=outs,
        in_specs=[smem_spec()] * scalars + [vmem_spec()] * (len(args) - scalars),
        out_specs=[vmem_spec()] * len(outs),
        scratch_shapes=scratch,
        compiler_params=pltpu.CompilerParams(vmem_limit_bytes=VMEM_BYTES),
        cost_estimate=pl.CostEstimate(flops=flops, bytes_accessed=moved, transcendentals=0),
    )(*args)


def dot(a, b):
    return lax.dot_general(a, b, (((1,), (0,)), ((), ())), preferred_element_type=jnp.float32)


def dot_t(a, b):
    return lax.dot_general(a, b, (((0,), (0,)), ((), ())), preferred_element_type=jnp.float32)


def band(where_ref, list_ref, count_ref, sigma_ref, panels, acc_ref):
    member = where_ref[0] % 4
    across = jnp.where(member < 2, 2, -2)
    beside = jnp.where(member % 2 == 0, 1, -1)
    offsets = (0, beside, across, -across, -beside)
    acc_ref[...] = jnp.zeros_like(acc_ref)
    for offset, panel in zip(offsets, panels):
        slot = jnp.int32(0)
        live = jnp.int32(0)
        for s in range(sigma_ref.shape[0]):
            hit = (list_ref[s] == offset) & (s < count_ref[0])
            slot = jnp.where(hit, s, slot)
            live = jnp.where(hit, 1, live)

        @pl.when(live == 1)
        def _(slot=slot, panel=panel):
            acc_ref[...] += dot(sigma_ref[slot], panel[...])


def first_kernel(where_ref, list_ref, count_ref, sigma_ref, own, beside, across, far, rest, second_ref,
                 column_ref, parts_ref, acc_ref):
    band(where_ref, list_ref, count_ref, sigma_ref, (own, beside, across, far, rest), acc_ref)
    column = (-acc_ref[...]).astype(jnp.bfloat16)
    column_ref[...] = column
    chunks, _, rows, width = parts_ref.shape
    diag = -dot_t(own[...], column)
    parts_ref[:, 0] = diag.astype(jnp.bfloat16).reshape(chunks, rows, width)
    cross = dot_t(column, second_ref[...])
    parts_ref[:, 1] = cross.astype(jnp.bfloat16).reshape(chunks, rows, width)


def second_kernel(where_ref, list_ref, count_ref, sigma_ref, own, beside, across, far, rest, column_first_ref,
                  lower_ref, column_ref, parts_ref, acc_ref):
    band(where_ref, list_ref, count_ref, sigma_ref, (own, beside, across, far, rest), acc_ref)
    total = acc_ref[...] + dot(column_first_ref[...], lower_ref[...])
    column = (-total).astype(jnp.bfloat16)
    column_ref[...] = column
    chunks, rows, width = parts_ref.shape
    parts_ref[...] = (-dot_t(own[...], column)).astype(jnp.bfloat16).reshape(chunks, rows, width)


def split(value):
    high = value.astype(jnp.bfloat16)
    low = (value - high.astype(jnp.float32)).astype(jnp.bfloat16)
    return high, low


def final_kernel(sums_ref, second_sum_ref, lower_ref, first_diag_ref, second_diag_ref, first_ref, link_ref, second_ref):
    size = lower_ref.shape
    lower = lower_ref[...]
    block_first = first_diag_ref[...] + sums_ref[:, 0].astype(jnp.float32).reshape(size)
    first_ref[...] = block_first
    high, low = split(block_first)
    link = dot(high, lower) + dot(low, lower) + sums_ref[:, 1].astype(jnp.float32).reshape(size)
    link_ref[...] = -link
    high, low = split(link)
    second_ref[...] = (
        second_diag_ref[...]
        + dot_t(lower, high)
        + dot_t(lower, low)
        + second_sum_ref[...].astype(jnp.float32).reshape(size)
    )


def exchange(panel, member, devices):
    beside = lax.ppermute(panel, "row", [(i, i ^ 1) for i in range(devices)])
    across = lax.ppermute(panel, "row", [(i, i ^ 2) for i in range(devices)])
    hops = [(i, i + 4 if i % 4 < 2 else i - 4) for i in range(devices)]
    far = lax.ppermute(across, "row", [(a, b) for a, b in hops if 0 <= b < devices])
    give_across = (member == 0) | (member == 3)
    rest = lax.ppermute(jnp.where(give_across, across, far), "row", [(i, i ^ 1) for i in range(devices)])
    return beside, across, far, rest


def summed(parts):
    devices = parts.shape[0]
    mine = lax.all_to_all(parts, "row", 0, 0, tiled=True)
    total = jnp.sum(mine.astype(jnp.float32), axis=0).astype(jnp.bfloat16)
    return lax.all_to_all(jnp.broadcast_to(total[None], (devices,) + total.shape), "row", 0, 0, tiled=True)


def shards(sigma_blocks, first_panel, second_panel, lower_panel, first_diag, second_diag, task_list, task_count):
    devices = lax.axis_size("row")
    position = lax.axis_index("row").astype(jnp.int32)
    member = position % 4
    slots, size, width = sigma_blocks.shape[-3:]
    sigma = sigma_blocks.reshape((slots, size, width))
    first = first_panel.reshape((size, width))
    second = second_panel.reshape((size, width))
    where = position.reshape((1,))
    listed = task_list.reshape((slots,))
    count = task_count.reshape((1,))
    one = 2 * size * size * width
    rows = size // devices

    first_near = exchange(first, member, devices)
    second_near = exchange(second, member, devices)
    column_first, parts = call(
        first_kernel,
        [jax.ShapeDtypeStruct((size, width), jnp.bfloat16), jax.ShapeDtypeStruct((devices, 2, rows, width), jnp.bfloat16)],
        [where, listed, count, sigma, first, *first_near, second],
        3,
        [pltpu.VMEM((size, width), jnp.float32)],
        7 * one,
    )
    column_second, second_parts = call(
        second_kernel,
        [jax.ShapeDtypeStruct((size, width), jnp.bfloat16), jax.ShapeDtypeStruct((devices, rows, width), jnp.bfloat16)],
        [where, listed, count, sigma, second, *second_near, column_first, lower_panel],
        3,
        [pltpu.VMEM((size, width), jnp.float32)],
        7 * one,
    )
    sums = summed(parts)
    second_sum = summed(second_parts)
    wide = jax.ShapeDtypeStruct((size, width), jnp.float32)
    block_first, block_link, block_second = call(
        final_kernel,
        [wide] * 3,
        [sums, second_sum, lower_panel, first_diag, second_diag],
        0,
        [],
        4 * one,
    )
    shape = first_panel.shape
    return column_first.reshape(shape), block_first, block_link, column_second.reshape(shape), block_second


def solution(mesh):
    return jax.shard_map(
        shards,
        mesh=mesh,
        in_specs=(
            P("groups", "row", None, None, None),
            P("groups", "row", None, None),
            P("groups", "row", None, None),
            P("groups", None),
            P("groups", None),
            P("groups", None),
            P("groups", "row", None),
            P("groups", "row"),
        ),
        out_specs=(
            P("groups", "row", None, None),
            P("groups", None),
            P("groups", None),
            P("groups", "row", None, None),
            P("groups", None),
        ),
        check_vma=False,
    )
```

time: 256 us -> 157 us (0.61)
  waiting for transfers between devices: 180 us -> 64.6 us
  blocking collectives: 0 us -> 51.6 us
  between operations: 14.2 us -> 1.43 us
  matrix products: 11.1 us -> 0 us
  Pallas kernels: 0 us -> 8.01 us
  loops' own time: 6.54 us -> 0 us
  starting transfers between devices: 28.5 us -> 22.8 us
  local copies, waits for them, and re-layouts: 11.1 us -> 5.85 us
  other arithmetic: 4.26 us -> 1.57 us
    psum x1 -> x0, waiting for transfers between devices: 136 us -> none  [shards(): sum_diag, sum_cross = lax.psum((part_diag, part_cross), 'row')]
    all_to_all x0 -> x2, blocking collectives: none -> 51.6 us  [the longest x1 28.7 us: summed(): lax.all_to_all(jnp.broadcast_to(total[None], (devices,) + total.shape), '...]
    all_to_all x0 -> x2, waiting for transfers between devices: none -> 35.9 us  [the longest x1 22.9 us: summed(): mine = lax.all_to_all(parts, 'row', 0, 0, tiled=True)]
    ppermute x8, starting transfers between devices: 28.5 us -> 11.7 us  [the longest x2 7.82 us: exchange(): lax.ppermute(across, 'row', [(a, b) for a, b in hops if 0 <= b < devices])]
    ppermute x8, waiting for transfers between devices: 44.1 us -> 28.7 us  [the longest x2 19.2 us: exchange(): across = lax.ppermute(panel, 'row', [(i, i ^ 2) for i in range(devices)])]
    dot_general x8 -> x0, matrix products: 11.1 us -> none  [the longest x2 3.33 us: add_slot(): jnp.dot(sigma_block, panel_block, preferred_element_type=jnp.float32)]
    all_to_all x0 -> x2, starting transfers between devices: none -> 11.1 us  [the longest x1 7 us: summed(): lax.all_to_all(jnp.broadcast_to(total[None], (devices,) + total.shape), '...]
    pallas_call x0 -> x3, Pallas kernels: none -> 8.01 us  [call(): pl.pallas_call(body, out_shape=outs, in_specs=[smem_spec()] * scalars + [...]
  transfers between devices with their start and end apart: 9 -> 10, of which waited for: 6 -> 5; matrix products, arithmetic and copies ran while one was open for 3% -> 1% of each run, Pallas kernels for 0% -> 2%
where the time goes in v1:
time: 157 us; the launch traced here: 156 us
  waiting for transfers between devices  64.6 us (41%)
  blocking collectives  51.6 us (33%)
  starting transfers between devices  22.8 us (15%)
  Pallas kernels  8.01 us (5%)
  local copies, waits for them, and re-layouts  5.85 us (4%)
  other arithmetic  1.57 us (1%)
    all_to_all x1, blocking collectives, summed(): lax.all_to_all(jnp.broadcast_to(total[None], (devices,) + total.shape), '...  28.7 us
    all_to_all x1, waiting for transfers between devices, summed(): mine = lax.all_to_all(parts, 'row', 0, 0, tiled=True)  22.9 us
    all_to_all x1, blocking collectives, summed(): mine = lax.all_to_all(parts, 'row', 0, 0, tiled=True)  22.8 us
    ppermute x2, waiting for transfers between devices, exchange(): across = lax.ppermute(panel, 'row', [(i, i ^ 2) for i in range(devices)])  19.2 us
    all_to_all x1, waiting for transfers between devices, summed(): lax.all_to_all(jnp.broadcast_to(total[None], (devices,) + total.shape), '...  13.1 us
    ppermute x2, waiting for transfers between devices, exchange(): lax.ppermute(across, 'row', [(a, b) for a, b in hops if 0 <= b < devices])  9.48 us
    pallas_call x3, Pallas kernels, call(): pl.pallas_call(body, out_shape=outs, in_specs=[smem_spec()] * scalars + [...  8.01 us
    ppermute x2, starting transfers between devices, exchange(): lax.ppermute(across, 'row', [(a, b) for a, b in hops if 0 <= b < devices])  7.82 us
  transfers between devices with their start and end apart: 10, of which 5 were waited for; matrix products, arithmetic and copies ran while one was open for 1% of the time, Pallas kernels for 2%

profile of v1, /device:TPU:0, one launch (start us, length us, event | category | flops | bytes accessed | tf_op | source)
XLA Modules:
  0.0 155.8 jit_solution(3304675357958539792)
XLA Ops:
  0.7 3.0 %collective-permute-start.1 = (bf16[512,512]{1,0:T(8,128)(2,1)}, bf16[512,512]{1,0:T(8,128)(2,1)S(1)}, u32[]{:S(2)}, u32[]{:S(2)}) collective-permute-start(bf16[512,512]{1,0:T(8,128)(2,1)} %bitcast.12), channel_id=1, source_target_pairs={{0,2},{1,3},{2,0},{3,1},{4,6},{5,7},{6,4},{7,5},{8,10},{9,11},{10,... | collective-permute-start | bytes 1572872 | tf_op jit(solution)/shard_map/ppermute | solution.py:108
  3.7 0.1 collective-permute-start.5
  3.7 12.9 %collective-permute-done.1.across = bf16[512,512]{1,0:T(8,128)(2,1)S(1)} collective-permute-done((bf16[512,512]{1,0:T(8,128)(2,1)}, bf16[512,512]{1,0:T(8,128)(2,1)S(1)}, u32[]{:S(2)}, u32[]{:S(2)}) %collective-permute-start.1) | collective-permute-done | bytes 524320 | tf_op jit(solution)/shard_map/ppermute | solution.py:108
  16.6 4.1 %collective-permute-start.2 = (bf16[512,512]{1,0:T(8,128)(2,1)S(1)}, bf16[512,512]{1,0:T(8,128)(2,1)S(1)}, u32[]{:S(2)}, u32[]{:S(2)}) collective-permute-start(bf16[512,512]{1,0:T(8,128)(2,1)S(1)} %collective-permute-done.1.across), channel_id=1, source_target_pairs={{0,4},{1,5},{4,8},{5,9},{6,2},{7,3},{8,12},{9,13},{10,6},{11,7},{1... | collective-permute-start | bytes 1572872 | tf_op jit(solution)/shard_map/ppermute | solution.py:110
  20.7 6.3 %collective-permute-done.5.across = bf16[512,512]{1,0:T(8,128)(2,1)S(1)} collective-permute-done((bf16[512,512]{1,0:T(8,128)(2,1)}, bf16[512,512]{1,0:T(8,128)(2,1)S(1)}, u32[]{:S(2)}, u32[]{:S(2)}) %collective-permute-start.5) | collective-permute-done | bytes 524320 | tf_op jit(solution)/shard_map/ppermute | solution.py:108
  27.0 3.8 %collective-permute-start.6 = (bf16[512,512]{1,0:T(8,128)(2,1)S(1)}, bf16[512,512]{1,0:T(8,128)(2,1)S(1)}, u32[]{:S(2)}, u32[]{:S(2)}) collective-permute-start(bf16[512,512]{1,0:T(8,128)(2,1)S(1)} %collective-permute-done.5.across), channel_id=1, source_target_pairs={{0,4},{1,5},{4,8},{5,9},{6,2},{7,3},{8,12},{9,13},{10,6},{11,7},{1... | collective-permute-start | bytes 1572872 | tf_op jit(solution)/shard_map/ppermute | solution.py:110
  30.8 0.1 collective-permute-start
  30.9 0.5 collective-permute-start.4
  31.4 0.1 broadcast_select_fusion.1
  31.4 0.1 collective-permute-start.3
  31.6 9.5 %collective-permute-done.6.far = bf16[512,512]{1,0:T(8,128)(2,1)S(1)} collective-permute-done((bf16[512,512]{1,0:T(8,128)(2,1)S(1)}, bf16[512,512]{1,0:T(8,128)(2,1)S(1)}, u32[]{:S(2)}, u32[]{:S(2)}) %collective-permute-start.6) | collective-permute-done | bytes 524320 | tf_op jit(solution)/shard_map/ppermute | solution.py:110
  41.0 0.1 broadcast_select_fusion
  41.1 0.1 collective-permute-start.7
  41.9 0.8 copy-done.7
  42.7 1.0 copy-done.5
  43.7 1.0 copy-done.8
  44.7 2.8 %shard_map.119 = (bf16[512,512]{1,0:T(8,128)(2,1)}, bf16[16,2,32,512]{3,2,1,0:T(8,128)(2,1)}) custom-call(s32[1]{0:T(128)} %bitcast.where_ref, s32[5]{0:T(128)S(1)} %bitcast.19, s32[1]{0:T(128)} %bitcast.8.count_ref, bf16[5,512,512]{2,1,0:T(8,128)(2,1)S(1)} %bitcast.10, bf16[512,512]{1,0:T(8,128)(2,1)S(1)} %bitcast.14, bf16[512,512]{1,0:T(8,128)(2,1)S(1)} %copy-done.8, ...), custom_call_target="tpu_custom_call" | custom-call | flops 1879048192 | bytes 7340060 | tf_op jit(solution)/shard_map/pallas_call | solution.py:23
  47.6 0.0 copy-start.10
  47.6 1.0 copy-done.10
  48.6 2.8 %shard_map.120 = (bf16[512,512]{1,0:T(8,128)(2,1)}, bf16[16,32,512]{2,1,0:T(8,128)(2,1)S(1)}) custom-call(s32[1]{0:T(128)} %bitcast.where_ref, s32[5]{0:T(128)S(1)} %bitcast.20, s32[1]{0:T(128)} %bitcast.9.count_ref, bf16[5,512,512]{2,1,0:T(8,128)(2,1)S(1)} %bitcast.11, bf16[512,512]{1,0:T(8,128)(2,1)S(1)} %bitcast.18, ...), custom_call_target="tpu_custom_call" | custom-call | flops 1879048192 | bytes 7340060 | tf_op jit(solution)/shard_map/pallas_call | solution.py:23
  51.5 22.8 %all_to_all.20 = bf16[16,32,512]{2,1,0:T(8,128)(2,1)S(1)} all-to-all(bf16[16,32,512]{2,1,0:T(8,128)(2,1)S(1)} %get-tuple-element.14), channel_id=1, replica_groups=mesh['groups'=2,'row'=16] {'row'}, dimensions={0} | all-to-all | bytes 1048576 | tf_op jit(solution)/shard_map/all_to_all | solution.py:118
  74.3 4.1 %all-to-all-start = ((bf16[16,2,32,512]{3,2,1,0:T(8,128)(2,1)}), bf16[16,2,32,512]{3,2,1,0:T(8,128)(2,1)S(1)}, u32[]{:S(2)}, u32[]{:S(2)}) async-start(bf16[16,2,32,512]{3,2,1,0:T(8,128)(2,1)} %get-tuple-element.13), calls=%async_computation | async-start | bytes 2097152 | tf_op jit(solution)/shard_map/all_to_all | solution.py:118
  78.4 0.1 reduce_sum.25
  78.5 22.9 %all-to-all-done = bf16[16,2,32,512]{3,2,1,0:T(8,128)(2,1)S(1)} async-done(((bf16[16,2,32,512]{3,2,1,0:T(8,128)(2,1)}), bf16[16,2,32,512]{3,2,1,0:T(8,128)(2,1)S(1)}, u32[]{:S(2)}, u32[]{:S(2)}) %all-to-all-start) | async-done | bytes 1048608 | tf_op jit(solution)/shard_map/all_to_all | solution.py:118
  101.3 1.0 copy-done.11
  102.3 0.8 broadcast_in_dim.5
  103.1 7.0 %all-to-all-start.3 = ((bf16[16,32,512]{2,1,0:T(8,128)(2,1)}), bf16[16,32,512]{2,1,0:T(8,128)(2,1)S(1)}, u32[]{:S(2)}, u32[]{:S(2)}) async-start(bf16[16,32,512]{2,1,0:T(8,128)(2,1)} %broadcast_in_dim.5), calls=%async_computation.3 | async-start | bytes 1048576 | tf_op jit(solution)/shard_map/all_to_all | solution.py:120
  110.1 1.4 reduce_sum.24
  111.5 13.1 %all-to-all-done.3.second_sum_ref = bf16[16,32,512]{2,1,0:T(8,128)(2,1)S(1)} async-done(((bf16[16,32,512]{2,1,0:T(8,128)(2,1)}), bf16[16,32,512]{2,1,0:T(8,128)(2,1)S(1)}, u32[]{:S(2)}, u32[]{:S(2)}) %all-to-all-start.3) | async-done | bytes 524320 | tf_op jit(solution)/shard_map/all_to_all | solution.py:120
  124.6 0.1 broadcast_in_dim.4
  124.7 28.7 %all_to_all.21.sums_ref = bf16[16,2,32,512]{3,2,1,0:T(8,128)(2,1)S(1)} all-to-all(bf16[16,2,32,512]{3,2,1,0:T(8,128)(2,1)S(1)} %broadcast_in_dim.4), channel_id=1, replica_groups=mesh['groups'=2,'row'=16] {'row'}, dimensions={0} | all-to-all | bytes 2097152 | tf_op jit(solution)/shard_map/all_to_all | solution.py:120
  153.5 2.4 %shard_map.121 = (f32[512,512]{1,0:T(8,128)}, f32[512,512]{1,0:T(8,128)}, f32[512,512]{1,0:T(8,128)}) custom-call(bf16[16,2,32,512]{3,2,1,0:T(8,128)(2,1)S(1)} %all_to_all.21.sums_ref, bf16[16,32,512]{2,1,0:T(8,128)(2,1)S(1)} %all-to-all-done.3.second_sum_ref, bf16[512,512]{1,0:T(8,128)(2,1)S(1)} %copy-done.2, f32[512,512]{1,0:T(8,128)S(1)} %copy-done, ...), custom_call_target="tpu_custom_call" | custom-call | flops 1073741824 | bytes 7340032 | tf_op jit(solution)/shard_map/pallas_call | solution.py:23
  (23 shorter events, 0.1 us)
Async XLA Ops:
  0.6 42.0 %copy-start.4 = (bf16[1,1,512,512]{3,2,1,0:T(8,128)(2,1)S(1)}, bf16[1,1,512,512]{3,2,1,0:T(8,128)(2,1)}, u32[]{:S(2)}) copy-start(bf16[1,1,512,512]{3,2,1,0:T(8,128)(2,1)} %param.9) | copy-start | bytes 1572868
  0.6 42.0 %copy-start.9 = (s32[1,1,5]{2,1,0:T(1,128)S(1)}, s32[1,1,5]{2,1,0:T(1,128)}, u32[]{:S(2)}) copy-start(s32[1,1,5]{2,1,0:T(1,128)} %param.14) | copy-start | bytes 64
  0.7 16.0 %collective-permute-start.1 = (bf16[512,512]{1,0:T(8,128)(2,1)}, bf16[512,512]{1,0:T(8,128)(2,1)S(1)}, u32[]{:S(2)}, u32[]{:S(2)}) collective-permute-start(bf16[512,512]{1,0:T(8,128)(2,1)} %bitcast.12), channel_id=1, source_target_pairs={{0,2},{1,3},{2,0},{3,1},{4,6},{5,7},{6,4},{7,5},{8,10},{9,11},{10,... | collective-permute-start | bytes 1572872 | tf_op jit(solution)/shard_map/ppermute | solution.py:108
  3.7 23.4 %collective-permute-start.5 = (bf16[512,512]{1,0:T(8,128)(2,1)}, bf16[512,512]{1,0:T(8,128)(2,1)S(1)}, u32[]{:S(2)}, u32[]{:S(2)}) collective-permute-start(bf16[512,512]{1,0:T(8,128)(2,1)} %bitcast.15), channel_id=1, source_target_pairs={{0,2},{1,3},{2,0},{3,1},{4,6},{5,7},{6,4},{7,5},{8,10},{9,11},{10,... | collective-permute-start | bytes 1572872 | tf_op jit(solution)/shard_map/ppermute | solution.py:108
  16.6 14.7 %collective-permute-start.2 = (bf16[512,512]{1,0:T(8,128)(2,1)S(1)}, bf16[512,512]{1,0:T(8,128)(2,1)S(1)}, u32[]{:S(2)}, u32[]{:S(2)}) collective-permute-start(bf16[512,512]{1,0:T(8,128)(2,1)S(1)} %collective-permute-done.1.across), channel_id=1, source_target_pairs={{0,4},{1,5},{4,8},{5,9},{6,2},{7,3},{8,12},{9,13},{10,6},{11,7},{1... | collective-permute-start | bytes 1572872 | tf_op jit(solution)/shard_map/ppermute | solution.py:110
  27.0 14.0 %collective-permute-start.6 = (bf16[512,512]{1,0:T(8,128)(2,1)S(1)}, bf16[512,512]{1,0:T(8,128)(2,1)S(1)}, u32[]{:S(2)}, u32[]{:S(2)}) collective-permute-start(bf16[512,512]{1,0:T(8,128)(2,1)S(1)} %collective-permute-done.5.across), channel_id=1, source_target_pairs={{0,4},{1,5},{4,8},{5,9},{6,2},{7,3},{8,12},{9,13},{10,6},{11,7},{1... | collective-permute-start | bytes 1572872 | tf_op jit(solution)/shard_map/ppermute | solution.py:110
  30.8 11.0 %collective-permute-start = (bf16[512,512]{1,0:T(8,128)(2,1)}, bf16[512,512]{1,0:T(8,128)(2,1)S(1)}, u32[]{:S(2)}, u32[]{:S(2)}) collective-permute-start(bf16[512,512]{1,0:T(8,128)(2,1)} %bitcast.13), channel_id=1, source_target_pairs={{0,1},{1,0},{2,3},{3,2},{4,5},{5,4},{6,7},{7,6},{8,9},{9,8},{10,11... | collective-permute-start | bytes 1572872 | tf_op jit(solution)/shard_map/ppermute | solution.py:107
  30.9 16.7 %collective-permute-start.4 = (bf16[512,512]{1,0:T(8,128)(2,1)}, bf16[512,512]{1,0:T(8,128)(2,1)}, u32[]{:S(2)}, u32[]{:S(2)}) collective-permute-start(bf16[512,512]{1,0:T(8,128)(2,1)} %bitcast.16), channel_id=1, source_target_pairs={{0,1},{1,0},{2,3},{3,2},{4,5},{5,4},{6,7},{7,6},{8,9},{9,8},{10,11... | collective-permute-start | bytes 1572872 | tf_op jit(solution)/shard_map/ppermute | solution.py:107
  31.4 11.3 %copy-start.3 = (bf16[1,1,5,512,512]{4,3,2,1,0:T(8,128)(2,1)S(1)}, bf16[1,1,5,512,512]{4,3,2,1,0:T(8,128)(2,1)}, u32[]{:S(2)}) copy-start(bf16[1,1,5,512,512]{4,3,2,1,0:T(8,128)(2,1)} %param.8) | copy-start | bytes 7864324
  31.4 11.2 %collective-permute-start.3 = (bf16[512,512]{1,0:T(8,128)(2,1)S(1)}, bf16[512,512]{1,0:T(8,128)(2,1)S(1)}, u32[]{:S(2)}, u32[]{:S(2)}) collective-permute-start(bf16[512,512]{1,0:T(8,128)(2,1)S(1)} %broadcast_select_fusion.1), channel_id=1, source_target_pairs={{0,1},{1,0},{2,3},{3,2},{4,5},{5,4},{6,7},{7,6},{8,9},{9,8},{10,11... | collective-permute-start | bytes 1572872 | tf_op jit(solution)/shard_map/ppermute | solution.py:112
  41.1 6.4 %collective-permute-start.7 = (bf16[512,512]{1,0:T(8,128)(2,1)S(1)}, bf16[512,512]{1,0:T(8,128)(2,1)S(1)}, u32[]{:S(2)}, u32[]{:S(2)}) collective-permute-start(bf16[512,512]{1,0:T(8,128)(2,1)S(1)} %broadcast_select_fusion), channel_id=1, source_target_pairs={{0,1},{1,0},{2,3},{3,2},{4,5},{5,4},{6,7},{7,6},{8,9},{9,8},{10,11... | collective-permute-start | bytes 1572872 | tf_op jit(solution)/shard_map/ppermute | solution.py:112
  41.8 0.8 copy-start.7
  42.7 1.0 copy-start.5
  43.7 1.0 copy-start.8
  44.7 2.8 %copy-start.2 = (bf16[512,512]{1,0:T(8,128)(2,1)S(1)}, bf16[512,512]{1,0:T(8,128)(2,1)}, u32[]{:S(2)}) copy-start(bf16[512,512]{1,0:T(8,128)(2,1)} %lower_ref.3) | copy-start | bytes 1572868
  44.7 2.8 %copy-start.6 = (bf16[1,1,512,512]{3,2,1,0:T(8,128)(2,1)S(1)}, bf16[1,1,512,512]{3,2,1,0:T(8,128)(2,1)}, u32[]{:S(2)}) copy-start(bf16[1,1,512,512]{3,2,1,0:T(8,128)(2,1)} %param.10) | copy-start | bytes 1572868
  47.6 1.0 copy-start.10
  74.3 27.0 %all-to-all-start = ((bf16[16,2,32,512]{3,2,1,0:T(8,128)(2,1)}), bf16[16,2,32,512]{3,2,1,0:T(8,128)(2,1)S(1)}, u32[]{:S(2)}, u32[]{:S(2)}) async-start(bf16[16,2,32,512]{3,2,1,0:T(8,128)(2,1)} %get-tuple-element.13), calls=%async_computation | async-start | bytes 2097152 | tf_op jit(solution)/shard_map/all_to_all | solution.py:118
  101.3 1.0 copy-start.11
  103.1 50.3 %copy-start = (f32[512,512]{1,0:T(8,128)S(1)}, f32[512,512]{1,0:T(8,128)}, u32[]{:S(2)}) copy-start(f32[512,512]{1,0:T(8,128)} %first_diag_ref.1) | copy-start | bytes 3145732
  103.1 50.3 %copy-start.1 = (f32[512,512]{1,0:T(8,128)S(1)}, f32[512,512]{1,0:T(8,128)}, u32[]{:S(2)}) copy-start(f32[512,512]{1,0:T(8,128)} %second_diag_ref.1) | copy-start | bytes 3145732
  103.1 21.5 %all-to-all-start.3 = ((bf16[16,32,512]{2,1,0:T(8,128)(2,1)}), bf16[16,32,512]{2,1,0:T(8,128)(2,1)S(1)}, u32[]{:S(2)}, u32[]{:S(2)}) async-start(bf16[16,32,512]{2,1,0:T(8,128)(2,1)} %broadcast_in_dim.5), calls=%async_computation.3 | async-start | bytes 1048576 | tf_op jit(solution)/shard_map/all_to_all | solution.py:120

commit v2 on v1

v2 whole, which is shorter than its diff:
```python
import functools

import jax
import jax.numpy as jnp
from jax import lax
from jax.experimental import pallas as pl
from jax.experimental.pallas import tpu as pltpu
from jax.sharding import PartitionSpec as P

VMEM_BYTES = 40 * 1024 * 1024


def vmem_spec():
    return pl.BlockSpec(memory_space=pltpu.VMEM)


def smem_spec():
    return pl.BlockSpec(memory_space=pltpu.SMEM)


def call(body, outs, args, scalars, scratch, flops):
    moved = sum(a.size * a.dtype.itemsize for a in args) + sum(o.size * o.dtype.itemsize for o in outs)
    return pl.pallas_call(
        body,
        out_shape=outs,
        in_specs=[smem_spec()] * scalars + [vmem_spec()] * (len(args) - scalars),
        out_specs=[vmem_spec()] * len(outs),
        scratch_shapes=scratch,
        compiler_params=pltpu.CompilerParams(vmem_limit_bytes=VMEM_BYTES),
        cost_estimate=pl.CostEstimate(flops=flops, bytes_accessed=moved, transcendentals=0),
    )(*args)


def dot(a, b):
    return lax.dot_general(a, b, (((1,), (0,)), ((), ())), preferred_element_type=jnp.float32)


def dot_t(a, b):
    return lax.dot_general(a, b, (((0,), (0,)), ((), ())), preferred_element_type=jnp.float32)


def band(where_ref, list_ref, count_ref, sigma_ref, panels, acc_ref):
    member = where_ref[0] % 4
    across = jnp.where(member < 2, 2, -2)
    beside = jnp.where(member % 2 == 0, 1, -1)
    offsets = (0, beside, across, -across, -beside)
    acc_ref[...] = jnp.zeros_like(acc_ref)
    for offset, panel in zip(offsets, panels):
        slot = jnp.int32(0)
        live = jnp.int32(0)
        for s in range(sigma_ref.shape[0]):
            hit = (list_ref[s] == offset) & (s < count_ref[0])
            slot = jnp.where(hit, s, slot)
            live = jnp.where(hit, 1, live)

        @pl.when(live == 1)
        def _(slot=slot, panel=panel):
            acc_ref[...] += dot(sigma_ref[slot], panel[...])


def halves(value, where_ref, scratch_ref, give_ref, keep_ref, index):
    scratch_ref[...] = value
    half = value.shape[0] // 2
    core = where_ref[0] % 2
    keep_ref[index] = scratch_ref[pl.ds(pl.multiple_of(core * half, half), half)]
    give_ref[index] = scratch_ref[pl.ds(pl.multiple_of((1 - core) * half, half), half)].astype(jnp.bfloat16)


def first_kernel(where_ref, list_ref, count_ref, sigma_ref, own, beside, across, far, rest, second_ref,
                 column_ref, give_ref, keep_ref, acc_ref):
    band(where_ref, list_ref, count_ref, sigma_ref, (own, beside, across, far, rest), acc_ref)
    column = (-acc_ref[...]).astype(jnp.bfloat16)
    column_ref[...] = column
    halves(-dot_t(own[...], column), where_ref, acc_ref, give_ref, keep_ref, 0)
    halves(dot_t(column, second_ref[...]), where_ref, acc_ref, give_ref, keep_ref, 1)


def second_kernel(where_ref, list_ref, count_ref, sigma_ref, own, beside, across, far, rest, column_first_ref,
                  lower_ref, column_ref, give_ref, keep_ref, acc_ref):
    band(where_ref, list_ref, count_ref, sigma_ref, (own, beside, across, far, rest), acc_ref)
    total = acc_ref[...] + dot(column_first_ref[...], lower_ref[...])
    column = (-total).astype(jnp.bfloat16)
    column_ref[...] = column
    halves(-dot_t(own[...], column), where_ref, acc_ref, give_ref, keep_ref, 0)


def split(value):
    high = value.astype(jnp.bfloat16)
    low = (value - high.astype(jnp.float32)).astype(jnp.bfloat16)
    return high, low


def place(where_ref, mine_ref, other_ref, index, out_ref):
    half = mine_ref.shape[1]
    core = where_ref[0] % 2
    out_ref[pl.ds(pl.multiple_of(core * half, half), half)] = mine_ref[index].astype(jnp.float32)
    out_ref[pl.ds(pl.multiple_of((1 - core) * half, half), half)] = other_ref[index].astype(jnp.float32)


def link_kernel(where_ref, mine_ref, other_ref, lower_ref, first_diag_ref, second_diag_ref,
                first_ref, link_ref, base_ref, sum_ref):
    lower = lower_ref[...]
    place(where_ref, mine_ref, other_ref, 0, sum_ref)
    block_first = first_diag_ref[...] + sum_ref[...]
    first_ref[...] = block_first
    place(where_ref, mine_ref, other_ref, 1, sum_ref)
    high, low = split(block_first)
    link = dot(high, lower) + dot(low, lower) + sum_ref[...]
    link_ref[...] = -link
    high, low = split(link)
    base_ref[...] = second_diag_ref[...] + dot_t(lower, high) + dot_t(lower, low)


def last_kernel(where_ref, mine_ref, other_ref, base_ref, second_ref):
    place(where_ref, mine_ref, other_ref, 0, second_ref)
    second_ref[...] += base_ref[...]


def swapped(value, bit, devices):
    return lax.ppermute(value, "row", [(i, i ^ bit) for i in range(devices)])


def far_of(across, devices):
    hops = [(i, i + 4 if i % 4 < 2 else i - 4) for i in range(devices)]
    return lax.ppermute(across, "row", [(a, b) for a, b in hops if 0 <= b < devices])


def rest_of(across, far, member, devices):
    give_across = (member == 0) | (member == 3)
    return swapped(jnp.where(give_across, across, far), 1, devices)


def summed(give, keep, position, devices):
    total = keep + swapped(give, 1, devices).astype(jnp.float32)
    bits = [2 ** b for b in range(1, devices.bit_length() - 1)]
    for bit in bits:
        k, rows, width = total.shape
        pair = total.reshape((k, 2, rows // 2, width))
        mine = (position // bit) % 2
        give = lax.dynamic_index_in_dim(pair, 1 - mine, 1, keepdims=False).astype(jnp.bfloat16)
        keep = lax.dynamic_index_in_dim(pair, mine, 1, keepdims=False)
        total = keep + swapped(give, bit, devices).astype(jnp.float32)
    gathered = total.astype(jnp.bfloat16)
    for bit in bits[::-1]:
        other = swapped(gathered, bit, devices)
        mine = (position // bit) % 2
        low = jnp.where(mine == 0, gathered, other)
        high = jnp.where(mine == 0, other, gathered)
        gathered = jnp.concatenate([low, high], axis=1)
    return gathered, swapped(gathered, 1, devices)


def shards(sigma_blocks, first_panel, second_panel, lower_panel, first_diag, second_diag, task_list, task_count):
    devices = lax.axis_size("row")
    position = lax.axis_index("row").astype(jnp.int32)
    member = position % 4
    slots, size, width = sigma_blocks.shape[-3:]
    sigma = sigma_blocks.reshape((slots, size, width))
    first = first_panel.reshape((size, width))
    second = second_panel.reshape((size, width))
    where = position.reshape((1,))
    listed = task_list.reshape((slots,))
    count = task_count.reshape((1,))
    one = 2 * size * size * width
    half = size // 2
    narrow = jax.ShapeDtypeStruct((size, width), jnp.bfloat16)
    wide = jax.ShapeDtypeStruct((size, width), jnp.float32)
    scratch = [pltpu.VMEM((size, width), jnp.float32)]

    def parts(k):
        return [jax.ShapeDtypeStruct((k, half, width), t) for t in (jnp.bfloat16, jnp.float32)]

    across = swapped(first, 2, devices)
    beside = swapped(first, 1, devices)
    across, later = lax.optimization_barrier((across, second))
    far = far_of(across, devices)
    second_across = swapped(later, 2, devices)
    second_beside = swapped(later, 1, devices)
    rest = rest_of(across, far, member, devices)
    second_far = far_of(second_across, devices)
    second_rest = rest_of(second_across, second_far, member, devices)
    column_first, give, keep = call(
        first_kernel,
        [narrow] + parts(2),
        [where, listed, count, sigma, first, beside, across, far, rest, second],
        3,
        scratch,
        7 * one,
    )
    column_second, second_give, second_keep = call(
        second_kernel,
        [narrow] + parts(1),
        [where, listed, count, sigma, second, second_beside, second_across, second_far, second_rest,
         column_first, lower_panel],
        3,
        scratch,
        7 * one,
    )
    mine, other = summed(give, keep, position, devices)
    second_mine, second_other = summed(second_give, second_keep, position, devices)
    block_first, block_link, base = call(
        link_kernel, [wide] * 3, [where, mine, other, lower_panel, first_diag, second_diag], 1, scratch, 4 * one
    )
    (block_second,) = call(last_kernel, [wide], [where, second_mine, second_other, base], 1, [], size * width)
    shape = first_panel.shape
    return column_first.reshape(shape), block_first, block_link, column_second.reshape(shape), block_second


def solution(mesh):
    return jax.shard_map(
        shards,
        mesh=mesh,
        in_specs=(
            P("groups", "row", None, None, None),
            P("groups", "row", None, None),
            P("groups", "row", None, None),
            P("groups", None),
            P("groups", None),
            P("groups", None),
            P("groups", "row", None),
            P("groups", "row"),
        ),
        out_specs=(
            P("groups", "row", None, None),
            P("groups", None),
            P("groups", None),
            P("groups", "row", None, None),
            P("groups", None),
        ),
        check_vma=False,
    )
```

time: 157 us -> 105 us (0.67)
  blocking collectives: 51.6 us -> 0 us
  waiting for transfers between devices: 64.6 us -> 45.2 us
  starting transfers between devices: 22.8 us -> 38.7 us
  local copies, waits for them, and re-layouts: 5.85 us -> 7.91 us
    all_to_all x2 -> x0, blocking collectives: 51.6 us -> none  [the longest x1 28.7 us: summed(): lax.all_to_all(jnp.broadcast_to(total[None], (devices,) + total.shape), '...]
    all_to_all x2 -> x0, waiting for transfers between devices: 35.9 us -> none  [the longest x1 22.9 us: summed(): mine = lax.all_to_all(parts, 'row', 0, 0, tiled=True)]
    ppermute x8 -> x24, starting transfers between devices: 11.7 us -> 38.7 us  [the longest x22 31.8 us: swapped(): return lax.ppermute(value, 'row', [(i, i ^ bit) for i in range(devices)])]
    ppermute x8 -> x24, waiting for transfers between devices: 28.7 us -> 45.2 us  [the longest x22 36.9 us: swapped(): return lax.ppermute(value, 'row', [(i, i ^ bit) for i in range(devices)])]
    all_to_all x2 -> x0, starting transfers between devices: 11.1 us -> none  [the longest x1 7 us: summed(): lax.all_to_all(jnp.broadcast_to(total[None], (devices,) + total.shape), '...]
    unnamed x24 -> x26, local copies, waits for them, and re-layouts: 4.9 us -> 7.76 us
    pallas_call x3 -> x4, Pallas kernels: 8.01 us -> 9.09 us  [call(): pl.pallas_call(body, out_shape=outs, in_specs=[smem_spec()] * scalars + [...]
  transfers between devices with their start and end apart: 10 -> 24, of which waited for: 5 -> 13; matrix products, arithmetic and copies ran while one was open for 1% -> 2% of each run, Pallas kernels for 2% -> 8%
where the time goes in v2:
time: 105 us; the launch traced here: 104 us
  waiting for transfers between devices  45.2 us (43%)
  starting transfers between devices  38.7 us (37%)
  Pallas kernels  9.09 us (9%)
  local copies, waits for them, and re-layouts  7.91 us (8%)
  between operations  1.78 us (2%)
  other arithmetic  1.64 us (2%)
    ppermute x22, waiting for transfers between devices, swapped(): return lax.ppermute(value, 'row', [(i, i ^ bit) for i in range(devices)])  36.9 us
    ppermute x22, starting transfers between devices, swapped(): return lax.ppermute(value, 'row', [(i, i ^ bit) for i in range(devices)])  31.8 us
    pallas_call x4, Pallas kernels, call(): pl.pallas_call(body, out_shape=outs, in_specs=[smem_spec()] * scalars + [...  9.09 us
    ppermute x2, waiting for transfers between devices, far_of(): lax.ppermute(across, 'row', [(a, b) for a, b in hops if 0 <= b < devices])  8.31 us
    unnamed x26, local copies, waits for them, and re-layouts  7.76 us
    ppermute x2, starting transfers between devices, far_of(): lax.ppermute(across, 'row', [(a, b) for a, b in hops if 0 <= b < devices])  6.93 us
  transfers between devices with their start and end apart: 24, of which 13 were waited for; matrix products, arithmetic and copies ran while one was open for 2% of the time, Pallas kernels for 8%

profile of v2, /device:TPU:0, one launch (start us, length us, event | category | flops | bytes accessed | tf_op | source)
XLA Modules:
  0.0 104.3 jit_solution(806714134189852088)
XLA Ops:
  0.6 3.0 %collective-permute-start.1 = (bf16[512,512]{1,0:T(8,128)(2,1)}, bf16[512,512]{1,0:T(8,128)(2,1)S(1)}, u32[]{:S(2)}, u32[]{:S(2)}) collective-permute-start(bf16[512,512]{1,0:T(8,128)(2,1)} %bitcast.54), channel_id=1, source_target_pairs={{0,2},{1,3},{2,0},{3,1},{4,6},{5,7},{6,4},{7,5},{8,10},{9,11},{10,... | collective-permute-start | bytes 1572872 | tf_op jit(solution)/shard_map/ppermute | solution.py:120
  3.6 12.1 %collective-permute-done.1.across = bf16[512,512]{1,0:T(8,128)(2,1)S(1)} collective-permute-done((bf16[512,512]{1,0:T(8,128)(2,1)}, bf16[512,512]{1,0:T(8,128)(2,1)S(1)}, u32[]{:S(2)}, u32[]{:S(2)}) %collective-permute-start.1) | collective-permute-done | bytes 524320 | tf_op jit(solution)/shard_map/ppermute | solution.py:120
  15.8 1.7 %collective-permute-start.13 = (bf16[512,512]{1,0:T(8,128)(2,1)}, bf16[512,512]{1,0:T(8,128)(2,1)S(1)}, u32[]{:S(2)}, u32[]{:S(2)}) collective-permute-start(bf16[512,512]{1,0:T(8,128)(2,1)} %bitcast.57), channel_id=1, source_target_pairs={{0,2},{1,3},{2,0},{3,1},{4,6},{5,7},{6,4},{7,5},{8,10},{9,11},{10,... | collective-permute-start | bytes 1572872 | tf_op jit(solution)/shard_map/ppermute | solution.py:120
  17.5 3.5 %collective-permute-start.2 = (bf16[512,512]{1,0:T(8,128)(2,1)S(1)}, bf16[512,512]{1,0:T(8,128)(2,1)S(1)}, u32[]{:S(2)}, u32[]{:S(2)}) collective-permute-start(bf16[512,512]{1,0:T(8,128)(2,1)S(1)} %collective-permute-done.1.across), channel_id=1, source_target_pairs={{0,4},{1,5},{4,8},{5,9},{6,2},{7,3},{8,12},{9,13},{10,6},{11,7},{1... | collective-permute-start | bytes 1572872 | tf_op jit(solution)/shard_map/ppermute | solution.py:125
  21.1 8.0 %collective-permute-done.13.across = bf16[512,512]{1,0:T(8,128)(2,1)S(1)} collective-permute-done((bf16[512,512]{1,0:T(8,128)(2,1)}, bf16[512,512]{1,0:T(8,128)(2,1)S(1)}, u32[]{:S(2)}, u32[]{:S(2)}) %collective-permute-start.13) | collective-permute-done | bytes 524320 | tf_op jit(solution)/shard_map/ppermute | solution.py:120
  29.1 3.4 %collective-permute-start.14 = (bf16[512,512]{1,0:T(8,128)(2,1)S(1)}, bf16[512,512]{1,0:T(8,128)(2,1)S(1)}, u32[]{:S(2)}, u32[]{:S(2)}) collective-permute-start(bf16[512,512]{1,0:T(8,128)(2,1)S(1)} %collective-permute-done.13.across), channel_id=1, source_target_pairs={{0,4},{1,5},{4,8},{5,9},{6,2},{7,3},{8,12},{9,13},{10,6},{11,7},{1... | collective-permute-start | bytes 1572872 | tf_op jit(solution)/shard_map/ppermute | solution.py:125
  33.9 8.3 %collective-permute-done.14.far = bf16[512,512]{1,0:T(8,128)(2,1)S(1)} collective-permute-done((bf16[512,512]{1,0:T(8,128)(2,1)S(1)}, bf16[512,512]{1,0:T(8,128)(2,1)S(1)}, u32[]{:S(2)}, u32[]{:S(2)}) %collective-permute-start.14) | collective-permute-done | bytes 524320 | tf_op jit(solution)/shard_map/ppermute | solution.py:125
  45.0 1.0 copy-done.10
  46.0 2.8 %shard_map.119 = (bf16[512,512]{1,0:T(8,128)(2,1)}, bf16[2,256,512]{2,1,0:T(8,128)(2,1)}, f32[2,256,512]{2,1,0:T(8,128)S(1)}) custom-call(s32[1]{0:T(128)} %bitcast.where_ref, s32[5]{0:T(128)S(1)} %bitcast.61, s32[1]{0:T(128)} %bitcast.50.count_ref, bf16[5,512,512]{2,1,0:T(8,128)(2,1)S(1)} %bitcast.52, bf16[512,512]{1,0:T(8,128)(2,1)S(1)} %bitcast.56, ...), custom_call_target="tpu_custom_call" | custom-call | flops 1879048192 | bytes 7864348 | tf_op jit(solution)/shard_map/pallas_call | solution.py:23
  48.8 1.4 %collective-permute-start.4 = (bf16[2,256,512]{2,1,0:T(8,128)(2,1)}, bf16[2,256,512]{2,1,0:T(8,128)(2,1)S(1)}, u32[]{:S(2)}, u32[]{:S(2)}) collective-permute-start(bf16[2,256,512]{2,1,0:T(8,128)(2,1)} %get-tuple-element.19), channel_id=1, source_target_pairs={{0,1},{1,0},{2,3},{3,2},{4,5},{5,4},{6,7},{7,6},{8,9},{9,8},{10,11... | collective-permute-start | bytes 1572872 | tf_op jit(solution)/shard_map/ppermute | solution.py:120
  50.2 1.7 %copy-done.1 = bf16[1,1,5,512,512]{4,3,2,1,0:T(8,128)(2,1)S(1)} copy-done((bf16[1,1,5,512,512]{4,3,2,1,0:T(8,128)(2,1)S(1)}, bf16[1,1,5,512,512]{4,3,2,1,0:T(8,128)(2,1)}, u32[]{:S(2)}) %copy-start.1) | copy-done | bytes 2621464
  53.0 1.0 copy-done.7
  54.0 1.0 copy-done.12
  55.0 3.0 %shard_map.121 = (bf16[512,512]{1,0:T(8,128)(2,1)}, bf16[1,256,512]{2,1,0:T(8,128)(2,1)S(1)}, f32[1,256,512]{2,1,0:T(8,128)S(1)}) custom-call(s32[1]{0:T(128)} %bitcast.where_ref, s32[5]{0:T(128)S(1)} %bitcast.62, s32[1]{0:T(128)} %bitcast.51.count_ref, bf16[5,512,512]{2,1,0:T(8,128)(2,1)S(1)} %bitcast.53, bf16[512,512]{1,0:T(8,128)(2,1)S(1)} %bitcast.60, ...), custom_call_target="tpu_custom_call" | custom-call | flops 1879048192 | bytes 7602204 | tf_op jit(solution)/shard_map/pallas_call | solution.py:23
  59.1 3.0 %collective-permute-start.5 = (bf16[2,128,512]{2,1,0:T(8,128)(2,1)S(1)}, bf16[2,128,512]{2,1,0:T(8,128)(2,1)S(1)}, u32[]{:S(2)}, u32[]{:S(2)}) collective-permute-start(bf16[2,128,512]{2,1,0:T(8,128)(2,1)S(1)} %fusion), channel_id=1, source_target_pairs={{0,2},{1,3},{2,0},{3,1},{4,6},{5,7},{6,4},{7,5},{8,10},{9,11},{10,... | collective-permute-start | bytes 786440 | tf_op jit(solution)/shard_map/ppermute | solution.py:120
  63.2 6.0 %collective-permute-done.5 = bf16[2,128,512]{2,1,0:T(8,128)(2,1)S(1)} collective-permute-done((bf16[2,128,512]{2,1,0:T(8,128)(2,1)S(1)}, bf16[2,128,512]{2,1,0:T(8,128)(2,1)S(1)}, u32[]{:S(2)}, u32[]{:S(2)}) %collective-permute-start.5) | collective-permute-done | bytes 262176 | tf_op jit(solution)/shard_map/ppermute | solution.py:120
  69.3 2.5 %collective-permute-start.6 = (bf16[2,64,512]{2,1,0:T(8,128)(2,1)S(1)}, bf16[2,64,512]{2,1,0:T(8,128)(2,1)S(1)}, u32[]{:S(2)}, u32[]{:S(2)}) collective-permute-start(bf16[2,64,512]{2,1,0:T(8,128)(2,1)S(1)} %fusion.1), channel_id=1, source_target_pairs={{0,4},{1,5},{2,6},{3,7},{4,0},{5,1},{6,2},{7,3},{8,12},{9,13},{10,... | collective-permute-start | bytes 393224 | tf_op jit(solution)/shard_map/ppermute | solution.py:120
  71.9 2.1 %collective-permute-start.18 = (bf16[1,64,512]{2,1,0:T(8,128)(2,1)S(1)}, bf16[1,64,512]{2,1,0:T(8,128)(2,1)S(1)}, u32[]{:S(2)}, u32[]{:S(2)}) collective-permute-start(bf16[1,64,512]{2,1,0:T(8,128)(2,1)S(1)} %fusion.4), channel_id=1, source_target_pairs={{0,4},{1,5},{2,6},{3,7},{4,0},{5,1},{6,2},{7,3},{8,12},{9,13},{10,... | collective-permute-start | bytes 196616 | tf_op jit(solution)/shard_map/ppermute | solution.py:120
  73.9 1.4 %collective-permute-done.6 = bf16[2,64,512]{2,1,0:T(8,128)(2,1)S(1)} collective-permute-done((bf16[2,64,512]{2,1,0:T(8,128)(2,1)S(1)}, bf16[2,64,512]{2,1,0:T(8,128)(2,1)S(1)}, u32[]{:S(2)}, u32[]{:S(2)}) %collective-permute-start.6) | collective-permute-done | bytes 131104 | tf_op jit(solution)/shard_map/ppermute | solution.py:120
  75.3 3.3 %collective-permute-start.7 = (bf16[2,32,512]{2,1,0:T(8,128)(2,1)S(1)}, bf16[2,32,512]{2,1,0:T(8,128)(2,1)S(1)}, u32[]{:S(2)}, u32[]{:S(2)}) collective-permute-start(bf16[2,32,512]{2,1,0:T(8,128)(2,1)S(1)} %fusion.5), channel_id=1, source_target_pairs={{0,8},{1,9},{2,10},{3,11},{4,12},{5,13},{6,14},{7,15},{8,0},{9,1},... | collective-permute-start | bytes 196616 | tf_op jit(solution)/shard_map/ppermute | solution.py:120
  78.7 1.8 %collective-permute-start.19 = (bf16[1,32,512]{2,1,0:T(8,128)(2,1)S(1)}, bf16[1,32,512]{2,1,0:T(8,128)(2,1)S(1)}, u32[]{:S(2)}, u32[]{:S(2)}) collective-permute-start(bf16[1,32,512]{2,1,0:T(8,128)(2,1)S(1)} %fusion.7), channel_id=1, source_target_pairs={{0,8},{1,9},{2,10},{3,11},{4,12},{5,13},{6,14},{7,15},{8,0},{9,1},... | collective-permute-start | bytes 98312 | tf_op jit(solution)/shard_map/ppermute | solution.py:120
  81.3 2.6 %collective-permute-start.8 = (bf16[2,32,512]{2,1,0:T(8,128)(2,1)S(1)}, bf16[2,32,512]{2,1,0:T(8,128)(2,1)S(1)}, u32[]{:S(2)}, u32[]{:S(2)}) collective-permute-start(bf16[2,32,512]{2,1,0:T(8,128)(2,1)S(1)} %fusion.3), channel_id=1, source_target_pairs={{0,8},{1,9},{2,10},{3,11},{4,12},{5,13},{6,14},{7,15},{8,0},{9,1},... | collective-permute-start | bytes 196616 | tf_op jit(solution)/shard_map/ppermute | solution.py:120
  85.5 1.2 %collective-permute-done.8 = bf16[2,32,512]{2,1,0:T(8,128)(2,1)S(1)} collective-permute-done((bf16[2,32,512]{2,1,0:T(8,128)(2,1)S(1)}, bf16[2,32,512]{2,1,0:T(8,128)(2,1)S(1)}, u32[]{:S(2)}, u32[]{:S(2)}) %collective-permute-start.8) | collective-permute-done | bytes 65568 | tf_op jit(solution)/shard_map/ppermute | solution.py:120
  86.7 1.5 %collective-permute-start.9 = (bf16[2,64,512]{2,1,0:T(8,128)(2,1)S(1)}, bf16[2,64,512]{2,1,0:T(8,128)(2,1)S(1)}, u32[]{:S(2)}, u32[]{:S(2)}) collective-permute-start(bf16[2,64,512]{2,1,0:T(8,128)(2,1)S(1)} %pad_maximum_fusion.3), channel_id=1, source_target_pairs={{0,4},{1,5},{2,6},{3,7},{4,0},{5,1},{6,2},{7,3},{8,12},{9,13},{10,... | collective-permute-start | bytes 393224 | tf_op jit(solution)/shard_map/ppermute | solution.py:120
  88.2 1.2 %collective-permute-done.20 = bf16[1,32,512]{2,1,0:T(8,128)(2,1)S(1)} collective-permute-done((bf16[1,32,512]{2,1,0:T(8,128)(2,1)S(1)}, bf16[1,32,512]{2,1,0:T(8,128)(2,1)S(1)}, u32[]{:S(2)}, u32[]{:S(2)}) %collective-permute-start.20) | collective-permute-done | bytes 32800 | tf_op jit(solution)/shard_map/ppermute | solution.py:120
  89.4 1.5 %collective-permute-start.21 = (bf16[1,64,512]{2,1,0:T(8,128)(2,1)S(1)}, bf16[1,64,512]{2,1,0:T(8,128)(2,1)S(1)}, u32[]{:S(2)}, u32[]{:S(2)}) collective-permute-start(bf16[1,64,512]{2,1,0:T(8,128)(2,1)S(1)} %pad_maximum_fusion.5), channel_id=1, source_target_pairs={{0,4},{1,5},{2,6},{3,7},{4,0},{5,1},{6,2},{7,3},{8,12},{9,13},{10,... | collective-permute-start | bytes 196616 | tf_op jit(solution)/shard_map/ppermute | solution.py:120
  91.8 2.7 %collective-permute-start.10 = (bf16[2,128,512]{2,1,0:T(8,128)(2,1)S(1)}, bf16[2,128,512]{2,1,0:T(8,128)(2,1)S(1)}, u32[]{:S(2)}, u32[]{:S(2)}) collective-permute-start(bf16[2,128,512]{2,1,0:T(8,128)(2,1)S(1)} %pad_maximum_fusion.1), channel_id=1, source_target_pairs={{0,2},{1,3},{2,0},{3,1},{4,6},{5,7},{6,4},{7,5},{8,10},{9,11},{10,... | collective-permute-start | bytes 786440 | tf_op jit(solution)/shard_map/ppermute | solution.py:120
  94.6 1.3 %collective-permute-start.22 = (bf16[1,128,512]{2,1,0:T(8,128)(2,1)S(1)}, bf16[1,128,512]{2,1,0:T(8,128)(2,1)S(1)}, u32[]{:S(2)}, u32[]{:S(2)}) collective-permute-start(bf16[1,128,512]{2,1,0:T(8,128)(2,1)S(1)} %pad_maximum_fusion.4), channel_id=1, source_target_pairs={{0,2},{1,3},{2,0},{3,1},{4,6},{5,7},{6,4},{7,5},{8,10},{9,11},{10,... | collective-permute-start | bytes 393224 | tf_op jit(solution)/shard_map/ppermute | solution.py:120
  95.9 3.0 %collective-permute-done.10 = bf16[2,128,512]{2,1,0:T(8,128)(2,1)S(1)} collective-permute-done((bf16[2,128,512]{2,1,0:T(8,128)(2,1)S(1)}, bf16[2,128,512]{2,1,0:T(8,128)(2,1)S(1)}, u32[]{:S(2)}, u32[]{:S(2)}) %collective-permute-start.10) | collective-permute-done | bytes 262176 | tf_op jit(solution)/shard_map/ppermute | solution.py:120
  99.1 1.2 %collective-permute-done.22 = bf16[1,128,512]{2,1,0:T(8,128)(2,1)S(1)} collective-permute-done((bf16[1,128,512]{2,1,0:T(8,128)(2,1)S(1)}, bf16[1,128,512]{2,1,0:T(8,128)(2,1)S(1)}, u32[]{:S(2)}, u32[]{:S(2)}) %collective-permute-start.22) | collective-permute-done | bytes 131104 | tf_op jit(solution)/shard_map/ppermute | solution.py:120
  101.0 2.1 %shard_map.120 = (f32[512,512]{1,0:T(8,128)}, f32[512,512]{1,0:T(8,128)}, f32[512,512]{1,0:T(8,128)S(1)}) custom-call(s32[1]{0:T(128)} %bitcast.where_ref, bf16[2,256,512]{2,1,0:T(8,128)(2,1)S(1)} %pad_maximum_fusion.mine_ref, bf16[2,256,512]{2,1,0:T(8,128)(2,1)S(1)} %collective-permute-done.11.other_ref, bf16[512,512]{1,0:T(8,128)(2,1)S(1)} %copy-done.8, ...), custom_call_target="tpu_custom_call" | custom-call | flops 1073741824 | bytes 6815748 | tf_op jit(solution)/shard_map/pallas_call | solution.py:23
  103.2 1.2 %shard_map.122 = f32[512,512]{1,0:T(8,128)} custom-call(s32[1]{0:T(128)} %bitcast.where_ref, bf16[1,256,512]{2,1,0:T(8,128)(2,1)S(1)} %pad_maximum_fusion.2.mine_ref, bf16[1,256,512]{2,1,0:T(8,128)(2,1)S(1)} %collective-permute-done.23.other_ref, f32[512,512]{1,0:T(8,128)S(1)} %get-tuple-element.26.base_ref), custom_call_target="tpu_custom_call" | custom-call | flops 262144 | bytes 2621444 | tf_op jit(solution)/shard_map/pallas_call | solution.py:23
  (74 shorter events, 11.0 us)
Async XLA Ops:
  0.6 43.3 %copy-start.11 = (s32[1,1,5]{2,1,0:T(1,128)S(1)}, s32[1,1,5]{2,1,0:T(1,128)}, u32[]{:S(2)}) copy-start(s32[1,1,5]{2,1,0:T(1,128)} %param.14) | copy-start | bytes 64
  0.6 15.1 %collective-permute-start.1 = (bf16[512,512]{1,0:T(8,128)(2,1)}, bf16[512,512]{1,0:T(8,128)(2,1)S(1)}, u32[]{:S(2)}, u32[]{:S(2)}) collective-permute-start(bf16[512,512]{1,0:T(8,128)(2,1)} %bitcast.54), channel_id=1, source_target_pairs={{0,2},{1,3},{2,0},{3,1},{4,6},{5,7},{6,4},{7,5},{8,10},{9,11},{10,... | collective-permute-start | bytes 1572872 | tf_op jit(solution)/shard_map/ppermute | solution.py:120
  15.8 13.3 %collective-permute-start.13 = (bf16[512,512]{1,0:T(8,128)(2,1)}, bf16[512,512]{1,0:T(8,128)(2,1)S(1)}, u32[]{:S(2)}, u32[]{:S(2)}) collective-permute-start(bf16[512,512]{1,0:T(8,128)(2,1)} %bitcast.57), channel_id=1, source_target_pairs={{0,2},{1,3},{2,0},{3,1},{4,6},{5,7},{6,4},{7,5},{8,10},{9,11},{10,... | collective-permute-start | bytes 1572872 | tf_op jit(solution)/shard_map/ppermute | solution.py:120
  17.5 15.0 %collective-permute-start.2 = (bf16[512,512]{1,0:T(8,128)(2,1)S(1)}, bf16[512,512]{1,0:T(8,128)(2,1)S(1)}, u32[]{:S(2)}, u32[]{:S(2)}) collective-permute-start(bf16[512,512]{1,0:T(8,128)(2,1)S(1)} %collective-permute-done.1.across), channel_id=1, source_target_pairs={{0,4},{1,5},{4,8},{5,9},{6,2},{7,3},{8,12},{9,13},{10,6},{11,7},{1... | collective-permute-start | bytes 1572872 | tf_op jit(solution)/shard_map/ppermute | solution.py:125
  21.0 22.1 %collective-permute-start = (bf16[512,512]{1,0:T(8,128)(2,1)}, bf16[512,512]{1,0:T(8,128)(2,1)S(1)}, u32[]{:S(2)}, u32[]{:S(2)}) collective-permute-start(bf16[512,512]{1,0:T(8,128)(2,1)} %bitcast.55), channel_id=1, source_target_pairs={{0,1},{1,0},{2,3},{3,2},{4,5},{5,4},{6,7},{7,6},{8,9},{9,8},{10,11... | collective-permute-start | bytes 1572872 | tf_op jit(solution)/shard_map/ppermute | solution.py:120
  29.1 13.1 %collective-permute-start.14 = (bf16[512,512]{1,0:T(8,128)(2,1)S(1)}, bf16[512,512]{1,0:T(8,128)(2,1)S(1)}, u32[]{:S(2)}, u32[]{:S(2)}) collective-permute-start(bf16[512,512]{1,0:T(8,128)(2,1)S(1)} %collective-permute-done.13.across), channel_id=1, source_target_pairs={{0,4},{1,5},{4,8},{5,9},{6,2},{7,3},{8,12},{9,13},{10,6},{11,7},{1... | collective-permute-start | bytes 1572872 | tf_op jit(solution)/shard_map/ppermute | solution.py:125
  32.5 11.4 %copy-start = (bf16[1,1,5,512,512]{4,3,2,1,0:T(8,128)(2,1)S(1)}, bf16[1,1,5,512,512]{4,3,2,1,0:T(8,128)(2,1)}, u32[]{:S(2)}) copy-start(bf16[1,1,5,512,512]{4,3,2,1,0:T(8,128)(2,1)} %param.8) | copy-start | bytes 7864324
  32.6 11.4 %copy-start.4 = (bf16[1,1,512,512]{3,2,1,0:T(8,128)(2,1)S(1)}, bf16[1,1,512,512]{3,2,1,0:T(8,128)(2,1)}, u32[]{:S(2)}) copy-start(bf16[1,1,512,512]{3,2,1,0:T(8,128)(2,1)} %param.9) | copy-start | bytes 1572868
  32.6 11.3 %collective-permute-start.3 = (bf16[512,512]{1,0:T(8,128)(2,1)S(1)}, bf16[512,512]{1,0:T(8,128)(2,1)S(1)}, u32[]{:S(2)}, u32[]{:S(2)}) collective-permute-start(bf16[512,512]{1,0:T(8,128)(2,1)S(1)} %broadcast_select_fusion.1), channel_id=1, source_target_pairs={{0,1},{1,0},{2,3},{3,2},{4,5},{5,4},{6,7},{7,6},{8,9},{9,8},{10,11... | collective-permute-start | bytes 1572872 | tf_op jit(solution)/shard_map/ppermute | solution.py:120
  33.5 16.7 %collective-permute-start.12 = (bf16[512,512]{1,0:T(8,128)(2,1)}, bf16[512,512]{1,0:T(8,128)(2,1)}, u32[]{:S(2)}, u32[]{:S(2)}) collective-permute-start(bf16[512,512]{1,0:T(8,128)(2,1)} %bitcast.58), channel_id=1, source_target_pairs={{0,1},{1,0},{2,3},{3,2},{4,5},{5,4},{6,7},{7,6},{8,9},{9,8},{10,11... | collective-permute-start | bytes 1572872 | tf_op jit(solution)/shard_map/ppermute | solution.py:120
  43.1 7.1 %collective-permute-start.15 = (bf16[512,512]{1,0:T(8,128)(2,1)}, bf16[512,512]{1,0:T(8,128)(2,1)}, u32[]{:S(2)}, u32[]{:S(2)}) collective-permute-start(bf16[512,512]{1,0:T(8,128)(2,1)} %broadcast_select_fusion), channel_id=1, source_target_pairs={{0,1},{1,0},{2,3},{3,2},{4,5},{5,4},{6,7},{7,6},{8,9},{9,8},{10,11... | collective-permute-start | bytes 1572872 | tf_op jit(solution)/shard_map/ppermute | solution.py:120
  43.9 1.0 %copy-start.5 = (bf16[1,1,512,512]{3,2,1,0:T(8,128)(2,1)S(1)}, bf16[1,1,512,512]{3,2,1,0:T(8,128)(2,1)}, u32[]{:S(2)}) copy-start(bf16[1,1,512,512]{3,2,1,0:T(8,128)(2,1)} %param.10) | copy-start | bytes 1572868
  48.8 10.1 %collective-permute-start.4 = (bf16[2,256,512]{2,1,0:T(8,128)(2,1)}, bf16[2,256,512]{2,1,0:T(8,128)(2,1)S(1)}, u32[]{:S(2)}, u32[]{:S(2)}) collective-permute-start(bf16[2,256,512]{2,1,0:T(8,128)(2,1)} %get-tuple-element.19), channel_id=1, source_target_pairs={{0,1},{1,0},{2,3},{3,2},{4,5},{5,4},{6,7},{7,6},{8,9},{9,8},{10,11... | collective-permute-start | bytes 1572872 | tf_op jit(solution)/shard_map/ppermute | solution.py:120
  50.2 1.7 %copy-start.1 = (bf16[1,1,5,512,512]{4,3,2,1,0:T(8,128)(2,1)S(1)}, bf16[1,1,5,512,512]{4,3,2,1,0:T(8,128)(2,1)}, u32[]{:S(2)}) copy-start(bf16[1,1,5,512,512]{4,3,2,1,0:T(8,128)(2,1)} %param.8) | copy-start | bytes 7864324
  58.0 4.0 %collective-permute-start.16 = (bf16[1,256,512]{2,1,0:T(8,128)(2,1)S(1)}, bf16[1,256,512]{2,1,0:T(8,128)(2,1)S(1)}, u32[]{:S(2)}, u32[]{:S(2)}) collective-permute-start(bf16[1,256,512]{2,1,0:T(8,128)(2,1)S(1)} %get-tuple-element.25), channel_id=1, source_target_pairs={{0,1},{1,0},{2,3},{3,2},{4,5},{5,4},{6,7},{7,6},{8,9},{9,8},{10,11... | collective-permute-start | bytes 786440 | tf_op jit(solution)/shard_map/ppermute | solution.py:120
  59.1 10.1 %collective-permute-start.5 = (bf16[2,128,512]{2,1,0:T(8,128)(2,1)S(1)}, bf16[2,128,512]{2,1,0:T(8,128)(2,1)S(1)}, u32[]{:S(2)}, u32[]{:S(2)}) collective-permute-start(bf16[2,128,512]{2,1,0:T(8,128)(2,1)S(1)} %fusion), channel_id=1, source_target_pairs={{0,2},{1,3},{2,0},{3,1},{4,6},{5,7},{6,4},{7,5},{8,10},{9,11},{10,... | collective-permute-start | bytes 786440 | tf_op jit(solution)/shard_map/ppermute | solution.py:120
  62.2 9.6 %collective-permute-start.17 = (bf16[1,128,512]{2,1,0:T(8,128)(2,1)S(1)}, bf16[1,128,512]{2,1,0:T(8,128)(2,1)S(1)}, u32[]{:S(2)}, u32[]{:S(2)}) collective-permute-start(bf16[1,128,512]{2,1,0:T(8,128)(2,1)S(1)} %fusion.2), channel_id=1, source_target_pairs={{0,2},{1,3},{2,0},{3,1},{4,6},{5,7},{6,4},{7,5},{8,10},{9,11},{10,... | collective-permute-start | bytes 393224 | tf_op jit(solution)/shard_map/ppermute | solution.py:120
  69.3 6.0 %collective-permute-start.6 = (bf16[2,64,512]{2,1,0:T(8,128)(2,1)S(1)}, bf16[2,64,512]{2,1,0:T(8,128)(2,1)S(1)}, u32[]{:S(2)}, u32[]{:S(2)}) collective-permute-start(bf16[2,64,512]{2,1,0:T(8,128)(2,1)S(1)} %fusion.1), channel_id=1, source_target_pairs={{0,4},{1,5},{2,6},{3,7},{4,0},{5,1},{6,2},{7,3},{8,12},{9,13},{10,... | collective-permute-start | bytes 393224 | tf_op jit(solution)/shard_map/ppermute | solution.py:120
  71.9 6.7 %collective-permute-start.18 = (bf16[1,64,512]{2,1,0:T(8,128)(2,1)S(1)}, bf16[1,64,512]{2,1,0:T(8,128)(2,1)S(1)}, u32[]{:S(2)}, u32[]{:S(2)}) collective-permute-start(bf16[1,64,512]{2,1,0:T(8,128)(2,1)S(1)} %fusion.4), channel_id=1, source_target_pairs={{0,4},{1,5},{2,6},{3,7},{4,0},{5,1},{6,2},{7,3},{8,12},{9,13},{10,... | collective-permute-start | bytes 196616 | tf_op jit(solution)/shard_map/ppermute | solution.py:120
  75.3 5.9 %collective-permute-start.7 = (bf16[2,32,512]{2,1,0:T(8,128)(2,1)S(1)}, bf16[2,32,512]{2,1,0:T(8,128)(2,1)S(1)}, u32[]{:S(2)}, u32[]{:S(2)}) collective-permute-start(bf16[2,32,512]{2,1,0:T(8,128)(2,1)S(1)} %fusion.5), channel_id=1, source_target_pairs={{0,8},{1,9},{2,10},{3,11},{4,12},{5,13},{6,14},{7,15},{8,0},{9,1},... | collective-permute-start | bytes 196616 | tf_op jit(solution)/shard_map/ppermute | solution.py:120
  78.7 5.9 %collective-permute-start.19 = (bf16[1,32,512]{2,1,0:T(8,128)(2,1)S(1)}, bf16[1,32,512]{2,1,0:T(8,128)(2,1)S(1)}, u32[]{:S(2)}, u32[]{:S(2)}) collective-permute-start(bf16[1,32,512]{2,1,0:T(8,128)(2,1)S(1)} %fusion.7), channel_id=1, source_target_pairs={{0,8},{1,9},{2,10},{3,11},{4,12},{5,13},{6,14},{7,15},{8,0},{9,1},... | collective-permute-start | bytes 98312 | tf_op jit(solution)/shard_map/ppermute | solution.py:120
  81.3 5.3 %collective-permute-start.8 = (bf16[2,32,512]{2,1,0:T(8,128)(2,1)S(1)}, bf16[2,32,512]{2,1,0:T(8,128)(2,1)S(1)}, u32[]{:S(2)}, u32[]{:S(2)}) collective-permute-start(bf16[2,32,512]{2,1,0:T(8,128)(2,1)S(1)} %fusion.3), channel_id=1, source_target_pairs={{0,8},{1,9},{2,10},{3,11},{4,12},{5,13},{6,14},{7,15},{8,0},{9,1},... | collective-permute-start | bytes 196616 | tf_op jit(solution)/shard_map/ppermute | solution.py:120
  84.5 4.9 %collective-permute-start.20 = (bf16[1,32,512]{2,1,0:T(8,128)(2,1)S(1)}, bf16[1,32,512]{2,1,0:T(8,128)(2,1)S(1)}, u32[]{:S(2)}, u32[]{:S(2)}) collective-permute-start(bf16[1,32,512]{2,1,0:T(8,128)(2,1)S(1)} %fusion.6), channel_id=1, source_target_pairs={{0,8},{1,9},{2,10},{3,11},{4,12},{5,13},{6,14},{7,15},{8,0},{9,1},... | collective-permute-start | bytes 98312 | tf_op jit(solution)/shard_map/ppermute | solution.py:120
  86.6 14.4 %copy-start.2 = (f32[512,512]{1,0:T(8,128)S(1)}, f32[512,512]{1,0:T(8,128)}, u32[]{:S(2)}) copy-start(f32[512,512]{1,0:T(8,128)} %first_diag_ref.1) | copy-start | bytes 3145732
  86.7 14.4 %copy-start.3 = (f32[512,512]{1,0:T(8,128)S(1)}, f32[512,512]{1,0:T(8,128)}, u32[]{:S(2)}) copy-start(f32[512,512]{1,0:T(8,128)} %second_diag_ref.1) | copy-start | bytes 3145732
  86.7 14.4 %copy-start.8 = (bf16[512,512]{1,0:T(8,128)(2,1)S(1)}, bf16[512,512]{1,0:T(8,128)(2,1)}, u32[]{:S(2)}) copy-start(bf16[512,512]{1,0:T(8,128)(2,1)} %lower_ref.3) | copy-start | bytes 1572868
  86.7 5.0 %collective-permute-start.9 = (bf16[2,64,512]{2,1,0:T(8,128)(2,1)S(1)}, bf16[2,64,512]{2,1,0:T(8,128)(2,1)S(1)}, u32[]{:S(2)}, u32[]{:S(2)}) collective-permute-start(bf16[2,64,512]{2,1,0:T(8,128)(2,1)S(1)} %pad_maximum_fusion.3), channel_id=1, source_target_pairs={{0,4},{1,5},{2,6},{3,7},{4,0},{5,1},{6,2},{7,3},{8,12},{9,13},{10,... | collective-permute-start | bytes 393224 | tf_op jit(solution)/shard_map/ppermute | solution.py:120
  89.4 5.1 %collective-permute-start.21 = (bf16[1,64,512]{2,1,0:T(8,128)(2,1)S(1)}, bf16[1,64,512]{2,1,0:T(8,128)(2,1)S(1)}, u32[]{:S(2)}, u32[]{:S(2)}) collective-permute-start(bf16[1,64,512]{2,1,0:T(8,128)(2,1)S(1)} %pad_maximum_fusion.5), channel_id=1, source_target_pairs={{0,4},{1,5},{2,6},{3,7},{4,0},{5,1},{6,2},{7,3},{8,12},{9,13},{10,... | collective-permute-start | bytes 196616 | tf_op jit(solution)/shard_map/ppermute | solution.py:120
  91.8 7.1 %collective-permute-start.10 = (bf16[2,128,512]{2,1,0:T(8,128)(2,1)S(1)}, bf16[2,128,512]{2,1,0:T(8,128)(2,1)S(1)}, u32[]{:S(2)}, u32[]{:S(2)}) collective-permute-start(bf16[2,128,512]{2,1,0:T(8,128)(2,1)S(1)} %pad_maximum_fusion.1), channel_id=1, source_target_pairs={{0,2},{1,3},{2,0},{3,1},{4,6},{5,7},{6,4},{7,5},{8,10},{9,11},{10,... | collective-permute-start | bytes 786440 | tf_op jit(solution)/shard_map/ppermute | solution.py:120
  94.6 5.7 %collective-permute-start.22 = (bf16[1,128,512]{2,1,0:T(8,128)(2,1)S(1)}, bf16[1,128,512]{2,1,0:T(8,128)(2,1)S(1)}, u32[]{:S(2)}, u32[]{:S(2)}) collective-permute-start(bf16[1,128,512]{2,1,0:T(8,128)(2,1)S(1)} %pad_maximum_fusion.4), channel_id=1, source_target_pairs={{0,2},{1,3},{2,0},{3,1},{4,6},{5,7},{6,4},{7,5},{8,10},{9,11},{10,... | collective-permute-start | bytes 393224 | tf_op jit(solution)/shard_map/ppermute | solution.py:120
  99.0 2.0 %collective-permute-start.11 = (bf16[2,256,512]{2,1,0:T(8,128)(2,1)S(1)}, bf16[2,256,512]{2,1,0:T(8,128)(2,1)S(1)}, u32[]{:S(2)}, u32[]{:S(2)}) collective-permute-start(bf16[2,256,512]{2,1,0:T(8,128)(2,1)S(1)} %pad_maximum_fusion.mine_ref), channel_id=1, source_target_pairs={{0,1},{1,0},{2,3},{3,2},{4,5},{5,4},{6,7},{7,6},{8,9},{9,8},{10,11... | collective-permute-start | bytes 1572872 | tf_op jit(solution)/shard_map/ppermute | solution.py:120
  100.4 2.8 %collective-permute-start.23 = (bf16[1,256,512]{2,1,0:T(8,128)(2,1)S(1)}, bf16[1,256,512]{2,1,0:T(8,128)(2,1)S(1)}, u32[]{:S(2)}, u32[]{:S(2)}) collective-permute-start(bf16[1,256,512]{2,1,0:T(8,128)(2,1)S(1)} %pad_maximum_fusion.2.mine_ref), channel_id=1, source_target_pairs={{0,1},{1,0},{2,3},{3,2},{4,5},{5,4},{6,7},{7,6},{8,9},{9,8},{10,11... | collective-permute-start | bytes 786440 | tf_op jit(solution)/shard_map/ppermute | solution.py:120
  (5 other events, 5.0 us)

commit v3 on v2

--- a/solution.py
+++ b/solution.py
@@ -7,7 +7,7 @@
 from jax.experimental.pallas import tpu as pltpu
 from jax.sharding import PartitionSpec as P
 
-VMEM_BYTES = 40 * 1024 * 1024
+VMEM_BYTES = 24 * 1024 * 1024
 
 
 def vmem_spec():
@@ -18,14 +18,14 @@
     return pl.BlockSpec(memory_space=pltpu.SMEM)
 
 
-def call(body, outs, args, scalars, scratch, flops):
+def call(body, outs, args, scalars, flops, scratch=()):
     moved = sum(a.size * a.dtype.itemsize for a in args) + sum(o.size * o.dtype.itemsize for o in outs)
     return pl.pallas_call(
         body,
         out_shape=outs,
         in_specs=[smem_spec()] * scalars + [vmem_spec()] * (len(args) - scalars),
         out_specs=[vmem_spec()] * len(outs),
-        scratch_shapes=scratch,
+        scratch_shapes=list(scratch),
         compiler_params=pltpu.CompilerParams(vmem_limit_bytes=VMEM_BYTES),
         cost_estimate=pl.CostEstimate(flops=flops, bytes_accessed=moved, transcendentals=0),
     )(*args)
@@ -39,23 +39,45 @@
     return lax.dot_general(a, b, (((0,), (0,)), ((), ())), preferred_element_type=jnp.float32)
 
 
-def band(where_ref, list_ref, count_ref, sigma_ref, panels, acc_ref):
+def offsets_of(where_ref):
     member = where_ref[0] % 4
     across = jnp.where(member < 2, 2, -2)
     beside = jnp.where(member % 2 == 0, 1, -1)
-    offsets = (0, beside, across, -across, -beside)
-    acc_ref[...] = jnp.zeros_like(acc_ref)
-    for offset, panel in zip(offsets, panels):
-        slot = jnp.int32(0)
-        live = jnp.int32(0)
-        for s in range(sigma_ref.shape[0]):
-            hit = (list_ref[s] == offset) & (s < count_ref[0])
-            slot = jnp.where(hit, s, slot)
-            live = jnp.where(hit, 1, live)
-
-        @pl.when(live == 1)
-        def _(slot=slot, panel=panel):
-            acc_ref[...] += dot(sigma_ref[slot], panel[...])
+    return jnp.int32(0), beside, across, -across, -beside
+
+
+def add_products(list_ref, count_ref, sigma_ref, offset, pairs):
+    slot = jnp.int32(0)
+    live = jnp.int32(0)
+    for s in range(sigma_ref.shape[0]):
+        hit = (list_ref[s] == offset) & (s < count_ref[0])
+        slot = jnp.where(hit, s, slot)
+        live = jnp.where(hit, 1, live)
+
+    @pl.when(live == 1)
+    def _():
+        for acc_ref, panel_ref in pairs:
+            acc_ref[...] += dot(sigma_ref[slot], panel_ref[...])
+
+
+def near_kernel(where_ref, list_ref, count_ref, sigma_ref, first, second, first_beside, second_beside,
+                first_acc, second_acc, turned_ref):
+    own, beside = offsets_of(where_ref)[:2]
+    first_acc[...] = jnp.zeros_like(first_acc)
+    second_acc[...] = jnp.zeros_like(second_acc)
+    add_products(list_ref, count_ref, sigma_ref, own, ((first_acc, first), (second_acc, second)))
+    add_products(list_ref, count_ref, sigma_ref, beside, ((first_acc, first_beside), (second_acc, second_beside)))
+    size = first.shape[0]
+    turned_ref[:size] = first[...].T
+    turned_ref[size:] = second[...].T
+
+
+def across_kernel(where_ref, list_ref, count_ref, sigma_ref, first_in, second_in, first_across, second_across,
+                  first_acc, second_acc):
+    first_acc[...] = first_in[...]
+    second_acc[...] = second_in[...]
+    across = offsets_of(where_ref)[2]
+    add_products(list_ref, count_ref, sigma_ref, across, ((first_acc, first_across), (second_acc, second_across)))
 
 
 def halves(value, where_ref, scratch_ref, give_ref, keep_ref, index):
@@ -66,22 +88,33 @@
     give_ref[index] = scratch_ref[pl.ds(pl.multiple_of((1 - core) * half, half), half)].astype(jnp.bfloat16)
 
 
-def first_kernel(where_ref, list_ref, count_ref, sigma_ref, own, beside, across, far, rest, second_ref,
+def first_kernel(where_ref, list_ref, count_ref, sigma_ref, acc_in, far, rest, turned_ref,
                  column_ref, give_ref, keep_ref, acc_ref):
-    band(where_ref, list_ref, count_ref, sigma_ref, (own, beside, across, far, rest), acc_ref)
+    acc_ref[...] = acc_in[...]
+    offsets = offsets_of(where_ref)
+    add_products(list_ref, count_ref, sigma_ref, offsets[3], ((acc_ref, far),))
+    add_products(list_ref, count_ref, sigma_ref, offsets[4], ((acc_ref, rest),))
     column = (-acc_ref[...]).astype(jnp.bfloat16)
     column_ref[...] = column
-    halves(-dot_t(own[...], column), where_ref, acc_ref, give_ref, keep_ref, 0)
-    halves(dot_t(column, second_ref[...]), where_ref, acc_ref, give_ref, keep_ref, 1)
-
-
-def second_kernel(where_ref, list_ref, count_ref, sigma_ref, own, beside, across, far, rest, column_first_ref,
-                  lower_ref, column_ref, give_ref, keep_ref, acc_ref):
-    band(where_ref, list_ref, count_ref, sigma_ref, (own, beside, across, far, rest), acc_ref)
-    total = acc_ref[...] + dot(column_first_ref[...], lower_ref[...])
-    column = (-total).astype(jnp.bfloat16)
+    size = column.shape[0]
+    halves(-dot(turned_ref[:size], column), where_ref, acc_ref, give_ref, keep_ref, 0)
+    halves(dot(turned_ref[size:], column), where_ref, acc_ref, give_ref, keep_ref, 1)
+
+
+def lower_kernel(acc_in, column_ref, lower_ref, acc_ref):
+    acc_ref[...] = acc_in[...] + dot(column_ref[...], lower_ref[...])
+
+
+def second_kernel(where_ref, list_ref, count_ref, sigma_ref, acc_in, far, rest, turned_ref,
+                  column_ref, give_ref, keep_ref, acc_ref):
+    acc_ref[...] = acc_in[...]
+    offsets = offsets_of(where_ref)
+    add_products(list_ref, count_ref, sigma_ref, offsets[3], ((acc_ref, far),))
+    add_products(list_ref, count_ref, sigma_ref, offsets[4], ((acc_ref, rest),))
+    column = (-acc_ref[...]).astype(jnp.bfloat16)
     column_ref[...] = column
-    halves(-dot_t(own[...], column), where_ref, acc_ref, give_ref, keep_ref, 0)
+    size = column.shape[0]
+    halves(-dot(turned_ref[size:], column), where_ref, acc_ref, give_ref, keep_ref, 0)
 
 
 def split(value):
@@ -105,7 +138,7 @@
     first_ref[...] = block_first
     place(where_ref, mine_ref, other_ref, 1, sum_ref)
     high, low = split(block_first)
-    link = dot(high, lower) + dot(low, lower) + sum_ref[...]
+    link = dot(high, lower) + dot(low, lower) + sum_ref[...].T
     link_ref[...] = -link
     high, low = split(link)
     base_ref[...] = second_diag_ref[...] + dot_t(lower, high) + dot_t(lower, low)
@@ -130,16 +163,24 @@
     return swapped(jnp.where(give_across, across, far), 1, devices)
 
 
+def core_summed(give, keep, position, devices):
+    return halved(keep + swapped(give, 1, devices).astype(jnp.float32), 2, position)
+
+
+def halved(total, bit, position):
+    k, rows, width = total.shape
+    pair = total.reshape((k, 2, rows // 2, width))
+    mine = (position // bit) % 2
+    give = lax.dynamic_index_in_dim(pair, 1 - mine, 1, keepdims=False).astype(jnp.bfloat16)
+    return give, lax.dynamic_index_in_dim(pair, mine, 1, keepdims=False)
+
+
 def summed(give, keep, position, devices):
-    total = keep + swapped(give, 1, devices).astype(jnp.float32)
     bits = [2 ** b for b in range(1, devices.bit_length() - 1)]
     for bit in bits:
-        k, rows, width = total.shape
-        pair = total.reshape((k, 2, rows // 2, width))
-        mine = (position // bit) % 2
-        give = lax.dynamic_index_in_dim(pair, 1 - mine, 1, keepdims=False).astype(jnp.bfloat16)
-        keep = lax.dynamic_index_in_dim(pair, mine, 1, keepdims=False)
         total = keep + swapped(give, bit, devices).astype(jnp.float32)
+        if bit != bits[-1]:
+            give, keep = halved(total, 2 * bit, position)
     gathered = total.astype(jnp.bfloat16)
     for bit in bits[::-1]:
         other = swapped(gathered, bit, devices)
@@ -170,38 +211,43 @@
     def parts(k):
         return [jax.ShapeDtypeStruct((k, half, width), t) for t in (jnp.bfloat16, jnp.float32)]
 
+    scalars = [where, listed, count, sigma]
     across = swapped(first, 2, devices)
     beside = swapped(first, 1, devices)
+    second_beside = swapped(second, 1, devices)
+    first_acc, second_acc, turned = call(
+        near_kernel,
+        [wide, wide, jax.ShapeDtypeStruct((2 * size, width), jnp.bfloat16)],
+        scalars + [first, second, beside, second_beside],
+        3,
+        4 * one,
+    )
     across, later = lax.optimization_barrier((across, second))
     far = far_of(across, devices)
     second_across = swapped(later, 2, devices)
-    second_beside = swapped(later, 1, devices)
     rest = rest_of(across, far, member, devices)
     second_far = far_of(second_across, devices)
+    first_acc, second_acc = call(
+        across_kernel, [wide, wide], scalars + [first_acc, second_acc, across, second_across], 3, 2 * one
+    )
+    column_first, give, keep = call(
+        first_kernel, [narrow] + parts(2), scalars + [first_acc, far, rest, turned], 3, 4 * one, scratch
+    )
+    give, second_across = lax.optimization_barrier((give, second_across))
     second_rest = rest_of(second_across, second_far, member, devices)
-    column_first, give, keep = call(
-        first_kernel,
-        [narrow] + parts(2),
-        [where, listed, count, sigma, first, beside, across, far, rest, second],
-        3,
-        scratch,
-        7 * one,
-    )
+    give, keep = core_summed(give, keep, position, devices)
+    (second_acc,) = call(lower_kernel, [wide], [second_acc, column_first, lower_panel], 0, one)
+    give, second_rest = lax.optimization_barrier((give, second_rest))
     column_second, second_give, second_keep = call(
-        second_kernel,
-        [narrow] + parts(1),
-        [where, listed, count, sigma, second, second_beside, second_across, second_far, second_rest,
-         column_first, lower_panel],
-        3,
-        scratch,
-        7 * one,
+        second_kernel, [narrow] + parts(1), scalars + [second_acc, second_far, second_rest, turned], 3, 3 * one, scratch
     )
     mine, other = summed(give, keep, position, devices)
+    second_give, second_keep = core_summed(second_give, second_keep, position, devices)
     second_mine, second_other = summed(second_give, second_keep, position, devices)
     block_first, block_link, base = call(
-        link_kernel, [wide] * 3, [where, mine, other, lower_panel, first_diag, second_diag], 1, scratch, 4 * one
-    )
-    (block_second,) = call(last_kernel, [wide], [where, second_mine, second_other, base], 1, [], size * width)
+        link_kernel, [wide] * 3, [where, mine, other, lower_panel, first_diag, second_diag], 1, 4 * one, scratch
+    )
+    (block_second,) = call(last_kernel, [wide], [where, second_mine, second_other, base], 1, size * width)
     shape = first_panel.shape
     return column_first.reshape(shape), block_first, block_link, column_second.reshape(shape), block_second
 

time: 105 us -> 106 us (level)
  starting transfers between devices: 38.7 us -> 27.1 us
  local copies, waits for them, and re-layouts: 7.91 us -> 12.7 us
  waiting for transfers between devices: 45.2 us -> 49.9 us
  other arithmetic: 1.64 us -> 4.39 us
  Pallas kernels: 9.09 us -> 10.3 us
    ppermute x22, starting transfers between devices: 31.8 us -> 19.8 us  [swapped(): return lax.ppermute(value, 'row', [(i, i ^ bit) for i in range(devices)])]
    unnamed x26 -> x36, local copies, waits for them, and re-layouts: 7.76 us -> 11.8 us
    ppermute x22, waiting for transfers between devices: 36.9 us -> 40.3 us  [swapped(): return lax.ppermute(value, 'row', [(i, i ^ bit) for i in range(devices)])]
    add x2, other arithmetic: 0.23 us -> 1.82 us  [core_summed(): keep + swapped(give, 1, devices).astype(jnp.float32)]
    ppermute x2, waiting for transfers between devices: 8.31 us -> 9.61 us  [far_of(): lax.ppermute(across, 'row', [(a, b) for a, b in hops if 0 <= b < devices])]
    pallas_call x4 -> x7, Pallas kernels: 9.09 us -> 10.3 us  [call(): pl.pallas_call(body, out_shape=outs, in_specs=[smem_spec()] * scalars + [...]
  transfers between devices with their start and end apart: 24 -> 24, of which waited for: 13 -> 14; matrix products, arithmetic and copies ran while one was open for 2% -> 5% of each run, Pallas kernels for 8% -> 7%
where the time goes in v3:
time: 106 us
  waiting for transfers between devices  49.9 us (47%)
  starting transfers between devices  27.1 us (26%)
  local copies, waits for them, and re-layouts  12.7 us (12%)
  Pallas kernels  10.3 us (10%)
  other arithmetic  4.39 us (4%)
  between operations  1.62 us (2%)
    ppermute x22, waiting for transfers between devices, swapped(): return lax.ppermute(value, 'row', [(i, i ^ bit) for i in range(devices)])  40.3 us
    ppermute x22, starting transfers between devices, swapped(): return lax.ppermute(value, 'row', [(i, i ^ bit) for i in range(devices)])  19.8 us
    unnamed x36, local copies, waits for them, and re-layouts  11.8 us
    pallas_call x7, Pallas kernels, call(): pl.pallas_call(body, out_shape=outs, in_specs=[smem_spec()] * scalars + [...  10.3 us
    ppermute x2, waiting for transfers between devices, far_of(): lax.ppermute(across, 'row', [(a, b) for a, b in hops if 0 <= b < devices])  9.61 us
    ppermute x2, starting transfers between devices, far_of(): lax.ppermute(across, 'row', [(a, b) for a, b in hops if 0 <= b < devices])  7.22 us
  transfers between devices with their start and end apart: 24, of which 14 were waited for; matrix products, arithmetic and copies ran while one was open for 5% of the time, Pallas kernels for 7%

profile of v3, /device:TPU:0, one launch (start us, length us, event | category | flops | bytes accessed | tf_op | source)
XLA Modules:
  0.0 105.9 jit_solution(16361894689231359198)
XLA Ops:
  0.6 3.0 %collective-permute-start.2 = (bf16[512,512]{1,0:T(8,128)(2,1)}, bf16[512,512]{1,0:T(8,128)(2,1)S(1)}, u32[]{:S(2)}, u32[]{:S(2)}) collective-permute-start(bf16[512,512]{1,0:T(8,128)(2,1)} %bitcast.59), channel_id=1, source_target_pairs={{0,2},{1,3},{2,0},{3,1},{4,6},{5,7},{6,4},{7,5},{8,10},{9,11},{10,... | collective-permute-start | bytes 1572872 | tf_op jit(solution)/shard_map/ppermute | solution.py:153
  3.6 12.1 %collective-permute-done.2.first_across = bf16[512,512]{1,0:T(8,128)(2,1)S(1)} collective-permute-done((bf16[512,512]{1,0:T(8,128)(2,1)}, bf16[512,512]{1,0:T(8,128)(2,1)S(1)}, u32[]{:S(2)}, u32[]{:S(2)}) %collective-permute-start.2) | collective-permute-done | bytes 524320 | tf_op jit(solution)/shard_map/ppermute | solution.py:153
  15.8 3.7 %collective-permute-start.4 = (bf16[512,512]{1,0:T(8,128)(2,1)S(1)}, bf16[512,512]{1,0:T(8,128)(2,1)S(1)}, u32[]{:S(2)}, u32[]{:S(2)}) collective-permute-start(bf16[512,512]{1,0:T(8,128)(2,1)S(1)} %collective-permute-done.2.first_across), channel_id=1, source_target_pairs={{0,4},{1,5},{4,8},{5,9},{6,2},{7,3},{8,12},{9,13},{10,6},{11,7},{1... | collective-permute-start | bytes 1572872 | tf_op jit(solution)/shard_map/ppermute | solution.py:158
  20.2 9.6 %collective-permute-done.4.far = bf16[512,512]{1,0:T(8,128)(2,1)S(1)} collective-permute-done((bf16[512,512]{1,0:T(8,128)(2,1)S(1)}, bf16[512,512]{1,0:T(8,128)(2,1)S(1)}, u32[]{:S(2)}, u32[]{:S(2)}) %collective-permute-start.4) | collective-permute-done | bytes 524320 | tf_op jit(solution)/shard_map/ppermute | solution.py:158
  29.9 2.4 %collective-permute-done.3.second_across = bf16[512,512]{1,0:T(8,128)(2,1)S(1)} collective-permute-done((bf16[512,512]{1,0:T(8,128)(2,1)}, bf16[512,512]{1,0:T(8,128)(2,1)S(1)}, u32[]{:S(2)}, u32[]{:S(2)}) %collective-permute-start.3) | collective-permute-done | bytes 524320 | tf_op jit(solution)/shard_map/ppermute | solution.py:153
  32.3 3.5 %collective-permute-start.7 = (bf16[512,512]{1,0:T(8,128)(2,1)S(1)}, bf16[512,512]{1,0:T(8,128)(2,1)S(1)}, u32[]{:S(2)}, u32[]{:S(2)}) collective-permute-start(bf16[512,512]{1,0:T(8,128)(2,1)S(1)} %collective-permute-done.3.second_across), channel_id=1, source_target_pairs={{0,4},{1,5},{4,8},{5,9},{6,2},{7,3},{8,12},{9,13},{10,6},{11,7},{1... | collective-permute-start | bytes 1572872 | tf_op jit(solution)/shard_map/ppermute | solution.py:158
  38.0 1.7 %copy-done = bf16[1,1,5,512,512]{4,3,2,1,0:T(8,128)(2,1)S(1)} copy-done((bf16[1,1,5,512,512]{4,3,2,1,0:T(8,128)(2,1)S(1)}, bf16[1,1,5,512,512]{4,3,2,1,0:T(8,128)(2,1)}, u32[]{:S(2)}) %copy-start) | copy-done | bytes 2621464
  40.8 1.0 copy-done.8
  41.9 1.0 copy-done.10
  44.6 1.7 %shard_map.119 = (f32[512,512]{1,0:T(8,128)S(1)}, f32[512,512]{1,0:T(8,128)S(1)}, bf16[1024,512]{1,0:T(8,128)(2,1)S(1)}) custom-call(s32[1]{0:T(128)} %bitcast.where_ref, s32[5]{0:T(128)S(1)} %bitcast.65, s32[1]{0:T(128)} %bitcast.50.count_ref, bf16[5,512,512]{2,1,0:T(8,128)(2,1)S(1)} %bitcast.54, bf16[512,512]{1,0:T(8,128)(2,1)S(1)} %bitcast.61, ...), custom_call_target="tpu_custom_call" | custom-call | flops 1073741824 | bytes 7864348 | tf_op jit(solution)/shard_map/pallas_call | solution.py:23
  48.0 2.4 %shard_map.121 = (bf16[512,512]{1,0:T(8,128)(2,1)}, bf16[2,256,512]{2,1,0:T(8,128)(2,1)}, f32[2,256,512]{2,1,0:T(8,128)S(1)}) custom-call(s32[1]{0:T(128)} %bitcast.where_ref, s32[5]{0:T(128)S(1)} %bitcast.67, s32[1]{0:T(128)} %bitcast.52.count_ref, bf16[5,512,512]{2,1,0:T(8,128)(2,1)S(1)} %bitcast.56, f32[512,512]{1,0:T(8,128)S(1)} %get-tuple-element.29.acc_in, ...), custom_call_target="tpu_custom_call" | custom-call | flops 1073741824 | bytes 7864348 | tf_op jit(solution)/shard_map/pallas_call | solution.py:23
  51.7 1.2 %copy-done.3 = f32[512,512]{1,0:T(8,128)S(1)} copy-done((f32[512,512]{1,0:T(8,128)S(1)}, f32[512,512]{1,0:T(8,128)}, u32[]{:S(2)}) %copy-start.3) | copy-done | bytes 1048600
  53.0 1.0 copy-done.6
  54.5 1.8 %convert_add_fusion = f32[2,256,512]{2,1,0:T(8,128)S(1)} fusion(f32[2,256,512]{2,1,0:T(8,128)} %copy-done.4, bf16[2,256,512]{2,1,0:T(8,128)(2,1)} %collective-permute-done.6), kind=kLoop, calls=%fused_computation | loop fusion | flops 524288 | bytes 2621440 | tf_op jit(solution)/shard_map/add | solution.py:167
  57.3 1.7 %shard_map.124 = (bf16[512,512]{1,0:T(8,128)(2,1)}, bf16[1,256,512]{2,1,0:T(8,128)(2,1)S(1)}, f32[1,256,512]{2,1,0:T(8,128)S(1)}) custom-call(s32[1]{0:T(128)} %bitcast.where_ref, s32[5]{0:T(128)S(1)} %bitcast.68, s32[1]{0:T(128)} %bitcast.53.count_ref, bf16[5,512,512]{2,1,0:T(8,128)(2,1)S(1)} %bitcast.57, f32[512,512]{1,0:T(8,128)S(1)} %shard_map.123.acc_in, ...), custom_call_target="tpu_custom_call" | custom-call | flops 805306368 | bytes 7077916 | tf_op jit(solution)/shard_map/pallas_call | solution.py:23
  59.7 1.2 %collective-permute-done.16 = bf16[1,256,512]{2,1,0:T(8,128)(2,1)S(1)} collective-permute-done((bf16[1,256,512]{2,1,0:T(8,128)(2,1)S(1)}, bf16[1,256,512]{2,1,0:T(8,128)(2,1)S(1)}, u32[]{:S(2)}, u32[]{:S(2)}) %collective-permute-start.16) | collective-permute-done | bytes 262176 | tf_op jit(solution)/shard_map/ppermute | solution.py:153
  61.9 7.2 %collective-permute-done.9 = bf16[2,128,512]{2,1,0:T(8,128)(2,1)S(1)} collective-permute-done((bf16[2,128,512]{2,1,0:T(8,128)(2,1)}, bf16[2,128,512]{2,1,0:T(8,128)(2,1)S(1)}, u32[]{:S(2)}, u32[]{:S(2)}) %collective-permute-start.9) | collective-permute-done | bytes 262176 | tf_op jit(solution)/shard_map/ppermute | solution.py:153
  69.1 1.1 %bitcast_add_fusion = f32[2,128,512]{2,1,0:T(8,128)S(1)} fusion(bf16[2,128,512]{2,1,0:T(8,128)(2,1)S(1)} %collective-permute-done.9, f32[2,2,128,512]{3,2,1,0:T(8,128)} %bitcast.70, s32[]{:T(128)S(6)} %select_n.182), kind=kLoop, calls=%fused_computation.3 | loop fusion | flops 262144 | bytes 1310724 | tf_op jit(solution)/shard_map/add | solution.py:181
  70.3 2.9 %collective-permute-start.10 = (bf16[2,64,512]{2,1,0:T(8,128)(2,1)S(1)}, bf16[2,64,512]{2,1,0:T(8,128)(2,1)S(1)}, u32[]{:S(2)}, u32[]{:S(2)}) collective-permute-start(bf16[2,64,512]{2,1,0:T(8,128)(2,1)S(1)} %fusion.1), channel_id=1, source_target_pairs={{0,4},{1,5},{2,6},{3,7},{4,0},{5,1},{6,2},{7,3},{8,12},{9,13},{10,... | collective-permute-start | bytes 393224 | tf_op jit(solution)/shard_map/ppermute | solution.py:153
  74.2 2.4 %collective-permute-done.10 = bf16[2,64,512]{2,1,0:T(8,128)(2,1)S(1)} collective-permute-done((bf16[2,64,512]{2,1,0:T(8,128)(2,1)S(1)}, bf16[2,64,512]{2,1,0:T(8,128)(2,1)S(1)}, u32[]{:S(2)}, u32[]{:S(2)}) %collective-permute-start.10) | collective-permute-done | bytes 131104 | tf_op jit(solution)/shard_map/ppermute | solution.py:153
  76.6 3.4 %collective-permute-start.11 = (bf16[2,32,512]{2,1,0:T(8,128)(2,1)S(1)}, bf16[2,32,512]{2,1,0:T(8,128)(2,1)S(1)}, u32[]{:S(2)}, u32[]{:S(2)}) collective-permute-start(bf16[2,32,512]{2,1,0:T(8,128)(2,1)S(1)} %fusion.5), channel_id=1, source_target_pairs={{0,8},{1,9},{2,10},{3,11},{4,12},{5,13},{6,14},{7,15},{8,0},{9,1},... | collective-permute-start | bytes 196616 | tf_op jit(solution)/shard_map/ppermute | solution.py:153
  80.1 1.1 %collective-permute-start.19 = (bf16[1,32,512]{2,1,0:T(8,128)(2,1)S(1)}, bf16[1,32,512]{2,1,0:T(8,128)(2,1)S(1)}, u32[]{:S(2)}, u32[]{:S(2)}) collective-permute-start(bf16[1,32,512]{2,1,0:T(8,128)(2,1)S(1)} %fusion.7), channel_id=1, source_target_pairs={{0,8},{1,9},{2,10},{3,11},{4,12},{5,13},{6,14},{7,15},{8,0},{9,1},... | collective-permute-start | bytes 98312 | tf_op jit(solution)/shard_map/ppermute | solution.py:153
  81.1 1.1 %collective-permute-done.11 = bf16[2,32,512]{2,1,0:T(8,128)(2,1)S(1)} collective-permute-done((bf16[2,32,512]{2,1,0:T(8,128)(2,1)S(1)}, bf16[2,32,512]{2,1,0:T(8,128)(2,1)S(1)}, u32[]{:S(2)}, u32[]{:S(2)}) %collective-permute-start.11) | collective-permute-done | bytes 65568 | tf_op jit(solution)/shard_map/ppermute | solution.py:153
  82.3 3.5 %collective-permute-start.12 = (bf16[2,32,512]{2,1,0:T(8,128)(2,1)S(1)}, bf16[2,32,512]{2,1,0:T(8,128)(2,1)S(1)}, u32[]{:S(2)}, u32[]{:S(2)}) collective-permute-start(bf16[2,32,512]{2,1,0:T(8,128)(2,1)S(1)} %fusion.3), channel_id=1, source_target_pairs={{0,8},{1,9},{2,10},{3,11},{4,12},{5,13},{6,14},{7,15},{8,0},{9,1},... | collective-permute-start | bytes 196616 | tf_op jit(solution)/shard_map/ppermute | solution.py:153
  86.4 2.4 %collective-permute-done.12 = bf16[2,32,512]{2,1,0:T(8,128)(2,1)S(1)} collective-permute-done((bf16[2,32,512]{2,1,0:T(8,128)(2,1)S(1)}, bf16[2,32,512]{2,1,0:T(8,128)(2,1)S(1)}, u32[]{:S(2)}, u32[]{:S(2)}) %collective-permute-start.12) | collective-permute-done | bytes 65568 | tf_op jit(solution)/shard_map/ppermute | solution.py:153
  89.1 1.6 %collective-permute-done.20 = bf16[1,32,512]{2,1,0:T(8,128)(2,1)S(1)} collective-permute-done((bf16[1,32,512]{2,1,0:T(8,128)(2,1)S(1)}, bf16[1,32,512]{2,1,0:T(8,128)(2,1)S(1)}, u32[]{:S(2)}, u32[]{:S(2)}) %collective-permute-start.20) | collective-permute-done | bytes 32800 | tf_op jit(solution)/shard_map/ppermute | solution.py:153
  91.1 2.8 %collective-permute-done.13 = bf16[2,64,512]{2,1,0:T(8,128)(2,1)S(1)} collective-permute-done((bf16[2,64,512]{2,1,0:T(8,128)(2,1)S(1)}, bf16[2,64,512]{2,1,0:T(8,128)(2,1)S(1)}, u32[]{:S(2)}, u32[]{:S(2)}) %collective-permute-start.13) | collective-permute-done | bytes 131104 | tf_op jit(solution)/shard_map/ppermute | solution.py:153
  95.1 1.1 %collective-permute-start.22 = (bf16[1,128,512]{2,1,0:T(8,128)(2,1)S(1)}, bf16[1,128,512]{2,1,0:T(8,128)(2,1)S(1)}, u32[]{:S(2)}, u32[]{:S(2)}) collective-permute-start(bf16[1,128,512]{2,1,0:T(8,128)(2,1)S(1)} %pad_maximum_fusion.4), channel_id=1, source_target_pairs={{0,2},{1,3},{2,0},{3,1},{4,6},{5,7},{6,4},{7,5},{8,10},{9,11},{10,... | collective-permute-start | bytes 393224 | tf_op jit(solution)/shard_map/ppermute | solution.py:153
  96.2 4.2 %collective-permute-done.14 = bf16[2,128,512]{2,1,0:T(8,128)(2,1)S(1)} collective-permute-done((bf16[2,128,512]{2,1,0:T(8,128)(2,1)S(1)}, bf16[2,128,512]{2,1,0:T(8,128)(2,1)S(1)}, u32[]{:S(2)}, u32[]{:S(2)}) %collective-permute-start.14) | collective-permute-done | bytes 262176 | tf_op jit(solution)/shard_map/ppermute | solution.py:153
  100.7 1.2 %collective-permute-done.22 = bf16[1,128,512]{2,1,0:T(8,128)(2,1)S(1)} collective-permute-done((bf16[1,128,512]{2,1,0:T(8,128)(2,1)S(1)}, bf16[1,128,512]{2,1,0:T(8,128)(2,1)S(1)}, u32[]{:S(2)}, u32[]{:S(2)}) %collective-permute-start.22) | collective-permute-done | bytes 131104 | tf_op jit(solution)/shard_map/ppermute | solution.py:153
  102.6 2.2 %shard_map.122 = (f32[512,512]{1,0:T(8,128)}, f32[512,512]{1,0:T(8,128)}, f32[512,512]{1,0:T(8,128)S(1)}) custom-call(s32[1]{0:T(128)} %bitcast.where_ref, bf16[2,256,512]{2,1,0:T(8,128)(2,1)S(1)} %pad_maximum_fusion.mine_ref, bf16[2,256,512]{2,1,0:T(8,128)(2,1)S(1)} %collective-permute-done.15.other_ref, bf16[512,512]{1,0:T(8,128)(2,1)S(1)} %copy-done.5, ...), custom_call_target="tpu_custom_call" | custom-call | flops 1073741824 | bytes 6815748 | tf_op jit(solution)/shard_map/pallas_call | solution.py:23
  104.8 1.1 %shard_map.125 = f32[512,512]{1,0:T(8,128)} custom-call(s32[1]{0:T(128)} %bitcast.where_ref, bf16[1,256,512]{2,1,0:T(8,128)(2,1)S(1)} %pad_maximum_fusion.2.mine_ref, bf16[1,256,512]{2,1,0:T(8,128)(2,1)S(1)} %collective-permute-done.23.other_ref, f32[512,512]{1,0:T(8,128)S(1)} %get-tuple-element.44.base_ref), custom_call_target="tpu_custom_call" | custom-call | flops 262144 | bytes 2621444 | tf_op jit(solution)/shard_map/pallas_call | solution.py:23
  (87 shorter events, 15.8 us)
Async XLA Ops:
  0.6 15.1 %collective-permute-start.2 = (bf16[512,512]{1,0:T(8,128)(2,1)}, bf16[512,512]{1,0:T(8,128)(2,1)S(1)}, u32[]{:S(2)}, u32[]{:S(2)}) collective-permute-start(bf16[512,512]{1,0:T(8,128)(2,1)} %bitcast.59), channel_id=1, source_target_pairs={{0,2},{1,3},{2,0},{3,1},{4,6},{5,7},{6,4},{7,5},{8,10},{9,11},{10,... | collective-permute-start | bytes 1572872 | tf_op jit(solution)/shard_map/ppermute | solution.py:153
  15.8 14.0 %collective-permute-start.4 = (bf16[512,512]{1,0:T(8,128)(2,1)S(1)}, bf16[512,512]{1,0:T(8,128)(2,1)S(1)}, u32[]{:S(2)}, u32[]{:S(2)}) collective-permute-start(bf16[512,512]{1,0:T(8,128)(2,1)S(1)} %collective-permute-done.2.first_across), channel_id=1, source_target_pairs={{0,4},{1,5},{4,8},{5,9},{6,2},{7,3},{8,12},{9,13},{10,6},{11,7},{1... | collective-permute-start | bytes 1572872 | tf_op jit(solution)/shard_map/ppermute | solution.py:158
  19.5 12.8 %collective-permute-start.3 = (bf16[512,512]{1,0:T(8,128)(2,1)}, bf16[512,512]{1,0:T(8,128)(2,1)S(1)}, u32[]{:S(2)}, u32[]{:S(2)}) collective-permute-start(bf16[512,512]{1,0:T(8,128)(2,1)} %bitcast.62), channel_id=1, source_target_pairs={{0,2},{1,3},{2,0},{3,1},{4,6},{5,7},{6,4},{7,5},{8,10},{9,11},{10,... | collective-permute-start | bytes 1572872 | tf_op jit(solution)/shard_map/ppermute | solution.py:153
  19.6 16.8 %collective-permute-start = (bf16[512,512]{1,0:T(8,128)(2,1)}, bf16[512,512]{1,0:T(8,128)(2,1)S(1)}, u32[]{:S(2)}, u32[]{:S(2)}) collective-permute-start(bf16[512,512]{1,0:T(8,128)(2,1)} %bitcast.60), channel_id=1, source_target_pairs={{0,1},{1,0},{2,3},{3,2},{4,5},{5,4},{6,7},{7,6},{8,9},{9,8},{10,11... | collective-permute-start | bytes 1572872 | tf_op jit(solution)/shard_map/ppermute | solution.py:153
  19.7 17.6 %collective-permute-start.1 = (bf16[512,512]{1,0:T(8,128)(2,1)}, bf16[512,512]{1,0:T(8,128)(2,1)S(1)}, u32[]{:S(2)}, u32[]{:S(2)}) collective-permute-start(bf16[512,512]{1,0:T(8,128)(2,1)} %bitcast.63), channel_id=1, source_target_pairs={{0,1},{1,0},{2,3},{3,2},{4,5},{5,4},{6,7},{7,6},{8,9},{9,8},{10,11... | collective-permute-start | bytes 1572872 | tf_op jit(solution)/shard_map/ppermute | solution.py:153
  29.8 18.1 %collective-permute-start.5 = (bf16[512,512]{1,0:T(8,128)(2,1)S(1)}, bf16[512,512]{1,0:T(8,128)(2,1)S(1)}, u32[]{:S(2)}, u32[]{:S(2)}) collective-permute-start(bf16[512,512]{1,0:T(8,128)(2,1)S(1)} %broadcast_select_fusion.1), channel_id=1, source_target_pairs={{0,1},{1,0},{2,3},{3,2},{4,5},{5,4},{6,7},{7,6},{8,9},{9,8},{10,11... | collective-permute-start | bytes 1572872 | tf_op jit(solution)/shard_map/ppermute | solution.py:153
  32.3 18.1 %collective-permute-start.7 = (bf16[512,512]{1,0:T(8,128)(2,1)S(1)}, bf16[512,512]{1,0:T(8,128)(2,1)S(1)}, u32[]{:S(2)}, u32[]{:S(2)}) collective-permute-start(bf16[512,512]{1,0:T(8,128)(2,1)S(1)} %collective-permute-done.3.second_across), channel_id=1, source_target_pairs={{0,4},{1,5},{4,8},{5,9},{6,2},{7,3},{8,12},{9,13},{10,6},{11,7},{1... | collective-permute-start | bytes 1572872 | tf_op jit(solution)/shard_map/ppermute | solution.py:158
  38.0 1.7 %copy-start = (bf16[1,1,5,512,512]{4,3,2,1,0:T(8,128)(2,1)S(1)}, bf16[1,1,5,512,512]{4,3,2,1,0:T(8,128)(2,1)}, u32[]{:S(2)}) copy-start(bf16[1,1,5,512,512]{4,3,2,1,0:T(8,128)(2,1)} %param.8) | copy-start | bytes 7864324
  48.0 3.8 %copy-start.5 = (bf16[512,512]{1,0:T(8,128)(2,1)S(1)}, bf16[512,512]{1,0:T(8,128)(2,1)}, u32[]{:S(2)}) copy-start(bf16[512,512]{1,0:T(8,128)(2,1)} %lower_ref.3) | copy-start | bytes 1572868
  50.4 1.1 %copy-start.4 = (f32[2,256,512]{2,1,0:T(8,128)}, f32[2,256,512]{2,1,0:T(8,128)S(1)}, u32[]{:S(2)}) copy-start(f32[2,256,512]{2,1,0:T(8,128)S(1)} %get-tuple-element.32) | copy-start | bytes 3145732
  50.4 4.1 %collective-permute-start.6 = (bf16[2,256,512]{2,1,0:T(8,128)(2,1)}, bf16[2,256,512]{2,1,0:T(8,128)(2,1)}, u32[]{:S(2)}, u32[]{:S(2)}) collective-permute-start(bf16[2,256,512]{2,1,0:T(8,128)(2,1)} %get-tuple-element.34), channel_id=1, source_target_pairs={{0,1},{1,0},{2,3},{3,2},{4,5},{5,4},{6,7},{7,6},{8,9},{9,8},{10,11... | collective-permute-start | bytes 1572872 | tf_op jit(solution)/shard_map/ppermute | solution.py:153
  51.5 5.5 %collective-permute-start.8 = (bf16[512,512]{1,0:T(8,128)(2,1)}, bf16[512,512]{1,0:T(8,128)(2,1)S(1)}, u32[]{:S(2)}, u32[]{:S(2)}) collective-permute-start(bf16[512,512]{1,0:T(8,128)(2,1)} %broadcast_select_fusion), channel_id=1, source_target_pairs={{0,1},{1,0},{2,3},{3,2},{4,5},{5,4},{6,7},{7,6},{8,9},{9,8},{10,11... | collective-permute-start | bytes 1572872 | tf_op jit(solution)/shard_map/ppermute | solution.py:153
  51.7 1.2 %copy-start.3 = (f32[512,512]{1,0:T(8,128)S(1)}, f32[512,512]{1,0:T(8,128)}, u32[]{:S(2)}) copy-start(f32[512,512]{1,0:T(8,128)} %copy-done.2) | copy-start | bytes 3145732
  54.0 3.3 %copy-start.1 = (bf16[1,1,5,512,512]{4,3,2,1,0:T(8,128)(2,1)S(1)}, bf16[1,1,5,512,512]{4,3,2,1,0:T(8,128)(2,1)}, u32[]{:S(2)}) copy-start(bf16[1,1,5,512,512]{4,3,2,1,0:T(8,128)(2,1)} %param.8) | copy-start | bytes 7864324
  54.0 3.3 %copy-start.14 = (s32[1,1,5]{2,1,0:T(1,128)S(1)}, s32[1,1,5]{2,1,0:T(1,128)}, u32[]{:S(2)}) copy-start(s32[1,1,5]{2,1,0:T(1,128)} %param.14) | copy-start | bytes 64
  59.0 1.9 %collective-permute-start.16 = (bf16[1,256,512]{2,1,0:T(8,128)(2,1)S(1)}, bf16[1,256,512]{2,1,0:T(8,128)(2,1)S(1)}, u32[]{:S(2)}, u32[]{:S(2)}) collective-permute-start(bf16[1,256,512]{2,1,0:T(8,128)(2,1)S(1)} %get-tuple-element.43), channel_id=1, source_target_pairs={{0,1},{1,0},{2,3},{3,2},{4,5},{5,4},{6,7},{7,6},{8,9},{9,8},{10,11... | collective-permute-start | bytes 786440 | tf_op jit(solution)/shard_map/ppermute | solution.py:153
  59.7 9.4 %collective-permute-start.9 = (bf16[2,128,512]{2,1,0:T(8,128)(2,1)}, bf16[2,128,512]{2,1,0:T(8,128)(2,1)S(1)}, u32[]{:S(2)}, u32[]{:S(2)}) collective-permute-start(bf16[2,128,512]{2,1,0:T(8,128)(2,1)} %fusion), channel_id=1, source_target_pairs={{0,2},{1,3},{2,0},{3,1},{4,6},{5,7},{6,4},{7,5},{8,10},{9,11},{10,... | collective-permute-start | bytes 786440 | tf_op jit(solution)/shard_map/ppermute | solution.py:153
  61.0 12.2 %collective-permute-start.17 = (bf16[1,128,512]{2,1,0:T(8,128)(2,1)S(1)}, bf16[1,128,512]{2,1,0:T(8,128)(2,1)S(1)}, u32[]{:S(2)}, u32[]{:S(2)}) collective-permute-start(bf16[1,128,512]{2,1,0:T(8,128)(2,1)S(1)} %fusion.2), channel_id=1, source_target_pairs={{0,2},{1,3},{2,0},{3,1},{4,6},{5,7},{6,4},{7,5},{8,10},{9,11},{10,... | collective-permute-start | bytes 393224 | tf_op jit(solution)/shard_map/ppermute | solution.py:153
  70.3 6.3 %collective-permute-start.10 = (bf16[2,64,512]{2,1,0:T(8,128)(2,1)S(1)}, bf16[2,64,512]{2,1,0:T(8,128)(2,1)S(1)}, u32[]{:S(2)}, u32[]{:S(2)}) collective-permute-start(bf16[2,64,512]{2,1,0:T(8,128)(2,1)S(1)} %fusion.1), channel_id=1, source_target_pairs={{0,4},{1,5},{2,6},{3,7},{4,0},{5,1},{6,2},{7,3},{8,12},{9,13},{10,... | collective-permute-start | bytes 393224 | tf_op jit(solution)/shard_map/ppermute | solution.py:153
  73.2 6.8 %collective-permute-start.18 = (bf16[1,64,512]{2,1,0:T(8,128)(2,1)S(1)}, bf16[1,64,512]{2,1,0:T(8,128)(2,1)S(1)}, u32[]{:S(2)}, u32[]{:S(2)}) collective-permute-start(bf16[1,64,512]{2,1,0:T(8,128)(2,1)S(1)} %fusion.4), channel_id=1, source_target_pairs={{0,4},{1,5},{2,6},{3,7},{4,0},{5,1},{6,2},{7,3},{8,12},{9,13},{10,... | collective-permute-start | bytes 196616 | tf_op jit(solution)/shard_map/ppermute | solution.py:153
  76.6 5.7 %collective-permute-start.11 = (bf16[2,32,512]{2,1,0:T(8,128)(2,1)S(1)}, bf16[2,32,512]{2,1,0:T(8,128)(2,1)S(1)}, u32[]{:S(2)}, u32[]{:S(2)}) collective-permute-start(bf16[2,32,512]{2,1,0:T(8,128)(2,1)S(1)} %fusion.5), channel_id=1, source_target_pairs={{0,8},{1,9},{2,10},{3,11},{4,12},{5,13},{6,14},{7,15},{8,0},{9,1},... | collective-permute-start | bytes 196616 | tf_op jit(solution)/shard_map/ppermute | solution.py:153
  80.1 5.8 %collective-permute-start.19 = (bf16[1,32,512]{2,1,0:T(8,128)(2,1)S(1)}, bf16[1,32,512]{2,1,0:T(8,128)(2,1)S(1)}, u32[]{:S(2)}, u32[]{:S(2)}) collective-permute-start(bf16[1,32,512]{2,1,0:T(8,128)(2,1)S(1)} %fusion.7), channel_id=1, source_target_pairs={{0,8},{1,9},{2,10},{3,11},{4,12},{5,13},{6,14},{7,15},{8,0},{9,1},... | collective-permute-start | bytes 98312 | tf_op jit(solution)/shard_map/ppermute | solution.py:153
  82.3 6.6 %collective-permute-start.12 = (bf16[2,32,512]{2,1,0:T(8,128)(2,1)S(1)}, bf16[2,32,512]{2,1,0:T(8,128)(2,1)S(1)}, u32[]{:S(2)}, u32[]{:S(2)}) collective-permute-start(bf16[2,32,512]{2,1,0:T(8,128)(2,1)S(1)} %fusion.3), channel_id=1, source_target_pairs={{0,8},{1,9},{2,10},{3,11},{4,12},{5,13},{6,14},{7,15},{8,0},{9,1},... | collective-permute-start | bytes 196616 | tf_op jit(solution)/shard_map/ppermute | solution.py:153
  85.8 4.9 %collective-permute-start.20 = (bf16[1,32,512]{2,1,0:T(8,128)(2,1)S(1)}, bf16[1,32,512]{2,1,0:T(8,128)(2,1)S(1)}, u32[]{:S(2)}, u32[]{:S(2)}) collective-permute-start(bf16[1,32,512]{2,1,0:T(8,128)(2,1)S(1)} %fusion.6), channel_id=1, source_target_pairs={{0,8},{1,9},{2,10},{3,11},{4,12},{5,13},{6,14},{7,15},{8,0},{9,1},... | collective-permute-start | bytes 98312 | tf_op jit(solution)/shard_map/ppermute | solution.py:153
  88.9 13.7 %copy-start.15 = (f32[512,512]{1,0:T(8,128)S(1)}, f32[512,512]{1,0:T(8,128)}, u32[]{:S(2)}) copy-start(f32[512,512]{1,0:T(8,128)} %first_diag_ref.1) | copy-start | bytes 3145732
  88.9 13.7 %copy-start.16 = (f32[512,512]{1,0:T(8,128)S(1)}, f32[512,512]{1,0:T(8,128)}, u32[]{:S(2)}) copy-start(f32[512,512]{1,0:T(8,128)} %second_diag_ref.1) | copy-start | bytes 3145732
  88.9 5.0 %collective-permute-start.13 = (bf16[2,64,512]{2,1,0:T(8,128)(2,1)S(1)}, bf16[2,64,512]{2,1,0:T(8,128)(2,1)S(1)}, u32[]{:S(2)}, u32[]{:S(2)}) collective-permute-start(bf16[2,64,512]{2,1,0:T(8,128)(2,1)S(1)} %pad_maximum_fusion.3), channel_id=1, source_target_pairs={{0,4},{1,5},{2,6},{3,7},{4,0},{5,1},{6,2},{7,3},{8,12},{9,13},{10,... | collective-permute-start | bytes 393224 | tf_op jit(solution)/shard_map/ppermute | solution.py:153
  90.8 4.3 %collective-permute-start.21 = (bf16[1,64,512]{2,1,0:T(8,128)(2,1)S(1)}, bf16[1,64,512]{2,1,0:T(8,128)(2,1)S(1)}, u32[]{:S(2)}, u32[]{:S(2)}) collective-permute-start(bf16[1,64,512]{2,1,0:T(8,128)(2,1)S(1)} %pad_maximum_fusion.5), channel_id=1, source_target_pairs={{0,4},{1,5},{2,6},{3,7},{4,0},{5,1},{6,2},{7,3},{8,12},{9,13},{10,... | collective-permute-start | bytes 196616 | tf_op jit(solution)/shard_map/ppermute | solution.py:153
  94.0 6.4 %collective-permute-start.14 = (bf16[2,128,512]{2,1,0:T(8,128)(2,1)S(1)}, bf16[2,128,512]{2,1,0:T(8,128)(2,1)S(1)}, u32[]{:S(2)}, u32[]{:S(2)}) collective-permute-start(bf16[2,128,512]{2,1,0:T(8,128)(2,1)S(1)} %pad_maximum_fusion.1), channel_id=1, source_target_pairs={{0,2},{1,3},{2,0},{3,1},{4,6},{5,7},{6,4},{7,5},{8,10},{9,11},{10,... | collective-permute-start | bytes 786440 | tf_op jit(solution)/shard_map/ppermute | solution.py:153
  95.1 6.7 %collective-permute-start.22 = (bf16[1,128,512]{2,1,0:T(8,128)(2,1)S(1)}, bf16[1,128,512]{2,1,0:T(8,128)(2,1)S(1)}, u32[]{:S(2)}, u32[]{:S(2)}) collective-permute-start(bf16[1,128,512]{2,1,0:T(8,128)(2,1)S(1)} %pad_maximum_fusion.4), channel_id=1, source_target_pairs={{0,2},{1,3},{2,0},{3,1},{4,6},{5,7},{6,4},{7,5},{8,10},{9,11},{10,... | collective-permute-start | bytes 393224 | tf_op jit(solution)/shard_map/ppermute | solution.py:153
  100.6 2.0 %collective-permute-start.15 = (bf16[2,256,512]{2,1,0:T(8,128)(2,1)S(1)}, bf16[2,256,512]{2,1,0:T(8,128)(2,1)S(1)}, u32[]{:S(2)}, u32[]{:S(2)}) collective-permute-start(bf16[2,256,512]{2,1,0:T(8,128)(2,1)S(1)} %pad_maximum_fusion.mine_ref), channel_id=1, source_target_pairs={{0,1},{1,0},{2,3},{3,2},{4,5},{5,4},{6,7},{7,6},{8,9},{9,8},{10,11... | collective-permute-start | bytes 1572872 | tf_op jit(solution)/shard_map/ppermute | solution.py:153
  101.9 2.8 %collective-permute-start.23 = (bf16[1,256,512]{2,1,0:T(8,128)(2,1)S(1)}, bf16[1,256,512]{2,1,0:T(8,128)(2,1)S(1)}, u32[]{:S(2)}, u32[]{:S(2)}) collective-permute-start(bf16[1,256,512]{2,1,0:T(8,128)(2,1)S(1)} %pad_maximum_fusion.2.mine_ref), channel_id=1, source_target_pairs={{0,1},{1,0},{2,3},{3,2},{4,5},{5,4},{6,7},{7,6},{8,9},{9,8},{10,11... | collective-permute-start | bytes 786440 | tf_op jit(solution)/shard_map/ppermute | solution.py:153
  (10 other events, 9.5 us)

commit v4 on v3

--- a/solution.py
+++ b/solution.py
@@ -7,24 +7,17 @@
 from jax.experimental.pallas import tpu as pltpu
 from jax.sharding import PartitionSpec as P
 
-VMEM_BYTES = 24 * 1024 * 1024
-
-
-def vmem_spec():
-    return pl.BlockSpec(memory_space=pltpu.VMEM)
-
-
-def smem_spec():
-    return pl.BlockSpec(memory_space=pltpu.SMEM)
-
-
-def call(body, outs, args, scalars, flops, scratch=()):
+VMEM_BYTES = 14 * 1024 * 1024
+
+
+def call(body, outs, args, spaces, flops, scratch=()):
+    kinds = {"s": pltpu.SMEM, "v": pltpu.VMEM, "h": pltpu.HBM}
     moved = sum(a.size * a.dtype.itemsize for a in args) + sum(o.size * o.dtype.itemsize for o in outs)
     return pl.pallas_call(
         body,
         out_shape=outs,
-        in_specs=[smem_spec()] * scalars + [vmem_spec()] * (len(args) - scalars),
-        out_specs=[vmem_spec()] * len(outs),
+        in_specs=[pl.BlockSpec(memory_space=kinds[c]) for c in spaces],
+        out_specs=[pl.BlockSpec(memory_space=pltpu.VMEM)] * len(outs),
         scratch_shapes=list(scratch),
         compiler_params=pltpu.CompilerParams(vmem_limit_bytes=VMEM_BYTES),
         cost_estimate=pl.CostEstimate(flops=flops, bytes_accessed=moved, transcendentals=0),
@@ -46,38 +39,56 @@
     return jnp.int32(0), beside, across, -across, -beside
 
 
-def add_products(list_ref, count_ref, sigma_ref, offset, pairs):
-    slot = jnp.int32(0)
-    live = jnp.int32(0)
-    for s in range(sigma_ref.shape[0]):
-        hit = (list_ref[s] == offset) & (s < count_ref[0])
-        slot = jnp.where(hit, s, slot)
-        live = jnp.where(hit, 1, live)
-
-    @pl.when(live == 1)
-    def _():
-        for acc_ref, panel_ref in pairs:
-            acc_ref[...] += dot(sigma_ref[slot], panel_ref[...])
-
-
-def near_kernel(where_ref, list_ref, count_ref, sigma_ref, first, second, first_beside, second_beside,
-                first_acc, second_acc, turned_ref):
-    own, beside = offsets_of(where_ref)[:2]
-    first_acc[...] = jnp.zeros_like(first_acc)
-    second_acc[...] = jnp.zeros_like(second_acc)
-    add_products(list_ref, count_ref, sigma_ref, own, ((first_acc, first), (second_acc, second)))
-    add_products(list_ref, count_ref, sigma_ref, beside, ((first_acc, first_beside), (second_acc, second_beside)))
+def near_kernel(where_ref, list_ref, count_ref, sigma_hbm, first_hbm, second_hbm, lower_hbm, first_beside, second_beside,
+                first_acc, second_acc, turned_ref, sigma_ref, lower_ref, near_ref, first, second, sems):
+    lives = []
+    copies = []
+    for index, offset in enumerate(offsets_of(where_ref)):
+        slot = jnp.int32(0)
+        live = jnp.int32(0)
+        for s in range(sigma_hbm.shape[0]):
+            hit = (list_ref[s] == offset) & (s < count_ref[0])
+            slot = jnp.where(hit, s, slot)
+            live = jnp.where(hit, 1, live)
+        target = near_ref.at[index] if index < 2 else sigma_ref.at[index - 2]
+        lives.append((live, target))
+        copies.append(pltpu.make_async_copy(sigma_hbm.at[slot], target, sems.at[index]))
+    copies.append(pltpu.make_async_copy(first_hbm, first, sems.at[5]))
+    copies.append(pltpu.make_async_copy(second_hbm, second, sems.at[6]))
+    copies.append(pltpu.make_async_copy(lower_hbm, lower_ref, sems.at[7]))
+    for index in (0, 5, 6, 1, 2, 3, 4, 7):
+        copies[index].start()
+
+    def arrived(index):
+        copies[index].wait()
+        live, target = lives[index]
+
+        @pl.when(live == 0)
+        def _():
+            target[...] = jnp.zeros(target.shape, target.dtype)
+
+    copies[5].wait()
+    copies[6].wait()
+    arrived(0)
+    first_acc[...] = dot(near_ref[0], first[...])
+    second_acc[...] = dot(near_ref[0], second[...])
     size = first.shape[0]
     turned_ref[:size] = first[...].T
     turned_ref[size:] = second[...].T
-
-
-def across_kernel(where_ref, list_ref, count_ref, sigma_ref, first_in, second_in, first_across, second_across,
-                  first_acc, second_acc):
-    first_acc[...] = first_in[...]
-    second_acc[...] = second_in[...]
-    across = offsets_of(where_ref)[2]
-    add_products(list_ref, count_ref, sigma_ref, across, ((first_acc, first_across), (second_acc, second_across)))
+    arrived(1)
+    first_acc[...] += dot(near_ref[1], first_beside[...])
+    second_acc[...] += dot(near_ref[1], second_beside[...])
+    for index in (2, 3, 4):
+        arrived(index)
+    copies[7].wait()
+
+
+def add_far(acc_ref, sigma_ref, index, parts):
+    start = 0
+    for part in parts:
+        rows = part.shape[0]
+        acc_ref[...] += dot(sigma_ref[index, :, start : start + rows], part[...])
+        start += rows
 
 
 def halves(value, where_ref, scratch_ref, give_ref, keep_ref, index):
@@ -88,29 +99,30 @@
     give_ref[index] = scratch_ref[pl.ds(pl.multiple_of((1 - core) * half, half), half)].astype(jnp.bfloat16)
 
 
-def first_kernel(where_ref, list_ref, count_ref, sigma_ref, acc_in, far, rest, turned_ref,
-                 column_ref, give_ref, keep_ref, acc_ref):
+def first_kernel(where_ref, acc_in, across_0, across_1, far_0, far_1, rest, sigma_ref, turned_ref,
+                 column_ref, again_ref, give_ref, keep_ref, acc_ref):
     acc_ref[...] = acc_in[...]
-    offsets = offsets_of(where_ref)
-    add_products(list_ref, count_ref, sigma_ref, offsets[3], ((acc_ref, far),))
-    add_products(list_ref, count_ref, sigma_ref, offsets[4], ((acc_ref, rest),))
+    add_far(acc_ref, sigma_ref, 0, (across_0, across_1))
+    add_far(acc_ref, sigma_ref, 1, (far_0, far_1))
+    add_far(acc_ref, sigma_ref, 2, (rest,))
     column = (-acc_ref[...]).astype(jnp.bfloat16)
     column_ref[...] = column
+    again_ref[...] = column
     size = column.shape[0]
     halves(-dot(turned_ref[:size], column), where_ref, acc_ref, give_ref, keep_ref, 0)
     halves(dot(turned_ref[size:], column), where_ref, acc_ref, give_ref, keep_ref, 1)
 
 
-def lower_kernel(acc_in, column_ref, lower_ref, acc_ref):
+def across_kernel(acc_in, column_ref, lower_ref, across_0, across_1, sigma_ref, acc_ref):
     acc_ref[...] = acc_in[...] + dot(column_ref[...], lower_ref[...])
-
-
-def second_kernel(where_ref, list_ref, count_ref, sigma_ref, acc_in, far, rest, turned_ref,
+    add_far(acc_ref, sigma_ref, 0, (across_0, across_1))
+
+
+def second_kernel(where_ref, acc_in, far_0, far_1, rest, sigma_ref, turned_ref,
                   column_ref, give_ref, keep_ref, acc_ref):
     acc_ref[...] = acc_in[...]
-    offsets = offsets_of(where_ref)
-    add_products(list_ref, count_ref, sigma_ref, offsets[3], ((acc_ref, far),))
-    add_products(list_ref, count_ref, sigma_ref, offsets[4], ((acc_ref, rest),))
+    add_far(acc_ref, sigma_ref, 1, (far_0, far_1))
+    add_far(acc_ref, sigma_ref, 2, (rest,))
     column = (-acc_ref[...]).astype(jnp.bfloat16)
     column_ref[...] = column
     size = column.shape[0]
@@ -160,7 +172,8 @@
 
 def rest_of(across, far, member, devices):
     give_across = (member == 0) | (member == 3)
-    return swapped(jnp.where(give_across, across, far), 1, devices)
+    pieces = [jnp.where(give_across, a, f) for a, f in zip(across, far)]
+    return swapped(jnp.concatenate(pieces, axis=0), 1, devices)
 
 
 def core_summed(give, keep, position, devices):
@@ -211,43 +224,60 @@
     def parts(k):
         return [jax.ShapeDtypeStruct((k, half, width), t) for t in (jnp.bfloat16, jnp.float32)]
 
-    scalars = [where, listed, count, sigma]
-    across = swapped(first, 2, devices)
+    barrier = lax.optimization_barrier
+
+    across = [swapped(first[:half], 2, devices), swapped(first[half:], 2, devices)]
     beside = swapped(first, 1, devices)
     second_beside = swapped(second, 1, devices)
-    first_acc, second_acc, turned = call(
+    first_acc, second_acc, turned, sorted_sigma, lower = call(
         near_kernel,
-        [wide, wide, jax.ShapeDtypeStruct((2 * size, width), jnp.bfloat16)],
-        scalars + [first, second, beside, second_beside],
-        3,
+        [wide, wide, jax.ShapeDtypeStruct((2 * size, width), jnp.bfloat16),
+         jax.ShapeDtypeStruct((3, size, width), jnp.bfloat16), narrow],
+        [where, listed, count, sigma, first, second, lower_panel, beside, second_beside],
+        "ssshhhhvv",
         4 * one,
-    )
-    across, later = lax.optimization_barrier((across, second))
-    far = far_of(across, devices)
-    second_across = swapped(later, 2, devices)
+        [pltpu.VMEM((2, size, width), jnp.bfloat16), pltpu.VMEM((size, width), jnp.bfloat16),
+         pltpu.VMEM((size, width), jnp.bfloat16), pltpu.SemaphoreType.DMA((8,))],
+    )
+    across[0], turned, later_0 = barrier((across[0], turned, second[:half]))
+    far = [far_of(across[0], devices)]
+    second_across = [swapped(later_0, 2, devices)]
+    across[1], later_1 = barrier((across[1], second[half:]))
+    far.append(far_of(across[1], devices))
+    second_across.append(swapped(later_1, 2, devices))
+    far, second_across = barrier((far, second_across))
     rest = rest_of(across, far, member, devices)
-    second_far = far_of(second_across, devices)
-    first_acc, second_acc = call(
-        across_kernel, [wide, wide], scalars + [first_acc, second_acc, across, second_across], 3, 2 * one
-    )
-    column_first, give, keep = call(
-        first_kernel, [narrow] + parts(2), scalars + [first_acc, far, rest, turned], 3, 4 * one, scratch
-    )
-    give, second_across = lax.optimization_barrier((give, second_across))
+    second_far = [far_of(piece, devices) for piece in second_across]
+    column_first, column_again, give, keep = call(
+        first_kernel,
+        [narrow, narrow] + parts(2),
+        [where, first_acc, *across, *far, rest, sorted_sigma, turned],
+        "svvvvvvvv",
+        5 * one,
+        scratch,
+    )
+    give, second_across = barrier((give, second_across))
     second_rest = rest_of(second_across, second_far, member, devices)
     give, keep = core_summed(give, keep, position, devices)
-    (second_acc,) = call(lower_kernel, [wide], [second_acc, column_first, lower_panel], 0, one)
-    give, second_rest = lax.optimization_barrier((give, second_rest))
+    (second_acc,) = call(
+        across_kernel, [wide], [second_acc, column_again, lower, *second_across, sorted_sigma], "vvvvvv", 2 * one
+    )
+    give, second_rest = barrier((give, second_rest))
     column_second, second_give, second_keep = call(
-        second_kernel, [narrow] + parts(1), scalars + [second_acc, second_far, second_rest, turned], 3, 3 * one, scratch
+        second_kernel,
+        [narrow] + parts(1),
+        [where, second_acc, *second_far, second_rest, sorted_sigma, turned],
+        "svvvvvv",
+        3 * one,
+        scratch,
     )
     mine, other = summed(give, keep, position, devices)
     second_give, second_keep = core_summed(second_give, second_keep, position, devices)
     second_mine, second_other = summed(second_give, second_keep, position, devices)
     block_first, block_link, base = call(
-        link_kernel, [wide] * 3, [where, mine, other, lower_panel, first_diag, second_diag], 1, 4 * one, scratch
-    )
-    (block_second,) = call(last_kernel, [wide], [where, second_mine, second_other, base], 1, size * width)
+        link_kernel, [wide] * 3, [where, mine, other, lower, first_diag, second_diag], "svvvvv", 4 * one, scratch
+    )
+    (block_second,) = call(last_kernel, [wide], [where, second_mine, second_other, base], "svvv", size * width)
     shape = first_panel.shape
     return column_first.reshape(shape), block_first, block_link, column_second.reshape(shape), block_second
 

time: 106 us -> 120 us (1.13); the launches traced: 106 us -> 119 us
  waiting for transfers between devices: 49.9 us -> 36.3 us
  starting transfers between devices: 27.1 us -> 38.4 us
  local copies, waits for them, and re-layouts: 12.7 us -> 23.7 us
  Pallas kernels: 10.3 us -> 12.7 us
  other arithmetic: 4.39 us -> 5.81 us
    ppermute x22 -> x24, waiting for transfers between devices: 40.3 us -> 30.8 us  [swapped(): return lax.ppermute(value, 'row', [(i, i ^ bit) for i in range(devices)])]
    ppermute x2 -> x4, starting transfers between devices: 7.22 us -> 15.5 us  [far_of(): lax.ppermute(across, 'row', [(a, b) for a, b in hops if 0 <= b < devices])]
    unnamed x36 -> x56, local copies, waits for them, and re-layouts: 11.8 us -> 19.2 us
    ppermute x2 -> x4, waiting for transfers between devices: 9.61 us -> 5.45 us  [far_of(): lax.ppermute(across, 'row', [(a, b) for a, b in hops if 0 <= b < devices])]
    slice x0 -> x2, local copies, waits for them, and re-layouts: none -> 3.64 us  [the longest x1 1.86 us: shards(): across[1], later_1 = barrier((across[1], second[half:]))]
    ppermute x22 -> x24, starting transfers between devices: 19.8 us -> 22.8 us  [swapped(): return lax.ppermute(value, 'row', [(i, i ^ bit) for i in range(devices)])]
    pallas_call x7 -> x6, Pallas kernels: 10.3 us -> 12.7 us  [call(): pl.pallas_call(body, out_shape=outs, in_specs=[pl.BlockSpec(memory_space=...]
  transfers between devices with their start and end apart: 24 -> 28, of which waited for: 14 -> 14; matrix products, arithmetic and copies ran while one was open for 5% -> 8% of each run, Pallas kernels for 7% -> 8%
where the time goes in v4:
time: 120 us; the launch traced here: 119 us
  starting transfers between devices  38.4 us (32%)
  waiting for transfers between devices  36.3 us (30%)
  local copies, waits for them, and re-layouts  23.7 us (20%)
  Pallas kernels  12.7 us (11%)
  other arithmetic  5.81 us (5%)
  between operations  1.68 us (1%)
    ppermute x24, waiting for transfers between devices, swapped(): return lax.ppermute(value, 'row', [(i, i ^ bit) for i in range(devices)])  30.8 us
    ppermute x24, starting transfers between devices, swapped(): return lax.ppermute(value, 'row', [(i, i ^ bit) for i in range(devices)])  22.8 us
    unnamed x56, local copies, waits for them, and re-layouts  19.2 us
    ppermute x4, starting transfers between devices, far_of(): lax.ppermute(across, 'row', [(a, b) for a, b in hops if 0 <= b < devices])  15.5 us
    pallas_call x6, Pallas kernels, call(): pl.pallas_call(body, out_shape=outs, in_specs=[pl.BlockSpec(memory_space=...  12.7 us
    ppermute x4, waiting for transfers between devices, far_of(): lax.ppermute(across, 'row', [(a, b) for a, b in hops if 0 <= b < devices])  5.45 us
  transfers between devices with their start and end apart: 28, of which 14 were waited for; matrix products, arithmetic and copies ran while one was open for 8% of the time, Pallas kernels for 8%

profile of v4, /device:TPU:0, one launch (start us, length us, event | category | flops | bytes accessed | tf_op | source)
XLA Modules:
  0.0 118.6 jit_solution(11792418971765290054)
XLA Ops:
  1.2 1.8 %slice_bitcast_fusion.1 = (bf16[256,512]{1,0:T(8,128)(2,1)S(1)}, bf16[256,512]{1,0:T(8,128)(2,1)}) fusion(bf16[1,1,512,512]{3,2,1,0:T(8,128)(2,1)} %param.9), kind=kLoop, calls=%fused_computation.15 | loop fusion | bytes 1048576 | tf_op jit(solution)/shard_map/slice | solution.py:229
  3.0 2.9 %collective-permute-start.3 = (bf16[256,512]{1,0:T(8,128)(2,1)S(1)}, bf16[256,512]{1,0:T(8,128)(2,1)S(1)}, u32[]{:S(2)}, u32[]{:S(2)}) collective-permute-start(bf16[256,512]{1,0:T(8,128)(2,1)S(1)} %get-tuple-element.67), channel_id=1, source_target_pairs={{0,2},{1,3},{2,0},{3,1},{4,6},{5,7},{6,4},{7,5},{8,10},{9,11},{10,... | collective-permute-start | bytes 786440 | tf_op jit(solution)/shard_map/ppermute | solution.py:165
  6.6 1.9 %slice_bitcast_fusion = (bf16[256,512]{1,0:T(8,128)(2,1)}, bf16[256,512]{1,0:T(8,128)(2,1)}) fusion(bf16[1,1,512,512]{3,2,1,0:T(8,128)(2,1)} %param.10), kind=kLoop, calls=%fused_computation.14 | loop fusion | bytes 1048576 | tf_op jit(solution)/shard_map/slice | solution.py:245
  8.5 4.6 %collective-permute-done.3.across_1 = bf16[256,512]{1,0:T(8,128)(2,1)S(1)} collective-permute-done((bf16[256,512]{1,0:T(8,128)(2,1)S(1)}, bf16[256,512]{1,0:T(8,128)(2,1)S(1)}, u32[]{:S(2)}, u32[]{:S(2)}) %collective-permute-start.3) | collective-permute-done | bytes 262176 | tf_op jit(solution)/shard_map/ppermute | solution.py:165
  13.0 4.7 %collective-permute-start.5 = (bf16[256,512]{1,0:T(8,128)(2,1)S(1)}, bf16[256,512]{1,0:T(8,128)(2,1)}, u32[]{:S(2)}, u32[]{:S(2)}) collective-permute-start(bf16[256,512]{1,0:T(8,128)(2,1)S(1)} %collective-permute-done.3.across_1), channel_id=1, source_target_pairs={{0,4},{1,5},{4,8},{5,9},{6,2},{7,3},{8,12},{9,13},{10,6},{11,7},{1... | collective-permute-start | bytes 786440 | tf_op jit(solution)/shard_map/ppermute | solution.py:170
  19.4 1.7 %copy-done = bf16[1,1,5,512,512]{4,3,2,1,0:T(8,128)(2,1)S(1)} copy-done((bf16[1,1,5,512,512]{4,3,2,1,0:T(8,128)(2,1)S(1)}, bf16[1,1,5,512,512]{4,3,2,1,0:T(8,128)(2,1)}, u32[]{:S(2)}) %copy-start) | copy-done | bytes 2621464
  27.0 2.4 %shard_map.119 = (f32[512,512]{1,0:T(8,128)S(1)}, f32[512,512]{1,0:T(8,128)S(1)}, bf16[1024,512]{1,0:T(8,128)(2,1)S(1)}, bf16[3,512,512]{2,1,0:T(8,128)(2,1)S(1)}, bf16[512,512]{1,0:T(8,128)(2,1)S(1)}) custom-call(s32[1]{0:T(128)} %bitcast.where_ref, s32[5]{0:T(128)S(1)} %bitcast.64, s32[1]{0:T(128)} %bitcast.58.count_ref, ...), custom_call_target="tpu_custom_call" | custom-call | flops 1073741824 | bytes 10485788 | tf_op jit(solution)/shard_map/pallas_call | solution.py:16
  32.1 3.8 %collective-permute-start.4 = (bf16[256,512]{1,0:T(8,128)(2,1)}, bf16[256,512]{1,0:T(8,128)(2,1)}, u32[]{:S(2)}, u32[]{:S(2)}) collective-permute-start(bf16[256,512]{1,0:T(8,128)(2,1)} %collective-permute-done.2.across_0), channel_id=1, source_target_pairs={{0,4},{1,5},{4,8},{5,9},{6,2},{7,3},{8,12},{9,13},{10,6},{11,7},{1... | collective-permute-start | bytes 786440 | tf_op jit(solution)/shard_map/ppermute | solution.py:170
  36.0 3.5 %collective-permute-done.4.far_0 = bf16[256,512]{1,0:T(8,128)(2,1)} collective-permute-done((bf16[256,512]{1,0:T(8,128)(2,1)}, bf16[256,512]{1,0:T(8,128)(2,1)}, u32[]{:S(2)}, u32[]{:S(2)}) %collective-permute-start.4) | collective-permute-done | bytes 262176 | tf_op jit(solution)/shard_map/ppermute | solution.py:170
  39.4 3.1 %collective-permute-done.6.across_0 = bf16[256,512]{1,0:T(8,128)(2,1)S(1)} collective-permute-done((bf16[256,512]{1,0:T(8,128)(2,1)}, bf16[256,512]{1,0:T(8,128)(2,1)S(1)}, u32[]{:S(2)}, u32[]{:S(2)}) %collective-permute-start.6) | collective-permute-done | bytes 262176 | tf_op jit(solution)/shard_map/ppermute | solution.py:165
  43.7 2.8 %collective-permute-start.10 = (bf16[256,512]{1,0:T(8,128)(2,1)S(1)}, bf16[256,512]{1,0:T(8,128)(2,1)S(1)}, u32[]{:S(2)}, u32[]{:S(2)}) collective-permute-start(bf16[256,512]{1,0:T(8,128)(2,1)S(1)} %collective-permute-done.6.across_0), channel_id=1, source_target_pairs={{0,4},{1,5},{4,8},{5,9},{6,2},{7,3},{8,12},{9,13},{10,6},{11,7},{1... | collective-permute-start | bytes 786440 | tf_op jit(solution)/shard_map/ppermute | solution.py:170
  46.5 4.1 %collective-permute-start.11 = (bf16[256,512]{1,0:T(8,128)(2,1)S(1)}, bf16[256,512]{1,0:T(8,128)(2,1)S(1)}, u32[]{:S(2)}, u32[]{:S(2)}) collective-permute-start(bf16[256,512]{1,0:T(8,128)(2,1)S(1)} %collective-permute-done.7.across_1), channel_id=1, source_target_pairs={{0,4},{1,5},{4,8},{5,9},{6,2},{7,3},{8,12},{9,13},{10,6},{11,7},{1... | collective-permute-start | bytes 786440 | tf_op jit(solution)/shard_map/ppermute | solution.py:170
  51.6 3.7 %shard_map.120 = (bf16[512,512]{1,0:T(8,128)(2,1)}, bf16[512,512]{1,0:T(8,128)(2,1)S(1)}, bf16[2,256,512]{2,1,0:T(8,128)(2,1)}, f32[2,256,512]{2,1,0:T(8,128)S(1)}) custom-call(s32[1]{0:T(128)} %bitcast.where_ref, f32[512,512]{1,0:T(8,128)S(1)} %copy-done.10, bf16[256,512]{1,0:T(8,128)(2,1)} %collective-permute-done.2.across_0, ...), custom_call_target="tpu_custom_call" | custom-call | flops 1342177280 | bytes 7864324 | tf_op jit(solution)/shard_map/pallas_call | solution.py:16
  56.3 2.0 %collective-permute-done.11.far_1 = bf16[256,512]{1,0:T(8,128)(2,1)S(1)} collective-permute-done((bf16[256,512]{1,0:T(8,128)(2,1)S(1)}, bf16[256,512]{1,0:T(8,128)(2,1)S(1)}, u32[]{:S(2)}, u32[]{:S(2)}) %collective-permute-start.11) | collective-permute-done | bytes 262176 | tf_op jit(solution)/shard_map/ppermute | solution.py:170
  59.9 1.2 %copy-done.4 = f32[512,512]{1,0:T(8,128)S(1)} copy-done((f32[512,512]{1,0:T(8,128)S(1)}, f32[512,512]{1,0:T(8,128)}, u32[]{:S(2)}) %copy-start.4) | copy-done | bytes 1048600
  64.4 1.2 %convert_add_fusion = f32[2,256,512]{2,1,0:T(8,128)S(1)} fusion(f32[2,256,512]{2,1,0:T(8,128)S(1)} %copy-done.6, bf16[2,256,512]{2,1,0:T(8,128)(2,1)} %collective-permute-done.9), kind=kLoop, calls=%fused_computation | loop fusion | flops 524288 | bytes 2621440 | tf_op jit(solution)/shard_map/add | solution.py:180
  66.5 2.6 %shard_map.123 = (bf16[512,512]{1,0:T(8,128)(2,1)}, bf16[1,256,512]{2,1,0:T(8,128)(2,1)S(1)}, f32[1,256,512]{2,1,0:T(8,128)S(1)}) custom-call(s32[1]{0:T(128)} %bitcast.where_ref, f32[512,512]{1,0:T(8,128)S(1)} %shard_map.122.acc_in, bf16[256,512]{1,0:T(8,128)(2,1)S(1)} %collective-permute-done.10.far_0, bf16[256,512]{1,0:T(8,128)(2,1)S(1)} %copy-done.8, ...), custom_call_target="tpu_custom_call" | custom-call | flops 805306368 | bytes 6029316 | tf_op jit(solution)/shard_map/pallas_call | solution.py:16
  70.4 2.1 %collective-permute-start.13 = (bf16[2,128,512]{2,1,0:T(8,128)(2,1)}, bf16[2,128,512]{2,1,0:T(8,128)(2,1)S(1)}, u32[]{:S(2)}, u32[]{:S(2)}) collective-permute-start(bf16[2,128,512]{2,1,0:T(8,128)(2,1)} %fusion), channel_id=1, source_target_pairs={{0,2},{1,3},{2,0},{3,1},{4,6},{5,7},{6,4},{7,5},{8,10},{9,11},{10,... | collective-permute-start | bytes 786440 | tf_op jit(solution)/shard_map/ppermute | solution.py:165
  73.6 1.2 %collective-permute-start.21 = (bf16[1,128,512]{2,1,0:T(8,128)(2,1)S(1)}, bf16[1,128,512]{2,1,0:T(8,128)(2,1)S(1)}, u32[]{:S(2)}, u32[]{:S(2)}) collective-permute-start(bf16[1,128,512]{2,1,0:T(8,128)(2,1)S(1)} %fusion.2), channel_id=1, source_target_pairs={{0,2},{1,3},{2,0},{3,1},{4,6},{5,7},{6,4},{7,5},{8,10},{9,11},{10,... | collective-permute-start | bytes 393224 | tf_op jit(solution)/shard_map/ppermute | solution.py:165
  74.8 4.9 %collective-permute-done.13 = bf16[2,128,512]{2,1,0:T(8,128)(2,1)S(1)} collective-permute-done((bf16[2,128,512]{2,1,0:T(8,128)(2,1)}, bf16[2,128,512]{2,1,0:T(8,128)(2,1)S(1)}, u32[]{:S(2)}, u32[]{:S(2)}) %collective-permute-start.13) | collective-permute-done | bytes 262176 | tf_op jit(solution)/shard_map/ppermute | solution.py:165
  80.9 2.6 %collective-permute-start.14 = (bf16[2,64,512]{2,1,0:T(8,128)(2,1)S(1)}, bf16[2,64,512]{2,1,0:T(8,128)(2,1)S(1)}, u32[]{:S(2)}, u32[]{:S(2)}) collective-permute-start(bf16[2,64,512]{2,1,0:T(8,128)(2,1)S(1)} %fusion.1), channel_id=1, source_target_pairs={{0,4},{1,5},{2,6},{3,7},{4,0},{5,1},{6,2},{7,3},{8,12},{9,13},{10,... | collective-permute-start | bytes 393224 | tf_op jit(solution)/shard_map/ppermute | solution.py:165
  84.2 2.2 %collective-permute-done.14 = bf16[2,64,512]{2,1,0:T(8,128)(2,1)S(1)} collective-permute-done((bf16[2,64,512]{2,1,0:T(8,128)(2,1)S(1)}, bf16[2,64,512]{2,1,0:T(8,128)(2,1)S(1)}, u32[]{:S(2)}, u32[]{:S(2)}) %collective-permute-start.14) | collective-permute-done | bytes 131104 | tf_op jit(solution)/shard_map/ppermute | solution.py:165
  86.5 4.4 %collective-permute-start.15 = (bf16[2,32,512]{2,1,0:T(8,128)(2,1)S(1)}, bf16[2,32,512]{2,1,0:T(8,128)(2,1)S(1)}, u32[]{:S(2)}, u32[]{:S(2)}) collective-permute-start(bf16[2,32,512]{2,1,0:T(8,128)(2,1)S(1)} %fusion.5), channel_id=1, source_target_pairs={{0,8},{1,9},{2,10},{3,11},{4,12},{5,13},{6,14},{7,15},{8,0},{9,1},... | collective-permute-start | bytes 196616 | tf_op jit(solution)/shard_map/ppermute | solution.py:165
  91.9 3.9 %collective-permute-done.15 = bf16[2,32,512]{2,1,0:T(8,128)(2,1)S(1)} collective-permute-done((bf16[2,32,512]{2,1,0:T(8,128)(2,1)S(1)}, bf16[2,32,512]{2,1,0:T(8,128)(2,1)S(1)}, u32[]{:S(2)}, u32[]{:S(2)}) %collective-permute-start.15) | collective-permute-done | bytes 65568 | tf_op jit(solution)/shard_map/ppermute | solution.py:165
  96.9 2.1 %collective-permute-start.24 = (bf16[1,32,512]{2,1,0:T(8,128)(2,1)S(1)}, bf16[1,32,512]{2,1,0:T(8,128)(2,1)S(1)}, u32[]{:S(2)}, u32[]{:S(2)}) collective-permute-start(bf16[1,32,512]{2,1,0:T(8,128)(2,1)S(1)} %fusion.6), channel_id=1, source_target_pairs={{0,8},{1,9},{2,10},{3,11},{4,12},{5,13},{6,14},{7,15},{8,0},{9,1},... | collective-permute-start | bytes 98312 | tf_op jit(solution)/shard_map/ppermute | solution.py:165
  99.0 2.5 %collective-permute-done.16 = bf16[2,32,512]{2,1,0:T(8,128)(2,1)S(1)} collective-permute-done((bf16[2,32,512]{2,1,0:T(8,128)(2,1)S(1)}, bf16[2,32,512]{2,1,0:T(8,128)(2,1)S(1)}, u32[]{:S(2)}, u32[]{:S(2)}) %collective-permute-start.16) | collective-permute-done | bytes 65568 | tf_op jit(solution)/shard_map/ppermute | solution.py:165
  101.9 1.9 %collective-permute-start.25 = (bf16[1,64,512]{2,1,0:T(8,128)(2,1)S(1)}, bf16[1,64,512]{2,1,0:T(8,128)(2,1)S(1)}, u32[]{:S(2)}, u32[]{:S(2)}) collective-permute-start(bf16[1,64,512]{2,1,0:T(8,128)(2,1)S(1)} %pad_maximum_fusion.7), channel_id=1, source_target_pairs={{0,4},{1,5},{2,6},{3,7},{4,0},{5,1},{6,2},{7,3},{8,12},{9,13},{10,... | collective-permute-start | bytes 196616 | tf_op jit(solution)/shard_map/ppermute | solution.py:165
  103.7 2.8 %collective-permute-done.17 = bf16[2,64,512]{2,1,0:T(8,128)(2,1)S(1)} collective-permute-done((bf16[2,64,512]{2,1,0:T(8,128)(2,1)S(1)}, bf16[2,64,512]{2,1,0:T(8,128)(2,1)S(1)}, u32[]{:S(2)}, u32[]{:S(2)}) %collective-permute-start.17) | collective-permute-done | bytes 131104 | tf_op jit(solution)/shard_map/ppermute | solution.py:165
  107.3 1.5 %collective-permute-start.26 = (bf16[1,128,512]{2,1,0:T(8,128)(2,1)S(1)}, bf16[1,128,512]{2,1,0:T(8,128)(2,1)S(1)}, u32[]{:S(2)}, u32[]{:S(2)}) collective-permute-start(bf16[1,128,512]{2,1,0:T(8,128)(2,1)S(1)} %pad_maximum_fusion.6), channel_id=1, source_target_pairs={{0,2},{1,3},{2,0},{3,1},{4,6},{5,7},{6,4},{7,5},{8,10},{9,11},{10,... | collective-permute-start | bytes 393224 | tf_op jit(solution)/shard_map/ppermute | solution.py:165
  108.9 4.2 %collective-permute-done.18 = bf16[2,128,512]{2,1,0:T(8,128)(2,1)S(1)} collective-permute-done((bf16[2,128,512]{2,1,0:T(8,128)(2,1)S(1)}, bf16[2,128,512]{2,1,0:T(8,128)(2,1)S(1)}, u32[]{:S(2)}, u32[]{:S(2)}) %collective-permute-start.18) | collective-permute-done | bytes 262176 | tf_op jit(solution)/shard_map/ppermute | solution.py:165
  113.3 1.2 collective-permute-done.26
  115.2 2.2 %shard_map.121 = (f32[512,512]{1,0:T(8,128)}, f32[512,512]{1,0:T(8,128)}, f32[512,512]{1,0:T(8,128)S(1)}) custom-call(s32[1]{0:T(128)} %bitcast.where_ref, bf16[2,256,512]{2,1,0:T(8,128)(2,1)S(1)} %pad_maximum_fusion.2.mine_ref, bf16[2,256,512]{2,1,0:T(8,128)(2,1)S(1)} %collective-permute-done.19.other_ref, bf16[512,512]{1,0:T(8,128)(2,1)S(1)} %copy-done.16, ...), custom_call_target="tpu_custom_call" | custom-call | flops 1073741824 | bytes 6815748 | tf_op jit(solution)/shard_map/pallas_call | solution.py:16
  (119 shorter events, 29.1 us)
Async XLA Ops:
  0.6 17.2 %collective-permute-start = (bf16[512,512]{1,0:T(8,128)(2,1)}, bf16[512,512]{1,0:T(8,128)(2,1)S(1)}, u32[]{:S(2)}, u32[]{:S(2)}) collective-permute-start(bf16[512,512]{1,0:T(8,128)(2,1)} %bitcast.60), channel_id=1, source_target_pairs={{0,1},{1,0},{2,3},{3,2},{4,5},{5,4},{6,7},{7,6},{8,9},{9,8},{10,11... | collective-permute-start | bytes 1572872 | tf_op jit(solution)/shard_map/ppermute | solution.py:165
  1.1 17.4 %collective-permute-start.1 = (bf16[512,512]{1,0:T(8,128)(2,1)}, bf16[512,512]{1,0:T(8,128)(2,1)S(1)}, u32[]{:S(2)}, u32[]{:S(2)}) collective-permute-start(bf16[512,512]{1,0:T(8,128)(2,1)} %bitcast.62), channel_id=1, source_target_pairs={{0,1},{1,0},{2,3},{3,2},{4,5},{5,4},{6,7},{7,6},{8,9},{9,8},{10,11... | collective-permute-start | bytes 1572872 | tf_op jit(solution)/shard_map/ppermute | solution.py:165
  3.0 10.0 %collective-permute-start.3 = (bf16[256,512]{1,0:T(8,128)(2,1)S(1)}, bf16[256,512]{1,0:T(8,128)(2,1)S(1)}, u32[]{:S(2)}, u32[]{:S(2)}) collective-permute-start(bf16[256,512]{1,0:T(8,128)(2,1)S(1)} %get-tuple-element.67), channel_id=1, source_target_pairs={{0,2},{1,3},{2,0},{3,1},{4,6},{5,7},{6,4},{7,5},{8,10},{9,11},{10,... | collective-permute-start | bytes 786440 | tf_op jit(solution)/shard_map/ppermute | solution.py:165
  5.9 26.2 %collective-permute-start.2 = (bf16[256,512]{1,0:T(8,128)(2,1)}, bf16[256,512]{1,0:T(8,128)(2,1)}, u32[]{:S(2)}, u32[]{:S(2)}) collective-permute-start(bf16[256,512]{1,0:T(8,128)(2,1)} %get-tuple-element.68), channel_id=1, source_target_pairs={{0,2},{1,3},{2,0},{3,1},{4,6},{5,7},{6,4},{7,5},{8,10},{9,11},{10,... | collective-permute-start | bytes 786440 | tf_op jit(solution)/shard_map/ppermute | solution.py:165
  13.0 29.5 %copy-start.11 = (bf16[256,512]{1,0:T(8,128)(2,1)}, bf16[256,512]{1,0:T(8,128)(2,1)S(1)}, u32[]{:S(2)}) copy-start(bf16[256,512]{1,0:T(8,128)(2,1)S(1)} %collective-permute-done.3.across_1) | copy-start | bytes 786436
  13.0 22.9 %collective-permute-start.5 = (bf16[256,512]{1,0:T(8,128)(2,1)S(1)}, bf16[256,512]{1,0:T(8,128)(2,1)}, u32[]{:S(2)}, u32[]{:S(2)}) collective-permute-start(bf16[256,512]{1,0:T(8,128)(2,1)S(1)} %collective-permute-done.3.across_1), channel_id=1, source_target_pairs={{0,4},{1,5},{4,8},{5,9},{6,2},{7,3},{8,12},{9,13},{10,6},{11,7},{1... | collective-permute-start | bytes 786440 | tf_op jit(solution)/shard_map/ppermute | solution.py:170
  17.8 18.2 %collective-permute-start.7 = (bf16[256,512]{1,0:T(8,128)(2,1)}, bf16[256,512]{1,0:T(8,128)(2,1)S(1)}, u32[]{:S(2)}, u32[]{:S(2)}) collective-permute-start(bf16[256,512]{1,0:T(8,128)(2,1)} %get-tuple-element.39), channel_id=1, source_target_pairs={{0,2},{1,3},{2,0},{3,1},{4,6},{5,7},{6,4},{7,5},{8,10},{9,11},{10,... | collective-permute-start | bytes 786440 | tf_op jit(solution)/shard_map/ppermute | solution.py:165
  32.1 7.3 %collective-permute-start.4 = (bf16[256,512]{1,0:T(8,128)(2,1)}, bf16[256,512]{1,0:T(8,128)(2,1)}, u32[]{:S(2)}, u32[]{:S(2)}) collective-permute-start(bf16[256,512]{1,0:T(8,128)(2,1)} %collective-permute-done.2.across_0), channel_id=1, source_target_pairs={{0,4},{1,5},{4,8},{5,9},{6,2},{7,3},{8,12},{9,13},{10,6},{11,7},{1... | collective-permute-start | bytes 786440 | tf_op jit(solution)/shard_map/ppermute | solution.py:170
  36.0 6.6 %collective-permute-start.6 = (bf16[256,512]{1,0:T(8,128)(2,1)}, bf16[256,512]{1,0:T(8,128)(2,1)S(1)}, u32[]{:S(2)}, u32[]{:S(2)}) collective-permute-start(bf16[256,512]{1,0:T(8,128)(2,1)} %get-tuple-element.38), channel_id=1, source_target_pairs={{0,2},{1,3},{2,0},{3,1},{4,6},{5,7},{6,4},{7,5},{8,10},{9,11},{10,... | collective-permute-start | bytes 786440 | tf_op jit(solution)/shard_map/ppermute | solution.py:165
  36.0 14.7 %copy-start.10 = (f32[512,512]{1,0:T(8,128)S(1)}, f32[512,512]{1,0:T(8,128)}, u32[]{:S(2)}) copy-start(f32[512,512]{1,0:T(8,128)} %copy-done.9) | copy-start | bytes 3145732
  43.6 7.0 %collective-permute-start.8 = (bf16[512,512]{1,0:T(8,128)(2,1)S(1)}, bf16[512,512]{1,0:T(8,128)(2,1)S(1)}, u32[]{:S(2)}, u32[]{:S(2)}) collective-permute-start(bf16[512,512]{1,0:T(8,128)(2,1)S(1)} %pad_maximum_fusion), channel_id=1, source_target_pairs={{0,1},{1,0},{2,3},{3,2},{4,5},{5,4},{6,7},{7,6},{8,9},{9,8},{10,11... | collective-permute-start | bytes 1572872 | tf_op jit(solution)/shard_map/ppermute | solution.py:165
  43.7 12.6 %collective-permute-start.10 = (bf16[256,512]{1,0:T(8,128)(2,1)S(1)}, bf16[256,512]{1,0:T(8,128)(2,1)S(1)}, u32[]{:S(2)}, u32[]{:S(2)}) collective-permute-start(bf16[256,512]{1,0:T(8,128)(2,1)S(1)} %collective-permute-done.6.across_0), channel_id=1, source_target_pairs={{0,4},{1,5},{4,8},{5,9},{6,2},{7,3},{8,12},{9,13},{10,6},{11,7},{1... | collective-permute-start | bytes 786440 | tf_op jit(solution)/shard_map/ppermute | solution.py:170
  46.5 11.8 %collective-permute-start.11 = (bf16[256,512]{1,0:T(8,128)(2,1)S(1)}, bf16[256,512]{1,0:T(8,128)(2,1)S(1)}, u32[]{:S(2)}, u32[]{:S(2)}) collective-permute-start(bf16[256,512]{1,0:T(8,128)(2,1)S(1)} %collective-permute-done.7.across_1), channel_id=1, source_target_pairs={{0,4},{1,5},{4,8},{5,9},{6,2},{7,3},{8,12},{9,13},{10,6},{11,7},{1... | collective-permute-start | bytes 786440 | tf_op jit(solution)/shard_map/ppermute | solution.py:170
  56.3 7.7 %collective-permute-start.9 = (bf16[2,256,512]{2,1,0:T(8,128)(2,1)}, bf16[2,256,512]{2,1,0:T(8,128)(2,1)}, u32[]{:S(2)}, u32[]{:S(2)}) collective-permute-start(bf16[2,256,512]{2,1,0:T(8,128)(2,1)} %get-tuple-element.49), channel_id=1, source_target_pairs={{0,1},{1,0},{2,3},{3,2},{4,5},{5,4},{6,7},{7,6},{8,9},{9,8},{10,11... | collective-permute-start | bytes 1572872 | tf_op jit(solution)/shard_map/ppermute | solution.py:165
  59.9 6.6 %collective-permute-start.12 = (bf16[512,512]{1,0:T(8,128)(2,1)}, bf16[512,512]{1,0:T(8,128)(2,1)}, u32[]{:S(2)}, u32[]{:S(2)}) collective-permute-start(bf16[512,512]{1,0:T(8,128)(2,1)} %pad_maximum_fusion.1), channel_id=1, source_target_pairs={{0,1},{1,0},{2,3},{3,2},{4,5},{5,4},{6,7},{7,6},{8,9},{9,8},{10,11... | collective-permute-start | bytes 1572872 | tf_op jit(solution)/shard_map/ppermute | solution.py:165
  69.9 2.6 %collective-permute-start.20 = (bf16[1,256,512]{2,1,0:T(8,128)(2,1)S(1)}, bf16[1,256,512]{2,1,0:T(8,128)(2,1)S(1)}, u32[]{:S(2)}, u32[]{:S(2)}) collective-permute-start(bf16[1,256,512]{2,1,0:T(8,128)(2,1)S(1)} %get-tuple-element.61), channel_id=1, source_target_pairs={{0,1},{1,0},{2,3},{3,2},{4,5},{5,4},{6,7},{7,6},{8,9},{9,8},{10,11... | collective-permute-start | bytes 786440 | tf_op jit(solution)/shard_map/ppermute | solution.py:165
  70.4 9.4 %collective-permute-start.13 = (bf16[2,128,512]{2,1,0:T(8,128)(2,1)}, bf16[2,128,512]{2,1,0:T(8,128)(2,1)S(1)}, u32[]{:S(2)}, u32[]{:S(2)}) collective-permute-start(bf16[2,128,512]{2,1,0:T(8,128)(2,1)} %fusion), channel_id=1, source_target_pairs={{0,2},{1,3},{2,0},{3,1},{4,6},{5,7},{6,4},{7,5},{8,10},{9,11},{10,... | collective-permute-start | bytes 786440 | tf_op jit(solution)/shard_map/ppermute | solution.py:165
  73.6 9.9 %collective-permute-start.21 = (bf16[1,128,512]{2,1,0:T(8,128)(2,1)S(1)}, bf16[1,128,512]{2,1,0:T(8,128)(2,1)S(1)}, u32[]{:S(2)}, u32[]{:S(2)}) collective-permute-start(bf16[1,128,512]{2,1,0:T(8,128)(2,1)S(1)} %fusion.2), channel_id=1, source_target_pairs={{0,2},{1,3},{2,0},{3,1},{4,6},{5,7},{6,4},{7,5},{8,10},{9,11},{10,... | collective-permute-start | bytes 393224 | tf_op jit(solution)/shard_map/ppermute | solution.py:165
  80.9 5.5 %collective-permute-start.14 = (bf16[2,64,512]{2,1,0:T(8,128)(2,1)S(1)}, bf16[2,64,512]{2,1,0:T(8,128)(2,1)S(1)}, u32[]{:S(2)}, u32[]{:S(2)}) collective-permute-start(bf16[2,64,512]{2,1,0:T(8,128)(2,1)S(1)} %fusion.1), channel_id=1, source_target_pairs={{0,4},{1,5},{2,6},{3,7},{4,0},{5,1},{6,2},{7,3},{8,12},{9,13},{10,... | collective-permute-start | bytes 393224 | tf_op jit(solution)/shard_map/ppermute | solution.py:165
  83.5 7.4 %collective-permute-start.22 = (bf16[1,64,512]{2,1,0:T(8,128)(2,1)S(1)}, bf16[1,64,512]{2,1,0:T(8,128)(2,1)S(1)}, u32[]{:S(2)}, u32[]{:S(2)}) collective-permute-start(bf16[1,64,512]{2,1,0:T(8,128)(2,1)S(1)} %fusion.4), channel_id=1, source_target_pairs={{0,4},{1,5},{2,6},{3,7},{4,0},{5,1},{6,2},{7,3},{8,12},{9,13},{10,... | collective-permute-start | bytes 196616 | tf_op jit(solution)/shard_map/ppermute | solution.py:165
  86.5 9.4 %collective-permute-start.15 = (bf16[2,32,512]{2,1,0:T(8,128)(2,1)S(1)}, bf16[2,32,512]{2,1,0:T(8,128)(2,1)S(1)}, u32[]{:S(2)}, u32[]{:S(2)}) collective-permute-start(bf16[2,32,512]{2,1,0:T(8,128)(2,1)S(1)} %fusion.5), channel_id=1, source_target_pairs={{0,8},{1,9},{2,10},{3,11},{4,12},{5,13},{6,14},{7,15},{8,0},{9,1},... | collective-permute-start | bytes 196616 | tf_op jit(solution)/shard_map/ppermute | solution.py:165
  90.9 5.9 %collective-permute-start.23 = (bf16[1,32,512]{2,1,0:T(8,128)(2,1)S(1)}, bf16[1,32,512]{2,1,0:T(8,128)(2,1)S(1)}, u32[]{:S(2)}, u32[]{:S(2)}) collective-permute-start(bf16[1,32,512]{2,1,0:T(8,128)(2,1)S(1)} %fusion.7), channel_id=1, source_target_pairs={{0,8},{1,9},{2,10},{3,11},{4,12},{5,13},{6,14},{7,15},{8,0},{9,1},... | collective-permute-start | bytes 98312 | tf_op jit(solution)/shard_map/ppermute | solution.py:165
  95.9 5.6 %collective-permute-start.16 = (bf16[2,32,512]{2,1,0:T(8,128)(2,1)S(1)}, bf16[2,32,512]{2,1,0:T(8,128)(2,1)S(1)}, u32[]{:S(2)}, u32[]{:S(2)}) collective-permute-start(bf16[2,32,512]{2,1,0:T(8,128)(2,1)S(1)} %fusion.3), channel_id=1, source_target_pairs={{0,8},{1,9},{2,10},{3,11},{4,12},{5,13},{6,14},{7,15},{8,0},{9,1},... | collective-permute-start | bytes 196616 | tf_op jit(solution)/shard_map/ppermute | solution.py:165
  96.9 5.0 %collective-permute-start.24 = (bf16[1,32,512]{2,1,0:T(8,128)(2,1)S(1)}, bf16[1,32,512]{2,1,0:T(8,128)(2,1)S(1)}, u32[]{:S(2)}, u32[]{:S(2)}) collective-permute-start(bf16[1,32,512]{2,1,0:T(8,128)(2,1)S(1)} %fusion.6), channel_id=1, source_target_pairs={{0,8},{1,9},{2,10},{3,11},{4,12},{5,13},{6,14},{7,15},{8,0},{9,1},... | collective-permute-start | bytes 98312 | tf_op jit(solution)/shard_map/ppermute | solution.py:165
  101.5 13.7 %copy-start.16 = (bf16[512,512]{1,0:T(8,128)(2,1)S(1)}, bf16[512,512]{1,0:T(8,128)(2,1)}, u32[]{:S(2)}) copy-start(bf16[512,512]{1,0:T(8,128)(2,1)} %copy-done.14) | copy-start | bytes 1572868
  101.5 13.7 %copy-start.25 = (f32[512,512]{1,0:T(8,128)S(1)}, f32[512,512]{1,0:T(8,128)}, u32[]{:S(2)}) copy-start(f32[512,512]{1,0:T(8,128)} %first_diag_ref.1) | copy-start | bytes 3145732
  101.6 5.0 %collective-permute-start.17 = (bf16[2,64,512]{2,1,0:T(8,128)(2,1)S(1)}, bf16[2,64,512]{2,1,0:T(8,128)(2,1)S(1)}, u32[]{:S(2)}, u32[]{:S(2)}) collective-permute-start(bf16[2,64,512]{2,1,0:T(8,128)(2,1)S(1)} %pad_maximum_fusion.5), channel_id=1, source_target_pairs={{0,4},{1,5},{2,6},{3,7},{4,0},{5,1},{6,2},{7,3},{8,12},{9,13},{10,... | collective-permute-start | bytes 393224 | tf_op jit(solution)/shard_map/ppermute | solution.py:165
  101.9 5.4 %collective-permute-start.25 = (bf16[1,64,512]{2,1,0:T(8,128)(2,1)S(1)}, bf16[1,64,512]{2,1,0:T(8,128)(2,1)S(1)}, u32[]{:S(2)}, u32[]{:S(2)}) collective-permute-start(bf16[1,64,512]{2,1,0:T(8,128)(2,1)S(1)} %pad_maximum_fusion.7), channel_id=1, source_target_pairs={{0,4},{1,5},{2,6},{3,7},{4,0},{5,1},{6,2},{7,3},{8,12},{9,13},{10,... | collective-permute-start | bytes 196616 | tf_op jit(solution)/shard_map/ppermute | solution.py:165
  106.7 6.4 %collective-permute-start.18 = (bf16[2,128,512]{2,1,0:T(8,128)(2,1)S(1)}, bf16[2,128,512]{2,1,0:T(8,128)(2,1)S(1)}, u32[]{:S(2)}, u32[]{:S(2)}) collective-permute-start(bf16[2,128,512]{2,1,0:T(8,128)(2,1)S(1)} %pad_maximum_fusion.3), channel_id=1, source_target_pairs={{0,2},{1,3},{2,0},{3,1},{4,6},{5,7},{6,4},{7,5},{8,10},{9,11},{10,... | collective-permute-start | bytes 786440 | tf_op jit(solution)/shard_map/ppermute | solution.py:165
  107.3 7.2 %collective-permute-start.26 = (bf16[1,128,512]{2,1,0:T(8,128)(2,1)S(1)}, bf16[1,128,512]{2,1,0:T(8,128)(2,1)S(1)}, u32[]{:S(2)}, u32[]{:S(2)}) collective-permute-start(bf16[1,128,512]{2,1,0:T(8,128)(2,1)S(1)} %pad_maximum_fusion.6), channel_id=1, source_target_pairs={{0,2},{1,3},{2,0},{3,1},{4,6},{5,7},{6,4},{7,5},{8,10},{9,11},{10,... | collective-permute-start | bytes 393224 | tf_op jit(solution)/shard_map/ppermute | solution.py:165
  113.2 2.0 %collective-permute-start.19 = (bf16[2,256,512]{2,1,0:T(8,128)(2,1)S(1)}, bf16[2,256,512]{2,1,0:T(8,128)(2,1)S(1)}, u32[]{:S(2)}, u32[]{:S(2)}) collective-permute-start(bf16[2,256,512]{2,1,0:T(8,128)(2,1)S(1)} %pad_maximum_fusion.2.mine_ref), channel_id=1, source_target_pairs={{0,1},{1,0},{2,3},{3,2},{4,5},{5,4},{6,7},{7,6},{8,9},{9,8},{10,11... | collective-permute-start | bytes 1572872 | tf_op jit(solution)/shard_map/ppermute | solution.py:165
  114.6 2.9 %collective-permute-start.27 = (bf16[1,256,512]{2,1,0:T(8,128)(2,1)S(1)}, bf16[1,256,512]{2,1,0:T(8,128)(2,1)S(1)}, u32[]{:S(2)}, u32[]{:S(2)}) collective-permute-start(bf16[1,256,512]{2,1,0:T(8,128)(2,1)S(1)} %pad_maximum_fusion.4.mine_ref), channel_id=1, source_target_pairs={{0,1},{1,0},{2,3},{3,2},{4,5},{5,4},{6,7},{7,6},{8,9},{9,8},{10,11... | collective-permute-start | bytes 786440 | tf_op jit(solution)/shard_map/ppermute | solution.py:165
  (24 other events, 41.6 us)

commit v5 on v4

--- a/solution.py
+++ b/solution.py
@@ -39,8 +39,23 @@
     return jnp.int32(0), beside, across, -across, -beside
 
 
-def near_kernel(where_ref, list_ref, count_ref, sigma_hbm, first_hbm, second_hbm, lower_hbm, first_beside, second_beside,
-                first_acc, second_acc, turned_ref, sigma_ref, lower_ref, near_ref, first, second, sems):
+def split_kernel(first_hbm, second_hbm, first_0, first_1, second_0, second_1, sems):
+    half = first_0.shape[0]
+    copies = [
+        pltpu.make_async_copy(source.at[pl.ds(start, half)], target, sems.at[index])
+        for index, (source, start, target) in enumerate(
+            ((first_hbm, 0, first_0), (first_hbm, half, first_1), (second_hbm, 0, second_0), (second_hbm, half, second_1))
+        )
+    ]
+    for copy in copies:
+        copy.start()
+    for copy in copies:
+        copy.wait()
+
+
+def near_kernel(where_ref, list_ref, count_ref, sigma_hbm, lower_hbm, first_0, first_1, second_0, second_1,
+                first_beside, second_beside,
+                first_acc, second_acc, turned_ref, sigma_ref, lower_ref, near_ref, sems):
     lives = []
     copies = []
     for index, offset in enumerate(offsets_of(where_ref)):
@@ -53,11 +68,9 @@
         target = near_ref.at[index] if index < 2 else sigma_ref.at[index - 2]
         lives.append((live, target))
         copies.append(pltpu.make_async_copy(sigma_hbm.at[slot], target, sems.at[index]))
-    copies.append(pltpu.make_async_copy(first_hbm, first, sems.at[5]))
-    copies.append(pltpu.make_async_copy(second_hbm, second, sems.at[6]))
-    copies.append(pltpu.make_async_copy(lower_hbm, lower_ref, sems.at[7]))
-    for index in (0, 5, 6, 1, 2, 3, 4, 7):
-        copies[index].start()
+    copies.append(pltpu.make_async_copy(lower_hbm, lower_ref, sems.at[5]))
+    for copy in copies:
+        copy.start()
 
     def arrived(index):
         copies[index].wait()
@@ -67,20 +80,23 @@
         def _():
             target[...] = jnp.zeros(target.shape, target.dtype)
 
-    copies[5].wait()
-    copies[6].wait()
+    half = first_0.shape[0]
+    size = 2 * half
+    turned_ref[:size, :half] = first_0[...].T
+    turned_ref[:size, half:] = first_1[...].T
+    turned_ref[size:, :half] = second_0[...].T
+    turned_ref[size:, half:] = second_1[...].T
     arrived(0)
-    first_acc[...] = dot(near_ref[0], first[...])
-    second_acc[...] = dot(near_ref[0], second[...])
-    size = first.shape[0]
-    turned_ref[:size] = first[...].T
-    turned_ref[size:] = second[...].T
+    first_acc[...] = jnp.zeros_like(first_acc)
+    second_acc[...] = jnp.zeros_like(second_acc)
+    add_far(first_acc, near_ref, 0, (first_0, first_1))
+    add_far(second_acc, near_ref, 0, (second_0, second_1))
     arrived(1)
-    first_acc[...] += dot(near_ref[1], first_beside[...])
-    second_acc[...] += dot(near_ref[1], second_beside[...])
+    add_far(first_acc, near_ref, 1, (first_beside,))
+    add_far(second_acc, near_ref, 1, (second_beside,))
     for index in (2, 3, 4):
         arrived(index)
-    copies[7].wait()
+    copies[5].wait()
 
 
 def add_far(acc_ref, sigma_ref, index, parts):
@@ -170,49 +186,49 @@
     return lax.ppermute(across, "row", [(a, b) for a, b in hops if 0 <= b < devices])
 
 
-def rest_of(across, far, member, devices):
-    give_across = (member == 0) | (member == 3)
+def rest_of(across, far, give_across, devices):
     pieces = [jnp.where(give_across, a, f) for a, f in zip(across, far)]
     return swapped(jnp.concatenate(pieces, axis=0), 1, devices)
 
 
-def core_summed(give, keep, position, devices):
-    return halved(keep + swapped(give, 1, devices).astype(jnp.float32), 2, position)
-
-
-def halved(total, bit, position):
-    k, rows, width = total.shape
-    pair = total.reshape((k, 2, rows // 2, width))
-    mine = (position // bit) % 2
-    give = lax.dynamic_index_in_dim(pair, 1 - mine, 1, keepdims=False).astype(jnp.bfloat16)
-    return give, lax.dynamic_index_in_dim(pair, mine, 1, keepdims=False)
-
-
-def summed(give, keep, position, devices):
-    bits = [2 ** b for b in range(1, devices.bit_length() - 1)]
-    for bit in bits:
-        total = keep + swapped(give, bit, devices).astype(jnp.float32)
-        if bit != bits[-1]:
-            give, keep = halved(total, 2 * bit, position)
+def core_summed(give, keep, uppers, devices):
+    return halved(keep + swapped(give, 1, devices).astype(jnp.float32), uppers[1])
+
+
+def halved(total, upper):
+    half = total.shape[1] // 2
+    low, high = total[:, :half], total[:, half:]
+    return jnp.where(upper, low, high).astype(jnp.bfloat16), jnp.where(upper, high, low)
+
+
+def summed(give, keep, uppers, devices):
+    count = len(uppers)
+    for b in range(1, count):
+        total = keep + swapped(give, 2 ** b, devices).astype(jnp.float32)
+        if b + 1 < count:
+            give, keep = halved(total, uppers[b + 1])
     gathered = total.astype(jnp.bfloat16)
-    for bit in bits[::-1]:
-        other = swapped(gathered, bit, devices)
-        mine = (position // bit) % 2
-        low = jnp.where(mine == 0, gathered, other)
-        high = jnp.where(mine == 0, other, gathered)
+    for b in range(count - 1, 0, -1):
+        other = swapped(gathered, 2 ** b, devices)
+        low = jnp.where(uppers[b], other, gathered)
+        high = jnp.where(uppers[b], gathered, other)
         gathered = jnp.concatenate([low, high], axis=1)
     return gathered, swapped(gathered, 1, devices)
 
 
 def shards(sigma_blocks, first_panel, second_panel, lower_panel, first_diag, second_diag, task_list, task_count):
+    barrier = lax.optimization_barrier
     devices = lax.axis_size("row")
     position = lax.axis_index("row").astype(jnp.int32)
-    member = position % 4
     slots, size, width = sigma_blocks.shape[-3:]
     sigma = sigma_blocks.reshape((slots, size, width))
     first = first_panel.reshape((size, width))
     second = second_panel.reshape((size, width))
     where = position.reshape((1,))
+    bits = [(position >> b) & 1 for b in range(devices.bit_length() - 1)]
+    uppers = [bit == 1 for bit in bits]
+    give_across = bits[0] == bits[1]
+    where, uppers, give_across, first, second = barrier((where, uppers, give_across, first, second))
     listed = task_list.reshape((slots,))
     count = task_count.reshape((1,))
     one = 2 * size * size * width
@@ -224,29 +240,28 @@
     def parts(k):
         return [jax.ShapeDtypeStruct((k, half, width), t) for t in (jnp.bfloat16, jnp.float32)]
 
-    barrier = lax.optimization_barrier
-
-    across = [swapped(first[:half], 2, devices), swapped(first[half:], 2, devices)]
+    piece = jax.ShapeDtypeStruct((half, width), jnp.bfloat16)
+    pieces = call(split_kernel, [piece] * 4, [first, second], "hh", 1, [pltpu.SemaphoreType.DMA((4,))])
+    across = [swapped(pieces[0], 2, devices), swapped(pieces[1], 2, devices)]
     beside = swapped(first, 1, devices)
     second_beside = swapped(second, 1, devices)
     first_acc, second_acc, turned, sorted_sigma, lower = call(
         near_kernel,
         [wide, wide, jax.ShapeDtypeStruct((2 * size, width), jnp.bfloat16),
          jax.ShapeDtypeStruct((3, size, width), jnp.bfloat16), narrow],
-        [where, listed, count, sigma, first, second, lower_panel, beside, second_beside],
-        "ssshhhhvv",
+        [where, listed, count, sigma, lower_panel, *pieces, beside, second_beside],
+        "ssshhvvvvvv",
         4 * one,
-        [pltpu.VMEM((2, size, width), jnp.bfloat16), pltpu.VMEM((size, width), jnp.bfloat16),
-         pltpu.VMEM((size, width), jnp.bfloat16), pltpu.SemaphoreType.DMA((8,))],
-    )
-    across[0], turned, later_0 = barrier((across[0], turned, second[:half]))
+        [pltpu.VMEM((2, size, width), jnp.bfloat16), pltpu.SemaphoreType.DMA((6,))],
+    )
+    across[0], turned, later_0 = barrier((across[0], turned, pieces[2]))
     far = [far_of(across[0], devices)]
     second_across = [swapped(later_0, 2, devices)]
-    across[1], later_1 = barrier((across[1], second[half:]))
+    across[1], later_1 = barrier((across[1], pieces[3]))
     far.append(far_of(across[1], devices))
     second_across.append(swapped(later_1, 2, devices))
     far, second_across = barrier((far, second_across))
-    rest = rest_of(across, far, member, devices)
+    rest = rest_of(across, far, give_across, devices)
     second_far = [far_of(piece, devices) for piece in second_across]
     column_first, column_again, give, keep = call(
         first_kernel,
@@ -257,8 +272,8 @@
         scratch,
     )
     give, second_across = barrier((give, second_across))
-    second_rest = rest_of(second_across, second_far, member, devices)
-    give, keep = core_summed(give, keep, position, devices)
+    second_rest = rest_of(second_across, second_far, give_across, devices)
+    give, keep = core_summed(give, keep, uppers, devices)
     (second_acc,) = call(
         across_kernel, [wide], [second_acc, column_again, lower, *second_across, sorted_sigma], "vvvvvv", 2 * one
     )
@@ -271,9 +286,9 @@
         3 * one,
         scratch,
     )
-    mine, other = summed(give, keep, position, devices)
-    second_give, second_keep = core_summed(second_give, second_keep, position, devices)
-    second_mine, second_other = summed(second_give, second_keep, position, devices)
+    mine, other = summed(give, keep, uppers, devices)
+    second_give, second_keep = core_summed(second_give, second_keep, uppers, devices)
+    second_mine, second_other = summed(second_give, second_keep, uppers, devices)
     block_first, block_link, base = call(
         link_kernel, [wide] * 3, [where, mine, other, lower, first_diag, second_diag], "svvvvv", 4 * one, scratch
     )

time: 120 us -> 98.4 us (0.82)
  local copies, waits for them, and re-layouts: 23.7 us -> 5.53 us
  other arithmetic: 5.81 us -> 1.21 us
  waiting for transfers between devices: 36.3 us -> 38.4 us
  starting transfers between devices: 38.4 us -> 40.4 us
  Pallas kernels: 12.7 us -> 10.8 us
    unnamed x56 -> x14, local copies, waits for them, and re-layouts: 19.2 us -> 5.53 us
    ppermute x4, waiting for transfers between devices: 5.45 us -> 9.63 us  [far_of(): lax.ppermute(across, 'row', [(a, b) for a, b in hops if 0 <= b < devices])]
    slice x2 -> x0, local copies, waits for them, and re-layouts: 3.64 us -> none  [the longest x1 1.86 us: shards(): across[1], later_1 = barrier((across[1], second[half:]))]
    ppermute x24, starting transfers between devices: 22.8 us -> 25.6 us  [swapped(): return lax.ppermute(value, 'row', [(i, i ^ bit) for i in range(devices)])]
    ppermute x24, waiting for transfers between devices: 30.8 us -> 28.8 us  [swapped(): return lax.ppermute(value, 'row', [(i, i ^ bit) for i in range(devices)])]
    add x2, other arithmetic: 2.32 us -> 0.25 us  [core_summed(): keep + swapped(give, 1, devices).astype(jnp.float32)]
    pallas_call x6 -> x7, Pallas kernels: 12.7 us -> 10.8 us  [call(): pl.pallas_call(body, out_shape=outs, in_specs=[pl.BlockSpec(memory_space=...]
  transfers between devices with their start and end apart: 28 -> 28, of which waited for: 14 -> 17; matrix products, arithmetic and copies ran while one was open for 8% -> 1% of each run, Pallas kernels for 8% -> 8%
where the time goes in v5:
time: 98.4 us; the launch traced here: 98 us
  starting transfers between devices  40.4 us (41%)
  waiting for transfers between devices  38.4 us (39%)
  Pallas kernels  10.8 us (11%)
  local copies, waits for them, and re-layouts  5.53 us (6%)
  between operations  1.69 us (2%)
  other arithmetic  1.21 us (1%)
    ppermute x24, waiting for transfers between devices, swapped(): return lax.ppermute(value, 'row', [(i, i ^ bit) for i in range(devices)])  28.8 us
    ppermute x24, starting transfers between devices, swapped(): return lax.ppermute(value, 'row', [(i, i ^ bit) for i in range(devices)])  25.6 us
    ppermute x4, starting transfers between devices, far_of(): lax.ppermute(across, 'row', [(a, b) for a, b in hops if 0 <= b < devices])  14.8 us
    pallas_call x7, Pallas kernels, call(): pl.pallas_call(body, out_shape=outs, in_specs=[pl.BlockSpec(memory_space=...  10.8 us
    ppermute x4, waiting for transfers between devices, far_of(): lax.ppermute(across, 'row', [(a, b) for a, b in hops if 0 <= b < devices])  9.63 us
    unnamed x14, local copies, waits for them, and re-layouts  5.53 us
  transfers between devices with their start and end apart: 28, of which 17 were waited for; matrix products, arithmetic and copies ran while one was open for 1% of the time, Pallas kernels for 8%

profile of v5, /device:TPU:0, one launch (start us, length us, event | category | flops | bytes accessed | tf_op | source)
XLA Modules:
  0.0 98.0 jit_solution(6808783129198569579)
XLA Ops:
  1.2 1.0 %copy-done.2 = bf16[1,1,512,512]{3,2,1,0:T(8,128)(2,1)S(1)} copy-done((bf16[1,1,512,512]{3,2,1,0:T(8,128)(2,1)S(1)}, bf16[1,1,512,512]{3,2,1,0:T(8,128)(2,1)}, u32[]{:S(2)}) %copy-start.2) | copy-done | bytes 524312
  3.4 3.0 %collective-permute-start.3 = (bf16[256,512]{1,0:T(8,128)(2,1)S(1)}, bf16[256,512]{1,0:T(8,128)(2,1)S(1)}, u32[]{:S(2)}, u32[]{:S(2)}) collective-permute-start(bf16[256,512]{1,0:T(8,128)(2,1)S(1)} %get-tuple-element.49.first_1), channel_id=1, source_target_pairs={{0,2},{1,3},{2,0},{3,1},{4,6},{5,7},{6,4},{7,5},{8,10},{9,11},{10,... | collective-permute-start | bytes 786440 | tf_op jit(solution)/shard_map/ppermute | solution.py:181
  7.2 6.4 %collective-permute-done.3.across_1 = bf16[256,512]{1,0:T(8,128)(2,1)S(1)} collective-permute-done((bf16[256,512]{1,0:T(8,128)(2,1)S(1)}, bf16[256,512]{1,0:T(8,128)(2,1)S(1)}, u32[]{:S(2)}, u32[]{:S(2)}) %collective-permute-start.3) | collective-permute-done | bytes 262176 | tf_op jit(solution)/shard_map/ppermute | solution.py:181
  13.5 4.1 %collective-permute-start.5 = (bf16[256,512]{1,0:T(8,128)(2,1)S(1)}, bf16[256,512]{1,0:T(8,128)(2,1)S(1)}, u32[]{:S(2)}, u32[]{:S(2)}) collective-permute-start(bf16[256,512]{1,0:T(8,128)(2,1)S(1)} %collective-permute-done.3.across_1), channel_id=1, source_target_pairs={{0,4},{1,5},{4,8},{5,9},{6,2},{7,3},{8,12},{9,13},{10,6},{11,7},{1... | collective-permute-start | bytes 786440 | tf_op jit(solution)/shard_map/ppermute | solution.py:186
  17.7 1.7 %copy-done = bf16[1,1,5,512,512]{4,3,2,1,0:T(8,128)(2,1)S(1)} copy-done((bf16[1,1,5,512,512]{4,3,2,1,0:T(8,128)(2,1)S(1)}, bf16[1,1,5,512,512]{4,3,2,1,0:T(8,128)(2,1)}, u32[]{:S(2)}) %copy-start) | copy-done | bytes 2621464
  21.1 2.7 %shard_map.120 = (f32[512,512]{1,0:T(8,128)S(1)}, f32[512,512]{1,0:T(8,128)S(1)}, bf16[1024,512]{1,0:T(8,128)(2,1)S(1)}, bf16[3,512,512]{2,1,0:T(8,128)(2,1)S(1)}, bf16[512,512]{1,0:T(8,128)(2,1)S(1)}) custom-call(s32[1]{0:T(128)} %bitcast.where_ref, s32[5]{0:T(128)S(1)} %bitcast.14, s32[1]{0:T(128)} %bitcast.8.count_ref, bf16[5,512,512]{2,1,0:T(8,128)(2,1)S(1)} %bitcast.9, ...), custom_call_target="tpu_custom_call" | custom-call | flops 1073741824 | bytes 10485788 | tf_op jit(solution)/shard_map/pallas_call | solution.py:16
  23.9 3.7 %collective-permute-start.4 = (bf16[256,512]{1,0:T(8,128)(2,1)S(1)}, bf16[256,512]{1,0:T(8,128)(2,1)S(1)}, u32[]{:S(2)}, u32[]{:S(2)}) collective-permute-start(bf16[256,512]{1,0:T(8,128)(2,1)S(1)} %collective-permute-done.2.across_0), channel_id=1, source_target_pairs={{0,4},{1,5},{4,8},{5,9},{6,2},{7,3},{8,12},{9,13},{10,6},{11,7},{1... | collective-permute-start | bytes 786440 | tf_op jit(solution)/shard_map/ppermute | solution.py:186
  27.7 3.8 %collective-permute-done.4.far_0 = bf16[256,512]{1,0:T(8,128)(2,1)S(1)} collective-permute-done((bf16[256,512]{1,0:T(8,128)(2,1)S(1)}, bf16[256,512]{1,0:T(8,128)(2,1)S(1)}, u32[]{:S(2)}, u32[]{:S(2)}) %collective-permute-start.4) | collective-permute-done | bytes 262176 | tf_op jit(solution)/shard_map/ppermute | solution.py:186
  31.5 2.6 %collective-permute-done.6.across_0 = bf16[256,512]{1,0:T(8,128)(2,1)S(1)} collective-permute-done((bf16[256,512]{1,0:T(8,128)(2,1)S(1)}, bf16[256,512]{1,0:T(8,128)(2,1)S(1)}, u32[]{:S(2)}, u32[]{:S(2)}) %collective-permute-start.6) | collective-permute-done | bytes 262176 | tf_op jit(solution)/shard_map/ppermute | solution.py:181
  34.2 3.5 %collective-permute-start.10 = (bf16[256,512]{1,0:T(8,128)(2,1)S(1)}, bf16[256,512]{1,0:T(8,128)(2,1)S(1)}, u32[]{:S(2)}, u32[]{:S(2)}) collective-permute-start(bf16[256,512]{1,0:T(8,128)(2,1)S(1)} %collective-permute-done.6.across_0), channel_id=1, source_target_pairs={{0,4},{1,5},{4,8},{5,9},{6,2},{7,3},{8,12},{9,13},{10,6},{11,7},{1... | collective-permute-start | bytes 786440 | tf_op jit(solution)/shard_map/ppermute | solution.py:186
  37.7 3.6 %collective-permute-start.11 = (bf16[256,512]{1,0:T(8,128)(2,1)S(1)}, bf16[256,512]{1,0:T(8,128)(2,1)S(1)}, u32[]{:S(2)}, u32[]{:S(2)}) collective-permute-start(bf16[256,512]{1,0:T(8,128)(2,1)S(1)} %collective-permute-done.7.across_1), channel_id=1, source_target_pairs={{0,4},{1,5},{4,8},{5,9},{6,2},{7,3},{8,12},{9,13},{10,6},{11,7},{1... | collective-permute-start | bytes 786440 | tf_op jit(solution)/shard_map/ppermute | solution.py:186
  41.3 2.3 %shard_map.121 = (bf16[512,512]{1,0:T(8,128)(2,1)}, bf16[512,512]{1,0:T(8,128)(2,1)S(1)}, bf16[2,256,512]{2,1,0:T(8,128)(2,1)S(1)}, f32[2,256,512]{2,1,0:T(8,128)S(1)}) custom-call(s32[1]{0:T(128)} %bitcast.where_ref, f32[512,512]{1,0:T(8,128)S(1)} %get-tuple-element.52.acc_in, bf16[256,512]{1,0:T(8,128)(2,1)S(1)} %collective-permute-done.2.across_0, ...), custom_call_target="tpu_custom_call" | custom-call | flops 1342177280 | bytes 7864324 | tf_op jit(solution)/shard_map/pallas_call | solution.py:16
  44.3 5.2 %collective-permute-done.11.far_1 = bf16[256,512]{1,0:T(8,128)(2,1)S(1)} collective-permute-done((bf16[256,512]{1,0:T(8,128)(2,1)S(1)}, bf16[256,512]{1,0:T(8,128)(2,1)S(1)}, u32[]{:S(2)}, u32[]{:S(2)}) %collective-permute-start.11) | collective-permute-done | bytes 262176 | tf_op jit(solution)/shard_map/ppermute | solution.py:186
  51.6 1.6 %shard_map.124 = (bf16[512,512]{1,0:T(8,128)(2,1)}, bf16[1,256,512]{2,1,0:T(8,128)(2,1)S(1)}, f32[1,256,512]{2,1,0:T(8,128)S(1)}) custom-call(s32[1]{0:T(128)} %bitcast.where_ref, f32[512,512]{1,0:T(8,128)S(1)} %shard_map.123.acc_in, bf16[256,512]{1,0:T(8,128)(2,1)S(1)} %collective-permute-done.10.far_0, bf16[256,512]{1,0:T(8,128)(2,1)S(1)} %collective-permute-done.11.far_1, ...), custom_call_target="tpu_custom_call" | custom-call | flops 805306368 | bytes 6029316 | tf_op jit(solution)/shard_map/pallas_call | solution.py:16
  53.2 1.3 %collective-permute-start.13 = (bf16[2,128,512]{2,1,0:T(8,128)(2,1)S(1)}, bf16[2,128,512]{2,1,0:T(8,128)(2,1)S(1)}, u32[]{:S(2)}, u32[]{:S(2)}) collective-permute-start(bf16[2,128,512]{2,1,0:T(8,128)(2,1)S(1)} %select_convert_fusion), channel_id=1, source_target_pairs={{0,2},{1,3},{2,0},{3,1},{4,6},{5,7},{6,4},{7,5},{8,10},{9,11},{10,... | collective-permute-start | bytes 786440 | tf_op jit(solution)/shard_map/ppermute | solution.py:181
  54.8 1.4 %collective-permute-start.21 = (bf16[1,128,512]{2,1,0:T(8,128)(2,1)S(1)}, bf16[1,128,512]{2,1,0:T(8,128)(2,1)S(1)}, u32[]{:S(2)}, u32[]{:S(2)}) collective-permute-start(bf16[1,128,512]{2,1,0:T(8,128)(2,1)S(1)} %select_convert_fusion.1), channel_id=1, source_target_pairs={{0,2},{1,3},{2,0},{3,1},{4,6},{5,7},{6,4},{7,5},{8,10},{9,11},{10,... | collective-permute-start | bytes 393224 | tf_op jit(solution)/shard_map/ppermute | solution.py:181
  56.2 6.2 %collective-permute-done.13 = bf16[2,128,512]{2,1,0:T(8,128)(2,1)S(1)} collective-permute-done((bf16[2,128,512]{2,1,0:T(8,128)(2,1)S(1)}, bf16[2,128,512]{2,1,0:T(8,128)(2,1)S(1)}, u32[]{:S(2)}, u32[]{:S(2)}) %collective-permute-start.13) | collective-permute-done | bytes 262176 | tf_op jit(solution)/shard_map/ppermute | solution.py:181
  62.6 2.5 %collective-permute-start.14 = (bf16[2,64,512]{2,1,0:T(8,128)(2,1)S(1)}, bf16[2,64,512]{2,1,0:T(8,128)(2,1)S(1)}, u32[]{:S(2)}, u32[]{:S(2)}) collective-permute-start(bf16[2,64,512]{2,1,0:T(8,128)(2,1)S(1)} %select_convert_fusion.2), channel_id=1, source_target_pairs={{0,4},{1,5},{2,6},{3,7},{4,0},{5,1},{6,2},{7,3},{8,12},{9,13},{10,... | collective-permute-start | bytes 393224 | tf_op jit(solution)/shard_map/ppermute | solution.py:181
  65.2 2.1 %collective-permute-start.22 = (bf16[1,64,512]{2,1,0:T(8,128)(2,1)S(1)}, bf16[1,64,512]{2,1,0:T(8,128)(2,1)S(1)}, u32[]{:S(2)}, u32[]{:S(2)}) collective-permute-start(bf16[1,64,512]{2,1,0:T(8,128)(2,1)S(1)} %select_convert_fusion.3), channel_id=1, source_target_pairs={{0,4},{1,5},{2,6},{3,7},{4,0},{5,1},{6,2},{7,3},{8,12},{9,13},{10,... | collective-permute-start | bytes 196616 | tf_op jit(solution)/shard_map/ppermute | solution.py:181
  67.3 1.2 %collective-permute-done.14 = bf16[2,64,512]{2,1,0:T(8,128)(2,1)S(1)} collective-permute-done((bf16[2,64,512]{2,1,0:T(8,128)(2,1)S(1)}, bf16[2,64,512]{2,1,0:T(8,128)(2,1)S(1)}, u32[]{:S(2)}, u32[]{:S(2)}) %collective-permute-start.14) | collective-permute-done | bytes 131104 | tf_op jit(solution)/shard_map/ppermute | solution.py:181
  68.5 3.5 %collective-permute-start.15 = (bf16[2,32,512]{2,1,0:T(8,128)(2,1)S(1)}, bf16[2,32,512]{2,1,0:T(8,128)(2,1)S(1)}, u32[]{:S(2)}, u32[]{:S(2)}) collective-permute-start(bf16[2,32,512]{2,1,0:T(8,128)(2,1)S(1)} %select_convert_fusion.4), channel_id=1, source_target_pairs={{0,8},{1,9},{2,10},{3,11},{4,12},{5,13},{6,14},{7,15},{8,0},{9,1},... | collective-permute-start | bytes 196616 | tf_op jit(solution)/shard_map/ppermute | solution.py:181
  72.0 1.3 %collective-permute-start.23 = (bf16[1,32,512]{2,1,0:T(8,128)(2,1)S(1)}, bf16[1,32,512]{2,1,0:T(8,128)(2,1)S(1)}, u32[]{:S(2)}, u32[]{:S(2)}) collective-permute-start(bf16[1,32,512]{2,1,0:T(8,128)(2,1)S(1)} %select_convert_fusion.5), channel_id=1, source_target_pairs={{0,8},{1,9},{2,10},{3,11},{4,12},{5,13},{6,14},{7,15},{8,0},{9,1},... | collective-permute-start | bytes 98312 | tf_op jit(solution)/shard_map/ppermute | solution.py:181
  73.4 1.2 %collective-permute-done.15 = bf16[2,32,512]{2,1,0:T(8,128)(2,1)S(1)} collective-permute-done((bf16[2,32,512]{2,1,0:T(8,128)(2,1)S(1)}, bf16[2,32,512]{2,1,0:T(8,128)(2,1)S(1)}, u32[]{:S(2)}, u32[]{:S(2)}) %collective-permute-start.15) | collective-permute-done | bytes 65568 | tf_op jit(solution)/shard_map/ppermute | solution.py:181
  74.6 3.0 %collective-permute-start.16 = (bf16[2,32,512]{2,1,0:T(8,128)(2,1)S(1)}, bf16[2,32,512]{2,1,0:T(8,128)(2,1)S(1)}, u32[]{:S(2)}, u32[]{:S(2)}) collective-permute-start(bf16[2,32,512]{2,1,0:T(8,128)(2,1)S(1)} %add_convert_fusion), channel_id=1, source_target_pairs={{0,8},{1,9},{2,10},{3,11},{4,12},{5,13},{6,14},{7,15},{8,0},{9,1},... | collective-permute-start | bytes 196616 | tf_op jit(solution)/shard_map/ppermute | solution.py:181
  78.3 1.8 %collective-permute-done.16 = bf16[2,32,512]{2,1,0:T(8,128)(2,1)S(1)} collective-permute-done((bf16[2,32,512]{2,1,0:T(8,128)(2,1)S(1)}, bf16[2,32,512]{2,1,0:T(8,128)(2,1)S(1)}, u32[]{:S(2)}, u32[]{:S(2)}) %collective-permute-start.16) | collective-permute-done | bytes 65568 | tf_op jit(solution)/shard_map/ppermute | solution.py:181
  80.1 2.9 %collective-permute-start.17 = (bf16[2,64,512]{2,1,0:T(8,128)(2,1)S(1)}, bf16[2,64,512]{2,1,0:T(8,128)(2,1)S(1)}, u32[]{:S(2)}, u32[]{:S(2)}) collective-permute-start(bf16[2,64,512]{2,1,0:T(8,128)(2,1)S(1)} %pad_maximum_fusion.5), channel_id=1, source_target_pairs={{0,4},{1,5},{2,6},{3,7},{4,0},{5,1},{6,2},{7,3},{8,12},{9,13},{10,... | collective-permute-start | bytes 393224 | tf_op jit(solution)/shard_map/ppermute | solution.py:181
  83.1 2.0 %collective-permute-start.25 = (bf16[1,64,512]{2,1,0:T(8,128)(2,1)S(1)}, bf16[1,64,512]{2,1,0:T(8,128)(2,1)S(1)}, u32[]{:S(2)}, u32[]{:S(2)}) collective-permute-start(bf16[1,64,512]{2,1,0:T(8,128)(2,1)S(1)} %pad_maximum_fusion.7), channel_id=1, source_target_pairs={{0,4},{1,5},{2,6},{3,7},{4,0},{5,1},{6,2},{7,3},{8,12},{9,13},{10,... | collective-permute-start | bytes 196616 | tf_op jit(solution)/shard_map/ppermute | solution.py:181
  86.1 1.3 %collective-permute-done.25 = bf16[1,64,512]{2,1,0:T(8,128)(2,1)S(1)} collective-permute-done((bf16[1,64,512]{2,1,0:T(8,128)(2,1)S(1)}, bf16[1,64,512]{2,1,0:T(8,128)(2,1)S(1)}, u32[]{:S(2)}, u32[]{:S(2)}) %collective-permute-start.25) | collective-permute-done | bytes 65568 | tf_op jit(solution)/shard_map/ppermute | solution.py:181
  88.3 4.2 %collective-permute-done.18 = bf16[2,128,512]{2,1,0:T(8,128)(2,1)S(1)} collective-permute-done((bf16[2,128,512]{2,1,0:T(8,128)(2,1)S(1)}, bf16[2,128,512]{2,1,0:T(8,128)(2,1)S(1)}, u32[]{:S(2)}, u32[]{:S(2)}) %collective-permute-start.18) | collective-permute-done | bytes 262176 | tf_op jit(solution)/shard_map/ppermute | solution.py:181
  92.7 1.2 %collective-permute-done.26 = bf16[1,128,512]{2,1,0:T(8,128)(2,1)S(1)} collective-permute-done((bf16[1,128,512]{2,1,0:T(8,128)(2,1)S(1)}, bf16[1,128,512]{2,1,0:T(8,128)(2,1)S(1)}, u32[]{:S(2)}, u32[]{:S(2)}) %collective-permute-start.26) | collective-permute-done | bytes 131104 | tf_op jit(solution)/shard_map/ppermute | solution.py:181
  94.6 2.2 %shard_map.122 = (f32[512,512]{1,0:T(8,128)}, f32[512,512]{1,0:T(8,128)}, f32[512,512]{1,0:T(8,128)S(1)}) custom-call(s32[1]{0:T(128)} %bitcast.where_ref, bf16[2,256,512]{2,1,0:T(8,128)(2,1)S(1)} %pad_maximum_fusion.2.mine_ref, bf16[2,256,512]{2,1,0:T(8,128)(2,1)S(1)} %collective-permute-done.19.other_ref, ...), custom_call_target="tpu_custom_call" | custom-call | flops 1073741824 | bytes 6815748 | tf_op jit(solution)/shard_map/pallas_call | solution.py:16
  96.8 1.2 %shard_map.125 = f32[512,512]{1,0:T(8,128)} custom-call(s32[1]{0:T(128)} %bitcast.where_ref, bf16[1,256,512]{2,1,0:T(8,128)(2,1)S(1)} %pad_maximum_fusion.4.mine_ref, bf16[1,256,512]{2,1,0:T(8,128)(2,1)S(1)} %collective-permute-done.27.other_ref, f32[512,512]{1,0:T(8,128)S(1)} %get-tuple-element.84.base_ref), custom_call_target="tpu_custom_call" | custom-call | flops 262144 | bytes 2621444 | tf_op jit(solution)/shard_map/pallas_call | solution.py:16
  (76 shorter events, 10.8 us)
Async XLA Ops:
  0.6 17.0 %collective-permute-start = (bf16[512,512]{1,0:T(8,128)(2,1)}, bf16[512,512]{1,0:T(8,128)(2,1)S(1)}, u32[]{:S(2)}, u32[]{:S(2)}) collective-permute-start(bf16[512,512]{1,0:T(8,128)(2,1)} %bitcast.10), channel_id=1, source_target_pairs={{0,1},{1,0},{2,3},{3,2},{4,5},{5,4},{6,7},{7,6},{8,9},{9,8},{10,11... | collective-permute-start | bytes 1572872 | tf_op jit(solution)/shard_map/ppermute | solution.py:181
  1.2 16.5 %collective-permute-start.1 = (bf16[512,512]{1,0:T(8,128)(2,1)}, bf16[512,512]{1,0:T(8,128)(2,1)S(1)}, u32[]{:S(2)}, u32[]{:S(2)}) collective-permute-start(bf16[512,512]{1,0:T(8,128)(2,1)} %bitcast.12), channel_id=1, source_target_pairs={{0,1},{1,0},{2,3},{3,2},{4,5},{5,4},{6,7},{7,6},{8,9},{9,8},{10,11... | collective-permute-start | bytes 1572872 | tf_op jit(solution)/shard_map/ppermute | solution.py:181
  1.2 1.0 %copy-start.2 = (bf16[1,1,512,512]{3,2,1,0:T(8,128)(2,1)S(1)}, bf16[1,1,512,512]{3,2,1,0:T(8,128)(2,1)}, u32[]{:S(2)}) copy-start(bf16[1,1,512,512]{3,2,1,0:T(8,128)(2,1)} %param.9) | copy-start | bytes 1572868
  3.4 10.1 %collective-permute-start.3 = (bf16[256,512]{1,0:T(8,128)(2,1)S(1)}, bf16[256,512]{1,0:T(8,128)(2,1)S(1)}, u32[]{:S(2)}, u32[]{:S(2)}) collective-permute-start(bf16[256,512]{1,0:T(8,128)(2,1)S(1)} %get-tuple-element.49.first_1), channel_id=1, source_target_pairs={{0,2},{1,3},{2,0},{3,1},{4,6},{5,7},{6,4},{7,5},{8,10},{9,11},{10,... | collective-permute-start | bytes 786440 | tf_op jit(solution)/shard_map/ppermute | solution.py:181
  6.4 17.5 %collective-permute-start.2 = (bf16[256,512]{1,0:T(8,128)(2,1)S(1)}, bf16[256,512]{1,0:T(8,128)(2,1)S(1)}, u32[]{:S(2)}, u32[]{:S(2)}) collective-permute-start(bf16[256,512]{1,0:T(8,128)(2,1)S(1)} %get-tuple-element.48.first_0), channel_id=1, source_target_pairs={{0,2},{1,3},{2,0},{3,1},{4,6},{5,7},{6,4},{7,5},{8,10},{9,11},{10,... | collective-permute-start | bytes 786440 | tf_op jit(solution)/shard_map/ppermute | solution.py:181
  13.5 14.2 %collective-permute-start.5 = (bf16[256,512]{1,0:T(8,128)(2,1)S(1)}, bf16[256,512]{1,0:T(8,128)(2,1)S(1)}, u32[]{:S(2)}, u32[]{:S(2)}) collective-permute-start(bf16[256,512]{1,0:T(8,128)(2,1)S(1)} %collective-permute-done.3.across_1), channel_id=1, source_target_pairs={{0,4},{1,5},{4,8},{5,9},{6,2},{7,3},{8,12},{9,13},{10,6},{11,7},{1... | collective-permute-start | bytes 786440 | tf_op jit(solution)/shard_map/ppermute | solution.py:186
  17.6 10.1 %collective-permute-start.7 = (bf16[256,512]{1,0:T(8,128)(2,1)S(1)}, bf16[256,512]{1,0:T(8,128)(2,1)S(1)}, u32[]{:S(2)}, u32[]{:S(2)}) collective-permute-start(bf16[256,512]{1,0:T(8,128)(2,1)S(1)} %get-tuple-element.57.second_1), channel_id=1, source_target_pairs={{0,2},{1,3},{2,0},{3,1},{4,6},{5,7},{6,4},{7,5},{8,10},{9,11},{10,... | collective-permute-start | bytes 786440 | tf_op jit(solution)/shard_map/ppermute | solution.py:181
  17.7 1.7 %copy-start = (bf16[1,1,5,512,512]{4,3,2,1,0:T(8,128)(2,1)S(1)}, bf16[1,1,5,512,512]{4,3,2,1,0:T(8,128)(2,1)}, u32[]{:S(2)}) copy-start(bf16[1,1,5,512,512]{4,3,2,1,0:T(8,128)(2,1)} %param.8) | copy-start | bytes 7864324
  23.9 7.6 %collective-permute-start.4 = (bf16[256,512]{1,0:T(8,128)(2,1)S(1)}, bf16[256,512]{1,0:T(8,128)(2,1)S(1)}, u32[]{:S(2)}, u32[]{:S(2)}) collective-permute-start(bf16[256,512]{1,0:T(8,128)(2,1)S(1)} %collective-permute-done.2.across_0), channel_id=1, source_target_pairs={{0,4},{1,5},{4,8},{5,9},{6,2},{7,3},{8,12},{9,13},{10,6},{11,7},{1... | collective-permute-start | bytes 786440 | tf_op jit(solution)/shard_map/ppermute | solution.py:186
  27.6 6.4 %collective-permute-start.6 = (bf16[256,512]{1,0:T(8,128)(2,1)S(1)}, bf16[256,512]{1,0:T(8,128)(2,1)S(1)}, u32[]{:S(2)}, u32[]{:S(2)}) collective-permute-start(bf16[256,512]{1,0:T(8,128)(2,1)S(1)} %get-tuple-element.56.second_0), channel_id=1, source_target_pairs={{0,2},{1,3},{2,0},{3,1},{4,6},{5,7},{6,4},{7,5},{8,10},{9,11},{10,... | collective-permute-start | bytes 786440 | tf_op jit(solution)/shard_map/ppermute | solution.py:181
  34.2 7.1 %collective-permute-start.8 = (bf16[512,512]{1,0:T(8,128)(2,1)S(1)}, bf16[512,512]{1,0:T(8,128)(2,1)S(1)}, u32[]{:S(2)}, u32[]{:S(2)}) collective-permute-start(bf16[512,512]{1,0:T(8,128)(2,1)S(1)} %pad_maximum_fusion), channel_id=1, source_target_pairs={{0,1},{1,0},{2,3},{3,2},{4,5},{5,4},{6,7},{7,6},{8,9},{9,8},{10,11... | collective-permute-start | bytes 1572872 | tf_op jit(solution)/shard_map/ppermute | solution.py:181
  34.2 10.0 %collective-permute-start.10 = (bf16[256,512]{1,0:T(8,128)(2,1)S(1)}, bf16[256,512]{1,0:T(8,128)(2,1)S(1)}, u32[]{:S(2)}, u32[]{:S(2)}) collective-permute-start(bf16[256,512]{1,0:T(8,128)(2,1)S(1)} %collective-permute-done.6.across_0), channel_id=1, source_target_pairs={{0,4},{1,5},{4,8},{5,9},{6,2},{7,3},{8,12},{9,13},{10,6},{11,7},{1... | collective-permute-start | bytes 786440 | tf_op jit(solution)/shard_map/ppermute | solution.py:186
  37.7 11.8 %collective-permute-start.11 = (bf16[256,512]{1,0:T(8,128)(2,1)S(1)}, bf16[256,512]{1,0:T(8,128)(2,1)S(1)}, u32[]{:S(2)}, u32[]{:S(2)}) collective-permute-start(bf16[256,512]{1,0:T(8,128)(2,1)S(1)} %collective-permute-done.7.across_1), channel_id=1, source_target_pairs={{0,4},{1,5},{4,8},{5,9},{6,2},{7,3},{8,12},{9,13},{10,6},{11,7},{1... | collective-permute-start | bytes 786440 | tf_op jit(solution)/shard_map/ppermute | solution.py:186
  43.6 6.8 %collective-permute-start.9 = (bf16[2,256,512]{2,1,0:T(8,128)(2,1)S(1)}, bf16[2,256,512]{2,1,0:T(8,128)(2,1)S(1)}, u32[]{:S(2)}, u32[]{:S(2)}) collective-permute-start(bf16[2,256,512]{2,1,0:T(8,128)(2,1)S(1)} %get-tuple-element.71), channel_id=1, source_target_pairs={{0,1},{1,0},{2,3},{3,2},{4,5},{5,4},{6,7},{7,6},{8,9},{9,8},{10,11... | collective-permute-start | bytes 1572872 | tf_op jit(solution)/shard_map/ppermute | solution.py:181
  49.6 2.0 %collective-permute-start.12 = (bf16[512,512]{1,0:T(8,128)(2,1)S(1)}, bf16[512,512]{1,0:T(8,128)(2,1)S(1)}, u32[]{:S(2)}, u32[]{:S(2)}) collective-permute-start(bf16[512,512]{1,0:T(8,128)(2,1)S(1)} %pad_maximum_fusion.1), channel_id=1, source_target_pairs={{0,1},{1,0},{2,3},{3,2},{4,5},{5,4},{6,7},{7,6},{8,9},{9,8},{10,11... | collective-permute-start | bytes 1572872 | tf_op jit(solution)/shard_map/ppermute | solution.py:181
  53.1 1.5 %collective-permute-start.20 = (bf16[1,256,512]{2,1,0:T(8,128)(2,1)S(1)}, bf16[1,256,512]{2,1,0:T(8,128)(2,1)S(1)}, u32[]{:S(2)}, u32[]{:S(2)}) collective-permute-start(bf16[1,256,512]{2,1,0:T(8,128)(2,1)S(1)} %get-tuple-element.83), channel_id=1, source_target_pairs={{0,1},{1,0},{2,3},{3,2},{4,5},{5,4},{6,7},{7,6},{8,9},{9,8},{10,11... | collective-permute-start | bytes 786440 | tf_op jit(solution)/shard_map/ppermute | solution.py:181
  53.2 9.1 %collective-permute-start.13 = (bf16[2,128,512]{2,1,0:T(8,128)(2,1)S(1)}, bf16[2,128,512]{2,1,0:T(8,128)(2,1)S(1)}, u32[]{:S(2)}, u32[]{:S(2)}) collective-permute-start(bf16[2,128,512]{2,1,0:T(8,128)(2,1)S(1)} %select_convert_fusion), channel_id=1, source_target_pairs={{0,2},{1,3},{2,0},{3,1},{4,6},{5,7},{6,4},{7,5},{8,10},{9,11},{10,... | collective-permute-start | bytes 786440 | tf_op jit(solution)/shard_map/ppermute | solution.py:181
  54.8 10.3 %collective-permute-start.21 = (bf16[1,128,512]{2,1,0:T(8,128)(2,1)S(1)}, bf16[1,128,512]{2,1,0:T(8,128)(2,1)S(1)}, u32[]{:S(2)}, u32[]{:S(2)}) collective-permute-start(bf16[1,128,512]{2,1,0:T(8,128)(2,1)S(1)} %select_convert_fusion.1), channel_id=1, source_target_pairs={{0,2},{1,3},{2,0},{3,1},{4,6},{5,7},{6,4},{7,5},{8,10},{9,11},{10,... | collective-permute-start | bytes 393224 | tf_op jit(solution)/shard_map/ppermute | solution.py:181
  62.6 5.9 %collective-permute-start.14 = (bf16[2,64,512]{2,1,0:T(8,128)(2,1)S(1)}, bf16[2,64,512]{2,1,0:T(8,128)(2,1)S(1)}, u32[]{:S(2)}, u32[]{:S(2)}) collective-permute-start(bf16[2,64,512]{2,1,0:T(8,128)(2,1)S(1)} %select_convert_fusion.2), channel_id=1, source_target_pairs={{0,4},{1,5},{2,6},{3,7},{4,0},{5,1},{6,2},{7,3},{8,12},{9,13},{10,... | collective-permute-start | bytes 393224 | tf_op jit(solution)/shard_map/ppermute | solution.py:181
  65.2 6.8 %collective-permute-start.22 = (bf16[1,64,512]{2,1,0:T(8,128)(2,1)S(1)}, bf16[1,64,512]{2,1,0:T(8,128)(2,1)S(1)}, u32[]{:S(2)}, u32[]{:S(2)}) collective-permute-start(bf16[1,64,512]{2,1,0:T(8,128)(2,1)S(1)} %select_convert_fusion.3), channel_id=1, source_target_pairs={{0,4},{1,5},{2,6},{3,7},{4,0},{5,1},{6,2},{7,3},{8,12},{9,13},{10,... | collective-permute-start | bytes 196616 | tf_op jit(solution)/shard_map/ppermute | solution.py:181
  68.5 6.1 %collective-permute-start.15 = (bf16[2,32,512]{2,1,0:T(8,128)(2,1)S(1)}, bf16[2,32,512]{2,1,0:T(8,128)(2,1)S(1)}, u32[]{:S(2)}, u32[]{:S(2)}) collective-permute-start(bf16[2,32,512]{2,1,0:T(8,128)(2,1)S(1)} %select_convert_fusion.4), channel_id=1, source_target_pairs={{0,8},{1,9},{2,10},{3,11},{4,12},{5,13},{6,14},{7,15},{8,0},{9,1},... | collective-permute-start | bytes 196616 | tf_op jit(solution)/shard_map/ppermute | solution.py:181
  72.0 5.8 %collective-permute-start.23 = (bf16[1,32,512]{2,1,0:T(8,128)(2,1)S(1)}, bf16[1,32,512]{2,1,0:T(8,128)(2,1)S(1)}, u32[]{:S(2)}, u32[]{:S(2)}) collective-permute-start(bf16[1,32,512]{2,1,0:T(8,128)(2,1)S(1)} %select_convert_fusion.5), channel_id=1, source_target_pairs={{0,8},{1,9},{2,10},{3,11},{4,12},{5,13},{6,14},{7,15},{8,0},{9,1},... | collective-permute-start | bytes 98312 | tf_op jit(solution)/shard_map/ppermute | solution.py:181
  74.6 5.5 %collective-permute-start.16 = (bf16[2,32,512]{2,1,0:T(8,128)(2,1)S(1)}, bf16[2,32,512]{2,1,0:T(8,128)(2,1)S(1)}, u32[]{:S(2)}, u32[]{:S(2)}) collective-permute-start(bf16[2,32,512]{2,1,0:T(8,128)(2,1)S(1)} %add_convert_fusion), channel_id=1, source_target_pairs={{0,8},{1,9},{2,10},{3,11},{4,12},{5,13},{6,14},{7,15},{8,0},{9,1},... | collective-permute-start | bytes 196616 | tf_op jit(solution)/shard_map/ppermute | solution.py:181
  77.9 5.2 %collective-permute-start.24 = (bf16[1,32,512]{2,1,0:T(8,128)(2,1)S(1)}, bf16[1,32,512]{2,1,0:T(8,128)(2,1)S(1)}, u32[]{:S(2)}, u32[]{:S(2)}) collective-permute-start(bf16[1,32,512]{2,1,0:T(8,128)(2,1)S(1)} %add_convert_fusion.1), channel_id=1, source_target_pairs={{0,8},{1,9},{2,10},{3,11},{4,12},{5,13},{6,14},{7,15},{8,0},{9,1},... | collective-permute-start | bytes 98312 | tf_op jit(solution)/shard_map/ppermute | solution.py:181
  80.1 14.5 %copy-start.5 = (f32[512,512]{1,0:T(8,128)S(1)}, f32[512,512]{1,0:T(8,128)}, u32[]{:S(2)}) copy-start(f32[512,512]{1,0:T(8,128)} %first_diag_ref.1) | copy-start | bytes 3145732
  80.1 14.5 %copy-start.6 = (f32[512,512]{1,0:T(8,128)S(1)}, f32[512,512]{1,0:T(8,128)}, u32[]{:S(2)}) copy-start(f32[512,512]{1,0:T(8,128)} %second_diag_ref.1) | copy-start | bytes 3145732
  80.1 5.9 %collective-permute-start.17 = (bf16[2,64,512]{2,1,0:T(8,128)(2,1)S(1)}, bf16[2,64,512]{2,1,0:T(8,128)(2,1)S(1)}, u32[]{:S(2)}, u32[]{:S(2)}) collective-permute-start(bf16[2,64,512]{2,1,0:T(8,128)(2,1)S(1)} %pad_maximum_fusion.5), channel_id=1, source_target_pairs={{0,4},{1,5},{2,6},{3,7},{4,0},{5,1},{6,2},{7,3},{8,12},{9,13},{10,... | collective-permute-start | bytes 393224 | tf_op jit(solution)/shard_map/ppermute | solution.py:181
  83.1 4.3 %collective-permute-start.25 = (bf16[1,64,512]{2,1,0:T(8,128)(2,1)S(1)}, bf16[1,64,512]{2,1,0:T(8,128)(2,1)S(1)}, u32[]{:S(2)}, u32[]{:S(2)}) collective-permute-start(bf16[1,64,512]{2,1,0:T(8,128)(2,1)S(1)} %pad_maximum_fusion.7), channel_id=1, source_target_pairs={{0,4},{1,5},{2,6},{3,7},{4,0},{5,1},{6,2},{7,3},{8,12},{9,13},{10,... | collective-permute-start | bytes 196616 | tf_op jit(solution)/shard_map/ppermute | solution.py:181
  86.1 6.4 %collective-permute-start.18 = (bf16[2,128,512]{2,1,0:T(8,128)(2,1)S(1)}, bf16[2,128,512]{2,1,0:T(8,128)(2,1)S(1)}, u32[]{:S(2)}, u32[]{:S(2)}) collective-permute-start(bf16[2,128,512]{2,1,0:T(8,128)(2,1)S(1)} %pad_maximum_fusion.3), channel_id=1, source_target_pairs={{0,2},{1,3},{2,0},{3,1},{4,6},{5,7},{6,4},{7,5},{8,10},{9,11},{10,... | collective-permute-start | bytes 786440 | tf_op jit(solution)/shard_map/ppermute | solution.py:181
  87.4 6.5 %collective-permute-start.26 = (bf16[1,128,512]{2,1,0:T(8,128)(2,1)S(1)}, bf16[1,128,512]{2,1,0:T(8,128)(2,1)S(1)}, u32[]{:S(2)}, u32[]{:S(2)}) collective-permute-start(bf16[1,128,512]{2,1,0:T(8,128)(2,1)S(1)} %pad_maximum_fusion.6), channel_id=1, source_target_pairs={{0,2},{1,3},{2,0},{3,1},{4,6},{5,7},{6,4},{7,5},{8,10},{9,11},{10,... | collective-permute-start | bytes 393224 | tf_op jit(solution)/shard_map/ppermute | solution.py:181
  92.6 2.0 %collective-permute-start.19 = (bf16[2,256,512]{2,1,0:T(8,128)(2,1)S(1)}, bf16[2,256,512]{2,1,0:T(8,128)(2,1)S(1)}, u32[]{:S(2)}, u32[]{:S(2)}) collective-permute-start(bf16[2,256,512]{2,1,0:T(8,128)(2,1)S(1)} %pad_maximum_fusion.2.mine_ref), channel_id=1, source_target_pairs={{0,1},{1,0},{2,3},{3,2},{4,5},{5,4},{6,7},{7,6},{8,9},{9,8},{10,11... | collective-permute-start | bytes 1572872 | tf_op jit(solution)/shard_map/ppermute | solution.py:181
  94.0 2.9 %collective-permute-start.27 = (bf16[1,256,512]{2,1,0:T(8,128)(2,1)S(1)}, bf16[1,256,512]{2,1,0:T(8,128)(2,1)S(1)}, u32[]{:S(2)}, u32[]{:S(2)}) collective-permute-start(bf16[1,256,512]{2,1,0:T(8,128)(2,1)S(1)} %pad_maximum_fusion.4.mine_ref), channel_id=1, source_target_pairs={{0,1},{1,0},{2,3},{3,2},{4,5},{5,4},{6,7},{7,6},{8,9},{9,8},{10,11... | collective-permute-start | bytes 786440 | tf_op jit(solution)/shard_map/ppermute | solution.py:181
  (3 other events, 2.7 us)

commit v6 on v5

--- a/solution.py
+++ b/solution.py
@@ -39,21 +39,7 @@
     return jnp.int32(0), beside, across, -across, -beside
 
 
-def split_kernel(first_hbm, second_hbm, first_0, first_1, second_0, second_1, sems):
-    half = first_0.shape[0]
-    copies = [
-        pltpu.make_async_copy(source.at[pl.ds(start, half)], target, sems.at[index])
-        for index, (source, start, target) in enumerate(
-            ((first_hbm, 0, first_0), (first_hbm, half, first_1), (second_hbm, 0, second_0), (second_hbm, half, second_1))
-        )
-    ]
-    for copy in copies:
-        copy.start()
-    for copy in copies:
-        copy.wait()
-
-
-def near_kernel(where_ref, list_ref, count_ref, sigma_hbm, lower_hbm, first_0, first_1, second_0, second_1,
+def near_kernel(where_ref, list_ref, count_ref, sigma_hbm, lower_hbm, first, second,
                 first_beside, second_beside,
                 first_acc, second_acc, turned_ref, sigma_ref, lower_ref, near_ref, sems):
     lives = []
@@ -80,31 +66,18 @@
         def _():
             target[...] = jnp.zeros(target.shape, target.dtype)
 
-    half = first_0.shape[0]
-    size = 2 * half
-    turned_ref[:size, :half] = first_0[...].T
-    turned_ref[:size, half:] = first_1[...].T
-    turned_ref[size:, :half] = second_0[...].T
-    turned_ref[size:, half:] = second_1[...].T
+    size = first.shape[0]
+    turned_ref[:size] = first[...].T
+    turned_ref[size:] = second[...].T
     arrived(0)
-    first_acc[...] = jnp.zeros_like(first_acc)
-    second_acc[...] = jnp.zeros_like(second_acc)
-    add_far(first_acc, near_ref, 0, (first_0, first_1))
-    add_far(second_acc, near_ref, 0, (second_0, second_1))
+    first_acc[...] = dot(near_ref[0], first[...])
+    second_acc[...] = dot(near_ref[0], second[...])
     arrived(1)
-    add_far(first_acc, near_ref, 1, (first_beside,))
-    add_far(second_acc, near_ref, 1, (second_beside,))
+    first_acc[...] += dot(near_ref[1], first_beside[...])
+    second_acc[...] += dot(near_ref[1], second_beside[...])
     for index in (2, 3, 4):
         arrived(index)
     copies[5].wait()
-
-
-def add_far(acc_ref, sigma_ref, index, parts):
-    start = 0
-    for part in parts:
-        rows = part.shape[0]
-        acc_ref[...] += dot(sigma_ref[index, :, start : start + rows], part[...])
-        start += rows
 
 
 def halves(value, where_ref, scratch_ref, give_ref, keep_ref, index):
@@ -115,12 +88,12 @@
     give_ref[index] = scratch_ref[pl.ds(pl.multiple_of((1 - core) * half, half), half)].astype(jnp.bfloat16)
 
 
-def first_kernel(where_ref, acc_in, across_0, across_1, far_0, far_1, rest, sigma_ref, turned_ref,
+def first_kernel(where_ref, acc_in, across, far, rest, sigma_ref, turned_ref,
                  column_ref, again_ref, give_ref, keep_ref, acc_ref):
     acc_ref[...] = acc_in[...]
-    add_far(acc_ref, sigma_ref, 0, (across_0, across_1))
-    add_far(acc_ref, sigma_ref, 1, (far_0, far_1))
-    add_far(acc_ref, sigma_ref, 2, (rest,))
+    acc_ref[...] += dot(sigma_ref[0], across[...])
+    acc_ref[...] += dot(sigma_ref[1], far[...])
+    acc_ref[...] += dot(sigma_ref[2], rest[...])
     column = (-acc_ref[...]).astype(jnp.bfloat16)
     column_ref[...] = column
     again_ref[...] = column
@@ -129,16 +102,16 @@
     halves(dot(turned_ref[size:], column), where_ref, acc_ref, give_ref, keep_ref, 1)
 
 
-def across_kernel(acc_in, column_ref, lower_ref, across_0, across_1, sigma_ref, acc_ref):
+def across_kernel(acc_in, column_ref, lower_ref, across, sigma_ref, acc_ref):
     acc_ref[...] = acc_in[...] + dot(column_ref[...], lower_ref[...])
-    add_far(acc_ref, sigma_ref, 0, (across_0, across_1))
-
-
-def second_kernel(where_ref, acc_in, far_0, far_1, rest, sigma_ref, turned_ref,
+    acc_ref[...] += dot(sigma_ref[0], across[...])
+
+
+def second_kernel(where_ref, acc_in, far, rest, sigma_ref, turned_ref,
                   column_ref, give_ref, keep_ref, acc_ref):
     acc_ref[...] = acc_in[...]
-    add_far(acc_ref, sigma_ref, 1, (far_0, far_1))
-    add_far(acc_ref, sigma_ref, 2, (rest,))
+    acc_ref[...] += dot(sigma_ref[1], far[...])
+    acc_ref[...] += dot(sigma_ref[2], rest[...])
     column = (-acc_ref[...]).astype(jnp.bfloat16)
     column_ref[...] = column
     size = column.shape[0]
@@ -182,17 +155,20 @@
 
 
 def far_of(across, devices):
-    hops = [(i, i + 4 if i % 4 < 2 else i - 4) for i in range(devices)]
-    return lax.ppermute(across, "row", [(a, b) for a, b in hops if 0 <= b < devices])
+    hops = [(i, (i + (4 if i % 4 < 2 else -4)) % devices) for i in range(devices)]
+    return lax.ppermute(across, "row", hops)
 
 
 def rest_of(across, far, give_across, devices):
-    pieces = [jnp.where(give_across, a, f) for a, f in zip(across, far)]
-    return swapped(jnp.concatenate(pieces, axis=0), 1, devices)
+    return swapped(jnp.where(give_across, across, far), 1, devices)
 
 
 def core_summed(give, keep, uppers, devices):
     return halved(keep + swapped(give, 1, devices).astype(jnp.float32), uppers[1])
+
+
+def chip_summed(give, keep, devices):
+    return keep + swapped(give, 2, devices).astype(jnp.float32)
 
 
 def halved(total, upper):
@@ -201,12 +177,11 @@
     return jnp.where(upper, low, high).astype(jnp.bfloat16), jnp.where(upper, high, low)
 
 
-def summed(give, keep, uppers, devices):
+def summed(total, uppers, devices):
     count = len(uppers)
-    for b in range(1, count):
+    for b in range(2, count):
+        give, keep = halved(total, uppers[b])
         total = keep + swapped(give, 2 ** b, devices).astype(jnp.float32)
-        if b + 1 < count:
-            give, keep = halved(total, uppers[b + 1])
     gathered = total.astype(jnp.bfloat16)
     for b in range(count - 1, 0, -1):
         other = swapped(gathered, 2 ** b, devices)
@@ -240,55 +215,52 @@
     def parts(k):
         return [jax.ShapeDtypeStruct((k, half, width), t) for t in (jnp.bfloat16, jnp.float32)]
 
-    piece = jax.ShapeDtypeStruct((half, width), jnp.bfloat16)
-    pieces = call(split_kernel, [piece] * 4, [first, second], "hh", 1, [pltpu.SemaphoreType.DMA((4,))])
-    across = [swapped(pieces[0], 2, devices), swapped(pieces[1], 2, devices)]
+    across = swapped(first, 2, devices)
+    second_across = swapped(second, 2, devices)
     beside = swapped(first, 1, devices)
     second_beside = swapped(second, 1, devices)
     first_acc, second_acc, turned, sorted_sigma, lower = call(
         near_kernel,
         [wide, wide, jax.ShapeDtypeStruct((2 * size, width), jnp.bfloat16),
          jax.ShapeDtypeStruct((3, size, width), jnp.bfloat16), narrow],
-        [where, listed, count, sigma, lower_panel, *pieces, beside, second_beside],
-        "ssshhvvvvvv",
+        [where, listed, count, sigma, lower_panel, first, second, beside, second_beside],
+        "ssshhvvvv",
         4 * one,
         [pltpu.VMEM((2, size, width), jnp.bfloat16), pltpu.SemaphoreType.DMA((6,))],
     )
-    across[0], turned, later_0 = barrier((across[0], turned, pieces[2]))
-    far = [far_of(across[0], devices)]
-    second_across = [swapped(later_0, 2, devices)]
-    across[1], later_1 = barrier((across[1], pieces[3]))
-    far.append(far_of(across[1], devices))
-    second_across.append(swapped(later_1, 2, devices))
+    across, turned = barrier((across, turned))
+    far = far_of(across, devices)
     far, second_across = barrier((far, second_across))
+    second_far = far_of(second_across, devices)
     rest = rest_of(across, far, give_across, devices)
-    second_far = [far_of(piece, devices) for piece in second_across]
     column_first, column_again, give, keep = call(
         first_kernel,
         [narrow, narrow] + parts(2),
-        [where, first_acc, *across, *far, rest, sorted_sigma, turned],
-        "svvvvvvvv",
+        [where, first_acc, across, far, rest, sorted_sigma, turned],
+        "svvvvvv",
         5 * one,
         scratch,
     )
+    give, keep = core_summed(give, keep, uppers, devices)
     give, second_across = barrier((give, second_across))
     second_rest = rest_of(second_across, second_far, give_across, devices)
-    give, keep = core_summed(give, keep, uppers, devices)
+    total = chip_summed(give, keep, devices)
     (second_acc,) = call(
-        across_kernel, [wide], [second_acc, column_again, lower, *second_across, sorted_sigma], "vvvvvv", 2 * one
-    )
-    give, second_rest = barrier((give, second_rest))
+        across_kernel, [wide], [second_acc, column_again, lower, second_across, sorted_sigma], "vvvvv", 2 * one
+    )
+    total, second_rest = barrier((total, second_rest))
     column_second, second_give, second_keep = call(
         second_kernel,
         [narrow] + parts(1),
-        [where, second_acc, *second_far, second_rest, sorted_sigma, turned],
-        "svvvvvv",
+        [where, second_acc, second_far, second_rest, sorted_sigma, turned],
+        "svvvvv",
         3 * one,
         scratch,
     )
-    mine, other = summed(give, keep, uppers, devices)
+    mine, other = summed(total, uppers, devices)
     second_give, second_keep = core_summed(second_give, second_keep, uppers, devices)
-    second_mine, second_other = summed(second_give, second_keep, uppers, devices)
+    second_total = chip_summed(second_give, second_keep, devices)
+    second_mine, second_other = summed(second_total, uppers, devices)
     block_first, block_link, base = call(
         link_kernel, [wide] * 3, [where, mine, other, lower, first_diag, second_diag], "svvvvv", 4 * one, scratch
     )

time: 98.4 us -> 103 us (1.047)
  waiting for transfers between devices: 38.4 us -> 60.1 us
  starting transfers between devices: 40.4 us -> 23.7 us
    ppermute x24 -> x22, waiting for transfers between devices: 28.8 us -> 42.1 us  [swapped(): return lax.ppermute(value, 'row', [(i, i ^ bit) for i in range(devices)])]
    ppermute x4 -> x2, starting transfers between devices: 14.8 us -> 2.15 us  [far_of(): return lax.ppermute(across, 'row', hops)]
    ppermute x4 -> x2, waiting for transfers between devices: 9.63 us -> 17.9 us  [far_of(): return lax.ppermute(across, 'row', hops)]
    ppermute x24 -> x22, starting transfers between devices: 25.6 us -> 21.5 us  [swapped(): return lax.ppermute(value, 'row', [(i, i ^ bit) for i in range(devices)])]
    pallas_call x7 -> x6, Pallas kernels: 10.8 us -> 10.6 us  [call(): pl.pallas_call(body, out_shape=outs, in_specs=[pl.BlockSpec(memory_space=...]
  transfers between devices with their start and end apart: 28 -> 24, of which waited for: 17 -> 18; matrix products, arithmetic and copies ran while one was open for 1% -> 1% of each run, Pallas kernels for 8% -> 7%
where the time goes in v6:
time: 103 us
  waiting for transfers between devices  60.1 us (58%)
  starting transfers between devices  23.7 us (23%)
  Pallas kernels  10.6 us (10%)
  local copies, waits for them, and re-layouts  5.52 us (5%)
  between operations  1.58 us (2%)
  other arithmetic  1.13 us (1%)
    ppermute x22, waiting for transfers between devices, swapped(): return lax.ppermute(value, 'row', [(i, i ^ bit) for i in range(devices)])  42.1 us
    ppermute x22, starting transfers between devices, swapped(): return lax.ppermute(value, 'row', [(i, i ^ bit) for i in range(devices)])  21.5 us
    ppermute x2, waiting for transfers between devices, far_of(): return lax.ppermute(across, 'row', hops)  17.9 us
    pallas_call x6, Pallas kernels, call(): pl.pallas_call(body, out_shape=outs, in_specs=[pl.BlockSpec(memory_space=...  10.6 us
    unnamed x14, local copies, waits for them, and re-layouts  5.52 us
    ppermute x2, starting transfers between devices, far_of(): return lax.ppermute(across, 'row', hops)  2.15 us
  transfers between devices with their start and end apart: 24, of which 18 were waited for; matrix products, arithmetic and copies ran while one was open for 1% of the time, Pallas kernels for 7%

profile of v6, /device:TPU:0, one launch (start us, length us, event | category | flops | bytes accessed | tf_op | source)
XLA Modules:
  0.0 102.5 jit_solution(10811771338359934554)
XLA Ops:
  1.2 2.9 %collective-permute-start.2 = (bf16[512,512]{1,0:T(8,128)(2,1)}, bf16[512,512]{1,0:T(8,128)(2,1)S(1)}, u32[]{:S(2)}, u32[]{:S(2)}) collective-permute-start(bf16[512,512]{1,0:T(8,128)(2,1)} %bitcast.11), channel_id=1, source_target_pairs={{0,2},{1,3},{2,0},{3,1},{4,6},{5,7},{6,4},{7,5},{8,10},{9,11},{10,... | collective-permute-start | bytes 1572872 | tf_op jit(solution)/shard_map/ppermute | solution.py:154
  4.9 1.7 %copy-done = bf16[1,1,5,512,512]{4,3,2,1,0:T(8,128)(2,1)S(1)} copy-done((bf16[1,1,5,512,512]{4,3,2,1,0:T(8,128)(2,1)S(1)}, bf16[1,1,5,512,512]{4,3,2,1,0:T(8,128)(2,1)}, u32[]{:S(2)}) %copy-start) | copy-done | bytes 2621464
  6.6 1.0 %copy-done.1 = bf16[512,512]{1,0:T(8,128)(2,1)S(1)} copy-done((bf16[512,512]{1,0:T(8,128)(2,1)S(1)}, bf16[512,512]{1,0:T(8,128)(2,1)}, u32[]{:S(2)}) %copy-start.1) | copy-done | bytes 524312
  7.7 1.0 %copy-done.2 = bf16[1,1,512,512]{3,2,1,0:T(8,128)(2,1)S(1)} copy-done((bf16[1,1,512,512]{3,2,1,0:T(8,128)(2,1)S(1)}, bf16[1,1,512,512]{3,2,1,0:T(8,128)(2,1)}, u32[]{:S(2)}) %copy-start.2) | copy-done | bytes 524312
  10.4 2.6 %shard_map.119 = (f32[512,512]{1,0:T(8,128)S(1)}, f32[512,512]{1,0:T(8,128)S(1)}, bf16[1024,512]{1,0:T(8,128)(2,1)S(1)}, bf16[3,512,512]{2,1,0:T(8,128)(2,1)S(1)}, bf16[512,512]{1,0:T(8,128)(2,1)S(1)}) custom-call(s32[1]{0:T(128)} %bitcast.where_ref, s32[5]{0:T(128)S(1)} %bitcast.16, s32[1]{0:T(128)} %bitcast.8.count_ref, bf16[5,512,512]{2,1,0:T(8,128)(2,1)S(1)} %bitcast.9, ...), custom_call_target="tpu_custom_call" | custom-call | flops 1073741824 | bytes 10485788 | tf_op jit(solution)/shard_map/pallas_call | solution.py:16
  13.0 4.1 %collective-permute-done.2.across = bf16[512,512]{1,0:T(8,128)(2,1)S(1)} collective-permute-done((bf16[512,512]{1,0:T(8,128)(2,1)}, bf16[512,512]{1,0:T(8,128)(2,1)S(1)}, u32[]{:S(2)}, u32[]{:S(2)}) %collective-permute-start.2) | collective-permute-done | bytes 524320 | tf_op jit(solution)/shard_map/ppermute | solution.py:154
  17.1 2.1 %collective-permute-start.3 = (bf16[512,512]{1,0:T(8,128)(2,1)S(1)}, bf16[512,512]{1,0:T(8,128)(2,1)S(1)}, u32[]{:S(2)}, u32[]{:S(2)}) collective-permute-start(bf16[512,512]{1,0:T(8,128)(2,1)S(1)} %collective-permute-done.2.across), channel_id=1, source_target_pairs={{0,4},{1,5},{2,14},{3,15},{4,8},{5,9},{6,2},{7,3},{8,12},{9,13},{1... | collective-permute-start | bytes 1572872 | tf_op jit(solution)/shard_map/ppermute | solution.py:159
  19.2 8.5 %collective-permute-done.4.across = bf16[512,512]{1,0:T(8,128)(2,1)S(1)} collective-permute-done((bf16[512,512]{1,0:T(8,128)(2,1)}, bf16[512,512]{1,0:T(8,128)(2,1)S(1)}, u32[]{:S(2)}, u32[]{:S(2)}) %collective-permute-start.4) | collective-permute-done | bytes 524320 | tf_op jit(solution)/shard_map/ppermute | solution.py:154
  27.8 3.9 %collective-permute-done.3.far = bf16[512,512]{1,0:T(8,128)(2,1)S(1)} collective-permute-done((bf16[512,512]{1,0:T(8,128)(2,1)S(1)}, bf16[512,512]{1,0:T(8,128)(2,1)S(1)}, u32[]{:S(2)}, u32[]{:S(2)}) %collective-permute-start.3) | collective-permute-done | bytes 524320 | tf_op jit(solution)/shard_map/ppermute | solution.py:159
  31.9 1.9 %collective-permute-done.5.rest = bf16[512,512]{1,0:T(8,128)(2,1)S(1)} collective-permute-done((bf16[512,512]{1,0:T(8,128)(2,1)S(1)}, bf16[512,512]{1,0:T(8,128)(2,1)S(1)}, u32[]{:S(2)}, u32[]{:S(2)}) %collective-permute-start.5) | collective-permute-done | bytes 524320 | tf_op jit(solution)/shard_map/ppermute | solution.py:154
  33.8 2.3 %shard_map.120 = (bf16[512,512]{1,0:T(8,128)(2,1)}, bf16[512,512]{1,0:T(8,128)(2,1)S(1)}, bf16[2,256,512]{2,1,0:T(8,128)(2,1)S(1)}, f32[2,256,512]{2,1,0:T(8,128)S(1)}) custom-call(s32[1]{0:T(128)} %bitcast.where_ref, f32[512,512]{1,0:T(8,128)S(1)} %get-tuple-element.38.acc_in, bf16[512,512]{1,0:T(8,128)(2,1)S(1)} %collective-permute-done.2.across, ...), custom_call_target="tpu_custom_call" | custom-call | flops 1342177280 | bytes 7864324 | tf_op jit(solution)/shard_map/pallas_call | solution.py:16
  36.2 1.8 %collective-permute-done.6 = bf16[2,256,512]{2,1,0:T(8,128)(2,1)S(1)} collective-permute-done((bf16[2,256,512]{2,1,0:T(8,128)(2,1)S(1)}, bf16[2,256,512]{2,1,0:T(8,128)(2,1)S(1)}, u32[]{:S(2)}, u32[]{:S(2)}) %collective-permute-start.6) | collective-permute-done | bytes 524320 | tf_op jit(solution)/shard_map/ppermute | solution.py:154
  38.2 14.0 %collective-permute-done.8.far = bf16[512,512]{1,0:T(8,128)(2,1)S(1)} collective-permute-done((bf16[512,512]{1,0:T(8,128)(2,1)S(1)}, bf16[512,512]{1,0:T(8,128)(2,1)S(1)}, u32[]{:S(2)}, u32[]{:S(2)}) %collective-permute-start.8) | collective-permute-done | bytes 524320 | tf_op jit(solution)/shard_map/ppermute | solution.py:159
  53.2 7.9 %collective-permute-done.7 = bf16[2,128,512]{2,1,0:T(8,128)(2,1)S(1)} collective-permute-done((bf16[2,128,512]{2,1,0:T(8,128)(2,1)S(1)}, bf16[2,128,512]{2,1,0:T(8,128)(2,1)S(1)}, u32[]{:S(2)}, u32[]{:S(2)}) %collective-permute-start.7) | collective-permute-done | bytes 262176 | tf_op jit(solution)/shard_map/ppermute | solution.py:154
  62.0 1.6 %shard_map.123 = (bf16[512,512]{1,0:T(8,128)(2,1)}, bf16[1,256,512]{2,1,0:T(8,128)(2,1)S(1)}, f32[1,256,512]{2,1,0:T(8,128)S(1)}) custom-call(s32[1]{0:T(128)} %bitcast.where_ref, f32[512,512]{1,0:T(8,128)S(1)} %shard_map.122.acc_in, bf16[512,512]{1,0:T(8,128)(2,1)S(1)} %collective-permute-done.8.far, bf16[512,512]{1,0:T(8,128)(2,1)S(1)} %collective-permute-done.9.rest, ...), custom_call_target="tpu_custom_call" | custom-call | flops 805306368 | bytes 6029316 | tf_op jit(solution)/shard_map/pallas_call | solution.py:16
  63.6 2.8 %collective-permute-done.10 = bf16[2,64,512]{2,1,0:T(8,128)(2,1)S(1)} collective-permute-done((bf16[2,64,512]{2,1,0:T(8,128)(2,1)S(1)}, bf16[2,64,512]{2,1,0:T(8,128)(2,1)S(1)}, u32[]{:S(2)}, u32[]{:S(2)}) %collective-permute-start.10) | collective-permute-done | bytes 131104 | tf_op jit(solution)/shard_map/ppermute | solution.py:154
  66.4 2.4 %collective-permute-start.11 = (bf16[2,32,512]{2,1,0:T(8,128)(2,1)S(1)}, bf16[2,32,512]{2,1,0:T(8,128)(2,1)S(1)}, u32[]{:S(2)}, u32[]{:S(2)}) collective-permute-start(bf16[2,32,512]{2,1,0:T(8,128)(2,1)S(1)} %select_convert_fusion.4), channel_id=1, source_target_pairs={{0,8},{1,9},{2,10},{3,11},{4,12},{5,13},{6,14},{7,15},{8,0},{9,1},... | collective-permute-start | bytes 196616 | tf_op jit(solution)/shard_map/ppermute | solution.py:154
  68.9 1.6 %collective-permute-start.17 = (bf16[1,128,512]{2,1,0:T(8,128)(2,1)S(1)}, bf16[1,128,512]{2,1,0:T(8,128)(2,1)S(1)}, u32[]{:S(2)}, u32[]{:S(2)}) collective-permute-start(bf16[1,128,512]{2,1,0:T(8,128)(2,1)S(1)} %select_convert_fusion.1), channel_id=1, source_target_pairs={{0,2},{1,3},{2,0},{3,1},{4,6},{5,7},{6,4},{7,5},{8,10},{9,11},{10,... | collective-permute-start | bytes 393224 | tf_op jit(solution)/shard_map/ppermute | solution.py:154
  70.5 1.8 %collective-permute-done.11 = bf16[2,32,512]{2,1,0:T(8,128)(2,1)S(1)} collective-permute-done((bf16[2,32,512]{2,1,0:T(8,128)(2,1)S(1)}, bf16[2,32,512]{2,1,0:T(8,128)(2,1)S(1)}, u32[]{:S(2)}, u32[]{:S(2)}) %collective-permute-start.11) | collective-permute-done | bytes 65568 | tf_op jit(solution)/shard_map/ppermute | solution.py:154
  72.4 1.7 %collective-permute-start.12 = (bf16[2,32,512]{2,1,0:T(8,128)(2,1)S(1)}, bf16[2,32,512]{2,1,0:T(8,128)(2,1)S(1)}, u32[]{:S(2)}, u32[]{:S(2)}) collective-permute-start(bf16[2,32,512]{2,1,0:T(8,128)(2,1)S(1)} %add_convert_fusion), channel_id=1, source_target_pairs={{0,8},{1,9},{2,10},{3,11},{4,12},{5,13},{6,14},{7,15},{8,0},{9,1},... | collective-permute-start | bytes 196616 | tf_op jit(solution)/shard_map/ppermute | solution.py:154
  74.2 2.2 %collective-permute-start.18 = (bf16[1,64,512]{2,1,0:T(8,128)(2,1)S(1)}, bf16[1,64,512]{2,1,0:T(8,128)(2,1)S(1)}, u32[]{:S(2)}, u32[]{:S(2)}) collective-permute-start(bf16[1,64,512]{2,1,0:T(8,128)(2,1)S(1)} %select_convert_fusion.3), channel_id=1, source_target_pairs={{0,4},{1,5},{2,6},{3,7},{4,0},{5,1},{6,2},{7,3},{8,12},{9,13},{10,... | collective-permute-start | bytes 196616 | tf_op jit(solution)/shard_map/ppermute | solution.py:154
  76.4 2.1 %collective-permute-done.12 = bf16[2,32,512]{2,1,0:T(8,128)(2,1)S(1)} collective-permute-done((bf16[2,32,512]{2,1,0:T(8,128)(2,1)S(1)}, bf16[2,32,512]{2,1,0:T(8,128)(2,1)S(1)}, u32[]{:S(2)}, u32[]{:S(2)}) %collective-permute-start.12) | collective-permute-done | bytes 65568 | tf_op jit(solution)/shard_map/ppermute | solution.py:154
  80.0 1.7 %collective-permute-start.13 = (bf16[2,64,512]{2,1,0:T(8,128)(2,1)S(1)}, bf16[2,64,512]{2,1,0:T(8,128)(2,1)S(1)}, u32[]{:S(2)}, u32[]{:S(2)}) collective-permute-start(bf16[2,64,512]{2,1,0:T(8,128)(2,1)S(1)} %pad_maximum_fusion.3), channel_id=1, source_target_pairs={{0,4},{1,5},{2,6},{3,7},{4,0},{5,1},{6,2},{7,3},{8,12},{9,13},{10,... | collective-permute-start | bytes 393224 | tf_op jit(solution)/shard_map/ppermute | solution.py:154
  81.7 2.3 %collective-permute-done.19 = bf16[1,32,512]{2,1,0:T(8,128)(2,1)S(1)} collective-permute-done((bf16[1,32,512]{2,1,0:T(8,128)(2,1)S(1)}, bf16[1,32,512]{2,1,0:T(8,128)(2,1)S(1)}, u32[]{:S(2)}, u32[]{:S(2)}) %collective-permute-start.19) | collective-permute-done | bytes 32800 | tf_op jit(solution)/shard_map/ppermute | solution.py:154
  85.4 3.5 %collective-permute-done.20 = bf16[1,32,512]{2,1,0:T(8,128)(2,1)S(1)} collective-permute-done((bf16[1,32,512]{2,1,0:T(8,128)(2,1)S(1)}, bf16[1,32,512]{2,1,0:T(8,128)(2,1)S(1)}, u32[]{:S(2)}, u32[]{:S(2)}) %collective-permute-start.20) | collective-permute-done | bytes 32800 | tf_op jit(solution)/shard_map/ppermute | solution.py:154
  88.9 1.7 %collective-permute-start.21 = (bf16[1,64,512]{2,1,0:T(8,128)(2,1)S(1)}, bf16[1,64,512]{2,1,0:T(8,128)(2,1)S(1)}, u32[]{:S(2)}, u32[]{:S(2)}) collective-permute-start(bf16[1,64,512]{2,1,0:T(8,128)(2,1)S(1)} %pad_maximum_fusion.5), channel_id=1, source_target_pairs={{0,4},{1,5},{2,6},{3,7},{4,0},{5,1},{6,2},{7,3},{8,12},{9,13},{10,... | collective-permute-start | bytes 196616 | tf_op jit(solution)/shard_map/ppermute | solution.py:154
  90.6 2.0 %collective-permute-start.14 = (bf16[2,128,512]{2,1,0:T(8,128)(2,1)S(1)}, bf16[2,128,512]{2,1,0:T(8,128)(2,1)S(1)}, u32[]{:S(2)}, u32[]{:S(2)}) collective-permute-start(bf16[2,128,512]{2,1,0:T(8,128)(2,1)S(1)} %pad_maximum_fusion.1), channel_id=1, source_target_pairs={{0,2},{1,3},{2,0},{3,1},{4,6},{5,7},{6,4},{7,5},{8,10},{9,11},{10,... | collective-permute-start | bytes 786440 | tf_op jit(solution)/shard_map/ppermute | solution.py:154
  93.2 1.6 %collective-permute-start.22 = (bf16[1,128,512]{2,1,0:T(8,128)(2,1)S(1)}, bf16[1,128,512]{2,1,0:T(8,128)(2,1)S(1)}, u32[]{:S(2)}, u32[]{:S(2)}) collective-permute-start(bf16[1,128,512]{2,1,0:T(8,128)(2,1)S(1)} %pad_maximum_fusion.4), channel_id=1, source_target_pairs={{0,2},{1,3},{2,0},{3,1},{4,6},{5,7},{6,4},{7,5},{8,10},{9,11},{10,... | collective-permute-start | bytes 393224 | tf_op jit(solution)/shard_map/ppermute | solution.py:154
  94.8 2.2 %collective-permute-done.14 = bf16[2,128,512]{2,1,0:T(8,128)(2,1)S(1)} collective-permute-done((bf16[2,128,512]{2,1,0:T(8,128)(2,1)S(1)}, bf16[2,128,512]{2,1,0:T(8,128)(2,1)S(1)}, u32[]{:S(2)}, u32[]{:S(2)}) %collective-permute-start.14) | collective-permute-done | bytes 262176 | tf_op jit(solution)/shard_map/ppermute | solution.py:154
  97.2 1.2 %collective-permute-done.22 = bf16[1,128,512]{2,1,0:T(8,128)(2,1)S(1)} collective-permute-done((bf16[1,128,512]{2,1,0:T(8,128)(2,1)S(1)}, bf16[1,128,512]{2,1,0:T(8,128)(2,1)S(1)}, u32[]{:S(2)}, u32[]{:S(2)}) %collective-permute-start.22) | collective-permute-done | bytes 131104 | tf_op jit(solution)/shard_map/ppermute | solution.py:154
  99.1 2.2 %shard_map.121 = (f32[512,512]{1,0:T(8,128)}, f32[512,512]{1,0:T(8,128)}, f32[512,512]{1,0:T(8,128)S(1)}) custom-call(s32[1]{0:T(128)} %bitcast.where_ref, bf16[2,256,512]{2,1,0:T(8,128)(2,1)S(1)} %pad_maximum_fusion.mine_ref, bf16[2,256,512]{2,1,0:T(8,128)(2,1)S(1)} %collective-permute-done.15.other_ref, bf16[512,512]{1,0:T(8,128)(2,1)S(1)} %get-tuple-element.55.lower_ref, ...), custom_call_target="tpu_custom_call" | custom-call | flops 1073741824 | bytes 6815748 | tf_op jit(solution)/shard_map/pallas_call | solution.py:16
  101.4 1.2 %shard_map.124 = f32[512,512]{1,0:T(8,128)} custom-call(s32[1]{0:T(128)} %bitcast.where_ref, bf16[1,256,512]{2,1,0:T(8,128)(2,1)S(1)} %pad_maximum_fusion.2.mine_ref, bf16[1,256,512]{2,1,0:T(8,128)(2,1)S(1)} %collective-permute-done.23.other_ref, f32[512,512]{1,0:T(8,128)S(1)} %get-tuple-element.64.base_ref), custom_call_target="tpu_custom_call" | custom-call | flops 262144 | bytes 2621444 | tf_op jit(solution)/shard_map/pallas_call | solution.py:16
  (64 shorter events, 9.5 us)
Async XLA Ops:
  0.6 4.2 %collective-permute-start = (bf16[512,512]{1,0:T(8,128)(2,1)}, bf16[512,512]{1,0:T(8,128)(2,1)S(1)}, u32[]{:S(2)}, u32[]{:S(2)}) collective-permute-start(bf16[512,512]{1,0:T(8,128)(2,1)} %bitcast.10), channel_id=1, source_target_pairs={{0,1},{1,0},{2,3},{3,2},{4,5},{5,4},{6,7},{7,6},{8,9},{9,8},{10,11... | collective-permute-start | bytes 1572872 | tf_op jit(solution)/shard_map/ppermute | solution.py:154
  1.2 3.7 %collective-permute-start.1 = (bf16[512,512]{1,0:T(8,128)(2,1)}, bf16[512,512]{1,0:T(8,128)(2,1)S(1)}, u32[]{:S(2)}, u32[]{:S(2)}) collective-permute-start(bf16[512,512]{1,0:T(8,128)(2,1)} %bitcast.13), channel_id=1, source_target_pairs={{0,1},{1,0},{2,3},{3,2},{4,5},{5,4},{6,7},{7,6},{8,9},{9,8},{10,11... | collective-permute-start | bytes 1572872 | tf_op jit(solution)/shard_map/ppermute | solution.py:154
  1.2 15.8 %collective-permute-start.2 = (bf16[512,512]{1,0:T(8,128)(2,1)}, bf16[512,512]{1,0:T(8,128)(2,1)S(1)}, u32[]{:S(2)}, u32[]{:S(2)}) collective-permute-start(bf16[512,512]{1,0:T(8,128)(2,1)} %bitcast.11), channel_id=1, source_target_pairs={{0,2},{1,3},{2,0},{3,1},{4,6},{5,7},{6,4},{7,5},{8,10},{9,11},{10,... | collective-permute-start | bytes 1572872 | tf_op jit(solution)/shard_map/ppermute | solution.py:154
  4.2 23.6 %collective-permute-start.4 = (bf16[512,512]{1,0:T(8,128)(2,1)}, bf16[512,512]{1,0:T(8,128)(2,1)S(1)}, u32[]{:S(2)}, u32[]{:S(2)}) collective-permute-start(bf16[512,512]{1,0:T(8,128)(2,1)} %bitcast.14), channel_id=1, source_target_pairs={{0,2},{1,3},{2,0},{3,1},{4,6},{5,7},{6,4},{7,5},{8,10},{9,11},{10,... | collective-permute-start | bytes 1572872 | tf_op jit(solution)/shard_map/ppermute | solution.py:154
  4.9 1.7 %copy-start = (bf16[1,1,5,512,512]{4,3,2,1,0:T(8,128)(2,1)S(1)}, bf16[1,1,5,512,512]{4,3,2,1,0:T(8,128)(2,1)}, u32[]{:S(2)}) copy-start(bf16[1,1,5,512,512]{4,3,2,1,0:T(8,128)(2,1)} %param.8) | copy-start | bytes 7864324
  6.6 1.0 %copy-start.1 = (bf16[512,512]{1,0:T(8,128)(2,1)S(1)}, bf16[512,512]{1,0:T(8,128)(2,1)}, u32[]{:S(2)}) copy-start(bf16[512,512]{1,0:T(8,128)(2,1)} %lower_hbm.1) | copy-start | bytes 1572868
  7.7 1.0 %copy-start.2 = (bf16[1,1,512,512]{3,2,1,0:T(8,128)(2,1)S(1)}, bf16[1,1,512,512]{3,2,1,0:T(8,128)(2,1)}, u32[]{:S(2)}) copy-start(bf16[1,1,512,512]{3,2,1,0:T(8,128)(2,1)} %param.9) | copy-start | bytes 1572868
  8.7 1.0 %copy-start.3 = (bf16[1,1,512,512]{3,2,1,0:T(8,128)(2,1)S(1)}, bf16[1,1,512,512]{3,2,1,0:T(8,128)(2,1)}, u32[]{:S(2)}) copy-start(bf16[1,1,512,512]{3,2,1,0:T(8,128)(2,1)} %param.10) | copy-start | bytes 1572868
  9.7 0.7 copy-start.4
  17.1 14.6 %collective-permute-start.3 = (bf16[512,512]{1,0:T(8,128)(2,1)S(1)}, bf16[512,512]{1,0:T(8,128)(2,1)S(1)}, u32[]{:S(2)}, u32[]{:S(2)}) collective-permute-start(bf16[512,512]{1,0:T(8,128)(2,1)S(1)} %collective-permute-done.2.across), channel_id=1, source_target_pairs={{0,4},{1,5},{2,14},{3,15},{4,8},{5,9},{6,2},{7,3},{8,12},{9,13},{1... | collective-permute-start | bytes 1572872 | tf_op jit(solution)/shard_map/ppermute | solution.py:159
  31.8 2.0 %collective-permute-start.5 = (bf16[512,512]{1,0:T(8,128)(2,1)S(1)}, bf16[512,512]{1,0:T(8,128)(2,1)S(1)}, u32[]{:S(2)}, u32[]{:S(2)}) collective-permute-start(bf16[512,512]{1,0:T(8,128)(2,1)S(1)} %broadcast_select_fusion.1), channel_id=1, source_target_pairs={{0,1},{1,0},{2,3},{3,2},{4,5},{5,4},{6,7},{7,6},{8,9},{9,8},{10,11... | collective-permute-start | bytes 1572872 | tf_op jit(solution)/shard_map/ppermute | solution.py:154
  36.1 1.9 %collective-permute-start.6 = (bf16[2,256,512]{2,1,0:T(8,128)(2,1)S(1)}, bf16[2,256,512]{2,1,0:T(8,128)(2,1)S(1)}, u32[]{:S(2)}, u32[]{:S(2)}) collective-permute-start(bf16[2,256,512]{2,1,0:T(8,128)(2,1)S(1)} %get-tuple-element.50), channel_id=1, source_target_pairs={{0,1},{1,0},{2,3},{3,2},{4,5},{5,4},{6,7},{7,6},{8,9},{9,8},{10,11... | collective-permute-start | bytes 1572872 | tf_op jit(solution)/shard_map/ppermute | solution.py:154
  36.2 16.0 %collective-permute-start.8 = (bf16[512,512]{1,0:T(8,128)(2,1)S(1)}, bf16[512,512]{1,0:T(8,128)(2,1)S(1)}, u32[]{:S(2)}, u32[]{:S(2)}) collective-permute-start(bf16[512,512]{1,0:T(8,128)(2,1)S(1)} %collective-permute-done.4.across), channel_id=1, source_target_pairs={{0,4},{1,5},{2,14},{3,15},{4,8},{5,9},{6,2},{7,3},{8,12},{9,13},{1... | collective-permute-start | bytes 1572872 | tf_op jit(solution)/shard_map/ppermute | solution.py:159
  52.3 8.9 %collective-permute-start.9 = (bf16[512,512]{1,0:T(8,128)(2,1)S(1)}, bf16[512,512]{1,0:T(8,128)(2,1)S(1)}, u32[]{:S(2)}, u32[]{:S(2)}) collective-permute-start(bf16[512,512]{1,0:T(8,128)(2,1)S(1)} %broadcast_select_fusion), channel_id=1, source_target_pairs={{0,1},{1,0},{2,3},{3,2},{4,5},{5,4},{6,7},{7,6},{8,9},{9,8},{10,11... | collective-permute-start | bytes 1572872 | tf_op jit(solution)/shard_map/ppermute | solution.py:154
  52.3 8.7 %collective-permute-start.7 = (bf16[2,128,512]{2,1,0:T(8,128)(2,1)S(1)}, bf16[2,128,512]{2,1,0:T(8,128)(2,1)S(1)}, u32[]{:S(2)}, u32[]{:S(2)}) collective-permute-start(bf16[2,128,512]{2,1,0:T(8,128)(2,1)S(1)} %select_convert_fusion), channel_id=1, source_target_pairs={{0,2},{1,3},{2,0},{3,1},{4,6},{5,7},{6,4},{7,5},{8,10},{9,11},{10,... | collective-permute-start | bytes 786440 | tf_op jit(solution)/shard_map/ppermute | solution.py:154
  61.2 5.1 %collective-permute-start.10 = (bf16[2,64,512]{2,1,0:T(8,128)(2,1)S(1)}, bf16[2,64,512]{2,1,0:T(8,128)(2,1)S(1)}, u32[]{:S(2)}, u32[]{:S(2)}) collective-permute-start(bf16[2,64,512]{2,1,0:T(8,128)(2,1)S(1)} %select_convert_fusion.2), channel_id=1, source_target_pairs={{0,4},{1,5},{2,6},{3,7},{4,0},{5,1},{6,2},{7,3},{8,12},{9,13},{10,... | collective-permute-start | bytes 393224 | tf_op jit(solution)/shard_map/ppermute | solution.py:154
  63.6 5.2 %collective-permute-start.16 = (bf16[1,256,512]{2,1,0:T(8,128)(2,1)S(1)}, bf16[1,256,512]{2,1,0:T(8,128)(2,1)S(1)}, u32[]{:S(2)}, u32[]{:S(2)}) collective-permute-start(bf16[1,256,512]{2,1,0:T(8,128)(2,1)S(1)} %get-tuple-element.63), channel_id=1, source_target_pairs={{0,1},{1,0},{2,3},{3,2},{4,5},{5,4},{6,7},{7,6},{8,9},{9,8},{10,11... | collective-permute-start | bytes 786440 | tf_op jit(solution)/shard_map/ppermute | solution.py:154
  66.4 5.9 %collective-permute-start.11 = (bf16[2,32,512]{2,1,0:T(8,128)(2,1)S(1)}, bf16[2,32,512]{2,1,0:T(8,128)(2,1)S(1)}, u32[]{:S(2)}, u32[]{:S(2)}) collective-permute-start(bf16[2,32,512]{2,1,0:T(8,128)(2,1)S(1)} %select_convert_fusion.4), channel_id=1, source_target_pairs={{0,8},{1,9},{2,10},{3,11},{4,12},{5,13},{6,14},{7,15},{8,0},{9,1},... | collective-permute-start | bytes 196616 | tf_op jit(solution)/shard_map/ppermute | solution.py:154
  68.9 5.2 %collective-permute-start.17 = (bf16[1,128,512]{2,1,0:T(8,128)(2,1)S(1)}, bf16[1,128,512]{2,1,0:T(8,128)(2,1)S(1)}, u32[]{:S(2)}, u32[]{:S(2)}) collective-permute-start(bf16[1,128,512]{2,1,0:T(8,128)(2,1)S(1)} %select_convert_fusion.1), channel_id=1, source_target_pairs={{0,2},{1,3},{2,0},{3,1},{4,6},{5,7},{6,4},{7,5},{8,10},{9,11},{10,... | collective-permute-start | bytes 393224 | tf_op jit(solution)/shard_map/ppermute | solution.py:154
  72.4 6.0 %collective-permute-start.12 = (bf16[2,32,512]{2,1,0:T(8,128)(2,1)S(1)}, bf16[2,32,512]{2,1,0:T(8,128)(2,1)S(1)}, u32[]{:S(2)}, u32[]{:S(2)}) collective-permute-start(bf16[2,32,512]{2,1,0:T(8,128)(2,1)S(1)} %add_convert_fusion), channel_id=1, source_target_pairs={{0,8},{1,9},{2,10},{3,11},{4,12},{5,13},{6,14},{7,15},{8,0},{9,1},... | collective-permute-start | bytes 196616 | tf_op jit(solution)/shard_map/ppermute | solution.py:154
  74.2 4.8 %collective-permute-start.18 = (bf16[1,64,512]{2,1,0:T(8,128)(2,1)S(1)}, bf16[1,64,512]{2,1,0:T(8,128)(2,1)S(1)}, u32[]{:S(2)}, u32[]{:S(2)}) collective-permute-start(bf16[1,64,512]{2,1,0:T(8,128)(2,1)S(1)} %select_convert_fusion.3), channel_id=1, source_target_pairs={{0,4},{1,5},{2,6},{3,7},{4,0},{5,1},{6,2},{7,3},{8,12},{9,13},{10,... | collective-permute-start | bytes 196616 | tf_op jit(solution)/shard_map/ppermute | solution.py:154
  79.0 4.9 %collective-permute-start.19 = (bf16[1,32,512]{2,1,0:T(8,128)(2,1)S(1)}, bf16[1,32,512]{2,1,0:T(8,128)(2,1)S(1)}, u32[]{:S(2)}, u32[]{:S(2)}) collective-permute-start(bf16[1,32,512]{2,1,0:T(8,128)(2,1)S(1)} %select_convert_fusion.5), channel_id=1, source_target_pairs={{0,8},{1,9},{2,10},{3,11},{4,12},{5,13},{6,14},{7,15},{8,0},{9,1},... | collective-permute-start | bytes 98312 | tf_op jit(solution)/shard_map/ppermute | solution.py:154
  79.9 19.2 %copy-start.5 = (f32[512,512]{1,0:T(8,128)S(1)}, f32[512,512]{1,0:T(8,128)}, u32[]{:S(2)}) copy-start(f32[512,512]{1,0:T(8,128)} %first_diag_ref.1) | copy-start | bytes 3145732
  80.0 19.2 %copy-start.6 = (f32[512,512]{1,0:T(8,128)S(1)}, f32[512,512]{1,0:T(8,128)}, u32[]{:S(2)}) copy-start(f32[512,512]{1,0:T(8,128)} %second_diag_ref.1) | copy-start | bytes 3145732
  80.0 5.3 %collective-permute-start.13 = (bf16[2,64,512]{2,1,0:T(8,128)(2,1)S(1)}, bf16[2,64,512]{2,1,0:T(8,128)(2,1)S(1)}, u32[]{:S(2)}, u32[]{:S(2)}) collective-permute-start(bf16[2,64,512]{2,1,0:T(8,128)(2,1)S(1)} %pad_maximum_fusion.3), channel_id=1, source_target_pairs={{0,4},{1,5},{2,6},{3,7},{4,0},{5,1},{6,2},{7,3},{8,12},{9,13},{10,... | collective-permute-start | bytes 393224 | tf_op jit(solution)/shard_map/ppermute | solution.py:154
  84.0 4.9 %collective-permute-start.20 = (bf16[1,32,512]{2,1,0:T(8,128)(2,1)S(1)}, bf16[1,32,512]{2,1,0:T(8,128)(2,1)S(1)}, u32[]{:S(2)}, u32[]{:S(2)}) collective-permute-start(bf16[1,32,512]{2,1,0:T(8,128)(2,1)S(1)} %add_convert_fusion.1), channel_id=1, source_target_pairs={{0,8},{1,9},{2,10},{3,11},{4,12},{5,13},{6,14},{7,15},{8,0},{9,1},... | collective-permute-start | bytes 98312 | tf_op jit(solution)/shard_map/ppermute | solution.py:154
  88.9 4.3 %collective-permute-start.21 = (bf16[1,64,512]{2,1,0:T(8,128)(2,1)S(1)}, bf16[1,64,512]{2,1,0:T(8,128)(2,1)S(1)}, u32[]{:S(2)}, u32[]{:S(2)}) collective-permute-start(bf16[1,64,512]{2,1,0:T(8,128)(2,1)S(1)} %pad_maximum_fusion.5), channel_id=1, source_target_pairs={{0,4},{1,5},{2,6},{3,7},{4,0},{5,1},{6,2},{7,3},{8,12},{9,13},{10,... | collective-permute-start | bytes 196616 | tf_op jit(solution)/shard_map/ppermute | solution.py:154
  90.6 6.4 %collective-permute-start.14 = (bf16[2,128,512]{2,1,0:T(8,128)(2,1)S(1)}, bf16[2,128,512]{2,1,0:T(8,128)(2,1)S(1)}, u32[]{:S(2)}, u32[]{:S(2)}) collective-permute-start(bf16[2,128,512]{2,1,0:T(8,128)(2,1)S(1)} %pad_maximum_fusion.1), channel_id=1, source_target_pairs={{0,2},{1,3},{2,0},{3,1},{4,6},{5,7},{6,4},{7,5},{8,10},{9,11},{10,... | collective-permute-start | bytes 786440 | tf_op jit(solution)/shard_map/ppermute | solution.py:154
  93.2 5.2 %collective-permute-start.22 = (bf16[1,128,512]{2,1,0:T(8,128)(2,1)S(1)}, bf16[1,128,512]{2,1,0:T(8,128)(2,1)S(1)}, u32[]{:S(2)}, u32[]{:S(2)}) collective-permute-start(bf16[1,128,512]{2,1,0:T(8,128)(2,1)S(1)} %pad_maximum_fusion.4), channel_id=1, source_target_pairs={{0,2},{1,3},{2,0},{3,1},{4,6},{5,7},{6,4},{7,5},{8,10},{9,11},{10,... | collective-permute-start | bytes 393224 | tf_op jit(solution)/shard_map/ppermute | solution.py:154
  97.2 2.0 %collective-permute-start.15 = (bf16[2,256,512]{2,1,0:T(8,128)(2,1)S(1)}, bf16[2,256,512]{2,1,0:T(8,128)(2,1)S(1)}, u32[]{:S(2)}, u32[]{:S(2)}) collective-permute-start(bf16[2,256,512]{2,1,0:T(8,128)(2,1)S(1)} %pad_maximum_fusion.mine_ref), channel_id=1, source_target_pairs={{0,1},{1,0},{2,3},{3,2},{4,5},{5,4},{6,7},{7,6},{8,9},{9,8},{10,11... | collective-permute-start | bytes 1572872 | tf_op jit(solution)/shard_map/ppermute | solution.py:154
  98.5 2.9 %collective-permute-start.23 = (bf16[1,256,512]{2,1,0:T(8,128)(2,1)S(1)}, bf16[1,256,512]{2,1,0:T(8,128)(2,1)S(1)}, u32[]{:S(2)}, u32[]{:S(2)}) collective-permute-start(bf16[1,256,512]{2,1,0:T(8,128)(2,1)S(1)} %pad_maximum_fusion.2.mine_ref), channel_id=1, source_target_pairs={{0,1},{1,0},{2,3},{3,2},{4,5},{5,4},{6,7},{7,6},{8,9},{9,8},{10,11... | collective-permute-start | bytes 786440 | tf_op jit(solution)/shard_map/ppermute | solution.py:154

commit v7 on v6

--- a/solution.py
+++ b/solution.py
@@ -241,14 +241,13 @@
         5 * one,
         scratch,
     )
+    give, second_across = barrier((give, second_across))
     give, keep = core_summed(give, keep, uppers, devices)
-    give, second_across = barrier((give, second_across))
     second_rest = rest_of(second_across, second_far, give_across, devices)
     total = chip_summed(give, keep, devices)
     (second_acc,) = call(
         across_kernel, [wide], [second_acc, column_again, lower, second_across, sorted_sigma], "vvvvv", 2 * one
     )
-    total, second_rest = barrier((total, second_rest))
     column_second, second_give, second_keep = call(
         second_kernel,
         [narrow] + parts(1),
@@ -257,8 +256,9 @@
         3 * one,
         scratch,
     )
+    second_give, total = barrier((second_give, total))
+    second_give, second_keep = core_summed(second_give, second_keep, uppers, devices)
     mine, other = summed(total, uppers, devices)
-    second_give, second_keep = core_summed(second_give, second_keep, uppers, devices)
     second_total = chip_summed(second_give, second_keep, devices)
     second_mine, second_other = summed(second_total, uppers, devices)
     block_first, block_link, base = call(

time: 103 us -> 99 us (0.961)
  waiting for transfers between devices: 60.1 us -> 56.6 us
    ppermute x2, waiting for transfers between devices: 17.9 us -> 15.7 us  [far_of(): return lax.ppermute(across, 'row', hops)]
    ppermute x22, waiting for transfers between devices: 42.1 us -> 40.9 us  [swapped(): return lax.ppermute(value, 'row', [(i, i ^ bit) for i in range(devices)])]
  transfers between devices with their start and end apart: 24 -> 24, of which waited for: 18 -> 18; matrix products, arithmetic and copies ran while one was open for 1% -> 1% of each run, Pallas kernels for 7% -> 10%
where the time goes in v7:
time: 99 us; the launch traced here: 98.7 us
  waiting for transfers between devices  56.6 us (57%)
  starting transfers between devices  23.2 us (23%)
  Pallas kernels  10.6 us (11%)
  local copies, waits for them, and re-layouts  5.52 us (6%)
  between operations  1.59 us (2%)
  other arithmetic  1.13 us (1%)
    ppermute x22, waiting for transfers between devices, swapped(): return lax.ppermute(value, 'row', [(i, i ^ bit) for i in range(devices)])  40.9 us
    ppermute x22, starting transfers between devices, swapped(): return lax.ppermute(value, 'row', [(i, i ^ bit) for i in range(devices)])  21 us
    ppermute x2, waiting for transfers between devices, far_of(): return lax.ppermute(across, 'row', hops)  15.7 us
    pallas_call x6, Pallas kernels, call(): pl.pallas_call(body, out_shape=outs, in_specs=[pl.BlockSpec(memory_space=...  10.6 us
    unnamed x14, local copies, waits for them, and re-layouts  5.52 us
    ppermute x2, starting transfers between devices, far_of(): return lax.ppermute(across, 'row', hops)  2.2 us
  transfers between devices with their start and end apart: 24, of which 18 were waited for; matrix products, arithmetic and copies ran while one was open for 1% of the time, Pallas kernels for 10%

profile of v7, /device:TPU:0, one launch (start us, length us, event | category | flops | bytes accessed | tf_op | source)
XLA Modules:
  0.0 98.7 jit_solution(15374588475390396110)
XLA Ops:
  1.2 2.9 %collective-permute-start.2 = (bf16[512,512]{1,0:T(8,128)(2,1)}, bf16[512,512]{1,0:T(8,128)(2,1)S(1)}, u32[]{:S(2)}, u32[]{:S(2)}) collective-permute-start(bf16[512,512]{1,0:T(8,128)(2,1)} %bitcast.11), channel_id=1, source_target_pairs={{0,2},{1,3},{2,0},{3,1},{4,6},{5,7},{6,4},{7,5},{8,10},{9,11},{10,... | collective-permute-start | bytes 1572872 | tf_op jit(solution)/shard_map/ppermute | solution.py:154
  4.9 1.7 %copy-done = bf16[1,1,5,512,512]{4,3,2,1,0:T(8,128)(2,1)S(1)} copy-done((bf16[1,1,5,512,512]{4,3,2,1,0:T(8,128)(2,1)S(1)}, bf16[1,1,5,512,512]{4,3,2,1,0:T(8,128)(2,1)}, u32[]{:S(2)}) %copy-start) | copy-done | bytes 2621464
  6.6 1.0 %copy-done.1 = bf16[512,512]{1,0:T(8,128)(2,1)S(1)} copy-done((bf16[512,512]{1,0:T(8,128)(2,1)S(1)}, bf16[512,512]{1,0:T(8,128)(2,1)}, u32[]{:S(2)}) %copy-start.1) | copy-done | bytes 524312
  7.7 1.0 %copy-done.2 = bf16[1,1,512,512]{3,2,1,0:T(8,128)(2,1)S(1)} copy-done((bf16[1,1,512,512]{3,2,1,0:T(8,128)(2,1)S(1)}, bf16[1,1,512,512]{3,2,1,0:T(8,128)(2,1)}, u32[]{:S(2)}) %copy-start.2) | copy-done | bytes 524312
  8.7 1.0 %copy-done.3 = bf16[1,1,512,512]{3,2,1,0:T(8,128)(2,1)S(1)} copy-done((bf16[1,1,512,512]{3,2,1,0:T(8,128)(2,1)S(1)}, bf16[1,1,512,512]{3,2,1,0:T(8,128)(2,1)}, u32[]{:S(2)}) %copy-start.3) | copy-done | bytes 524312
  10.4 2.6 %shard_map.119 = (f32[512,512]{1,0:T(8,128)S(1)}, f32[512,512]{1,0:T(8,128)S(1)}, bf16[1024,512]{1,0:T(8,128)(2,1)S(1)}, bf16[3,512,512]{2,1,0:T(8,128)(2,1)S(1)}, bf16[512,512]{1,0:T(8,128)(2,1)S(1)}) custom-call(s32[1]{0:T(128)} %bitcast.where_ref, s32[5]{0:T(128)S(1)} %bitcast.16, s32[1]{0:T(128)} %bitcast.8.count_ref, bf16[5,512,512]{2,1,0:T(8,128)(2,1)S(1)} %bitcast.9, ...), custom_call_target="tpu_custom_call" | custom-call | flops 1073741824 | bytes 10485788 | tf_op jit(solution)/shard_map/pallas_call | solution.py:16
  13.0 4.1 %collective-permute-done.2.across = bf16[512,512]{1,0:T(8,128)(2,1)S(1)} collective-permute-done((bf16[512,512]{1,0:T(8,128)(2,1)}, bf16[512,512]{1,0:T(8,128)(2,1)S(1)}, u32[]{:S(2)}, u32[]{:S(2)}) %collective-permute-start.2) | collective-permute-done | bytes 524320 | tf_op jit(solution)/shard_map/ppermute | solution.py:154
  17.1 2.1 %collective-permute-start.3 = (bf16[512,512]{1,0:T(8,128)(2,1)S(1)}, bf16[512,512]{1,0:T(8,128)(2,1)S(1)}, u32[]{:S(2)}, u32[]{:S(2)}) collective-permute-start(bf16[512,512]{1,0:T(8,128)(2,1)S(1)} %collective-permute-done.2.across), channel_id=1, source_target_pairs={{0,4},{1,5},{2,14},{3,15},{4,8},{5,9},{6,2},{7,3},{8,12},{9,13},{1... | collective-permute-start | bytes 1572872 | tf_op jit(solution)/shard_map/ppermute | solution.py:159
  19.2 8.5 %collective-permute-done.4.across = bf16[512,512]{1,0:T(8,128)(2,1)S(1)} collective-permute-done((bf16[512,512]{1,0:T(8,128)(2,1)}, bf16[512,512]{1,0:T(8,128)(2,1)S(1)}, u32[]{:S(2)}, u32[]{:S(2)}) %collective-permute-start.4) | collective-permute-done | bytes 524320 | tf_op jit(solution)/shard_map/ppermute | solution.py:154
  27.8 3.9 %collective-permute-done.3.far = bf16[512,512]{1,0:T(8,128)(2,1)S(1)} collective-permute-done((bf16[512,512]{1,0:T(8,128)(2,1)S(1)}, bf16[512,512]{1,0:T(8,128)(2,1)S(1)}, u32[]{:S(2)}, u32[]{:S(2)}) %collective-permute-start.3) | collective-permute-done | bytes 524320 | tf_op jit(solution)/shard_map/ppermute | solution.py:159
  31.9 1.8 %collective-permute-done.5.rest = bf16[512,512]{1,0:T(8,128)(2,1)S(1)} collective-permute-done((bf16[512,512]{1,0:T(8,128)(2,1)S(1)}, bf16[512,512]{1,0:T(8,128)(2,1)S(1)}, u32[]{:S(2)}, u32[]{:S(2)}) %collective-permute-start.5) | collective-permute-done | bytes 524320 | tf_op jit(solution)/shard_map/ppermute | solution.py:154
  33.8 2.3 %shard_map.120 = (bf16[512,512]{1,0:T(8,128)(2,1)}, bf16[512,512]{1,0:T(8,128)(2,1)S(1)}, bf16[2,256,512]{2,1,0:T(8,128)(2,1)S(1)}, f32[2,256,512]{2,1,0:T(8,128)S(1)}) custom-call(s32[1]{0:T(128)} %bitcast.where_ref, f32[512,512]{1,0:T(8,128)S(1)} %get-tuple-element.38.acc_in, bf16[512,512]{1,0:T(8,128)(2,1)S(1)} %collective-permute-done.2.across, ...), custom_call_target="tpu_custom_call" | custom-call | flops 1342177280 | bytes 7864324 | tf_op jit(solution)/shard_map/pallas_call | solution.py:16
  36.2 11.8 %collective-permute-done.6.far = bf16[512,512]{1,0:T(8,128)(2,1)S(1)} collective-permute-done((bf16[512,512]{1,0:T(8,128)(2,1)S(1)}, bf16[512,512]{1,0:T(8,128)(2,1)S(1)}, u32[]{:S(2)}, u32[]{:S(2)}) %collective-permute-start.6) | collective-permute-done | bytes 524320 | tf_op jit(solution)/shard_map/ppermute | solution.py:159
  50.0 1.6 %shard_map.122 = (bf16[512,512]{1,0:T(8,128)(2,1)}, bf16[1,256,512]{2,1,0:T(8,128)(2,1)S(1)}, f32[1,256,512]{2,1,0:T(8,128)S(1)}) custom-call(s32[1]{0:T(128)} %bitcast.where_ref, f32[512,512]{1,0:T(8,128)S(1)} %shard_map.121.acc_in, bf16[512,512]{1,0:T(8,128)(2,1)S(1)} %collective-permute-done.6.far, bf16[512,512]{1,0:T(8,128)(2,1)S(1)} %collective-permute-done.7.rest, ...), custom_call_target="tpu_custom_call" | custom-call | flops 805306368 | bytes 6029316 | tf_op jit(solution)/shard_map/pallas_call | solution.py:16
  51.6 5.6 %collective-permute-done.9 = bf16[2,128,512]{2,1,0:T(8,128)(2,1)S(1)} collective-permute-done((bf16[2,128,512]{2,1,0:T(8,128)(2,1)S(1)}, bf16[2,128,512]{2,1,0:T(8,128)(2,1)S(1)}, u32[]{:S(2)}, u32[]{:S(2)}) %collective-permute-start.9) | collective-permute-done | bytes 262176 | tf_op jit(solution)/shard_map/ppermute | solution.py:154
  57.5 5.0 %collective-permute-done.10 = bf16[2,64,512]{2,1,0:T(8,128)(2,1)S(1)} collective-permute-done((bf16[2,64,512]{2,1,0:T(8,128)(2,1)S(1)}, bf16[2,64,512]{2,1,0:T(8,128)(2,1)S(1)}, u32[]{:S(2)}, u32[]{:S(2)}) %collective-permute-start.10) | collective-permute-done | bytes 131104 | tf_op jit(solution)/shard_map/ppermute | solution.py:154
  62.6 2.4 %collective-permute-start.11 = (bf16[2,32,512]{2,1,0:T(8,128)(2,1)S(1)}, bf16[2,32,512]{2,1,0:T(8,128)(2,1)S(1)}, u32[]{:S(2)}, u32[]{:S(2)}) collective-permute-start(bf16[2,32,512]{2,1,0:T(8,128)(2,1)S(1)} %select_convert_fusion.4), channel_id=1, source_target_pairs={{0,8},{1,9},{2,10},{3,11},{4,12},{5,13},{6,14},{7,15},{8,0},{9,1},... | collective-permute-start | bytes 196616 | tf_op jit(solution)/shard_map/ppermute | solution.py:154
  65.1 1.6 %collective-permute-start.17 = (bf16[1,128,512]{2,1,0:T(8,128)(2,1)S(1)}, bf16[1,128,512]{2,1,0:T(8,128)(2,1)S(1)}, u32[]{:S(2)}, u32[]{:S(2)}) collective-permute-start(bf16[1,128,512]{2,1,0:T(8,128)(2,1)S(1)} %select_convert_fusion.1), channel_id=1, source_target_pairs={{0,2},{1,3},{2,0},{3,1},{4,6},{5,7},{6,4},{7,5},{8,10},{9,11},{10,... | collective-permute-start | bytes 393224 | tf_op jit(solution)/shard_map/ppermute | solution.py:154
  66.7 1.8 %collective-permute-done.11 = bf16[2,32,512]{2,1,0:T(8,128)(2,1)S(1)} collective-permute-done((bf16[2,32,512]{2,1,0:T(8,128)(2,1)S(1)}, bf16[2,32,512]{2,1,0:T(8,128)(2,1)S(1)}, u32[]{:S(2)}, u32[]{:S(2)}) %collective-permute-start.11) | collective-permute-done | bytes 65568 | tf_op jit(solution)/shard_map/ppermute | solution.py:154
  68.5 1.7 %collective-permute-start.12 = (bf16[2,32,512]{2,1,0:T(8,128)(2,1)S(1)}, bf16[2,32,512]{2,1,0:T(8,128)(2,1)S(1)}, u32[]{:S(2)}, u32[]{:S(2)}) collective-permute-start(bf16[2,32,512]{2,1,0:T(8,128)(2,1)S(1)} %add_convert_fusion), channel_id=1, source_target_pairs={{0,8},{1,9},{2,10},{3,11},{4,12},{5,13},{6,14},{7,15},{8,0},{9,1},... | collective-permute-start | bytes 196616 | tf_op jit(solution)/shard_map/ppermute | solution.py:154
  70.3 2.2 %collective-permute-start.18 = (bf16[1,64,512]{2,1,0:T(8,128)(2,1)S(1)}, bf16[1,64,512]{2,1,0:T(8,128)(2,1)S(1)}, u32[]{:S(2)}, u32[]{:S(2)}) collective-permute-start(bf16[1,64,512]{2,1,0:T(8,128)(2,1)S(1)} %select_convert_fusion.3), channel_id=1, source_target_pairs={{0,4},{1,5},{2,6},{3,7},{4,0},{5,1},{6,2},{7,3},{8,12},{9,13},{10,... | collective-permute-start | bytes 196616 | tf_op jit(solution)/shard_map/ppermute | solution.py:154
  72.5 2.1 %collective-permute-done.12 = bf16[2,32,512]{2,1,0:T(8,128)(2,1)S(1)} collective-permute-done((bf16[2,32,512]{2,1,0:T(8,128)(2,1)S(1)}, bf16[2,32,512]{2,1,0:T(8,128)(2,1)S(1)}, u32[]{:S(2)}, u32[]{:S(2)}) %collective-permute-start.12) | collective-permute-done | bytes 65568 | tf_op jit(solution)/shard_map/ppermute | solution.py:154
  76.1 1.7 %collective-permute-start.13 = (bf16[2,64,512]{2,1,0:T(8,128)(2,1)S(1)}, bf16[2,64,512]{2,1,0:T(8,128)(2,1)S(1)}, u32[]{:S(2)}, u32[]{:S(2)}) collective-permute-start(bf16[2,64,512]{2,1,0:T(8,128)(2,1)S(1)} %pad_maximum_fusion.3), channel_id=1, source_target_pairs={{0,4},{1,5},{2,6},{3,7},{4,0},{5,1},{6,2},{7,3},{8,12},{9,13},{10,... | collective-permute-start | bytes 393224 | tf_op jit(solution)/shard_map/ppermute | solution.py:154
  77.8 2.2 %collective-permute-done.19 = bf16[1,32,512]{2,1,0:T(8,128)(2,1)S(1)} collective-permute-done((bf16[1,32,512]{2,1,0:T(8,128)(2,1)S(1)}, bf16[1,32,512]{2,1,0:T(8,128)(2,1)S(1)}, u32[]{:S(2)}, u32[]{:S(2)}) %collective-permute-start.19) | collective-permute-done | bytes 32800 | tf_op jit(solution)/shard_map/ppermute | solution.py:154
  81.4 3.5 %collective-permute-done.20 = bf16[1,32,512]{2,1,0:T(8,128)(2,1)S(1)} collective-permute-done((bf16[1,32,512]{2,1,0:T(8,128)(2,1)S(1)}, bf16[1,32,512]{2,1,0:T(8,128)(2,1)S(1)}, u32[]{:S(2)}, u32[]{:S(2)}) %collective-permute-start.20) | collective-permute-done | bytes 32800 | tf_op jit(solution)/shard_map/ppermute | solution.py:154
  84.9 1.8 %collective-permute-start.21 = (bf16[1,64,512]{2,1,0:T(8,128)(2,1)S(1)}, bf16[1,64,512]{2,1,0:T(8,128)(2,1)S(1)}, u32[]{:S(2)}, u32[]{:S(2)}) collective-permute-start(bf16[1,64,512]{2,1,0:T(8,128)(2,1)S(1)} %pad_maximum_fusion.5), channel_id=1, source_target_pairs={{0,4},{1,5},{2,6},{3,7},{4,0},{5,1},{6,2},{7,3},{8,12},{9,13},{10,... | collective-permute-start | bytes 196616 | tf_op jit(solution)/shard_map/ppermute | solution.py:154
  86.7 1.6 %collective-permute-start.14 = (bf16[2,128,512]{2,1,0:T(8,128)(2,1)S(1)}, bf16[2,128,512]{2,1,0:T(8,128)(2,1)S(1)}, u32[]{:S(2)}, u32[]{:S(2)}) collective-permute-start(bf16[2,128,512]{2,1,0:T(8,128)(2,1)S(1)} %pad_maximum_fusion.1), channel_id=1, source_target_pairs={{0,2},{1,3},{2,0},{3,1},{4,6},{5,7},{6,4},{7,5},{8,10},{9,11},{10,... | collective-permute-start | bytes 786440 | tf_op jit(solution)/shard_map/ppermute | solution.py:154
  89.3 1.3 %collective-permute-start.22 = (bf16[1,128,512]{2,1,0:T(8,128)(2,1)S(1)}, bf16[1,128,512]{2,1,0:T(8,128)(2,1)S(1)}, u32[]{:S(2)}, u32[]{:S(2)}) collective-permute-start(bf16[1,128,512]{2,1,0:T(8,128)(2,1)S(1)} %pad_maximum_fusion.4), channel_id=1, source_target_pairs={{0,2},{1,3},{2,0},{3,1},{4,6},{5,7},{6,4},{7,5},{8,10},{9,11},{10,... | collective-permute-start | bytes 393224 | tf_op jit(solution)/shard_map/ppermute | solution.py:154
  90.6 2.6 %collective-permute-done.14 = bf16[2,128,512]{2,1,0:T(8,128)(2,1)S(1)} collective-permute-done((bf16[2,128,512]{2,1,0:T(8,128)(2,1)S(1)}, bf16[2,128,512]{2,1,0:T(8,128)(2,1)S(1)}, u32[]{:S(2)}, u32[]{:S(2)}) %collective-permute-start.14) | collective-permute-done | bytes 262176 | tf_op jit(solution)/shard_map/ppermute | solution.py:154
  93.4 1.2 %collective-permute-done.22 = bf16[1,128,512]{2,1,0:T(8,128)(2,1)S(1)} collective-permute-done((bf16[1,128,512]{2,1,0:T(8,128)(2,1)S(1)}, bf16[1,128,512]{2,1,0:T(8,128)(2,1)S(1)}, u32[]{:S(2)}, u32[]{:S(2)}) %collective-permute-start.22) | collective-permute-done | bytes 131104 | tf_op jit(solution)/shard_map/ppermute | solution.py:154
  95.3 2.2 %shard_map.123 = (f32[512,512]{1,0:T(8,128)}, f32[512,512]{1,0:T(8,128)}, f32[512,512]{1,0:T(8,128)S(1)}) custom-call(s32[1]{0:T(128)} %bitcast.where_ref, bf16[2,256,512]{2,1,0:T(8,128)(2,1)S(1)} %pad_maximum_fusion.mine_ref, bf16[2,256,512]{2,1,0:T(8,128)(2,1)S(1)} %collective-permute-done.15.other_ref, bf16[512,512]{1,0:T(8,128)(2,1)S(1)} %get-tuple-element.51.lower_ref, ...), custom_call_target="tpu_custom_call" | custom-call | flops 1073741824 | bytes 6815748 | tf_op jit(solution)/shard_map/pallas_call | solution.py:16
  97.5 1.2 %shard_map.124 = f32[512,512]{1,0:T(8,128)} custom-call(s32[1]{0:T(128)} %bitcast.where_ref, bf16[1,256,512]{2,1,0:T(8,128)(2,1)S(1)} %pad_maximum_fusion.2.mine_ref, bf16[1,256,512]{2,1,0:T(8,128)(2,1)S(1)} %collective-permute-done.23.other_ref, f32[512,512]{1,0:T(8,128)S(1)} %get-tuple-element.64.base_ref), custom_call_target="tpu_custom_call" | custom-call | flops 262144 | bytes 2621444 | tf_op jit(solution)/shard_map/pallas_call | solution.py:16
  (64 shorter events, 9.0 us)
Async XLA Ops:
  0.6 4.2 %collective-permute-start = (bf16[512,512]{1,0:T(8,128)(2,1)}, bf16[512,512]{1,0:T(8,128)(2,1)S(1)}, u32[]{:S(2)}, u32[]{:S(2)}) collective-permute-start(bf16[512,512]{1,0:T(8,128)(2,1)} %bitcast.10), channel_id=1, source_target_pairs={{0,1},{1,0},{2,3},{3,2},{4,5},{5,4},{6,7},{7,6},{8,9},{9,8},{10,11... | collective-permute-start | bytes 1572872 | tf_op jit(solution)/shard_map/ppermute | solution.py:154
  1.2 3.7 %collective-permute-start.1 = (bf16[512,512]{1,0:T(8,128)(2,1)}, bf16[512,512]{1,0:T(8,128)(2,1)S(1)}, u32[]{:S(2)}, u32[]{:S(2)}) collective-permute-start(bf16[512,512]{1,0:T(8,128)(2,1)} %bitcast.13), channel_id=1, source_target_pairs={{0,1},{1,0},{2,3},{3,2},{4,5},{5,4},{6,7},{7,6},{8,9},{9,8},{10,11... | collective-permute-start | bytes 1572872 | tf_op jit(solution)/shard_map/ppermute | solution.py:154
  1.2 15.8 %collective-permute-start.2 = (bf16[512,512]{1,0:T(8,128)(2,1)}, bf16[512,512]{1,0:T(8,128)(2,1)S(1)}, u32[]{:S(2)}, u32[]{:S(2)}) collective-permute-start(bf16[512,512]{1,0:T(8,128)(2,1)} %bitcast.11), channel_id=1, source_target_pairs={{0,2},{1,3},{2,0},{3,1},{4,6},{5,7},{6,4},{7,5},{8,10},{9,11},{10,... | collective-permute-start | bytes 1572872 | tf_op jit(solution)/shard_map/ppermute | solution.py:154
  4.2 23.6 %collective-permute-start.4 = (bf16[512,512]{1,0:T(8,128)(2,1)}, bf16[512,512]{1,0:T(8,128)(2,1)S(1)}, u32[]{:S(2)}, u32[]{:S(2)}) collective-permute-start(bf16[512,512]{1,0:T(8,128)(2,1)} %bitcast.14), channel_id=1, source_target_pairs={{0,2},{1,3},{2,0},{3,1},{4,6},{5,7},{6,4},{7,5},{8,10},{9,11},{10,... | collective-permute-start | bytes 1572872 | tf_op jit(solution)/shard_map/ppermute | solution.py:154
  4.9 1.7 %copy-start = (bf16[1,1,5,512,512]{4,3,2,1,0:T(8,128)(2,1)S(1)}, bf16[1,1,5,512,512]{4,3,2,1,0:T(8,128)(2,1)}, u32[]{:S(2)}) copy-start(bf16[1,1,5,512,512]{4,3,2,1,0:T(8,128)(2,1)} %param.8) | copy-start | bytes 7864324
  6.6 1.0 %copy-start.1 = (bf16[512,512]{1,0:T(8,128)(2,1)S(1)}, bf16[512,512]{1,0:T(8,128)(2,1)}, u32[]{:S(2)}) copy-start(bf16[512,512]{1,0:T(8,128)(2,1)} %lower_hbm.1) | copy-start | bytes 1572868
  7.7 1.0 %copy-start.2 = (bf16[1,1,512,512]{3,2,1,0:T(8,128)(2,1)S(1)}, bf16[1,1,512,512]{3,2,1,0:T(8,128)(2,1)}, u32[]{:S(2)}) copy-start(bf16[1,1,512,512]{3,2,1,0:T(8,128)(2,1)} %param.9) | copy-start | bytes 1572868
  8.7 1.0 %copy-start.3 = (bf16[1,1,512,512]{3,2,1,0:T(8,128)(2,1)S(1)}, bf16[1,1,512,512]{3,2,1,0:T(8,128)(2,1)}, u32[]{:S(2)}) copy-start(bf16[1,1,512,512]{3,2,1,0:T(8,128)(2,1)} %param.10) | copy-start | bytes 1572868
  9.7 0.7 copy-start.4
  17.1 14.6 %collective-permute-start.3 = (bf16[512,512]{1,0:T(8,128)(2,1)S(1)}, bf16[512,512]{1,0:T(8,128)(2,1)S(1)}, u32[]{:S(2)}, u32[]{:S(2)}) collective-permute-start(bf16[512,512]{1,0:T(8,128)(2,1)S(1)} %collective-permute-done.2.across), channel_id=1, source_target_pairs={{0,4},{1,5},{2,14},{3,15},{4,8},{5,9},{6,2},{7,3},{8,12},{9,13},{1... | collective-permute-start | bytes 1572872 | tf_op jit(solution)/shard_map/ppermute | solution.py:159
  31.8 2.0 %collective-permute-start.5 = (bf16[512,512]{1,0:T(8,128)(2,1)S(1)}, bf16[512,512]{1,0:T(8,128)(2,1)S(1)}, u32[]{:S(2)}, u32[]{:S(2)}) collective-permute-start(bf16[512,512]{1,0:T(8,128)(2,1)S(1)} %broadcast_select_fusion.1), channel_id=1, source_target_pairs={{0,1},{1,0},{2,3},{3,2},{4,5},{5,4},{6,7},{7,6},{8,9},{9,8},{10,11... | collective-permute-start | bytes 1572872 | tf_op jit(solution)/shard_map/ppermute | solution.py:154
  31.9 16.1 %collective-permute-start.6 = (bf16[512,512]{1,0:T(8,128)(2,1)S(1)}, bf16[512,512]{1,0:T(8,128)(2,1)S(1)}, u32[]{:S(2)}, u32[]{:S(2)}) collective-permute-start(bf16[512,512]{1,0:T(8,128)(2,1)S(1)} %collective-permute-done.4.across), channel_id=1, source_target_pairs={{0,4},{1,5},{2,14},{3,15},{4,8},{5,9},{6,2},{7,3},{8,12},{9,13},{1... | collective-permute-start | bytes 1572872 | tf_op jit(solution)/shard_map/ppermute | solution.py:159
  36.1 12.1 %collective-permute-start.8 = (bf16[2,256,512]{2,1,0:T(8,128)(2,1)S(1)}, bf16[2,256,512]{2,1,0:T(8,128)(2,1)S(1)}, u32[]{:S(2)}, u32[]{:S(2)}) collective-permute-start(bf16[2,256,512]{2,1,0:T(8,128)(2,1)S(1)} %get-tuple-element.57), channel_id=1, source_target_pairs={{0,1},{1,0},{2,3},{3,2},{4,5},{5,4},{6,7},{7,6},{8,9},{9,8},{10,11... | collective-permute-start | bytes 1572872 | tf_op jit(solution)/shard_map/ppermute | solution.py:154
  48.0 2.0 %collective-permute-start.7 = (bf16[512,512]{1,0:T(8,128)(2,1)S(1)}, bf16[512,512]{1,0:T(8,128)(2,1)S(1)}, u32[]{:S(2)}, u32[]{:S(2)}) collective-permute-start(bf16[512,512]{1,0:T(8,128)(2,1)S(1)} %broadcast_select_fusion), channel_id=1, source_target_pairs={{0,1},{1,0},{2,3},{3,2},{4,5},{5,4},{6,7},{7,6},{8,9},{9,8},{10,11... | collective-permute-start | bytes 1572872 | tf_op jit(solution)/shard_map/ppermute | solution.py:154
  48.4 8.8 %collective-permute-start.9 = (bf16[2,128,512]{2,1,0:T(8,128)(2,1)S(1)}, bf16[2,128,512]{2,1,0:T(8,128)(2,1)S(1)}, u32[]{:S(2)}, u32[]{:S(2)}) collective-permute-start(bf16[2,128,512]{2,1,0:T(8,128)(2,1)S(1)} %select_convert_fusion), channel_id=1, source_target_pairs={{0,2},{1,3},{2,0},{3,1},{4,6},{5,7},{6,4},{7,5},{8,10},{9,11},{10,... | collective-permute-start | bytes 786440 | tf_op jit(solution)/shard_map/ppermute | solution.py:154
  57.3 5.2 %collective-permute-start.10 = (bf16[2,64,512]{2,1,0:T(8,128)(2,1)S(1)}, bf16[2,64,512]{2,1,0:T(8,128)(2,1)S(1)}, u32[]{:S(2)}, u32[]{:S(2)}) collective-permute-start(bf16[2,64,512]{2,1,0:T(8,128)(2,1)S(1)} %select_convert_fusion.2), channel_id=1, source_target_pairs={{0,4},{1,5},{2,6},{3,7},{4,0},{5,1},{6,2},{7,3},{8,12},{9,13},{10,... | collective-permute-start | bytes 393224 | tf_op jit(solution)/shard_map/ppermute | solution.py:154
  57.4 7.6 %collective-permute-start.16 = (bf16[1,256,512]{2,1,0:T(8,128)(2,1)S(1)}, bf16[1,256,512]{2,1,0:T(8,128)(2,1)S(1)}, u32[]{:S(2)}, u32[]{:S(2)}) collective-permute-start(bf16[1,256,512]{2,1,0:T(8,128)(2,1)S(1)} %get-tuple-element.63), channel_id=1, source_target_pairs={{0,1},{1,0},{2,3},{3,2},{4,5},{5,4},{6,7},{7,6},{8,9},{9,8},{10,11... | collective-permute-start | bytes 786440 | tf_op jit(solution)/shard_map/ppermute | solution.py:154
  62.6 5.9 %collective-permute-start.11 = (bf16[2,32,512]{2,1,0:T(8,128)(2,1)S(1)}, bf16[2,32,512]{2,1,0:T(8,128)(2,1)S(1)}, u32[]{:S(2)}, u32[]{:S(2)}) collective-permute-start(bf16[2,32,512]{2,1,0:T(8,128)(2,1)S(1)} %select_convert_fusion.4), channel_id=1, source_target_pairs={{0,8},{1,9},{2,10},{3,11},{4,12},{5,13},{6,14},{7,15},{8,0},{9,1},... | collective-permute-start | bytes 196616 | tf_op jit(solution)/shard_map/ppermute | solution.py:154
  65.1 5.2 %collective-permute-start.17 = (bf16[1,128,512]{2,1,0:T(8,128)(2,1)S(1)}, bf16[1,128,512]{2,1,0:T(8,128)(2,1)S(1)}, u32[]{:S(2)}, u32[]{:S(2)}) collective-permute-start(bf16[1,128,512]{2,1,0:T(8,128)(2,1)S(1)} %select_convert_fusion.1), channel_id=1, source_target_pairs={{0,2},{1,3},{2,0},{3,1},{4,6},{5,7},{6,4},{7,5},{8,10},{9,11},{10,... | collective-permute-start | bytes 393224 | tf_op jit(solution)/shard_map/ppermute | solution.py:154
  68.5 6.0 %collective-permute-start.12 = (bf16[2,32,512]{2,1,0:T(8,128)(2,1)S(1)}, bf16[2,32,512]{2,1,0:T(8,128)(2,1)S(1)}, u32[]{:S(2)}, u32[]{:S(2)}) collective-permute-start(bf16[2,32,512]{2,1,0:T(8,128)(2,1)S(1)} %add_convert_fusion), channel_id=1, source_target_pairs={{0,8},{1,9},{2,10},{3,11},{4,12},{5,13},{6,14},{7,15},{8,0},{9,1},... | collective-permute-start | bytes 196616 | tf_op jit(solution)/shard_map/ppermute | solution.py:154
  70.3 4.7 %collective-permute-start.18 = (bf16[1,64,512]{2,1,0:T(8,128)(2,1)S(1)}, bf16[1,64,512]{2,1,0:T(8,128)(2,1)S(1)}, u32[]{:S(2)}, u32[]{:S(2)}) collective-permute-start(bf16[1,64,512]{2,1,0:T(8,128)(2,1)S(1)} %select_convert_fusion.3), channel_id=1, source_target_pairs={{0,4},{1,5},{2,6},{3,7},{4,0},{5,1},{6,2},{7,3},{8,12},{9,13},{10,... | collective-permute-start | bytes 196616 | tf_op jit(solution)/shard_map/ppermute | solution.py:154
  75.1 4.9 %collective-permute-start.19 = (bf16[1,32,512]{2,1,0:T(8,128)(2,1)S(1)}, bf16[1,32,512]{2,1,0:T(8,128)(2,1)S(1)}, u32[]{:S(2)}, u32[]{:S(2)}) collective-permute-start(bf16[1,32,512]{2,1,0:T(8,128)(2,1)S(1)} %select_convert_fusion.5), channel_id=1, source_target_pairs={{0,8},{1,9},{2,10},{3,11},{4,12},{5,13},{6,14},{7,15},{8,0},{9,1},... | collective-permute-start | bytes 98312 | tf_op jit(solution)/shard_map/ppermute | solution.py:154
  76.0 19.2 %copy-start.5 = (f32[512,512]{1,0:T(8,128)S(1)}, f32[512,512]{1,0:T(8,128)}, u32[]{:S(2)}) copy-start(f32[512,512]{1,0:T(8,128)} %first_diag_ref.1) | copy-start | bytes 3145732
  76.1 19.2 %copy-start.6 = (f32[512,512]{1,0:T(8,128)S(1)}, f32[512,512]{1,0:T(8,128)}, u32[]{:S(2)}) copy-start(f32[512,512]{1,0:T(8,128)} %second_diag_ref.1) | copy-start | bytes 3145732
  76.1 5.3 %collective-permute-start.13 = (bf16[2,64,512]{2,1,0:T(8,128)(2,1)S(1)}, bf16[2,64,512]{2,1,0:T(8,128)(2,1)S(1)}, u32[]{:S(2)}, u32[]{:S(2)}) collective-permute-start(bf16[2,64,512]{2,1,0:T(8,128)(2,1)S(1)} %pad_maximum_fusion.3), channel_id=1, source_target_pairs={{0,4},{1,5},{2,6},{3,7},{4,0},{5,1},{6,2},{7,3},{8,12},{9,13},{10,... | collective-permute-start | bytes 393224 | tf_op jit(solution)/shard_map/ppermute | solution.py:154
  80.0 4.9 %collective-permute-start.20 = (bf16[1,32,512]{2,1,0:T(8,128)(2,1)S(1)}, bf16[1,32,512]{2,1,0:T(8,128)(2,1)S(1)}, u32[]{:S(2)}, u32[]{:S(2)}) collective-permute-start(bf16[1,32,512]{2,1,0:T(8,128)(2,1)S(1)} %add_convert_fusion.1), channel_id=1, source_target_pairs={{0,8},{1,9},{2,10},{3,11},{4,12},{5,13},{6,14},{7,15},{8,0},{9,1},... | collective-permute-start | bytes 98312 | tf_op jit(solution)/shard_map/ppermute | solution.py:154
  84.9 4.3 %collective-permute-start.21 = (bf16[1,64,512]{2,1,0:T(8,128)(2,1)S(1)}, bf16[1,64,512]{2,1,0:T(8,128)(2,1)S(1)}, u32[]{:S(2)}, u32[]{:S(2)}) collective-permute-start(bf16[1,64,512]{2,1,0:T(8,128)(2,1)S(1)} %pad_maximum_fusion.5), channel_id=1, source_target_pairs={{0,4},{1,5},{2,6},{3,7},{4,0},{5,1},{6,2},{7,3},{8,12},{9,13},{10,... | collective-permute-start | bytes 196616 | tf_op jit(solution)/shard_map/ppermute | solution.py:154
  86.7 6.4 %collective-permute-start.14 = (bf16[2,128,512]{2,1,0:T(8,128)(2,1)S(1)}, bf16[2,128,512]{2,1,0:T(8,128)(2,1)S(1)}, u32[]{:S(2)}, u32[]{:S(2)}) collective-permute-start(bf16[2,128,512]{2,1,0:T(8,128)(2,1)S(1)} %pad_maximum_fusion.1), channel_id=1, source_target_pairs={{0,2},{1,3},{2,0},{3,1},{4,6},{5,7},{6,4},{7,5},{8,10},{9,11},{10,... | collective-permute-start | bytes 786440 | tf_op jit(solution)/shard_map/ppermute | solution.py:154
  89.3 5.2 %collective-permute-start.22 = (bf16[1,128,512]{2,1,0:T(8,128)(2,1)S(1)}, bf16[1,128,512]{2,1,0:T(8,128)(2,1)S(1)}, u32[]{:S(2)}, u32[]{:S(2)}) collective-permute-start(bf16[1,128,512]{2,1,0:T(8,128)(2,1)S(1)} %pad_maximum_fusion.4), channel_id=1, source_target_pairs={{0,2},{1,3},{2,0},{3,1},{4,6},{5,7},{6,4},{7,5},{8,10},{9,11},{10,... | collective-permute-start | bytes 393224 | tf_op jit(solution)/shard_map/ppermute | solution.py:154
  93.3 2.0 %collective-permute-start.15 = (bf16[2,256,512]{2,1,0:T(8,128)(2,1)S(1)}, bf16[2,256,512]{2,1,0:T(8,128)(2,1)S(1)}, u32[]{:S(2)}, u32[]{:S(2)}) collective-permute-start(bf16[2,256,512]{2,1,0:T(8,128)(2,1)S(1)} %pad_maximum_fusion.mine_ref), channel_id=1, source_target_pairs={{0,1},{1,0},{2,3},{3,2},{4,5},{5,4},{6,7},{7,6},{8,9},{9,8},{10,11... | collective-permute-start | bytes 1572872 | tf_op jit(solution)/shard_map/ppermute | solution.py:154
  94.6 2.9 %collective-permute-start.23 = (bf16[1,256,512]{2,1,0:T(8,128)(2,1)S(1)}, bf16[1,256,512]{2,1,0:T(8,128)(2,1)S(1)}, u32[]{:S(2)}, u32[]{:S(2)}) collective-permute-start(bf16[1,256,512]{2,1,0:T(8,128)(2,1)S(1)} %pad_maximum_fusion.2.mine_ref), channel_id=1, source_target_pairs={{0,1},{1,0},{2,3},{3,2},{4,5},{5,4},{6,7},{7,6},{8,9},{9,8},{10,11... | collective-permute-start | bytes 786440 | tf_op jit(solution)/shard_map/ppermute | solution.py:154

commit v8 on v7

--- a/solution.py
+++ b/solution.py
@@ -107,10 +107,12 @@
     acc_ref[...] += dot(sigma_ref[0], across[...])
 
 
-def second_kernel(where_ref, acc_in, far, rest, sigma_ref, turned_ref,
+def second_kernel(where_ref, acc_in, far_0, far_1, rest, sigma_ref, turned_ref,
                   column_ref, give_ref, keep_ref, acc_ref):
+    half = far_0.shape[0]
     acc_ref[...] = acc_in[...]
-    acc_ref[...] += dot(sigma_ref[1], far[...])
+    acc_ref[...] += dot(sigma_ref[1, :, :half], far_0[...])
+    acc_ref[...] += dot(sigma_ref[1, :, half:], far_1[...])
     acc_ref[...] += dot(sigma_ref[2], rest[...])
     column = (-acc_ref[...]).astype(jnp.bfloat16)
     column_ref[...] = column
@@ -160,7 +162,9 @@
 
 
 def rest_of(across, far, give_across, devices):
-    return swapped(jnp.where(give_across, across, far), 1, devices)
+    rows = across.shape[0] // len(far)
+    pieces = [jnp.where(give_across, across[i * rows : (i + 1) * rows], piece) for i, piece in enumerate(far)]
+    return swapped(jnp.concatenate(pieces, axis=0), 1, devices)
 
 
 def core_summed(give, keep, uppers, devices):
@@ -178,12 +182,13 @@
 
 
 def summed(total, uppers, devices):
-    count = len(uppers)
-    for b in range(2, count):
+    last = len(uppers) - 1
+    for b in range(2, last):
         give, keep = halved(total, uppers[b])
         total = keep + swapped(give, 2 ** b, devices).astype(jnp.float32)
-    gathered = total.astype(jnp.bfloat16)
-    for b in range(count - 1, 0, -1):
+    own = total.astype(jnp.bfloat16)
+    gathered = (own.astype(jnp.float32) + swapped(own, 2 ** last, devices).astype(jnp.float32)).astype(jnp.bfloat16)
+    for b in range(last - 1, 0, -1):
         other = swapped(gathered, 2 ** b, devices)
         low = jnp.where(uppers[b], other, gathered)
         high = jnp.where(uppers[b], gathered, other)
@@ -231,8 +236,8 @@
     across, turned = barrier((across, turned))
     far = far_of(across, devices)
     far, second_across = barrier((far, second_across))
-    second_far = far_of(second_across, devices)
-    rest = rest_of(across, far, give_across, devices)
+    second_far = [far_of(second_across[:half], devices), far_of(second_across[half:], devices)]
+    rest = rest_of(across, [far], give_across, devices)
     column_first, column_again, give, keep = call(
         first_kernel,
         [narrow, narrow] + parts(2),
@@ -241,22 +246,22 @@
         5 * one,
         scratch,
     )
-    give, second_across = barrier((give, second_across))
+    give, second_far[0] = barrier((give, second_far[0]))
     give, keep = core_summed(give, keep, uppers, devices)
+    total = chip_summed(give, keep, devices)
+    total, second_across = barrier((total, second_across))
     second_rest = rest_of(second_across, second_far, give_across, devices)
-    total = chip_summed(give, keep, devices)
     (second_acc,) = call(
         across_kernel, [wide], [second_acc, column_again, lower, second_across, sorted_sigma], "vvvvv", 2 * one
     )
     column_second, second_give, second_keep = call(
         second_kernel,
         [narrow] + parts(1),
-        [where, second_acc, second_far, second_rest, sorted_sigma, turned],
-        "svvvvv",
+        [where, second_acc, *second_far, second_rest, sorted_sigma, turned],
+        "svvvvvv",
         3 * one,
         scratch,
     )
-    second_give, total = barrier((second_give, total))
     second_give, second_keep = core_summed(second_give, second_keep, uppers, devices)
     mine, other = summed(total, uppers, devices)
     second_total = chip_summed(second_give, second_keep, devices)

time: 99 us -> 97 us (0.980)
  starting transfers between devices: 23.2 us -> 15.4 us
  waiting for transfers between devices: 56.6 us -> 62.4 us
    ppermute x22 -> x20, waiting for transfers between devices: 40.9 us -> 49.2 us  [swapped(): return lax.ppermute(value, 'row', [(i, i ^ bit) for i in range(devices)])]
    ppermute x22 -> x20, starting transfers between devices: 21 us -> 13.2 us  [swapped(): return lax.ppermute(value, 'row', [(i, i ^ bit) for i in range(devices)])]
    ppermute x2 -> x3, waiting for transfers between devices: 15.7 us -> 13.2 us  [far_of(): return lax.ppermute(across, 'row', hops)]
    ppermute x2 -> x3, starting transfers between devices: 2.2 us -> 2.21 us  [far_of(): return lax.ppermute(across, 'row', hops)]
  transfers between devices with their start and end apart: 24 -> 23, of which waited for: 18 -> 17; matrix products, arithmetic and copies ran while one was open for 1% -> 1% of each run, Pallas kernels for 10% -> 10%
where the time goes in v8:
time: 97 us; the launch traced here: 96.7 us
  waiting for transfers between devices  62.4 us (64%)
  starting transfers between devices  15.4 us (16%)
  Pallas kernels  10.6 us (11%)
  local copies, waits for them, and re-layouts  5.56 us (6%)
  between operations  1.6 us (2%)
  other arithmetic  1.1 us (1%)
    ppermute x20, waiting for transfers between devices, swapped(): return lax.ppermute(value, 'row', [(i, i ^ bit) for i in range(devices)])  49.2 us
    ppermute x3, waiting for transfers between devices, far_of(): return lax.ppermute(across, 'row', hops)  13.2 us
    ppermute x20, starting transfers between devices, swapped(): return lax.ppermute(value, 'row', [(i, i ^ bit) for i in range(devices)])  13.2 us
    pallas_call x6, Pallas kernels, call(): pl.pallas_call(body, out_shape=outs, in_specs=[pl.BlockSpec(memory_space=...  10.6 us
    unnamed x14, local copies, waits for them, and re-layouts  5.52 us
    ppermute x3, starting transfers between devices, far_of(): return lax.ppermute(across, 'row', hops)  2.21 us
  transfers between devices with their start and end apart: 23, of which 17 were waited for; matrix products, arithmetic and copies ran while one was open for 1% of the time, Pallas kernels for 10%

profile of v8, /device:TPU:0, one launch (start us, length us, event | category | flops | bytes accessed | tf_op | source)
XLA Modules:
  0.0 96.7 jit_solution(2287799635477107130)
XLA Ops:
  1.2 2.9 %collective-permute-start.2 = (bf16[512,512]{1,0:T(8,128)(2,1)}, bf16[512,512]{1,0:T(8,128)(2,1)S(1)}, u32[]{:S(2)}, u32[]{:S(2)}) collective-permute-start(bf16[512,512]{1,0:T(8,128)(2,1)} %bitcast.11), channel_id=1, source_target_pairs={{0,2},{1,3},{2,0},{3,1},{4,6},{5,7},{6,4},{7,5},{8,10},{9,11},{10,... | collective-permute-start | bytes 1572872 | tf_op jit(solution)/shard_map/ppermute | solution.py:156
  4.9 1.7 %copy-done = bf16[1,1,5,512,512]{4,3,2,1,0:T(8,128)(2,1)S(1)} copy-done((bf16[1,1,5,512,512]{4,3,2,1,0:T(8,128)(2,1)S(1)}, bf16[1,1,5,512,512]{4,3,2,1,0:T(8,128)(2,1)}, u32[]{:S(2)}) %copy-start) | copy-done | bytes 2621464
  6.6 1.0 %copy-done.1 = bf16[512,512]{1,0:T(8,128)(2,1)S(1)} copy-done((bf16[512,512]{1,0:T(8,128)(2,1)S(1)}, bf16[512,512]{1,0:T(8,128)(2,1)}, u32[]{:S(2)}) %copy-start.1) | copy-done | bytes 524312
  7.7 1.0 %copy-done.2 = bf16[1,1,512,512]{3,2,1,0:T(8,128)(2,1)S(1)} copy-done((bf16[1,1,512,512]{3,2,1,0:T(8,128)(2,1)S(1)}, bf16[1,1,512,512]{3,2,1,0:T(8,128)(2,1)}, u32[]{:S(2)}) %copy-start.2) | copy-done | bytes 524312
  8.7 1.0 %copy-done.3 = bf16[1,1,512,512]{3,2,1,0:T(8,128)(2,1)S(1)} copy-done((bf16[1,1,512,512]{3,2,1,0:T(8,128)(2,1)S(1)}, bf16[1,1,512,512]{3,2,1,0:T(8,128)(2,1)}, u32[]{:S(2)}) %copy-start.3) | copy-done | bytes 524312
  10.4 2.6 %shard_map.119 = (f32[512,512]{1,0:T(8,128)S(1)}, f32[512,512]{1,0:T(8,128)S(1)}, bf16[1024,512]{1,0:T(8,128)(2,1)S(1)}, bf16[3,512,512]{2,1,0:T(8,128)(2,1)S(1)}, bf16[512,512]{1,0:T(8,128)(2,1)S(1)}) custom-call(s32[1]{0:T(128)} %bitcast.where_ref, s32[5]{0:T(128)S(1)} %bitcast.16, s32[1]{0:T(128)} %bitcast.8.count_ref, bf16[5,512,512]{2,1,0:T(8,128)(2,1)S(1)} %bitcast.9, ...), custom_call_target="tpu_custom_call" | custom-call | flops 1073741824 | bytes 10485788 | tf_op jit(solution)/shard_map/pallas_call | solution.py:16
  13.0 4.1 %collective-permute-done.2.across = bf16[512,512]{1,0:T(8,128)(2,1)S(1)} collective-permute-done((bf16[512,512]{1,0:T(8,128)(2,1)}, bf16[512,512]{1,0:T(8,128)(2,1)S(1)}, u32[]{:S(2)}, u32[]{:S(2)}) %collective-permute-start.2) | collective-permute-done | bytes 524320 | tf_op jit(solution)/shard_map/ppermute | solution.py:156
  17.1 2.1 %collective-permute-start.3 = (bf16[512,512]{1,0:T(8,128)(2,1)S(1)}, bf16[512,512]{1,0:T(8,128)(2,1)S(1)}, u32[]{:S(2)}, u32[]{:S(2)}) collective-permute-start(bf16[512,512]{1,0:T(8,128)(2,1)S(1)} %collective-permute-done.2.across), channel_id=1, source_target_pairs={{0,4},{1,5},{2,14},{3,15},{4,8},{5,9},{6,2},{7,3},{8,12},{9,13},{1... | collective-permute-start | bytes 1572872 | tf_op jit(solution)/shard_map/ppermute | solution.py:161
  19.2 8.5 %collective-permute-done.4.across = bf16[512,512]{1,0:T(8,128)(2,1)S(1)} collective-permute-done((bf16[512,512]{1,0:T(8,128)(2,1)}, bf16[512,512]{1,0:T(8,128)(2,1)S(1)}, u32[]{:S(2)}, u32[]{:S(2)}) %collective-permute-start.4) | collective-permute-done | bytes 524320 | tf_op jit(solution)/shard_map/ppermute | solution.py:156
  27.8 3.9 %collective-permute-done.3.far = bf16[512,512]{1,0:T(8,128)(2,1)S(1)} collective-permute-done((bf16[512,512]{1,0:T(8,128)(2,1)S(1)}, bf16[512,512]{1,0:T(8,128)(2,1)S(1)}, u32[]{:S(2)}, u32[]{:S(2)}) %collective-permute-start.3) | collective-permute-done | bytes 524320 | tf_op jit(solution)/shard_map/ppermute | solution.py:161
  32.0 1.8 %collective-permute-done.5.rest = bf16[512,512]{1,0:T(8,128)(2,1)S(1)} collective-permute-done((bf16[512,512]{1,0:T(8,128)(2,1)S(1)}, bf16[512,512]{1,0:T(8,128)(2,1)S(1)}, u32[]{:S(2)}, u32[]{:S(2)}) %collective-permute-start.5) | collective-permute-done | bytes 524320 | tf_op jit(solution)/shard_map/ppermute | solution.py:156
  33.8 2.3 %shard_map.120 = (bf16[512,512]{1,0:T(8,128)(2,1)}, bf16[512,512]{1,0:T(8,128)(2,1)S(1)}, bf16[2,256,512]{2,1,0:T(8,128)(2,1)S(1)}, f32[2,256,512]{2,1,0:T(8,128)S(1)}) custom-call(s32[1]{0:T(128)} %bitcast.where_ref, f32[512,512]{1,0:T(8,128)S(1)} %get-tuple-element.37.acc_in, bf16[512,512]{1,0:T(8,128)(2,1)S(1)} %collective-permute-done.2.across, ...), custom_call_target="tpu_custom_call" | custom-call | flops 1342177280 | bytes 7864324 | tf_op jit(solution)/shard_map/pallas_call | solution.py:16
  36.1 6.4 %collective-permute-done.6.far_0 = bf16[256,512]{1,0:T(8,128)(2,1)S(1)} collective-permute-done((bf16[256,512]{1,0:T(8,128)(2,1)S(1)}, bf16[256,512]{1,0:T(8,128)(2,1)S(1)}, u32[]{:S(2)}, u32[]{:S(2)}) %collective-permute-start.6) | collective-permute-done | bytes 262176 | tf_op jit(solution)/shard_map/ppermute | solution.py:161
  42.5 1.9 %collective-permute-done.7 = bf16[2,256,512]{2,1,0:T(8,128)(2,1)S(1)} collective-permute-done((bf16[2,256,512]{2,1,0:T(8,128)(2,1)S(1)}, bf16[2,256,512]{2,1,0:T(8,128)(2,1)S(1)}, u32[]{:S(2)}, u32[]{:S(2)}) %collective-permute-start.7) | collective-permute-done | bytes 524320 | tf_op jit(solution)/shard_map/ppermute | solution.py:156
  44.6 0.8 collective-permute-start.8
  45.4 7.6 %collective-permute-done.8 = bf16[2,128,512]{2,1,0:T(8,128)(2,1)S(1)} collective-permute-done((bf16[2,128,512]{2,1,0:T(8,128)(2,1)S(1)}, bf16[2,128,512]{2,1,0:T(8,128)(2,1)S(1)}, u32[]{:S(2)}, u32[]{:S(2)}) %collective-permute-start.8) | collective-permute-done | bytes 262176 | tf_op jit(solution)/shard_map/ppermute | solution.py:156
  53.1 2.9 %collective-permute-done.14.far_1 = bf16[256,512]{1,0:T(8,128)(2,1)S(1)} collective-permute-done((bf16[256,512]{1,0:T(8,128)(2,1)S(1)}, bf16[256,512]{1,0:T(8,128)(2,1)S(1)}, u32[]{:S(2)}, u32[]{:S(2)}) %collective-permute-start.14) | collective-permute-done | bytes 262176 | tf_op jit(solution)/shard_map/ppermute | solution.py:161
  56.3 0.7 shard_map.122.acc_in
  57.0 1.1 %collective-permute-done.15.rest = bf16[512,512]{1,0:T(8,128)(2,1)S(1)} collective-permute-done((bf16[512,512]{1,0:T(8,128)(2,1)S(1)}, bf16[512,512]{1,0:T(8,128)(2,1)S(1)}, u32[]{:S(2)}, u32[]{:S(2)}) %collective-permute-start.15) | collective-permute-done | bytes 524320 | tf_op jit(solution)/shard_map/ppermute | solution.py:156
  58.1 1.5 %shard_map.123 = (bf16[512,512]{1,0:T(8,128)(2,1)}, bf16[1,256,512]{2,1,0:T(8,128)(2,1)S(1)}, f32[1,256,512]{2,1,0:T(8,128)S(1)}) custom-call(s32[1]{0:T(128)} %bitcast.where_ref, f32[512,512]{1,0:T(8,128)S(1)} %shard_map.122.acc_in, bf16[256,512]{1,0:T(8,128)(2,1)S(1)} %collective-permute-done.6.far_0, bf16[256,512]{1,0:T(8,128)(2,1)S(1)} %collective-permute-done.14.far_1, ...), custom_call_target="tpu_custom_call" | custom-call | flops 805306368 | bytes 6029316 | tf_op jit(solution)/shard_map/pallas_call | solution.py:16
  59.8 2.4 %collective-permute-done.9 = bf16[2,64,512]{2,1,0:T(8,128)(2,1)S(1)} collective-permute-done((bf16[2,64,512]{2,1,0:T(8,128)(2,1)S(1)}, bf16[2,64,512]{2,1,0:T(8,128)(2,1)S(1)}, u32[]{:S(2)}, u32[]{:S(2)}) %collective-permute-start.9) | collective-permute-done | bytes 131104 | tf_op jit(solution)/shard_map/ppermute | solution.py:156
  63.0 2.2 %collective-permute-start.17 = (bf16[1,128,512]{2,1,0:T(8,128)(2,1)S(1)}, bf16[1,128,512]{2,1,0:T(8,128)(2,1)S(1)}, u32[]{:S(2)}, u32[]{:S(2)}) collective-permute-start(bf16[1,128,512]{2,1,0:T(8,128)(2,1)S(1)} %select_convert_fusion.1), channel_id=1, source_target_pairs={{0,2},{1,3},{2,0},{3,1},{4,6},{5,7},{6,4},{7,5},{8,10},{9,11},{10,... | collective-permute-start | bytes 393224 | tf_op jit(solution)/shard_map/ppermute | solution.py:156
  65.2 5.8 %collective-permute-done.10 = bf16[2,64,512]{2,1,0:T(8,128)(2,1)S(1)} collective-permute-done((bf16[2,64,512]{2,1,0:T(8,128)(2,1)S(1)}, bf16[2,64,512]{2,1,0:T(8,128)(2,1)S(1)}, u32[]{:S(2)}, u32[]{:S(2)}) %collective-permute-start.10) | collective-permute-done | bytes 131104 | tf_op jit(solution)/shard_map/ppermute | solution.py:156
  71.3 2.1 %collective-permute-start.18 = (bf16[1,64,512]{2,1,0:T(8,128)(2,1)S(1)}, bf16[1,64,512]{2,1,0:T(8,128)(2,1)S(1)}, u32[]{:S(2)}, u32[]{:S(2)}) collective-permute-start(bf16[1,64,512]{2,1,0:T(8,128)(2,1)S(1)} %select_convert_fusion.3), channel_id=1, source_target_pairs={{0,4},{1,5},{2,6},{3,7},{4,0},{5,1},{6,2},{7,3},{8,12},{9,13},{10,... | collective-permute-start | bytes 196616 | tf_op jit(solution)/shard_map/ppermute | solution.py:156
  73.4 3.9 %collective-permute-done.11 = bf16[2,64,512]{2,1,0:T(8,128)(2,1)S(1)} collective-permute-done((bf16[2,64,512]{2,1,0:T(8,128)(2,1)S(1)}, bf16[2,64,512]{2,1,0:T(8,128)(2,1)S(1)}, u32[]{:S(2)}, u32[]{:S(2)}) %collective-permute-start.11) | collective-permute-done | bytes 131104 | tf_op jit(solution)/shard_map/ppermute | solution.py:156
  78.7 2.2 %collective-permute-start.12 = (bf16[2,128,512]{2,1,0:T(8,128)(2,1)S(1)}, bf16[2,128,512]{2,1,0:T(8,128)(2,1)S(1)}, u32[]{:S(2)}, u32[]{:S(2)}) collective-permute-start(bf16[2,128,512]{2,1,0:T(8,128)(2,1)S(1)} %pad_maximum_fusion.2), channel_id=1, source_target_pairs={{0,2},{1,3},{2,0},{3,1},{4,6},{5,7},{6,4},{7,5},{8,10},{9,11},{10,... | collective-permute-start | bytes 786440 | tf_op jit(solution)/shard_map/ppermute | solution.py:156
  80.9 2.8 %collective-permute-done.19 = bf16[1,64,512]{2,1,0:T(8,128)(2,1)S(1)} collective-permute-done((bf16[1,64,512]{2,1,0:T(8,128)(2,1)S(1)}, bf16[1,64,512]{2,1,0:T(8,128)(2,1)S(1)}, u32[]{:S(2)}, u32[]{:S(2)}) %collective-permute-start.19) | collective-permute-done | bytes 65568 | tf_op jit(solution)/shard_map/ppermute | solution.py:156
  83.8 2.8 %collective-permute-done.12 = bf16[2,128,512]{2,1,0:T(8,128)(2,1)S(1)} collective-permute-done((bf16[2,128,512]{2,1,0:T(8,128)(2,1)S(1)}, bf16[2,128,512]{2,1,0:T(8,128)(2,1)S(1)}, u32[]{:S(2)}, u32[]{:S(2)}) %collective-permute-start.12) | collective-permute-done | bytes 262176 | tf_op jit(solution)/shard_map/ppermute | solution.py:156
  86.7 1.4 %collective-permute-done.20 = bf16[1,64,512]{2,1,0:T(8,128)(2,1)S(1)} collective-permute-done((bf16[1,64,512]{2,1,0:T(8,128)(2,1)S(1)}, bf16[1,64,512]{2,1,0:T(8,128)(2,1)S(1)}, u32[]{:S(2)}, u32[]{:S(2)}) %collective-permute-start.20) | collective-permute-done | bytes 65568 | tf_op jit(solution)/shard_map/ppermute | solution.py:156
  88.6 4.5 %collective-permute-done.21 = bf16[1,128,512]{2,1,0:T(8,128)(2,1)S(1)} collective-permute-done((bf16[1,128,512]{2,1,0:T(8,128)(2,1)S(1)}, bf16[1,128,512]{2,1,0:T(8,128)(2,1)S(1)}, u32[]{:S(2)}, u32[]{:S(2)}) %collective-permute-start.21) | collective-permute-done | bytes 131104 | tf_op jit(solution)/shard_map/ppermute | solution.py:156
  93.3 2.2 %shard_map.121 = (f32[512,512]{1,0:T(8,128)}, f32[512,512]{1,0:T(8,128)}, f32[512,512]{1,0:T(8,128)S(1)}) custom-call(s32[1]{0:T(128)} %bitcast.where_ref, bf16[2,256,512]{2,1,0:T(8,128)(2,1)S(1)} %pad_maximum_fusion.mine_ref, bf16[2,256,512]{2,1,0:T(8,128)(2,1)S(1)} %collective-permute-done.13.other_ref, bf16[512,512]{1,0:T(8,128)(2,1)S(1)} %get-tuple-element.52.lower_ref, ...), custom_call_target="tpu_custom_call" | custom-call | flops 1073741824 | bytes 6815748 | tf_op jit(solution)/shard_map/pallas_call | solution.py:16
  95.5 1.2 %shard_map.124 = f32[512,512]{1,0:T(8,128)} custom-call(s32[1]{0:T(128)} %bitcast.where_ref, bf16[1,256,512]{2,1,0:T(8,128)(2,1)S(1)} %pad_maximum_fusion.3.mine_ref, bf16[1,256,512]{2,1,0:T(8,128)(2,1)S(1)} %collective-permute-done.22.other_ref, f32[512,512]{1,0:T(8,128)S(1)} %get-tuple-element.62.base_ref), custom_call_target="tpu_custom_call" | custom-call | flops 262144 | bytes 2621444 | tf_op jit(solution)/shard_map/pallas_call | solution.py:16
  (58 shorter events, 5.5 us)
Async XLA Ops:
  0.6 4.2 %collective-permute-start = (bf16[512,512]{1,0:T(8,128)(2,1)}, bf16[512,512]{1,0:T(8,128)(2,1)S(1)}, u32[]{:S(2)}, u32[]{:S(2)}) collective-permute-start(bf16[512,512]{1,0:T(8,128)(2,1)} %bitcast.10), channel_id=1, source_target_pairs={{0,1},{1,0},{2,3},{3,2},{4,5},{5,4},{6,7},{7,6},{8,9},{9,8},{10,11... | collective-permute-start | bytes 1572872 | tf_op jit(solution)/shard_map/ppermute | solution.py:156
  1.2 3.7 %collective-permute-start.1 = (bf16[512,512]{1,0:T(8,128)(2,1)}, bf16[512,512]{1,0:T(8,128)(2,1)S(1)}, u32[]{:S(2)}, u32[]{:S(2)}) collective-permute-start(bf16[512,512]{1,0:T(8,128)(2,1)} %bitcast.13), channel_id=1, source_target_pairs={{0,1},{1,0},{2,3},{3,2},{4,5},{5,4},{6,7},{7,6},{8,9},{9,8},{10,11... | collective-permute-start | bytes 1572872 | tf_op jit(solution)/shard_map/ppermute | solution.py:156
  1.2 15.8 %collective-permute-start.2 = (bf16[512,512]{1,0:T(8,128)(2,1)}, bf16[512,512]{1,0:T(8,128)(2,1)S(1)}, u32[]{:S(2)}, u32[]{:S(2)}) collective-permute-start(bf16[512,512]{1,0:T(8,128)(2,1)} %bitcast.11), channel_id=1, source_target_pairs={{0,2},{1,3},{2,0},{3,1},{4,6},{5,7},{6,4},{7,5},{8,10},{9,11},{10,... | collective-permute-start | bytes 1572872 | tf_op jit(solution)/shard_map/ppermute | solution.py:156
  4.2 23.6 %collective-permute-start.4 = (bf16[512,512]{1,0:T(8,128)(2,1)}, bf16[512,512]{1,0:T(8,128)(2,1)S(1)}, u32[]{:S(2)}, u32[]{:S(2)}) collective-permute-start(bf16[512,512]{1,0:T(8,128)(2,1)} %bitcast.14), channel_id=1, source_target_pairs={{0,2},{1,3},{2,0},{3,1},{4,6},{5,7},{6,4},{7,5},{8,10},{9,11},{10,... | collective-permute-start | bytes 1572872 | tf_op jit(solution)/shard_map/ppermute | solution.py:156
  4.9 1.7 %copy-start = (bf16[1,1,5,512,512]{4,3,2,1,0:T(8,128)(2,1)S(1)}, bf16[1,1,5,512,512]{4,3,2,1,0:T(8,128)(2,1)}, u32[]{:S(2)}) copy-start(bf16[1,1,5,512,512]{4,3,2,1,0:T(8,128)(2,1)} %param.8) | copy-start | bytes 7864324
  6.6 1.0 %copy-start.1 = (bf16[512,512]{1,0:T(8,128)(2,1)S(1)}, bf16[512,512]{1,0:T(8,128)(2,1)}, u32[]{:S(2)}) copy-start(bf16[512,512]{1,0:T(8,128)(2,1)} %lower_hbm.1) | copy-start | bytes 1572868
  7.6 1.0 %copy-start.2 = (bf16[1,1,512,512]{3,2,1,0:T(8,128)(2,1)S(1)}, bf16[1,1,512,512]{3,2,1,0:T(8,128)(2,1)}, u32[]{:S(2)}) copy-start(bf16[1,1,512,512]{3,2,1,0:T(8,128)(2,1)} %param.9) | copy-start | bytes 1572868
  8.7 1.0 %copy-start.3 = (bf16[1,1,512,512]{3,2,1,0:T(8,128)(2,1)S(1)}, bf16[1,1,512,512]{3,2,1,0:T(8,128)(2,1)}, u32[]{:S(2)}) copy-start(bf16[1,1,512,512]{3,2,1,0:T(8,128)(2,1)} %param.10) | copy-start | bytes 1572868
  9.7 0.7 copy-start.4
  17.1 14.6 %collective-permute-start.3 = (bf16[512,512]{1,0:T(8,128)(2,1)S(1)}, bf16[512,512]{1,0:T(8,128)(2,1)S(1)}, u32[]{:S(2)}, u32[]{:S(2)}) collective-permute-start(bf16[512,512]{1,0:T(8,128)(2,1)S(1)} %collective-permute-done.2.across), channel_id=1, source_target_pairs={{0,4},{1,5},{2,14},{3,15},{4,8},{5,9},{6,2},{7,3},{8,12},{9,13},{1... | collective-permute-start | bytes 1572872 | tf_op jit(solution)/shard_map/ppermute | solution.py:161
  31.8 2.0 %collective-permute-start.5 = (bf16[512,512]{1,0:T(8,128)(2,1)S(1)}, bf16[512,512]{1,0:T(8,128)(2,1)S(1)}, u32[]{:S(2)}, u32[]{:S(2)}) collective-permute-start(bf16[512,512]{1,0:T(8,128)(2,1)S(1)} %broadcast_select_fusion), channel_id=1, source_target_pairs={{0,1},{1,0},{2,3},{3,2},{4,5},{5,4},{6,7},{7,6},{8,9},{9,8},{10,11... | collective-permute-start | bytes 1572872 | tf_op jit(solution)/shard_map/ppermute | solution.py:156
  31.9 10.6 %collective-permute-start.6 = (bf16[256,512]{1,0:T(8,128)(2,1)S(1)}, bf16[256,512]{1,0:T(8,128)(2,1)S(1)}, u32[]{:S(2)}, u32[]{:S(2)}) collective-permute-start(bf16[256,512]{1,0:T(8,128)(2,1)S(1)} %get-tuple-element.66), channel_id=1, source_target_pairs={{0,4},{1,5},{2,14},{3,15},{4,8},{5,9},{6,2},{7,3},{8,12},{9,13},{1... | collective-permute-start | bytes 786440 | tf_op jit(solution)/shard_map/ppermute | solution.py:161
  42.5 1.9 %collective-permute-start.7 = (bf16[2,256,512]{2,1,0:T(8,128)(2,1)S(1)}, bf16[2,256,512]{2,1,0:T(8,128)(2,1)S(1)}, u32[]{:S(2)}, u32[]{:S(2)}) collective-permute-start(bf16[2,256,512]{2,1,0:T(8,128)(2,1)S(1)} %get-tuple-element.50), channel_id=1, source_target_pairs={{0,1},{1,0},{2,3},{3,2},{4,5},{5,4},{6,7},{7,6},{8,9},{9,8},{10,11... | collective-permute-start | bytes 1572872 | tf_op jit(solution)/shard_map/ppermute | solution.py:156
  44.6 8.4 %collective-permute-start.8 = (bf16[2,128,512]{2,1,0:T(8,128)(2,1)S(1)}, bf16[2,128,512]{2,1,0:T(8,128)(2,1)S(1)}, u32[]{:S(2)}, u32[]{:S(2)}) collective-permute-start(bf16[2,128,512]{2,1,0:T(8,128)(2,1)S(1)} %select_convert_fusion), channel_id=1, source_target_pairs={{0,2},{1,3},{2,0},{3,1},{4,6},{5,7},{6,4},{7,5},{8,10},{9,11},{10,... | collective-permute-start | bytes 786440 | tf_op jit(solution)/shard_map/ppermute | solution.py:156
  45.4 10.6 %collective-permute-start.14 = (bf16[256,512]{1,0:T(8,128)(2,1)S(1)}, bf16[256,512]{1,0:T(8,128)(2,1)S(1)}, u32[]{:S(2)}, u32[]{:S(2)}) collective-permute-start(bf16[256,512]{1,0:T(8,128)(2,1)S(1)} %get-tuple-element.65), channel_id=1, source_target_pairs={{0,4},{1,5},{2,14},{3,15},{4,8},{5,9},{6,2},{7,3},{8,12},{9,13},{1... | collective-permute-start | bytes 786440 | tf_op jit(solution)/shard_map/ppermute | solution.py:161
  56.1 2.0 %collective-permute-start.15 = (bf16[512,512]{1,0:T(8,128)(2,1)S(1)}, bf16[512,512]{1,0:T(8,128)(2,1)S(1)}, u32[]{:S(2)}, u32[]{:S(2)}) collective-permute-start(bf16[512,512]{1,0:T(8,128)(2,1)S(1)} %pad_maximum_fusion.1), channel_id=1, source_target_pairs={{0,1},{1,0},{2,3},{3,2},{4,5},{5,4},{6,7},{7,6},{8,9},{9,8},{10,11... | collective-permute-start | bytes 1572872 | tf_op jit(solution)/shard_map/ppermute | solution.py:156
  56.3 6.0 %collective-permute-start.9 = (bf16[2,64,512]{2,1,0:T(8,128)(2,1)S(1)}, bf16[2,64,512]{2,1,0:T(8,128)(2,1)S(1)}, u32[]{:S(2)}, u32[]{:S(2)}) collective-permute-start(bf16[2,64,512]{2,1,0:T(8,128)(2,1)S(1)} %select_convert_fusion.2), channel_id=1, source_target_pairs={{0,4},{1,5},{2,6},{3,7},{4,0},{5,1},{6,2},{7,3},{8,12},{9,13},{10,... | collective-permute-start | bytes 393224 | tf_op jit(solution)/shard_map/ppermute | solution.py:156
  59.7 3.2 %collective-permute-start.16 = (bf16[1,256,512]{2,1,0:T(8,128)(2,1)S(1)}, bf16[1,256,512]{2,1,0:T(8,128)(2,1)S(1)}, u32[]{:S(2)}, u32[]{:S(2)}) collective-permute-start(bf16[1,256,512]{2,1,0:T(8,128)(2,1)S(1)} %get-tuple-element.61), channel_id=1, source_target_pairs={{0,1},{1,0},{2,3},{3,2},{4,5},{5,4},{6,7},{7,6},{8,9},{9,8},{10,11... | collective-permute-start | bytes 786440 | tf_op jit(solution)/shard_map/ppermute | solution.py:156
  62.3 8.8 %collective-permute-start.10 = (bf16[2,64,512]{2,1,0:T(8,128)(2,1)S(1)}, bf16[2,64,512]{2,1,0:T(8,128)(2,1)S(1)}, u32[]{:S(2)}, u32[]{:S(2)}) collective-permute-start(bf16[2,64,512]{2,1,0:T(8,128)(2,1)S(1)} %add_convert_fusion.1), channel_id=1, source_target_pairs={{0,8},{1,9},{2,10},{3,11},{4,12},{5,13},{6,14},{7,15},{8,0},{9,1},... | collective-permute-start | bytes 393224 | tf_op jit(solution)/shard_map/ppermute | solution.py:156
  63.0 8.2 %collective-permute-start.17 = (bf16[1,128,512]{2,1,0:T(8,128)(2,1)S(1)}, bf16[1,128,512]{2,1,0:T(8,128)(2,1)S(1)}, u32[]{:S(2)}, u32[]{:S(2)}) collective-permute-start(bf16[1,128,512]{2,1,0:T(8,128)(2,1)S(1)} %select_convert_fusion.1), channel_id=1, source_target_pairs={{0,2},{1,3},{2,0},{3,1},{4,6},{5,7},{6,4},{7,5},{8,10},{9,11},{10,... | collective-permute-start | bytes 393224 | tf_op jit(solution)/shard_map/ppermute | solution.py:156
  71.1 6.2 %collective-permute-start.11 = (bf16[2,64,512]{2,1,0:T(8,128)(2,1)S(1)}, bf16[2,64,512]{2,1,0:T(8,128)(2,1)S(1)}, u32[]{:S(2)}, u32[]{:S(2)}) collective-permute-start(bf16[2,64,512]{2,1,0:T(8,128)(2,1)S(1)} %add_convert_fusion), channel_id=1, source_target_pairs={{0,4},{1,5},{2,6},{3,7},{4,0},{5,1},{6,2},{7,3},{8,12},{9,13},{10,... | collective-permute-start | bytes 393224 | tf_op jit(solution)/shard_map/ppermute | solution.py:156
  71.3 22.0 %copy-start.5 = (f32[512,512]{1,0:T(8,128)S(1)}, f32[512,512]{1,0:T(8,128)}, u32[]{:S(2)}) copy-start(f32[512,512]{1,0:T(8,128)} %first_diag_ref.1) | copy-start | bytes 3145732
  71.3 22.0 %copy-start.6 = (f32[512,512]{1,0:T(8,128)S(1)}, f32[512,512]{1,0:T(8,128)}, u32[]{:S(2)}) copy-start(f32[512,512]{1,0:T(8,128)} %second_diag_ref.1) | copy-start | bytes 3145732
  71.3 6.7 %collective-permute-start.18 = (bf16[1,64,512]{2,1,0:T(8,128)(2,1)S(1)}, bf16[1,64,512]{2,1,0:T(8,128)(2,1)S(1)}, u32[]{:S(2)}, u32[]{:S(2)}) collective-permute-start(bf16[1,64,512]{2,1,0:T(8,128)(2,1)S(1)} %select_convert_fusion.3), channel_id=1, source_target_pairs={{0,4},{1,5},{2,6},{3,7},{4,0},{5,1},{6,2},{7,3},{8,12},{9,13},{10,... | collective-permute-start | bytes 196616 | tf_op jit(solution)/shard_map/ppermute | solution.py:156
  78.0 5.7 %collective-permute-start.19 = (bf16[1,64,512]{2,1,0:T(8,128)(2,1)S(1)}, bf16[1,64,512]{2,1,0:T(8,128)(2,1)S(1)}, u32[]{:S(2)}, u32[]{:S(2)}) collective-permute-start(bf16[1,64,512]{2,1,0:T(8,128)(2,1)S(1)} %add_convert_fusion.3), channel_id=1, source_target_pairs={{0,8},{1,9},{2,10},{3,11},{4,12},{5,13},{6,14},{7,15},{8,0},{9,1},... | collective-permute-start | bytes 196616 | tf_op jit(solution)/shard_map/ppermute | solution.py:156
  78.7 7.9 %collective-permute-start.12 = (bf16[2,128,512]{2,1,0:T(8,128)(2,1)S(1)}, bf16[2,128,512]{2,1,0:T(8,128)(2,1)S(1)}, u32[]{:S(2)}, u32[]{:S(2)}) collective-permute-start(bf16[2,128,512]{2,1,0:T(8,128)(2,1)S(1)} %pad_maximum_fusion.2), channel_id=1, source_target_pairs={{0,2},{1,3},{2,0},{3,1},{4,6},{5,7},{6,4},{7,5},{8,10},{9,11},{10,... | collective-permute-start | bytes 786440 | tf_op jit(solution)/shard_map/ppermute | solution.py:156
  83.7 4.3 %collective-permute-start.20 = (bf16[1,64,512]{2,1,0:T(8,128)(2,1)S(1)}, bf16[1,64,512]{2,1,0:T(8,128)(2,1)S(1)}, u32[]{:S(2)}, u32[]{:S(2)}) collective-permute-start(bf16[1,64,512]{2,1,0:T(8,128)(2,1)S(1)} %add_convert_fusion.2), channel_id=1, source_target_pairs={{0,4},{1,5},{2,6},{3,7},{4,0},{5,1},{6,2},{7,3},{8,12},{9,13},{10,... | collective-permute-start | bytes 196616 | tf_op jit(solution)/shard_map/ppermute | solution.py:156
  88.1 5.0 %collective-permute-start.21 = (bf16[1,128,512]{2,1,0:T(8,128)(2,1)S(1)}, bf16[1,128,512]{2,1,0:T(8,128)(2,1)S(1)}, u32[]{:S(2)}, u32[]{:S(2)}) collective-permute-start(bf16[1,128,512]{2,1,0:T(8,128)(2,1)S(1)} %pad_maximum_fusion.4), channel_id=1, source_target_pairs={{0,2},{1,3},{2,0},{3,1},{4,6},{5,7},{6,4},{7,5},{8,10},{9,11},{10,... | collective-permute-start | bytes 393224 | tf_op jit(solution)/shard_map/ppermute | solution.py:156
  88.6 4.7 %collective-permute-start.13 = (bf16[2,256,512]{2,1,0:T(8,128)(2,1)S(1)}, bf16[2,256,512]{2,1,0:T(8,128)(2,1)S(1)}, u32[]{:S(2)}, u32[]{:S(2)}) collective-permute-start(bf16[2,256,512]{2,1,0:T(8,128)(2,1)S(1)} %pad_maximum_fusion.mine_ref), channel_id=1, source_target_pairs={{0,1},{1,0},{2,3},{3,2},{4,5},{5,4},{6,7},{7,6},{8,9},{9,8},{10,11... | collective-permute-start | bytes 1572872 | tf_op jit(solution)/shard_map/ppermute | solution.py:156
  93.2 2.3 %collective-permute-start.22 = (bf16[1,256,512]{2,1,0:T(8,128)(2,1)S(1)}, bf16[1,256,512]{2,1,0:T(8,128)(2,1)S(1)}, u32[]{:S(2)}, u32[]{:S(2)}) collective-permute-start(bf16[1,256,512]{2,1,0:T(8,128)(2,1)S(1)} %pad_maximum_fusion.3.mine_ref), channel_id=1, source_target_pairs={{0,1},{1,0},{2,3},{3,2},{4,5},{5,4},{6,7},{7,6},{8,9},{9,8},{10,11... | collective-permute-start | bytes 786440 | tf_op jit(solution)/shard_map/ppermute | solution.py:156

commit v9 on v7

--- a/solution.py
+++ b/solution.py
@@ -155,12 +155,14 @@
 
 
 def far_of(across, devices):
-    hops = [(i, (i + (4 if i % 4 < 2 else -4)) % devices) for i in range(devices)]
-    return lax.ppermute(across, "row", hops)
+    hops = [(i, i + 4 if i % 4 < 2 else i - 4) for i in range(devices)]
+    return lax.ppermute(across, "row", [(a, b) for a, b in hops if 0 <= b < devices])
 
 
 def rest_of(across, far, give_across, devices):
-    return swapped(jnp.where(give_across, across, far), 1, devices)
+    rows = across.shape[0] // len(far)
+    pieces = [jnp.where(give_across, across[i * rows : (i + 1) * rows], piece) for i, piece in enumerate(far)]
+    return swapped(jnp.concatenate(pieces, axis=0), 1, devices)
 
 
 def core_summed(give, keep, uppers, devices):
@@ -178,12 +180,13 @@
 
 
 def summed(total, uppers, devices):
-    count = len(uppers)
-    for b in range(2, count):
+    last = len(uppers) - 1
+    for b in range(2, last):
         give, keep = halved(total, uppers[b])
         total = keep + swapped(give, 2 ** b, devices).astype(jnp.float32)
-    gathered = total.astype(jnp.bfloat16)
-    for b in range(count - 1, 0, -1):
+    own = total.astype(jnp.bfloat16)
+    gathered = (own.astype(jnp.float32) + swapped(own, 2 ** last, devices).astype(jnp.float32)).astype(jnp.bfloat16)
+    for b in range(last - 1, 0, -1):
         other = swapped(gathered, 2 ** b, devices)
         low = jnp.where(uppers[b], other, gathered)
         high = jnp.where(uppers[b], gathered, other)
@@ -232,7 +235,7 @@
     far = far_of(across, devices)
     far, second_across = barrier((far, second_across))
     second_far = far_of(second_across, devices)
-    rest = rest_of(across, far, give_across, devices)
+    rest = rest_of(across, [far], give_across, devices)
     column_first, column_again, give, keep = call(
         first_kernel,
         [narrow, narrow] + parts(2),
@@ -243,7 +246,7 @@
     )
     give, second_across = barrier((give, second_across))
     give, keep = core_summed(give, keep, uppers, devices)
-    second_rest = rest_of(second_across, second_far, give_across, devices)
+    second_rest = rest_of(second_across, [second_far], give_across, devices)
     total = chip_summed(give, keep, devices)
     (second_acc,) = call(
         across_kernel, [wide], [second_acc, column_again, lower, second_across, sorted_sigma], "vvvvv", 2 * one

time: 99 us -> 96.5 us (0.975)
  waiting for transfers between devices: 56.6 us -> 47.2 us
  starting transfers between devices: 23.2 us -> 30.3 us
    ppermute x2, starting transfers between devices: 2.2 us -> 8.49 us  [far_of(): lax.ppermute(across, 'row', [(a, b) for a, b in hops if 0 <= b < devices])]
    ppermute x22 -> x20, waiting for transfers between devices: 40.9 us -> 34.9 us  [swapped(): return lax.ppermute(value, 'row', [(i, i ^ bit) for i in range(devices)])]
    ppermute x2, waiting for transfers between devices: 15.7 us -> 12.3 us  [far_of(): lax.ppermute(across, 'row', [(a, b) for a, b in hops if 0 <= b < devices])]
    ppermute x22 -> x20, starting transfers between devices: 21 us -> 21.8 us  [swapped(): return lax.ppermute(value, 'row', [(i, i ^ bit) for i in range(devices)])]
  transfers between devices with their start and end apart: 24 -> 22, of which waited for: 18 -> 13; matrix products, arithmetic and copies ran while one was open for 1% -> 1% of each run, Pallas kernels for 10% -> 10%
where the time goes in v9:
time: 96.5 us; the launch traced here: 96.2 us
  waiting for transfers between devices  47.2 us (49%)
  starting transfers between devices  30.3 us (31%)
  Pallas kernels  10.6 us (11%)
  local copies, waits for them, and re-layouts  5.52 us (6%)
  between operations  1.57 us (2%)
  other arithmetic  1.05 us (1%)
    ppermute x20, waiting for transfers between devices, swapped(): return lax.ppermute(value, 'row', [(i, i ^ bit) for i in range(devices)])  34.9 us
    ppermute x20, starting transfers between devices, swapped(): return lax.ppermute(value, 'row', [(i, i ^ bit) for i in range(devices)])  21.8 us
    ppermute x2, waiting for transfers between devices, far_of(): lax.ppermute(across, 'row', [(a, b) for a, b in hops if 0 <= b < devices])  12.3 us
    pallas_call x6, Pallas kernels, call(): pl.pallas_call(body, out_shape=outs, in_specs=[pl.BlockSpec(memory_space=...  10.6 us
    ppermute x2, starting transfers between devices, far_of(): lax.ppermute(across, 'row', [(a, b) for a, b in hops if 0 <= b < devices])  8.49 us
    unnamed x14, local copies, waits for them, and re-layouts  5.52 us
  transfers between devices with their start and end apart: 22, of which 13 were waited for; matrix products, arithmetic and copies ran while one was open for 1% of the time, Pallas kernels for 10%

profile of v9, /device:TPU:0, one launch (start us, length us, event | category | flops | bytes accessed | tf_op | source)
XLA Modules:
  0.0 96.2 jit_solution(12258867935853673399)
XLA Ops:
  1.2 2.9 %collective-permute-start.2 = (bf16[512,512]{1,0:T(8,128)(2,1)}, bf16[512,512]{1,0:T(8,128)(2,1)S(1)}, u32[]{:S(2)}, u32[]{:S(2)}) collective-permute-start(bf16[512,512]{1,0:T(8,128)(2,1)} %bitcast.11), channel_id=1, source_target_pairs={{0,2},{1,3},{2,0},{3,1},{4,6},{5,7},{6,4},{7,5},{8,10},{9,11},{10,... | collective-permute-start | bytes 1572872 | tf_op jit(solution)/shard_map/ppermute | solution.py:154
  4.9 1.7 %copy-done = bf16[1,1,5,512,512]{4,3,2,1,0:T(8,128)(2,1)S(1)} copy-done((bf16[1,1,5,512,512]{4,3,2,1,0:T(8,128)(2,1)S(1)}, bf16[1,1,5,512,512]{4,3,2,1,0:T(8,128)(2,1)}, u32[]{:S(2)}) %copy-start) | copy-done | bytes 2621464
  6.6 1.0 %copy-done.1 = bf16[512,512]{1,0:T(8,128)(2,1)S(1)} copy-done((bf16[512,512]{1,0:T(8,128)(2,1)S(1)}, bf16[512,512]{1,0:T(8,128)(2,1)}, u32[]{:S(2)}) %copy-start.1) | copy-done | bytes 524312
  7.7 1.0 %copy-done.2 = bf16[1,1,512,512]{3,2,1,0:T(8,128)(2,1)S(1)} copy-done((bf16[1,1,512,512]{3,2,1,0:T(8,128)(2,1)S(1)}, bf16[1,1,512,512]{3,2,1,0:T(8,128)(2,1)}, u32[]{:S(2)}) %copy-start.2) | copy-done | bytes 524312
  8.7 1.0 %copy-done.3 = bf16[1,1,512,512]{3,2,1,0:T(8,128)(2,1)S(1)} copy-done((bf16[1,1,512,512]{3,2,1,0:T(8,128)(2,1)S(1)}, bf16[1,1,512,512]{3,2,1,0:T(8,128)(2,1)}, u32[]{:S(2)}) %copy-start.3) | copy-done | bytes 524312
  10.4 2.6 %shard_map.119 = (f32[512,512]{1,0:T(8,128)S(1)}, f32[512,512]{1,0:T(8,128)S(1)}, bf16[1024,512]{1,0:T(8,128)(2,1)S(1)}, bf16[3,512,512]{2,1,0:T(8,128)(2,1)S(1)}, bf16[512,512]{1,0:T(8,128)(2,1)S(1)}) custom-call(s32[1]{0:T(128)} %bitcast.where_ref, s32[5]{0:T(128)S(1)} %bitcast.16, s32[1]{0:T(128)} %bitcast.8.count_ref, bf16[5,512,512]{2,1,0:T(8,128)(2,1)S(1)} %bitcast.9, ...), custom_call_target="tpu_custom_call" | custom-call | flops 1073741824 | bytes 10485788 | tf_op jit(solution)/shard_map/pallas_call | solution.py:16
  13.0 4.1 %collective-permute-done.2.across = bf16[512,512]{1,0:T(8,128)(2,1)S(1)} collective-permute-done((bf16[512,512]{1,0:T(8,128)(2,1)}, bf16[512,512]{1,0:T(8,128)(2,1)S(1)}, u32[]{:S(2)}, u32[]{:S(2)}) %collective-permute-start.2) | collective-permute-done | bytes 524320 | tf_op jit(solution)/shard_map/ppermute | solution.py:154
  17.1 4.1 %collective-permute-start.3 = (bf16[512,512]{1,0:T(8,128)(2,1)S(1)}, bf16[512,512]{1,0:T(8,128)(2,1)S(1)}, u32[]{:S(2)}, u32[]{:S(2)}) collective-permute-start(bf16[512,512]{1,0:T(8,128)(2,1)S(1)} %collective-permute-done.2.across), channel_id=1, source_target_pairs={{0,4},{1,5},{4,8},{5,9},{6,2},{7,3},{8,12},{9,13},{10,6},{11,7},{1... | collective-permute-start | bytes 1572872 | tf_op jit(solution)/shard_map/ppermute | solution.py:159
  21.2 6.6 %collective-permute-done.4.across = bf16[512,512]{1,0:T(8,128)(2,1)S(1)} collective-permute-done((bf16[512,512]{1,0:T(8,128)(2,1)}, bf16[512,512]{1,0:T(8,128)(2,1)S(1)}, u32[]{:S(2)}, u32[]{:S(2)}) %collective-permute-start.4) | collective-permute-done | bytes 524320 | tf_op jit(solution)/shard_map/ppermute | solution.py:154
  27.8 3.1 %collective-permute-done.3.far = bf16[512,512]{1,0:T(8,128)(2,1)S(1)} collective-permute-done((bf16[512,512]{1,0:T(8,128)(2,1)S(1)}, bf16[512,512]{1,0:T(8,128)(2,1)S(1)}, u32[]{:S(2)}, u32[]{:S(2)}) %collective-permute-start.3) | collective-permute-done | bytes 524320 | tf_op jit(solution)/shard_map/ppermute | solution.py:159
  31.0 4.4 %collective-permute-start.6 = (bf16[512,512]{1,0:T(8,128)(2,1)S(1)}, bf16[512,512]{1,0:T(8,128)(2,1)S(1)}, u32[]{:S(2)}, u32[]{:S(2)}) collective-permute-start(bf16[512,512]{1,0:T(8,128)(2,1)S(1)} %collective-permute-done.4.across), channel_id=1, source_target_pairs={{0,4},{1,5},{4,8},{5,9},{6,2},{7,3},{8,12},{9,13},{10,6},{11,7},{1... | collective-permute-start | bytes 1572872 | tf_op jit(solution)/shard_map/ppermute | solution.py:159
  35.4 2.3 %shard_map.120 = (bf16[512,512]{1,0:T(8,128)(2,1)}, bf16[512,512]{1,0:T(8,128)(2,1)S(1)}, bf16[2,256,512]{2,1,0:T(8,128)(2,1)S(1)}, f32[2,256,512]{2,1,0:T(8,128)S(1)}) custom-call(s32[1]{0:T(128)} %bitcast.where_ref, f32[512,512]{1,0:T(8,128)S(1)} %get-tuple-element.37.acc_in, bf16[512,512]{1,0:T(8,128)(2,1)S(1)} %collective-permute-done.2.across, ...), custom_call_target="tpu_custom_call" | custom-call | flops 1342177280 | bytes 7864324 | tf_op jit(solution)/shard_map/pallas_call | solution.py:16
  37.9 9.2 %collective-permute-done.6.far = bf16[512,512]{1,0:T(8,128)(2,1)S(1)} collective-permute-done((bf16[512,512]{1,0:T(8,128)(2,1)S(1)}, bf16[512,512]{1,0:T(8,128)(2,1)S(1)}, u32[]{:S(2)}, u32[]{:S(2)}) %collective-permute-start.6) | collective-permute-done | bytes 524320 | tf_op jit(solution)/shard_map/ppermute | solution.py:159
  47.6 2.5 %collective-permute-start.9 = (bf16[2,128,512]{2,1,0:T(8,128)(2,1)S(1)}, bf16[2,128,512]{2,1,0:T(8,128)(2,1)S(1)}, u32[]{:S(2)}, u32[]{:S(2)}) collective-permute-start(bf16[2,128,512]{2,1,0:T(8,128)(2,1)S(1)} %select_convert_fusion), channel_id=1, source_target_pairs={{0,2},{1,3},{2,0},{3,1},{4,6},{5,7},{6,4},{7,5},{8,10},{9,11},{10,... | collective-permute-start | bytes 786440 | tf_op jit(solution)/shard_map/ppermute | solution.py:154
  50.7 1.6 %shard_map.122 = (bf16[512,512]{1,0:T(8,128)(2,1)}, bf16[1,256,512]{2,1,0:T(8,128)(2,1)S(1)}, f32[1,256,512]{2,1,0:T(8,128)S(1)}) custom-call(s32[1]{0:T(128)} %bitcast.where_ref, f32[512,512]{1,0:T(8,128)S(1)} %shard_map.121.acc_in, bf16[512,512]{1,0:T(8,128)(2,1)S(1)} %collective-permute-done.6.far, bf16[512,512]{1,0:T(8,128)(2,1)S(1)} %collective-permute-done.7.rest, ...), custom_call_target="tpu_custom_call" | custom-call | flops 805306368 | bytes 6029316 | tf_op jit(solution)/shard_map/pallas_call | solution.py:16
  52.3 4.7 %collective-permute-done.9 = bf16[2,128,512]{2,1,0:T(8,128)(2,1)S(1)} collective-permute-done((bf16[2,128,512]{2,1,0:T(8,128)(2,1)S(1)}, bf16[2,128,512]{2,1,0:T(8,128)(2,1)S(1)}, u32[]{:S(2)}, u32[]{:S(2)}) %collective-permute-start.9) | collective-permute-done | bytes 262176 | tf_op jit(solution)/shard_map/ppermute | solution.py:154
  57.2 1.9 %collective-permute-start.10 = (bf16[2,64,512]{2,1,0:T(8,128)(2,1)S(1)}, bf16[2,64,512]{2,1,0:T(8,128)(2,1)S(1)}, u32[]{:S(2)}, u32[]{:S(2)}) collective-permute-start(bf16[2,64,512]{2,1,0:T(8,128)(2,1)S(1)} %select_convert_fusion.2), channel_id=1, source_target_pairs={{0,4},{1,5},{2,6},{3,7},{4,0},{5,1},{6,2},{7,3},{8,12},{9,13},{10,... | collective-permute-start | bytes 393224 | tf_op jit(solution)/shard_map/ppermute | solution.py:154
  59.2 1.6 %collective-permute-start.16 = (bf16[1,128,512]{2,1,0:T(8,128)(2,1)S(1)}, bf16[1,128,512]{2,1,0:T(8,128)(2,1)S(1)}, u32[]{:S(2)}, u32[]{:S(2)}) collective-permute-start(bf16[1,128,512]{2,1,0:T(8,128)(2,1)S(1)} %select_convert_fusion.1), channel_id=1, source_target_pairs={{0,2},{1,3},{2,0},{3,1},{4,6},{5,7},{6,4},{7,5},{8,10},{9,11},{10,... | collective-permute-start | bytes 393224 | tf_op jit(solution)/shard_map/ppermute | solution.py:154
  60.8 2.5 %collective-permute-done.10 = bf16[2,64,512]{2,1,0:T(8,128)(2,1)S(1)} collective-permute-done((bf16[2,64,512]{2,1,0:T(8,128)(2,1)S(1)}, bf16[2,64,512]{2,1,0:T(8,128)(2,1)S(1)}, u32[]{:S(2)}, u32[]{:S(2)}) %collective-permute-start.10) | collective-permute-done | bytes 131104 | tf_op jit(solution)/shard_map/ppermute | solution.py:154
  63.3 2.8 %collective-permute-start.11 = (bf16[2,64,512]{2,1,0:T(8,128)(2,1)S(1)}, bf16[2,64,512]{2,1,0:T(8,128)(2,1)S(1)}, u32[]{:S(2)}, u32[]{:S(2)}) collective-permute-start(bf16[2,64,512]{2,1,0:T(8,128)(2,1)S(1)} %add_convert_fusion.1), channel_id=1, source_target_pairs={{0,8},{1,9},{2,10},{3,11},{4,12},{5,13},{6,14},{7,15},{8,0},{9,1},... | collective-permute-start | bytes 393224 | tf_op jit(solution)/shard_map/ppermute | solution.py:154
  66.2 1.6 %collective-permute-start.17 = (bf16[1,64,512]{2,1,0:T(8,128)(2,1)S(1)}, bf16[1,64,512]{2,1,0:T(8,128)(2,1)S(1)}, u32[]{:S(2)}, u32[]{:S(2)}) collective-permute-start(bf16[1,64,512]{2,1,0:T(8,128)(2,1)S(1)} %select_convert_fusion.3), channel_id=1, source_target_pairs={{0,4},{1,5},{2,6},{3,7},{4,0},{5,1},{6,2},{7,3},{8,12},{9,13},{10,... | collective-permute-start | bytes 196616 | tf_op jit(solution)/shard_map/ppermute | solution.py:154
  67.9 4.5 %collective-permute-done.11 = bf16[2,64,512]{2,1,0:T(8,128)(2,1)S(1)} collective-permute-done((bf16[2,64,512]{2,1,0:T(8,128)(2,1)S(1)}, bf16[2,64,512]{2,1,0:T(8,128)(2,1)S(1)}, u32[]{:S(2)}, u32[]{:S(2)}) %collective-permute-start.11) | collective-permute-done | bytes 131104 | tf_op jit(solution)/shard_map/ppermute | solution.py:154
  72.4 0.8 collective-permute-start.12
  73.2 3.4 %collective-permute-start.18 = (bf16[1,64,512]{2,1,0:T(8,128)(2,1)S(1)}, bf16[1,64,512]{2,1,0:T(8,128)(2,1)S(1)}, u32[]{:S(2)}, u32[]{:S(2)}) collective-permute-start(bf16[1,64,512]{2,1,0:T(8,128)(2,1)S(1)} %add_convert_fusion.3), channel_id=1, source_target_pairs={{0,8},{1,9},{2,10},{3,11},{4,12},{5,13},{6,14},{7,15},{8,0},{9,1},... | collective-permute-start | bytes 196616 | tf_op jit(solution)/shard_map/ppermute | solution.py:154
  76.7 1.5 %collective-permute-done.12 = bf16[2,64,512]{2,1,0:T(8,128)(2,1)S(1)} collective-permute-done((bf16[2,64,512]{2,1,0:T(8,128)(2,1)S(1)}, bf16[2,64,512]{2,1,0:T(8,128)(2,1)S(1)}, u32[]{:S(2)}, u32[]{:S(2)}) %collective-permute-start.12) | collective-permute-done | bytes 131104 | tf_op jit(solution)/shard_map/ppermute | solution.py:154
  78.2 0.7 collective-permute-done.18
  78.9 2.8 %collective-permute-start.19 = (bf16[1,64,512]{2,1,0:T(8,128)(2,1)S(1)}, bf16[1,64,512]{2,1,0:T(8,128)(2,1)S(1)}, u32[]{:S(2)}, u32[]{:S(2)}) collective-permute-start(bf16[1,64,512]{2,1,0:T(8,128)(2,1)S(1)} %add_convert_fusion.2), channel_id=1, source_target_pairs={{0,4},{1,5},{2,6},{3,7},{4,0},{5,1},{6,2},{7,3},{8,12},{9,13},{10,... | collective-permute-start | bytes 196616 | tf_op jit(solution)/shard_map/ppermute | solution.py:154
  81.8 2.1 %collective-permute-done.19 = bf16[1,64,512]{2,1,0:T(8,128)(2,1)S(1)} collective-permute-done((bf16[1,64,512]{2,1,0:T(8,128)(2,1)S(1)}, bf16[1,64,512]{2,1,0:T(8,128)(2,1)S(1)}, u32[]{:S(2)}, u32[]{:S(2)}) %collective-permute-start.19) | collective-permute-done | bytes 65568 | tf_op jit(solution)/shard_map/ppermute | solution.py:154
  84.2 6.4 %collective-permute-done.13 = bf16[2,128,512]{2,1,0:T(8,128)(2,1)S(1)} collective-permute-done((bf16[2,128,512]{2,1,0:T(8,128)(2,1)S(1)}, bf16[2,128,512]{2,1,0:T(8,128)(2,1)S(1)}, u32[]{:S(2)}, u32[]{:S(2)}) %collective-permute-start.13) | collective-permute-done | bytes 262176 | tf_op jit(solution)/shard_map/ppermute | solution.py:154
  90.9 1.2 %collective-permute-done.20 = bf16[1,128,512]{2,1,0:T(8,128)(2,1)S(1)} collective-permute-done((bf16[1,128,512]{2,1,0:T(8,128)(2,1)S(1)}, bf16[1,128,512]{2,1,0:T(8,128)(2,1)S(1)}, u32[]{:S(2)}, u32[]{:S(2)}) %collective-permute-start.20) | collective-permute-done | bytes 131104 | tf_op jit(solution)/shard_map/ppermute | solution.py:154
  92.8 2.2 %shard_map.123 = (f32[512,512]{1,0:T(8,128)}, f32[512,512]{1,0:T(8,128)}, f32[512,512]{1,0:T(8,128)S(1)}) custom-call(s32[1]{0:T(128)} %bitcast.where_ref, bf16[2,256,512]{2,1,0:T(8,128)(2,1)S(1)} %pad_maximum_fusion.mine_ref, bf16[2,256,512]{2,1,0:T(8,128)(2,1)S(1)} %collective-permute-done.14.other_ref, bf16[512,512]{1,0:T(8,128)(2,1)S(1)} %get-tuple-element.49.lower_ref, ...), custom_call_target="tpu_custom_call" | custom-call | flops 1073741824 | bytes 6815748 | tf_op jit(solution)/shard_map/pallas_call | solution.py:16
  95.0 1.2 %shard_map.124 = f32[512,512]{1,0:T(8,128)} custom-call(s32[1]{0:T(128)} %bitcast.where_ref, bf16[1,256,512]{2,1,0:T(8,128)(2,1)S(1)} %pad_maximum_fusion.2.mine_ref, bf16[1,256,512]{2,1,0:T(8,128)(2,1)S(1)} %collective-permute-done.21.other_ref, f32[512,512]{1,0:T(8,128)S(1)} %get-tuple-element.62.base_ref), custom_call_target="tpu_custom_call" | custom-call | flops 262144 | bytes 2621444 | tf_op jit(solution)/shard_map/pallas_call | solution.py:16
  (54 shorter events, 4.5 us)
Async XLA Ops:
  0.6 4.2 %collective-permute-start = (bf16[512,512]{1,0:T(8,128)(2,1)}, bf16[512,512]{1,0:T(8,128)(2,1)S(1)}, u32[]{:S(2)}, u32[]{:S(2)}) collective-permute-start(bf16[512,512]{1,0:T(8,128)(2,1)} %bitcast.10), channel_id=1, source_target_pairs={{0,1},{1,0},{2,3},{3,2},{4,5},{5,4},{6,7},{7,6},{8,9},{9,8},{10,11... | collective-permute-start | bytes 1572872 | tf_op jit(solution)/shard_map/ppermute | solution.py:154
  1.2 3.7 %collective-permute-start.1 = (bf16[512,512]{1,0:T(8,128)(2,1)}, bf16[512,512]{1,0:T(8,128)(2,1)S(1)}, u32[]{:S(2)}, u32[]{:S(2)}) collective-permute-start(bf16[512,512]{1,0:T(8,128)(2,1)} %bitcast.13), channel_id=1, source_target_pairs={{0,1},{1,0},{2,3},{3,2},{4,5},{5,4},{6,7},{7,6},{8,9},{9,8},{10,11... | collective-permute-start | bytes 1572872 | tf_op jit(solution)/shard_map/ppermute | solution.py:154
  1.2 15.8 %collective-permute-start.2 = (bf16[512,512]{1,0:T(8,128)(2,1)}, bf16[512,512]{1,0:T(8,128)(2,1)S(1)}, u32[]{:S(2)}, u32[]{:S(2)}) collective-permute-start(bf16[512,512]{1,0:T(8,128)(2,1)} %bitcast.11), channel_id=1, source_target_pairs={{0,2},{1,3},{2,0},{3,1},{4,6},{5,7},{6,4},{7,5},{8,10},{9,11},{10,... | collective-permute-start | bytes 1572872 | tf_op jit(solution)/shard_map/ppermute | solution.py:154
  4.2 23.6 %collective-permute-start.4 = (bf16[512,512]{1,0:T(8,128)(2,1)}, bf16[512,512]{1,0:T(8,128)(2,1)S(1)}, u32[]{:S(2)}, u32[]{:S(2)}) collective-permute-start(bf16[512,512]{1,0:T(8,128)(2,1)} %bitcast.14), channel_id=1, source_target_pairs={{0,2},{1,3},{2,0},{3,1},{4,6},{5,7},{6,4},{7,5},{8,10},{9,11},{10,... | collective-permute-start | bytes 1572872 | tf_op jit(solution)/shard_map/ppermute | solution.py:154
  4.9 1.7 %copy-start = (bf16[1,1,5,512,512]{4,3,2,1,0:T(8,128)(2,1)S(1)}, bf16[1,1,5,512,512]{4,3,2,1,0:T(8,128)(2,1)}, u32[]{:S(2)}) copy-start(bf16[1,1,5,512,512]{4,3,2,1,0:T(8,128)(2,1)} %param.8) | copy-start | bytes 7864324
  6.6 1.0 %copy-start.1 = (bf16[512,512]{1,0:T(8,128)(2,1)S(1)}, bf16[512,512]{1,0:T(8,128)(2,1)}, u32[]{:S(2)}) copy-start(bf16[512,512]{1,0:T(8,128)(2,1)} %lower_hbm.1) | copy-start | bytes 1572868
  7.6 1.0 %copy-start.2 = (bf16[1,1,512,512]{3,2,1,0:T(8,128)(2,1)S(1)}, bf16[1,1,512,512]{3,2,1,0:T(8,128)(2,1)}, u32[]{:S(2)}) copy-start(bf16[1,1,512,512]{3,2,1,0:T(8,128)(2,1)} %param.9) | copy-start | bytes 1572868
  8.7 1.0 %copy-start.3 = (bf16[1,1,512,512]{3,2,1,0:T(8,128)(2,1)S(1)}, bf16[1,1,512,512]{3,2,1,0:T(8,128)(2,1)}, u32[]{:S(2)}) copy-start(bf16[1,1,512,512]{3,2,1,0:T(8,128)(2,1)} %param.10) | copy-start | bytes 1572868
  9.7 0.7 copy-start.4
  17.1 13.7 %collective-permute-start.3 = (bf16[512,512]{1,0:T(8,128)(2,1)S(1)}, bf16[512,512]{1,0:T(8,128)(2,1)S(1)}, u32[]{:S(2)}, u32[]{:S(2)}) collective-permute-start(bf16[512,512]{1,0:T(8,128)(2,1)S(1)} %collective-permute-done.2.across), channel_id=1, source_target_pairs={{0,4},{1,5},{4,8},{5,9},{6,2},{7,3},{8,12},{9,13},{10,6},{11,7},{1... | collective-permute-start | bytes 1572872 | tf_op jit(solution)/shard_map/ppermute | solution.py:159
  30.9 4.5 %collective-permute-start.5 = (bf16[512,512]{1,0:T(8,128)(2,1)S(1)}, bf16[512,512]{1,0:T(8,128)(2,1)S(1)}, u32[]{:S(2)}, u32[]{:S(2)}) collective-permute-start(bf16[512,512]{1,0:T(8,128)(2,1)S(1)} %broadcast_select_fusion.1), channel_id=1, source_target_pairs={{0,1},{1,0},{2,3},{3,2},{4,5},{5,4},{6,7},{7,6},{8,9},{9,8},{10,11... | collective-permute-start | bytes 1572872 | tf_op jit(solution)/shard_map/ppermute | solution.py:154
  31.0 16.2 %collective-permute-start.6 = (bf16[512,512]{1,0:T(8,128)(2,1)S(1)}, bf16[512,512]{1,0:T(8,128)(2,1)S(1)}, u32[]{:S(2)}, u32[]{:S(2)}) collective-permute-start(bf16[512,512]{1,0:T(8,128)(2,1)S(1)} %collective-permute-done.4.across), channel_id=1, source_target_pairs={{0,4},{1,5},{4,8},{5,9},{6,2},{7,3},{8,12},{9,13},{10,6},{11,7},{1... | collective-permute-start | bytes 1572872 | tf_op jit(solution)/shard_map/ppermute | solution.py:159
  37.7 9.6 %collective-permute-start.8 = (bf16[2,256,512]{2,1,0:T(8,128)(2,1)S(1)}, bf16[2,256,512]{2,1,0:T(8,128)(2,1)S(1)}, u32[]{:S(2)}, u32[]{:S(2)}) collective-permute-start(bf16[2,256,512]{2,1,0:T(8,128)(2,1)S(1)} %get-tuple-element.55), channel_id=1, source_target_pairs={{0,1},{1,0},{2,3},{3,2},{4,5},{5,4},{6,7},{7,6},{8,9},{9,8},{10,11... | collective-permute-start | bytes 1572872 | tf_op jit(solution)/shard_map/ppermute | solution.py:154
  47.2 3.5 %collective-permute-start.7 = (bf16[512,512]{1,0:T(8,128)(2,1)S(1)}, bf16[512,512]{1,0:T(8,128)(2,1)S(1)}, u32[]{:S(2)}, u32[]{:S(2)}) collective-permute-start(bf16[512,512]{1,0:T(8,128)(2,1)S(1)} %broadcast_select_fusion), channel_id=1, source_target_pairs={{0,1},{1,0},{2,3},{3,2},{4,5},{5,4},{6,7},{7,6},{8,9},{9,8},{10,11... | collective-permute-start | bytes 1572872 | tf_op jit(solution)/shard_map/ppermute | solution.py:154
  47.6 9.4 %collective-permute-start.9 = (bf16[2,128,512]{2,1,0:T(8,128)(2,1)S(1)}, bf16[2,128,512]{2,1,0:T(8,128)(2,1)S(1)}, u32[]{:S(2)}, u32[]{:S(2)}) collective-permute-start(bf16[2,128,512]{2,1,0:T(8,128)(2,1)S(1)} %select_convert_fusion), channel_id=1, source_target_pairs={{0,2},{1,3},{2,0},{3,1},{4,6},{5,7},{6,4},{7,5},{8,10},{9,11},{10,... | collective-permute-start | bytes 786440 | tf_op jit(solution)/shard_map/ppermute | solution.py:154
  57.1 2.0 %collective-permute-start.15 = (bf16[1,256,512]{2,1,0:T(8,128)(2,1)S(1)}, bf16[1,256,512]{2,1,0:T(8,128)(2,1)S(1)}, u32[]{:S(2)}, u32[]{:S(2)}) collective-permute-start(bf16[1,256,512]{2,1,0:T(8,128)(2,1)S(1)} %get-tuple-element.61), channel_id=1, source_target_pairs={{0,1},{1,0},{2,3},{3,2},{4,5},{5,4},{6,7},{7,6},{8,9},{9,8},{10,11... | collective-permute-start | bytes 786440 | tf_op jit(solution)/shard_map/ppermute | solution.py:154
  57.2 6.0 %collective-permute-start.10 = (bf16[2,64,512]{2,1,0:T(8,128)(2,1)S(1)}, bf16[2,64,512]{2,1,0:T(8,128)(2,1)S(1)}, u32[]{:S(2)}, u32[]{:S(2)}) collective-permute-start(bf16[2,64,512]{2,1,0:T(8,128)(2,1)S(1)} %select_convert_fusion.2), channel_id=1, source_target_pairs={{0,4},{1,5},{2,6},{3,7},{4,0},{5,1},{6,2},{7,3},{8,12},{9,13},{10,... | collective-permute-start | bytes 393224 | tf_op jit(solution)/shard_map/ppermute | solution.py:154
  59.2 6.9 %collective-permute-start.16 = (bf16[1,128,512]{2,1,0:T(8,128)(2,1)S(1)}, bf16[1,128,512]{2,1,0:T(8,128)(2,1)S(1)}, u32[]{:S(2)}, u32[]{:S(2)}) collective-permute-start(bf16[1,128,512]{2,1,0:T(8,128)(2,1)S(1)} %select_convert_fusion.1), channel_id=1, source_target_pairs={{0,2},{1,3},{2,0},{3,1},{4,6},{5,7},{6,4},{7,5},{8,10},{9,11},{10,... | collective-permute-start | bytes 393224 | tf_op jit(solution)/shard_map/ppermute | solution.py:154
  63.3 9.0 %collective-permute-start.11 = (bf16[2,64,512]{2,1,0:T(8,128)(2,1)S(1)}, bf16[2,64,512]{2,1,0:T(8,128)(2,1)S(1)}, u32[]{:S(2)}, u32[]{:S(2)}) collective-permute-start(bf16[2,64,512]{2,1,0:T(8,128)(2,1)S(1)} %add_convert_fusion.1), channel_id=1, source_target_pairs={{0,8},{1,9},{2,10},{3,11},{4,12},{5,13},{6,14},{7,15},{8,0},{9,1},... | collective-permute-start | bytes 393224 | tf_op jit(solution)/shard_map/ppermute | solution.py:154
  66.2 7.0 %collective-permute-start.17 = (bf16[1,64,512]{2,1,0:T(8,128)(2,1)S(1)}, bf16[1,64,512]{2,1,0:T(8,128)(2,1)S(1)}, u32[]{:S(2)}, u32[]{:S(2)}) collective-permute-start(bf16[1,64,512]{2,1,0:T(8,128)(2,1)S(1)} %select_convert_fusion.3), channel_id=1, source_target_pairs={{0,4},{1,5},{2,6},{3,7},{4,0},{5,1},{6,2},{7,3},{8,12},{9,13},{10,... | collective-permute-start | bytes 196616 | tf_op jit(solution)/shard_map/ppermute | solution.py:154
  72.4 20.4 %copy-start.5 = (f32[512,512]{1,0:T(8,128)S(1)}, f32[512,512]{1,0:T(8,128)}, u32[]{:S(2)}) copy-start(f32[512,512]{1,0:T(8,128)} %first_diag_ref.1) | copy-start | bytes 3145732
  72.4 20.4 %copy-start.6 = (f32[512,512]{1,0:T(8,128)S(1)}, f32[512,512]{1,0:T(8,128)}, u32[]{:S(2)}) copy-start(f32[512,512]{1,0:T(8,128)} %second_diag_ref.1) | copy-start | bytes 3145732
  72.4 5.7 %collective-permute-start.12 = (bf16[2,64,512]{2,1,0:T(8,128)(2,1)S(1)}, bf16[2,64,512]{2,1,0:T(8,128)(2,1)S(1)}, u32[]{:S(2)}, u32[]{:S(2)}) collective-permute-start(bf16[2,64,512]{2,1,0:T(8,128)(2,1)S(1)} %add_convert_fusion), channel_id=1, source_target_pairs={{0,4},{1,5},{2,6},{3,7},{4,0},{5,1},{6,2},{7,3},{8,12},{9,13},{10,... | collective-permute-start | bytes 393224 | tf_op jit(solution)/shard_map/ppermute | solution.py:154
  73.2 5.7 %collective-permute-start.18 = (bf16[1,64,512]{2,1,0:T(8,128)(2,1)S(1)}, bf16[1,64,512]{2,1,0:T(8,128)(2,1)S(1)}, u32[]{:S(2)}, u32[]{:S(2)}) collective-permute-start(bf16[1,64,512]{2,1,0:T(8,128)(2,1)S(1)} %add_convert_fusion.3), channel_id=1, source_target_pairs={{0,8},{1,9},{2,10},{3,11},{4,12},{5,13},{6,14},{7,15},{8,0},{9,1},... | collective-permute-start | bytes 196616 | tf_op jit(solution)/shard_map/ppermute | solution.py:154
  78.9 5.1 %collective-permute-start.19 = (bf16[1,64,512]{2,1,0:T(8,128)(2,1)S(1)}, bf16[1,64,512]{2,1,0:T(8,128)(2,1)S(1)}, u32[]{:S(2)}, u32[]{:S(2)}) collective-permute-start(bf16[1,64,512]{2,1,0:T(8,128)(2,1)S(1)} %add_convert_fusion.2), channel_id=1, source_target_pairs={{0,4},{1,5},{2,6},{3,7},{4,0},{5,1},{6,2},{7,3},{8,12},{9,13},{10,... | collective-permute-start | bytes 196616 | tf_op jit(solution)/shard_map/ppermute | solution.py:154
  81.8 8.9 %collective-permute-start.13 = (bf16[2,128,512]{2,1,0:T(8,128)(2,1)S(1)}, bf16[2,128,512]{2,1,0:T(8,128)(2,1)S(1)}, u32[]{:S(2)}, u32[]{:S(2)}) collective-permute-start(bf16[2,128,512]{2,1,0:T(8,128)(2,1)S(1)} %pad_maximum_fusion.1), channel_id=1, source_target_pairs={{0,2},{1,3},{2,0},{3,1},{4,6},{5,7},{6,4},{7,5},{8,10},{9,11},{10,... | collective-permute-start | bytes 786440 | tf_op jit(solution)/shard_map/ppermute | solution.py:154
  84.0 8.0 %collective-permute-start.20 = (bf16[1,128,512]{2,1,0:T(8,128)(2,1)S(1)}, bf16[1,128,512]{2,1,0:T(8,128)(2,1)S(1)}, u32[]{:S(2)}, u32[]{:S(2)}) collective-permute-start(bf16[1,128,512]{2,1,0:T(8,128)(2,1)S(1)} %pad_maximum_fusion.3), channel_id=1, source_target_pairs={{0,2},{1,3},{2,0},{3,1},{4,6},{5,7},{6,4},{7,5},{8,10},{9,11},{10,... | collective-permute-start | bytes 393224 | tf_op jit(solution)/shard_map/ppermute | solution.py:154
  90.8 2.0 %collective-permute-start.14 = (bf16[2,256,512]{2,1,0:T(8,128)(2,1)S(1)}, bf16[2,256,512]{2,1,0:T(8,128)(2,1)S(1)}, u32[]{:S(2)}, u32[]{:S(2)}) collective-permute-start(bf16[2,256,512]{2,1,0:T(8,128)(2,1)S(1)} %pad_maximum_fusion.mine_ref), channel_id=1, source_target_pairs={{0,1},{1,0},{2,3},{3,2},{4,5},{5,4},{6,7},{7,6},{8,9},{9,8},{10,11... | collective-permute-start | bytes 1572872 | tf_op jit(solution)/shard_map/ppermute | solution.py:154
  92.1 2.9 %collective-permute-start.21 = (bf16[1,256,512]{2,1,0:T(8,128)(2,1)S(1)}, bf16[1,256,512]{2,1,0:T(8,128)(2,1)S(1)}, u32[]{:S(2)}, u32[]{:S(2)}) collective-permute-start(bf16[1,256,512]{2,1,0:T(8,128)(2,1)S(1)} %pad_maximum_fusion.2.mine_ref), channel_id=1, source_target_pairs={{0,1},{1,0},{2,3},{3,2},{4,5},{5,4},{6,7},{7,6},{8,9},{9,8},{10,11... | collective-permute-start | bytes 786440 | tf_op jit(solution)/shard_map/ppermute | solution.py:154

commit v10 on v9

--- a/solution.py
+++ b/solution.py
@@ -39,7 +39,19 @@
     return jnp.int32(0), beside, across, -across, -beside
 
 
-def near_kernel(where_ref, list_ref, count_ref, sigma_hbm, lower_hbm, first, second,
+def split_kernel(panel_hbm, low, high, sems):
+    half = low.shape[0]
+    copies = [
+        pltpu.make_async_copy(panel_hbm.at[pl.ds(index * half, half)], target, sems.at[index])
+        for index, target in enumerate((low, high))
+    ]
+    for copy in copies:
+        copy.start()
+    for copy in copies:
+        copy.wait()
+
+
+def near_kernel(where_ref, list_ref, count_ref, sigma_hbm, lower_hbm, first_0, first_1, second,
                 first_beside, second_beside,
                 first_acc, second_acc, turned_ref, sigma_ref, lower_ref, near_ref, sems):
     lives = []
@@ -66,11 +78,14 @@
         def _():
             target[...] = jnp.zeros(target.shape, target.dtype)
 
-    size = first.shape[0]
-    turned_ref[:size] = first[...].T
+    half = first_0.shape[0]
+    size = 2 * half
+    turned_ref[:size, :half] = first_0[...].T
+    turned_ref[:size, half:] = first_1[...].T
     turned_ref[size:] = second[...].T
     arrived(0)
-    first_acc[...] = dot(near_ref[0], first[...])
+    first_acc[...] = dot(near_ref[0, :, :half], first_0[...])
+    first_acc[...] += dot(near_ref[0, :, half:], first_1[...])
     second_acc[...] = dot(near_ref[0], second[...])
     arrived(1)
     first_acc[...] += dot(near_ref[1], first_beside[...])
@@ -88,11 +103,14 @@
     give_ref[index] = scratch_ref[pl.ds(pl.multiple_of((1 - core) * half, half), half)].astype(jnp.bfloat16)
 
 
-def first_kernel(where_ref, acc_in, across, far, rest, sigma_ref, turned_ref,
+def first_kernel(where_ref, acc_in, across_0, across_1, far_0, far_1, rest, sigma_ref, turned_ref,
                  column_ref, again_ref, give_ref, keep_ref, acc_ref):
+    half = far_0.shape[0]
     acc_ref[...] = acc_in[...]
-    acc_ref[...] += dot(sigma_ref[0], across[...])
-    acc_ref[...] += dot(sigma_ref[1], far[...])
+    acc_ref[...] += dot(sigma_ref[0, :, :half], across_0[...])
+    acc_ref[...] += dot(sigma_ref[0, :, half:], across_1[...])
+    acc_ref[...] += dot(sigma_ref[1, :, :half], far_0[...])
+    acc_ref[...] += dot(sigma_ref[1, :, half:], far_1[...])
     acc_ref[...] += dot(sigma_ref[2], rest[...])
     column = (-acc_ref[...]).astype(jnp.bfloat16)
     column_ref[...] = column
@@ -160,8 +178,7 @@
 
 
 def rest_of(across, far, give_across, devices):
-    rows = across.shape[0] // len(far)
-    pieces = [jnp.where(give_across, across[i * rows : (i + 1) * rows], piece) for i, piece in enumerate(far)]
+    pieces = [jnp.where(give_across, a, f) for a, f in zip(across, far)]
     return swapped(jnp.concatenate(pieces, axis=0), 1, devices)
 
 
@@ -218,7 +235,9 @@
     def parts(k):
         return [jax.ShapeDtypeStruct((k, half, width), t) for t in (jnp.bfloat16, jnp.float32)]
 
-    across = swapped(first, 2, devices)
+    piece = jax.ShapeDtypeStruct((half, width), jnp.bfloat16)
+    pieces = call(split_kernel, [piece] * 2, [first], "h", 1, [pltpu.SemaphoreType.DMA((2,))])
+    across = [swapped(part, 2, devices) for part in pieces]
     second_across = swapped(second, 2, devices)
     beside = swapped(first, 1, devices)
     second_beside = swapped(second, 1, devices)
@@ -226,27 +245,27 @@
         near_kernel,
         [wide, wide, jax.ShapeDtypeStruct((2 * size, width), jnp.bfloat16),
          jax.ShapeDtypeStruct((3, size, width), jnp.bfloat16), narrow],
-        [where, listed, count, sigma, lower_panel, first, second, beside, second_beside],
-        "ssshhvvvv",
+        [where, listed, count, sigma, lower_panel, *pieces, second, beside, second_beside],
+        "ssshhvvvvv",
         4 * one,
         [pltpu.VMEM((2, size, width), jnp.bfloat16), pltpu.SemaphoreType.DMA((6,))],
     )
-    across, turned = barrier((across, turned))
-    far = far_of(across, devices)
+    across[1], turned = barrier((across[1], turned))
+    far = [far_of(part, devices) for part in across]
+    second_far = far_of(second_across, devices)
     far, second_across = barrier((far, second_across))
-    second_far = far_of(second_across, devices)
-    rest = rest_of(across, [far], give_across, devices)
+    rest = rest_of(across, far, give_across, devices)
     column_first, column_again, give, keep = call(
         first_kernel,
         [narrow, narrow] + parts(2),
-        [where, first_acc, across, far, rest, sorted_sigma, turned],
-        "svvvvvv",
+        [where, first_acc, *across, *far, rest, sorted_sigma, turned],
+        "svvvvvvvv",
         5 * one,
         scratch,
     )
     give, second_across = barrier((give, second_across))
     give, keep = core_summed(give, keep, uppers, devices)
-    second_rest = rest_of(second_across, [second_far], give_across, devices)
+    second_rest = rest_of([second_across], [second_far], give_across, devices)
     total = chip_summed(give, keep, devices)
     (second_acc,) = call(
         across_kernel, [wide], [second_acc, column_again, lower, second_across, sorted_sigma], "vvvvv", 2 * one

time: 96.5 us -> 93.7 us (0.971)
  waiting for transfers between devices: 47.2 us -> 43.8 us
    ppermute x2 -> x3, starting transfers between devices: 8.49 us -> 11.8 us  [far_of(): lax.ppermute(across, 'row', [(a, b) for a, b in hops if 0 <= b < devices])]
    ppermute x20 -> x21, starting transfers between devices: 21.8 us -> 18.8 us  [swapped(): return lax.ppermute(value, 'row', [(i, i ^ bit) for i in range(devices)])]
    ppermute x20 -> x21, waiting for transfers between devices: 34.9 us -> 32.4 us  [swapped(): return lax.ppermute(value, 'row', [(i, i ^ bit) for i in range(devices)])]
    ppermute x2 -> x3, waiting for transfers between devices: 12.3 us -> 11.4 us  [far_of(): lax.ppermute(across, 'row', [(a, b) for a, b in hops if 0 <= b < devices])]
    pallas_call x6 -> x7, Pallas kernels: 10.6 us -> 10.7 us  [call(): pl.pallas_call(body, out_shape=outs, in_specs=[pl.BlockSpec(memory_space=...]
  transfers between devices with their start and end apart: 22 -> 24, of which waited for: 13 -> 12; matrix products, arithmetic and copies ran while one was open for 1% -> 1% of each run, Pallas kernels for 10% -> 10%
where the time goes in v10:
time: 93.7 us; the launch traced here: 93.3 us
  waiting for transfers between devices  43.8 us (47%)
  starting transfers between devices  30.6 us (33%)
  Pallas kernels  10.7 us (11%)
  local copies, waits for them, and re-layouts  5.53 us (6%)
  between operations  1.63 us (2%)
  other arithmetic  1.12 us (1%)
    ppermute x21, waiting for transfers between devices, swapped(): return lax.ppermute(value, 'row', [(i, i ^ bit) for i in range(devices)])  32.4 us
    ppermute x21, starting transfers between devices, swapped(): return lax.ppermute(value, 'row', [(i, i ^ bit) for i in range(devices)])  18.8 us
    ppermute x3, starting transfers between devices, far_of(): lax.ppermute(across, 'row', [(a, b) for a, b in hops if 0 <= b < devices])  11.8 us
    ppermute x3, waiting for transfers between devices, far_of(): lax.ppermute(across, 'row', [(a, b) for a, b in hops if 0 <= b < devices])  11.4 us
    pallas_call x7, Pallas kernels, call(): pl.pallas_call(body, out_shape=outs, in_specs=[pl.BlockSpec(memory_space=...  10.7 us
    unnamed x14, local copies, waits for them, and re-layouts  5.53 us
  transfers between devices with their start and end apart: 24, of which 12 were waited for; matrix products, arithmetic and copies ran while one was open for 1% of the time, Pallas kernels for 10%

profile of v10, /device:TPU:0, one launch (start us, length us, event | category | flops | bytes accessed | tf_op | source)
XLA Modules:
  0.0 93.3 jit_solution(14318512865763414142)
XLA Ops:
  1.2 1.0 %copy-done.3 = bf16[1,1,512,512]{3,2,1,0:T(8,128)(2,1)S(1)} copy-done((bf16[1,1,512,512]{3,2,1,0:T(8,128)(2,1)S(1)}, bf16[1,1,512,512]{3,2,1,0:T(8,128)(2,1)}, u32[]{:S(2)}) %copy-start.3) | copy-done | bytes 524312
  2.3 3.0 %collective-permute-start.2 = (bf16[256,512]{1,0:T(8,128)(2,1)S(1)}, bf16[256,512]{1,0:T(8,128)(2,1)S(1)}, u32[]{:S(2)}, u32[]{:S(2)}) collective-permute-start(bf16[256,512]{1,0:T(8,128)(2,1)S(1)} %get-tuple-element.39.first_0), channel_id=1, source_target_pairs={{0,2},{1,3},{2,0},{3,1},{4,6},{5,7},{6,4},{7,5},{8,10},{9,11},{10,... | collective-permute-start | bytes 786440 | tf_op jit(solution)/shard_map/ppermute | solution.py:172
  5.4 1.9 %collective-permute-start.6 = (bf16[512,512]{1,0:T(8,128)(2,1)}, bf16[512,512]{1,0:T(8,128)(2,1)S(1)}, u32[]{:S(2)}, u32[]{:S(2)}) collective-permute-start(bf16[512,512]{1,0:T(8,128)(2,1)} %bitcast.11), channel_id=1, source_target_pairs={{0,2},{1,3},{2,0},{3,1},{4,6},{5,7},{6,4},{7,5},{8,10},{9,11},{10,... | collective-permute-start | bytes 1572872 | tf_op jit(solution)/shard_map/ppermute | solution.py:172
  8.0 4.4 %collective-permute-done.2.across_0 = bf16[256,512]{1,0:T(8,128)(2,1)S(1)} collective-permute-done((bf16[256,512]{1,0:T(8,128)(2,1)S(1)}, bf16[256,512]{1,0:T(8,128)(2,1)S(1)}, u32[]{:S(2)}, u32[]{:S(2)}) %collective-permute-start.2) | collective-permute-done | bytes 262176 | tf_op jit(solution)/shard_map/ppermute | solution.py:172
  12.4 4.1 %collective-permute-start.4 = (bf16[256,512]{1,0:T(8,128)(2,1)S(1)}, bf16[256,512]{1,0:T(8,128)(2,1)S(1)}, u32[]{:S(2)}, u32[]{:S(2)}) collective-permute-start(bf16[256,512]{1,0:T(8,128)(2,1)S(1)} %collective-permute-done.2.across_0), channel_id=1, source_target_pairs={{0,4},{1,5},{4,8},{5,9},{6,2},{7,3},{8,12},{9,13},{10,6},{11,7},{1... | collective-permute-start | bytes 786440 | tf_op jit(solution)/shard_map/ppermute | solution.py:177
  16.5 1.7 %copy-done = bf16[1,1,5,512,512]{4,3,2,1,0:T(8,128)(2,1)S(1)} copy-done((bf16[1,1,5,512,512]{4,3,2,1,0:T(8,128)(2,1)S(1)}, bf16[1,1,5,512,512]{4,3,2,1,0:T(8,128)(2,1)}, u32[]{:S(2)}) %copy-start) | copy-done | bytes 2621464
  18.3 1.0 %copy-done.1 = bf16[512,512]{1,0:T(8,128)(2,1)S(1)} copy-done((bf16[512,512]{1,0:T(8,128)(2,1)S(1)}, bf16[512,512]{1,0:T(8,128)(2,1)}, u32[]{:S(2)}) %copy-start.1) | copy-done | bytes 524312
  19.3 1.0 %copy-done.2 = bf16[1,1,512,512]{3,2,1,0:T(8,128)(2,1)S(1)} copy-done((bf16[1,1,512,512]{3,2,1,0:T(8,128)(2,1)S(1)}, bf16[1,1,512,512]{3,2,1,0:T(8,128)(2,1)}, u32[]{:S(2)}) %copy-start.2) | copy-done | bytes 524312
  20.3 0.7 copy-done.4
  21.0 2.6 %shard_map.120 = (f32[512,512]{1,0:T(8,128)S(1)}, f32[512,512]{1,0:T(8,128)S(1)}, bf16[1024,512]{1,0:T(8,128)(2,1)S(1)}, bf16[3,512,512]{2,1,0:T(8,128)(2,1)S(1)}, bf16[512,512]{1,0:T(8,128)(2,1)S(1)}) custom-call(s32[1]{0:T(128)} %bitcast.where_ref, s32[5]{0:T(128)S(1)} %bitcast.15, s32[1]{0:T(128)} %bitcast.8.count_ref, bf16[5,512,512]{2,1,0:T(8,128)(2,1)S(1)} %bitcast.9, ...), custom_call_target="tpu_custom_call" | custom-call | flops 1073741824 | bytes 10485788 | tf_op jit(solution)/shard_map/pallas_call | solution.py:16
  23.6 3.4 %collective-permute-start.5 = (bf16[256,512]{1,0:T(8,128)(2,1)S(1)}, bf16[256,512]{1,0:T(8,128)(2,1)S(1)}, u32[]{:S(2)}, u32[]{:S(2)}) collective-permute-start(bf16[256,512]{1,0:T(8,128)(2,1)S(1)} %collective-permute-done.3.across_1), channel_id=1, source_target_pairs={{0,4},{1,5},{4,8},{5,9},{6,2},{7,3},{8,12},{9,13},{10,6},{11,7},{1... | collective-permute-start | bytes 786440 | tf_op jit(solution)/shard_map/ppermute | solution.py:177
  27.0 1.7 %collective-permute-done.6.across = bf16[512,512]{1,0:T(8,128)(2,1)S(1)} collective-permute-done((bf16[512,512]{1,0:T(8,128)(2,1)}, bf16[512,512]{1,0:T(8,128)(2,1)S(1)}, u32[]{:S(2)}, u32[]{:S(2)}) %collective-permute-start.6) | collective-permute-done | bytes 524320 | tf_op jit(solution)/shard_map/ppermute | solution.py:172
  28.7 2.1 %collective-permute-done.5.far_1 = bf16[256,512]{1,0:T(8,128)(2,1)S(1)} collective-permute-done((bf16[256,512]{1,0:T(8,128)(2,1)S(1)}, bf16[256,512]{1,0:T(8,128)(2,1)S(1)}, u32[]{:S(2)}, u32[]{:S(2)}) %collective-permute-start.5) | collective-permute-done | bytes 262176 | tf_op jit(solution)/shard_map/ppermute | solution.py:177
  31.1 4.4 %collective-permute-start.8 = (bf16[512,512]{1,0:T(8,128)(2,1)S(1)}, bf16[512,512]{1,0:T(8,128)(2,1)S(1)}, u32[]{:S(2)}, u32[]{:S(2)}) collective-permute-start(bf16[512,512]{1,0:T(8,128)(2,1)S(1)} %collective-permute-done.6.across), channel_id=1, source_target_pairs={{0,4},{1,5},{4,8},{5,9},{6,2},{7,3},{8,12},{9,13},{10,6},{11,7},{1... | collective-permute-start | bytes 1572872 | tf_op jit(solution)/shard_map/ppermute | solution.py:177
  35.5 2.3 %shard_map.121 = (bf16[512,512]{1,0:T(8,128)(2,1)}, bf16[512,512]{1,0:T(8,128)(2,1)S(1)}, bf16[2,256,512]{2,1,0:T(8,128)(2,1)S(1)}, f32[2,256,512]{2,1,0:T(8,128)S(1)}) custom-call(s32[1]{0:T(128)} %bitcast.where_ref, f32[512,512]{1,0:T(8,128)S(1)} %get-tuple-element.42.acc_in, bf16[256,512]{1,0:T(8,128)(2,1)S(1)} %collective-permute-done.2.across_0, ...), custom_call_target="tpu_custom_call" | custom-call | flops 1342177280 | bytes 7864324 | tf_op jit(solution)/shard_map/pallas_call | solution.py:16
  38.0 9.2 %collective-permute-done.8.far = bf16[512,512]{1,0:T(8,128)(2,1)S(1)} collective-permute-done((bf16[512,512]{1,0:T(8,128)(2,1)S(1)}, bf16[512,512]{1,0:T(8,128)(2,1)S(1)}, u32[]{:S(2)}, u32[]{:S(2)}) %collective-permute-start.8) | collective-permute-done | bytes 524320 | tf_op jit(solution)/shard_map/ppermute | solution.py:177
  47.7 1.2 %collective-permute-start.11 = (bf16[2,128,512]{2,1,0:T(8,128)(2,1)S(1)}, bf16[2,128,512]{2,1,0:T(8,128)(2,1)S(1)}, u32[]{:S(2)}, u32[]{:S(2)}) collective-permute-start(bf16[2,128,512]{2,1,0:T(8,128)(2,1)S(1)} %select_convert_fusion), channel_id=1, source_target_pairs={{0,2},{1,3},{2,0},{3,1},{4,6},{5,7},{6,4},{7,5},{8,10},{9,11},{10,... | collective-permute-start | bytes 786440 | tf_op jit(solution)/shard_map/ppermute | solution.py:172
  48.9 0.7 shard_map.122.acc_in
  49.6 1.6 %shard_map.123 = (bf16[512,512]{1,0:T(8,128)(2,1)}, bf16[1,256,512]{2,1,0:T(8,128)(2,1)S(1)}, f32[1,256,512]{2,1,0:T(8,128)S(1)}) custom-call(s32[1]{0:T(128)} %bitcast.where_ref, f32[512,512]{1,0:T(8,128)S(1)} %shard_map.122.acc_in, bf16[512,512]{1,0:T(8,128)(2,1)S(1)} %collective-permute-done.8.far, bf16[512,512]{1,0:T(8,128)(2,1)S(1)} %collective-permute-done.9.rest, ...), custom_call_target="tpu_custom_call" | custom-call | flops 805306368 | bytes 6029316 | tf_op jit(solution)/shard_map/pallas_call | solution.py:16
  51.2 5.2 %collective-permute-done.11 = bf16[2,128,512]{2,1,0:T(8,128)(2,1)S(1)} collective-permute-done((bf16[2,128,512]{2,1,0:T(8,128)(2,1)S(1)}, bf16[2,128,512]{2,1,0:T(8,128)(2,1)S(1)}, u32[]{:S(2)}, u32[]{:S(2)}) %collective-permute-start.11) | collective-permute-done | bytes 262176 | tf_op jit(solution)/shard_map/ppermute | solution.py:172
  56.7 2.5 %collective-permute-start.12 = (bf16[2,64,512]{2,1,0:T(8,128)(2,1)S(1)}, bf16[2,64,512]{2,1,0:T(8,128)(2,1)S(1)}, u32[]{:S(2)}, u32[]{:S(2)}) collective-permute-start(bf16[2,64,512]{2,1,0:T(8,128)(2,1)S(1)} %select_convert_fusion.2), channel_id=1, source_target_pairs={{0,4},{1,5},{2,6},{3,7},{4,0},{5,1},{6,2},{7,3},{8,12},{9,13},{10,... | collective-permute-start | bytes 393224 | tf_op jit(solution)/shard_map/ppermute | solution.py:172
  59.8 3.5 %collective-permute-done.12 = bf16[2,64,512]{2,1,0:T(8,128)(2,1)S(1)} collective-permute-done((bf16[2,64,512]{2,1,0:T(8,128)(2,1)S(1)}, bf16[2,64,512]{2,1,0:T(8,128)(2,1)S(1)}, u32[]{:S(2)}, u32[]{:S(2)}) %collective-permute-start.12) | collective-permute-done | bytes 131104 | tf_op jit(solution)/shard_map/ppermute | solution.py:172
  63.4 2.8 %collective-permute-start.13 = (bf16[2,64,512]{2,1,0:T(8,128)(2,1)S(1)}, bf16[2,64,512]{2,1,0:T(8,128)(2,1)S(1)}, u32[]{:S(2)}, u32[]{:S(2)}) collective-permute-start(bf16[2,64,512]{2,1,0:T(8,128)(2,1)S(1)} %add_convert_fusion.1), channel_id=1, source_target_pairs={{0,8},{1,9},{2,10},{3,11},{4,12},{5,13},{6,14},{7,15},{8,0},{9,1},... | collective-permute-start | bytes 393224 | tf_op jit(solution)/shard_map/ppermute | solution.py:172
  66.7 5.8 %collective-permute-done.13 = bf16[2,64,512]{2,1,0:T(8,128)(2,1)S(1)} collective-permute-done((bf16[2,64,512]{2,1,0:T(8,128)(2,1)S(1)}, bf16[2,64,512]{2,1,0:T(8,128)(2,1)S(1)}, u32[]{:S(2)}, u32[]{:S(2)}) %collective-permute-start.13) | collective-permute-done | bytes 131104 | tf_op jit(solution)/shard_map/ppermute | solution.py:172
  72.7 2.9 %collective-permute-start.20 = (bf16[1,64,512]{2,1,0:T(8,128)(2,1)S(1)}, bf16[1,64,512]{2,1,0:T(8,128)(2,1)S(1)}, u32[]{:S(2)}, u32[]{:S(2)}) collective-permute-start(bf16[1,64,512]{2,1,0:T(8,128)(2,1)S(1)} %add_convert_fusion.3), channel_id=1, source_target_pairs={{0,8},{1,9},{2,10},{3,11},{4,12},{5,13},{6,14},{7,15},{8,0},{9,1},... | collective-permute-start | bytes 196616 | tf_op jit(solution)/shard_map/ppermute | solution.py:172
  75.6 2.9 %collective-permute-done.14 = bf16[2,64,512]{2,1,0:T(8,128)(2,1)S(1)} collective-permute-done((bf16[2,64,512]{2,1,0:T(8,128)(2,1)S(1)}, bf16[2,64,512]{2,1,0:T(8,128)(2,1)S(1)}, u32[]{:S(2)}, u32[]{:S(2)}) %collective-permute-start.14) | collective-permute-done | bytes 131104 | tf_op jit(solution)/shard_map/ppermute | solution.py:172
  78.6 1.4 %collective-permute-start.21 = (bf16[1,64,512]{2,1,0:T(8,128)(2,1)S(1)}, bf16[1,64,512]{2,1,0:T(8,128)(2,1)S(1)}, u32[]{:S(2)}, u32[]{:S(2)}) collective-permute-start(bf16[1,64,512]{2,1,0:T(8,128)(2,1)S(1)} %add_convert_fusion.2), channel_id=1, source_target_pairs={{0,4},{1,5},{2,6},{3,7},{4,0},{5,1},{6,2},{7,3},{8,12},{9,13},{10,... | collective-permute-start | bytes 196616 | tf_op jit(solution)/shard_map/ppermute | solution.py:172
  80.5 2.4 %collective-permute-done.21 = bf16[1,64,512]{2,1,0:T(8,128)(2,1)S(1)} collective-permute-done((bf16[1,64,512]{2,1,0:T(8,128)(2,1)S(1)}, bf16[1,64,512]{2,1,0:T(8,128)(2,1)S(1)}, u32[]{:S(2)}, u32[]{:S(2)}) %collective-permute-start.21) | collective-permute-done | bytes 65568 | tf_op jit(solution)/shard_map/ppermute | solution.py:172
  83.2 4.6 %collective-permute-done.15 = bf16[2,128,512]{2,1,0:T(8,128)(2,1)S(1)} collective-permute-done((bf16[2,128,512]{2,1,0:T(8,128)(2,1)S(1)}, bf16[2,128,512]{2,1,0:T(8,128)(2,1)S(1)}, u32[]{:S(2)}, u32[]{:S(2)}) %collective-permute-start.15) | collective-permute-done | bytes 262176 | tf_op jit(solution)/shard_map/ppermute | solution.py:172
  88.0 1.2 %collective-permute-done.22 = bf16[1,128,512]{2,1,0:T(8,128)(2,1)S(1)} collective-permute-done((bf16[1,128,512]{2,1,0:T(8,128)(2,1)S(1)}, bf16[1,128,512]{2,1,0:T(8,128)(2,1)S(1)}, u32[]{:S(2)}, u32[]{:S(2)}) %collective-permute-start.22) | collective-permute-done | bytes 131104 | tf_op jit(solution)/shard_map/ppermute | solution.py:172
  89.9 2.2 %shard_map.124 = (f32[512,512]{1,0:T(8,128)}, f32[512,512]{1,0:T(8,128)}, f32[512,512]{1,0:T(8,128)S(1)}) custom-call(s32[1]{0:T(128)} %bitcast.where_ref, bf16[2,256,512]{2,1,0:T(8,128)(2,1)S(1)} %pad_maximum_fusion.1.mine_ref, bf16[2,256,512]{2,1,0:T(8,128)(2,1)S(1)} %collective-permute-done.16.other_ref, ...), custom_call_target="tpu_custom_call" | custom-call | flops 1073741824 | bytes 6815748 | tf_op jit(solution)/shard_map/pallas_call | solution.py:16
  92.1 1.2 %shard_map.125 = f32[512,512]{1,0:T(8,128)} custom-call(s32[1]{0:T(128)} %bitcast.where_ref, bf16[1,256,512]{2,1,0:T(8,128)(2,1)S(1)} %pad_maximum_fusion.3.mine_ref, bf16[1,256,512]{2,1,0:T(8,128)(2,1)S(1)} %collective-permute-done.23.other_ref, f32[512,512]{1,0:T(8,128)S(1)} %get-tuple-element.68.base_ref), custom_call_target="tpu_custom_call" | custom-call | flops 262144 | bytes 2621444 | tf_op jit(solution)/shard_map/pallas_call | solution.py:16
  (60 shorter events, 4.7 us)
Async XLA Ops:
  0.6 15.9 %collective-permute-start.1 = (bf16[512,512]{1,0:T(8,128)(2,1)}, bf16[512,512]{1,0:T(8,128)(2,1)S(1)}, u32[]{:S(2)}, u32[]{:S(2)}) collective-permute-start(bf16[512,512]{1,0:T(8,128)(2,1)} %bitcast.10), channel_id=1, source_target_pairs={{0,1},{1,0},{2,3},{3,2},{4,5},{5,4},{6,7},{7,6},{8,9},{9,8},{10,11... | collective-permute-start | bytes 1572872 | tf_op jit(solution)/shard_map/ppermute | solution.py:172
  1.2 15.3 %collective-permute-start = (bf16[512,512]{1,0:T(8,128)(2,1)}, bf16[512,512]{1,0:T(8,128)(2,1)S(1)}, u32[]{:S(2)}, u32[]{:S(2)}) collective-permute-start(bf16[512,512]{1,0:T(8,128)(2,1)} %bitcast.13), channel_id=1, source_target_pairs={{0,1},{1,0},{2,3},{3,2},{4,5},{5,4},{6,7},{7,6},{8,9},{9,8},{10,11... | collective-permute-start | bytes 1572872 | tf_op jit(solution)/shard_map/ppermute | solution.py:172
  1.2 1.0 %copy-start.3 = (bf16[1,1,512,512]{3,2,1,0:T(8,128)(2,1)S(1)}, bf16[1,1,512,512]{3,2,1,0:T(8,128)(2,1)}, u32[]{:S(2)}) copy-start(bf16[1,1,512,512]{3,2,1,0:T(8,128)(2,1)} %param.9) | copy-start | bytes 1572868
  2.3 10.1 %collective-permute-start.2 = (bf16[256,512]{1,0:T(8,128)(2,1)S(1)}, bf16[256,512]{1,0:T(8,128)(2,1)S(1)}, u32[]{:S(2)}, u32[]{:S(2)}) collective-permute-start(bf16[256,512]{1,0:T(8,128)(2,1)S(1)} %get-tuple-element.39.first_0), channel_id=1, source_target_pairs={{0,2},{1,3},{2,0},{3,1},{4,6},{5,7},{6,4},{7,5},{8,10},{9,11},{10,... | collective-permute-start | bytes 786440 | tf_op jit(solution)/shard_map/ppermute | solution.py:172
  5.3 18.3 %collective-permute-start.3 = (bf16[256,512]{1,0:T(8,128)(2,1)S(1)}, bf16[256,512]{1,0:T(8,128)(2,1)S(1)}, u32[]{:S(2)}, u32[]{:S(2)}) collective-permute-start(bf16[256,512]{1,0:T(8,128)(2,1)S(1)} %get-tuple-element.40.first_1), channel_id=1, source_target_pairs={{0,2},{1,3},{2,0},{3,1},{4,6},{5,7},{6,4},{7,5},{8,10},{9,11},{10,... | collective-permute-start | bytes 786440 | tf_op jit(solution)/shard_map/ppermute | solution.py:172
  5.4 23.3 %collective-permute-start.6 = (bf16[512,512]{1,0:T(8,128)(2,1)}, bf16[512,512]{1,0:T(8,128)(2,1)S(1)}, u32[]{:S(2)}, u32[]{:S(2)}) collective-permute-start(bf16[512,512]{1,0:T(8,128)(2,1)} %bitcast.11), channel_id=1, source_target_pairs={{0,2},{1,3},{2,0},{3,1},{4,6},{5,7},{6,4},{7,5},{8,10},{9,11},{10,... | collective-permute-start | bytes 1572872 | tf_op jit(solution)/shard_map/ppermute | solution.py:172
  12.4 14.6 %collective-permute-start.4 = (bf16[256,512]{1,0:T(8,128)(2,1)S(1)}, bf16[256,512]{1,0:T(8,128)(2,1)S(1)}, u32[]{:S(2)}, u32[]{:S(2)}) collective-permute-start(bf16[256,512]{1,0:T(8,128)(2,1)S(1)} %collective-permute-done.2.across_0), channel_id=1, source_target_pairs={{0,4},{1,5},{4,8},{5,9},{6,2},{7,3},{8,12},{9,13},{10,6},{11,7},{1... | collective-permute-start | bytes 786440 | tf_op jit(solution)/shard_map/ppermute | solution.py:177
  16.5 1.7 %copy-start = (bf16[1,1,5,512,512]{4,3,2,1,0:T(8,128)(2,1)S(1)}, bf16[1,1,5,512,512]{4,3,2,1,0:T(8,128)(2,1)}, u32[]{:S(2)}) copy-start(bf16[1,1,5,512,512]{4,3,2,1,0:T(8,128)(2,1)} %param.8) | copy-start | bytes 7864324
  18.3 1.0 %copy-start.1 = (bf16[512,512]{1,0:T(8,128)(2,1)S(1)}, bf16[512,512]{1,0:T(8,128)(2,1)}, u32[]{:S(2)}) copy-start(bf16[512,512]{1,0:T(8,128)(2,1)} %lower_hbm.1) | copy-start | bytes 1572868
  19.3 1.0 %copy-start.2 = (bf16[1,1,512,512]{3,2,1,0:T(8,128)(2,1)S(1)}, bf16[1,1,512,512]{3,2,1,0:T(8,128)(2,1)}, u32[]{:S(2)}) copy-start(bf16[1,1,512,512]{3,2,1,0:T(8,128)(2,1)} %param.10) | copy-start | bytes 1572868
  20.3 0.7 copy-start.4
  23.6 7.2 %collective-permute-start.5 = (bf16[256,512]{1,0:T(8,128)(2,1)S(1)}, bf16[256,512]{1,0:T(8,128)(2,1)S(1)}, u32[]{:S(2)}, u32[]{:S(2)}) collective-permute-start(bf16[256,512]{1,0:T(8,128)(2,1)S(1)} %collective-permute-done.3.across_1), channel_id=1, source_target_pairs={{0,4},{1,5},{4,8},{5,9},{6,2},{7,3},{8,12},{9,13},{10,6},{11,7},{1... | collective-permute-start | bytes 786440 | tf_op jit(solution)/shard_map/ppermute | solution.py:177
  31.0 4.5 %collective-permute-start.7 = (bf16[512,512]{1,0:T(8,128)(2,1)S(1)}, bf16[512,512]{1,0:T(8,128)(2,1)S(1)}, u32[]{:S(2)}, u32[]{:S(2)}) collective-permute-start(bf16[512,512]{1,0:T(8,128)(2,1)S(1)} %pad_maximum_fusion), channel_id=1, source_target_pairs={{0,1},{1,0},{2,3},{3,2},{4,5},{5,4},{6,7},{7,6},{8,9},{9,8},{10,11... | collective-permute-start | bytes 1572872 | tf_op jit(solution)/shard_map/ppermute | solution.py:172
  31.1 16.2 %collective-permute-start.8 = (bf16[512,512]{1,0:T(8,128)(2,1)S(1)}, bf16[512,512]{1,0:T(8,128)(2,1)S(1)}, u32[]{:S(2)}, u32[]{:S(2)}) collective-permute-start(bf16[512,512]{1,0:T(8,128)(2,1)S(1)} %collective-permute-done.6.across), channel_id=1, source_target_pairs={{0,4},{1,5},{4,8},{5,9},{6,2},{7,3},{8,12},{9,13},{10,6},{11,7},{1... | collective-permute-start | bytes 1572872 | tf_op jit(solution)/shard_map/ppermute | solution.py:177
  37.8 9.6 %collective-permute-start.10 = (bf16[2,256,512]{2,1,0:T(8,128)(2,1)S(1)}, bf16[2,256,512]{2,1,0:T(8,128)(2,1)S(1)}, u32[]{:S(2)}, u32[]{:S(2)}) collective-permute-start(bf16[2,256,512]{2,1,0:T(8,128)(2,1)S(1)} %get-tuple-element.61), channel_id=1, source_target_pairs={{0,1},{1,0},{2,3},{3,2},{4,5},{5,4},{6,7},{7,6},{8,9},{9,8},{10,11... | collective-permute-start | bytes 1572872 | tf_op jit(solution)/shard_map/ppermute | solution.py:172
  47.3 2.3 %collective-permute-start.9 = (bf16[512,512]{1,0:T(8,128)(2,1)S(1)}, bf16[512,512]{1,0:T(8,128)(2,1)S(1)}, u32[]{:S(2)}, u32[]{:S(2)}) collective-permute-start(bf16[512,512]{1,0:T(8,128)(2,1)S(1)} %broadcast_select_fusion), channel_id=1, source_target_pairs={{0,1},{1,0},{2,3},{3,2},{4,5},{5,4},{6,7},{7,6},{8,9},{9,8},{10,11... | collective-permute-start | bytes 1572872 | tf_op jit(solution)/shard_map/ppermute | solution.py:172
  47.7 8.8 %collective-permute-start.11 = (bf16[2,128,512]{2,1,0:T(8,128)(2,1)S(1)}, bf16[2,128,512]{2,1,0:T(8,128)(2,1)S(1)}, u32[]{:S(2)}, u32[]{:S(2)}) collective-permute-start(bf16[2,128,512]{2,1,0:T(8,128)(2,1)S(1)} %select_convert_fusion), channel_id=1, source_target_pairs={{0,2},{1,3},{2,0},{3,1},{4,6},{5,7},{6,4},{7,5},{8,10},{9,11},{10,... | collective-permute-start | bytes 786440 | tf_op jit(solution)/shard_map/ppermute | solution.py:172
  56.6 2.7 %collective-permute-start.17 = (bf16[1,256,512]{2,1,0:T(8,128)(2,1)S(1)}, bf16[1,256,512]{2,1,0:T(8,128)(2,1)S(1)}, u32[]{:S(2)}, u32[]{:S(2)}) collective-permute-start(bf16[1,256,512]{2,1,0:T(8,128)(2,1)S(1)} %get-tuple-element.67), channel_id=1, source_target_pairs={{0,1},{1,0},{2,3},{3,2},{4,5},{5,4},{6,7},{7,6},{8,9},{9,8},{10,11... | collective-permute-start | bytes 786440 | tf_op jit(solution)/shard_map/ppermute | solution.py:172
  56.7 6.7 %collective-permute-start.12 = (bf16[2,64,512]{2,1,0:T(8,128)(2,1)S(1)}, bf16[2,64,512]{2,1,0:T(8,128)(2,1)S(1)}, u32[]{:S(2)}, u32[]{:S(2)}) collective-permute-start(bf16[2,64,512]{2,1,0:T(8,128)(2,1)S(1)} %select_convert_fusion.2), channel_id=1, source_target_pairs={{0,4},{1,5},{2,6},{3,7},{4,0},{5,1},{6,2},{7,3},{8,12},{9,13},{10,... | collective-permute-start | bytes 393224 | tf_op jit(solution)/shard_map/ppermute | solution.py:172
  59.3 6.9 %collective-permute-start.18 = (bf16[1,128,512]{2,1,0:T(8,128)(2,1)S(1)}, bf16[1,128,512]{2,1,0:T(8,128)(2,1)S(1)}, u32[]{:S(2)}, u32[]{:S(2)}) collective-permute-start(bf16[1,128,512]{2,1,0:T(8,128)(2,1)S(1)} %select_convert_fusion.1), channel_id=1, source_target_pairs={{0,2},{1,3},{2,0},{3,1},{4,6},{5,7},{6,4},{7,5},{8,10},{9,11},{10,... | collective-permute-start | bytes 393224 | tf_op jit(solution)/shard_map/ppermute | solution.py:172
  63.4 9.1 %collective-permute-start.13 = (bf16[2,64,512]{2,1,0:T(8,128)(2,1)S(1)}, bf16[2,64,512]{2,1,0:T(8,128)(2,1)S(1)}, u32[]{:S(2)}, u32[]{:S(2)}) collective-permute-start(bf16[2,64,512]{2,1,0:T(8,128)(2,1)S(1)} %add_convert_fusion.1), channel_id=1, source_target_pairs={{0,8},{1,9},{2,10},{3,11},{4,12},{5,13},{6,14},{7,15},{8,0},{9,1},... | collective-permute-start | bytes 393224 | tf_op jit(solution)/shard_map/ppermute | solution.py:172
  66.4 6.3 %collective-permute-start.19 = (bf16[1,64,512]{2,1,0:T(8,128)(2,1)S(1)}, bf16[1,64,512]{2,1,0:T(8,128)(2,1)S(1)}, u32[]{:S(2)}, u32[]{:S(2)}) collective-permute-start(bf16[1,64,512]{2,1,0:T(8,128)(2,1)S(1)} %select_convert_fusion.3), channel_id=1, source_target_pairs={{0,4},{1,5},{2,6},{3,7},{4,0},{5,1},{6,2},{7,3},{8,12},{9,13},{10,... | collective-permute-start | bytes 196616 | tf_op jit(solution)/shard_map/ppermute | solution.py:172
  72.6 17.3 %copy-start.5 = (f32[512,512]{1,0:T(8,128)S(1)}, f32[512,512]{1,0:T(8,128)}, u32[]{:S(2)}) copy-start(f32[512,512]{1,0:T(8,128)} %first_diag_ref.1) | copy-start | bytes 3145732
  72.6 17.3 %copy-start.6 = (f32[512,512]{1,0:T(8,128)S(1)}, f32[512,512]{1,0:T(8,128)}, u32[]{:S(2)}) copy-start(f32[512,512]{1,0:T(8,128)} %second_diag_ref.1) | copy-start | bytes 3145732
  72.6 5.9 %collective-permute-start.14 = (bf16[2,64,512]{2,1,0:T(8,128)(2,1)S(1)}, bf16[2,64,512]{2,1,0:T(8,128)(2,1)S(1)}, u32[]{:S(2)}, u32[]{:S(2)}) collective-permute-start(bf16[2,64,512]{2,1,0:T(8,128)(2,1)S(1)} %add_convert_fusion), channel_id=1, source_target_pairs={{0,4},{1,5},{2,6},{3,7},{4,0},{5,1},{6,2},{7,3},{8,12},{9,13},{10,... | collective-permute-start | bytes 393224 | tf_op jit(solution)/shard_map/ppermute | solution.py:172
  72.7 5.8 %collective-permute-start.20 = (bf16[1,64,512]{2,1,0:T(8,128)(2,1)S(1)}, bf16[1,64,512]{2,1,0:T(8,128)(2,1)S(1)}, u32[]{:S(2)}, u32[]{:S(2)}) collective-permute-start(bf16[1,64,512]{2,1,0:T(8,128)(2,1)S(1)} %add_convert_fusion.3), channel_id=1, source_target_pairs={{0,8},{1,9},{2,10},{3,11},{4,12},{5,13},{6,14},{7,15},{8,0},{9,1},... | collective-permute-start | bytes 196616 | tf_op jit(solution)/shard_map/ppermute | solution.py:172
  78.6 4.3 %collective-permute-start.21 = (bf16[1,64,512]{2,1,0:T(8,128)(2,1)S(1)}, bf16[1,64,512]{2,1,0:T(8,128)(2,1)S(1)}, u32[]{:S(2)}, u32[]{:S(2)}) collective-permute-start(bf16[1,64,512]{2,1,0:T(8,128)(2,1)S(1)} %add_convert_fusion.2), channel_id=1, source_target_pairs={{0,4},{1,5},{2,6},{3,7},{4,0},{5,1},{6,2},{7,3},{8,12},{9,13},{10,... | collective-permute-start | bytes 196616 | tf_op jit(solution)/shard_map/ppermute | solution.py:172
  80.0 7.7 %collective-permute-start.15 = (bf16[2,128,512]{2,1,0:T(8,128)(2,1)S(1)}, bf16[2,128,512]{2,1,0:T(8,128)(2,1)S(1)}, u32[]{:S(2)}, u32[]{:S(2)}) collective-permute-start(bf16[2,128,512]{2,1,0:T(8,128)(2,1)S(1)} %pad_maximum_fusion.2), channel_id=1, source_target_pairs={{0,2},{1,3},{2,0},{3,1},{4,6},{5,7},{6,4},{7,5},{8,10},{9,11},{10,... | collective-permute-start | bytes 786440 | tf_op jit(solution)/shard_map/ppermute | solution.py:172
  82.9 6.2 %collective-permute-start.22 = (bf16[1,128,512]{2,1,0:T(8,128)(2,1)S(1)}, bf16[1,128,512]{2,1,0:T(8,128)(2,1)S(1)}, u32[]{:S(2)}, u32[]{:S(2)}) collective-permute-start(bf16[1,128,512]{2,1,0:T(8,128)(2,1)S(1)} %pad_maximum_fusion.4), channel_id=1, source_target_pairs={{0,2},{1,3},{2,0},{3,1},{4,6},{5,7},{6,4},{7,5},{8,10},{9,11},{10,... | collective-permute-start | bytes 393224 | tf_op jit(solution)/shard_map/ppermute | solution.py:172
  87.9 2.0 %collective-permute-start.16 = (bf16[2,256,512]{2,1,0:T(8,128)(2,1)S(1)}, bf16[2,256,512]{2,1,0:T(8,128)(2,1)S(1)}, u32[]{:S(2)}, u32[]{:S(2)}) collective-permute-start(bf16[2,256,512]{2,1,0:T(8,128)(2,1)S(1)} %pad_maximum_fusion.1.mine_ref), channel_id=1, source_target_pairs={{0,1},{1,0},{2,3},{3,2},{4,5},{5,4},{6,7},{7,6},{8,9},{9,8},{10,11... | collective-permute-start | bytes 1572872 | tf_op jit(solution)/shard_map/ppermute | solution.py:172
  89.3 2.9 %collective-permute-start.23 = (bf16[1,256,512]{2,1,0:T(8,128)(2,1)S(1)}, bf16[1,256,512]{2,1,0:T(8,128)(2,1)S(1)}, u32[]{:S(2)}, u32[]{:S(2)}) collective-permute-start(bf16[1,256,512]{2,1,0:T(8,128)(2,1)S(1)} %pad_maximum_fusion.3.mine_ref), channel_id=1, source_target_pairs={{0,1},{1,0},{2,3},{3,2},{4,5},{5,4},{6,7},{7,6},{8,9},{9,8},{10,11... | collective-permute-start | bytes 786440 | tf_op jit(solution)/shard_map/ppermute | solution.py:172

commit v11 on v10

--- a/solution.py
+++ b/solution.py
@@ -172,9 +172,12 @@
     return lax.ppermute(value, "row", [(i, i ^ bit) for i in range(devices)])
 
 
-def far_of(across, devices):
+def far_of(across, devices, closed=False):
     hops = [(i, i + 4 if i % 4 < 2 else i - 4) for i in range(devices)]
-    return lax.ppermute(across, "row", [(a, b) for a, b in hops if 0 <= b < devices])
+    pairs = [(a, b if 0 <= b < devices else a ^ 2) for a, b in hops]
+    if not closed:
+        pairs = [(a, b) for a, b in hops if 0 <= b < devices]
+    return lax.ppermute(across, "row", pairs)
 
 
 def rest_of(across, far, give_across, devices):
@@ -250,10 +253,9 @@
         4 * one,
         [pltpu.VMEM((2, size, width), jnp.bfloat16), pltpu.SemaphoreType.DMA((6,))],
     )
-    across[1], turned = barrier((across[1], turned))
     far = [far_of(part, devices) for part in across]
-    second_far = far_of(second_across, devices)
-    far, second_across = barrier((far, second_across))
+    second_far = far_of(second_across, devices, closed=True)
+    far, second_across, turned = barrier((far, second_across, turned))
     rest = rest_of(across, far, give_across, devices)
     column_first, column_again, give, keep = call(
         first_kernel,

time: 93.7 us -> 91.7 us (0.979)
  waiting for transfers between devices: 43.8 us -> 41.6 us
    ppermute x21, starting transfers between devices: 18.8 us -> 21.2 us  [swapped(): return lax.ppermute(value, 'row', [(i, i ^ bit) for i in range(devices)])]
    ppermute x3, starting transfers between devices: 11.8 us -> 9.69 us  [far_of(): return lax.ppermute(across, 'row', pairs)]
    ppermute x3, waiting for transfers between devices: 11.4 us -> 9.99 us  [far_of(): return lax.ppermute(across, 'row', pairs)]
  transfers between devices with their start and end apart: 24 -> 24, of which waited for: 12 -> 14; matrix products, arithmetic and copies ran while one was open for 1% -> 1% of each run, Pallas kernels for 10% -> 10%
where the time goes in v11:
time: 91.7 us; the launch traced here: 91.3 us
  waiting for transfers between devices  41.6 us (45%)
  starting transfers between devices  30.9 us (34%)
  Pallas kernels  10.6 us (12%)
  local copies, waits for them, and re-layouts  5.53 us (6%)
  between operations  1.61 us (2%)
  other arithmetic  1.1 us (1%)
    ppermute x21, waiting for transfers between devices, swapped(): return lax.ppermute(value, 'row', [(i, i ^ bit) for i in range(devices)])  31.6 us
    ppermute x21, starting transfers between devices, swapped(): return lax.ppermute(value, 'row', [(i, i ^ bit) for i in range(devices)])  21.2 us
    pallas_call x7, Pallas kernels, call(): pl.pallas_call(body, out_shape=outs, in_specs=[pl.BlockSpec(memory_space=...  10.6 us
    ppermute x3, waiting for transfers between devices, far_of(): return lax.ppermute(across, 'row', pairs)  9.99 us
    ppermute x3, starting transfers between devices, far_of(): return lax.ppermute(across, 'row', pairs)  9.69 us
    unnamed x14, local copies, waits for them, and re-layouts  5.53 us
  transfers between devices with their start and end apart: 24, of which 14 were waited for; matrix products, arithmetic and copies ran while one was open for 1% of the time, Pallas kernels for 10%

profile of v11, /device:TPU:0, one launch (start us, length us, event | category | flops | bytes accessed | tf_op | source)
XLA Modules:
  0.0 91.3 jit_solution(558489988174034459)
XLA Ops:
  1.2 1.0 %copy-done.3 = bf16[1,1,512,512]{3,2,1,0:T(8,128)(2,1)S(1)} copy-done((bf16[1,1,512,512]{3,2,1,0:T(8,128)(2,1)S(1)}, bf16[1,1,512,512]{3,2,1,0:T(8,128)(2,1)}, u32[]{:S(2)}) %copy-start.3) | copy-done | bytes 524312
  2.3 3.0 %collective-permute-start.2 = (bf16[256,512]{1,0:T(8,128)(2,1)S(1)}, bf16[256,512]{1,0:T(8,128)(2,1)S(1)}, u32[]{:S(2)}, u32[]{:S(2)}) collective-permute-start(bf16[256,512]{1,0:T(8,128)(2,1)S(1)} %get-tuple-element.38.first_0), channel_id=1, source_target_pairs={{0,2},{1,3},{2,0},{3,1},{4,6},{5,7},{6,4},{7,5},{8,10},{9,11},{10,... | collective-permute-start | bytes 786440 | tf_op jit(solution)/shard_map/ppermute | solution.py:172
  5.4 1.9 %collective-permute-start.6 = (bf16[512,512]{1,0:T(8,128)(2,1)}, bf16[512,512]{1,0:T(8,128)(2,1)S(1)}, u32[]{:S(2)}, u32[]{:S(2)}) collective-permute-start(bf16[512,512]{1,0:T(8,128)(2,1)} %bitcast.11), channel_id=1, source_target_pairs={{0,2},{1,3},{2,0},{3,1},{4,6},{5,7},{6,4},{7,5},{8,10},{9,11},{10,... | collective-permute-start | bytes 1572872 | tf_op jit(solution)/shard_map/ppermute | solution.py:172
  7.4 5.1 %collective-permute-done.2.across_0 = bf16[256,512]{1,0:T(8,128)(2,1)S(1)} collective-permute-done((bf16[256,512]{1,0:T(8,128)(2,1)S(1)}, bf16[256,512]{1,0:T(8,128)(2,1)S(1)}, u32[]{:S(2)}, u32[]{:S(2)}) %collective-permute-start.2) | collective-permute-done | bytes 262176 | tf_op jit(solution)/shard_map/ppermute | solution.py:172
  12.4 4.1 %collective-permute-start.4 = (bf16[256,512]{1,0:T(8,128)(2,1)S(1)}, bf16[256,512]{1,0:T(8,128)(2,1)S(1)}, u32[]{:S(2)}, u32[]{:S(2)}) collective-permute-start(bf16[256,512]{1,0:T(8,128)(2,1)S(1)} %collective-permute-done.2.across_0), channel_id=1, source_target_pairs={{0,4},{1,5},{4,8},{5,9},{6,2},{7,3},{8,12},{9,13},{10,6},{11,7},{1... | collective-permute-start | bytes 786440 | tf_op jit(solution)/shard_map/ppermute | solution.py:180
  16.5 1.6 %collective-permute-done.3.across_1 = bf16[256,512]{1,0:T(8,128)(2,1)S(1)} collective-permute-done((bf16[256,512]{1,0:T(8,128)(2,1)S(1)}, bf16[256,512]{1,0:T(8,128)(2,1)S(1)}, u32[]{:S(2)}, u32[]{:S(2)}) %collective-permute-start.3) | collective-permute-done | bytes 262176 | tf_op jit(solution)/shard_map/ppermute | solution.py:172
  18.1 4.1 %collective-permute-start.5 = (bf16[256,512]{1,0:T(8,128)(2,1)S(1)}, bf16[256,512]{1,0:T(8,128)(2,1)S(1)}, u32[]{:S(2)}, u32[]{:S(2)}) collective-permute-start(bf16[256,512]{1,0:T(8,128)(2,1)S(1)} %collective-permute-done.3.across_1), channel_id=1, source_target_pairs={{0,4},{1,5},{4,8},{5,9},{6,2},{7,3},{8,12},{9,13},{10,6},{11,7},{1... | collective-permute-start | bytes 786440 | tf_op jit(solution)/shard_map/ppermute | solution.py:180
  22.8 1.7 %copy-done = bf16[1,1,5,512,512]{4,3,2,1,0:T(8,128)(2,1)S(1)} copy-done((bf16[1,1,5,512,512]{4,3,2,1,0:T(8,128)(2,1)S(1)}, bf16[1,1,5,512,512]{4,3,2,1,0:T(8,128)(2,1)}, u32[]{:S(2)}) %copy-start) | copy-done | bytes 2621464
  24.5 1.0 %copy-done.1 = bf16[512,512]{1,0:T(8,128)(2,1)S(1)} copy-done((bf16[512,512]{1,0:T(8,128)(2,1)S(1)}, bf16[512,512]{1,0:T(8,128)(2,1)}, u32[]{:S(2)}) %copy-start.1) | copy-done | bytes 524312
  25.6 1.0 %copy-done.2 = bf16[1,1,512,512]{3,2,1,0:T(8,128)(2,1)S(1)} copy-done((bf16[1,1,512,512]{3,2,1,0:T(8,128)(2,1)S(1)}, bf16[1,1,512,512]{3,2,1,0:T(8,128)(2,1)}, u32[]{:S(2)}) %copy-start.2) | copy-done | bytes 524312
  26.6 0.7 copy-done.4
  27.3 2.6 %shard_map.120 = (f32[512,512]{1,0:T(8,128)S(1)}, f32[512,512]{1,0:T(8,128)S(1)}, bf16[1024,512]{1,0:T(8,128)(2,1)S(1)}, bf16[3,512,512]{2,1,0:T(8,128)(2,1)S(1)}, bf16[512,512]{1,0:T(8,128)(2,1)S(1)}) custom-call(s32[1]{0:T(128)} %bitcast.where_ref, s32[5]{0:T(128)S(1)} %bitcast.15, s32[1]{0:T(128)} %bitcast.8.count_ref, bf16[5,512,512]{2,1,0:T(8,128)(2,1)S(1)} %bitcast.9, ...), custom_call_target="tpu_custom_call" | custom-call | flops 1073741824 | bytes 10485788 | tf_op jit(solution)/shard_map/pallas_call | solution.py:16
  30.1 1.6 %collective-permute-start.8 = (bf16[512,512]{1,0:T(8,128)(2,1)S(1)}, bf16[512,512]{1,0:T(8,128)(2,1)S(1)}, u32[]{:S(2)}, u32[]{:S(2)}) collective-permute-start(bf16[512,512]{1,0:T(8,128)(2,1)S(1)} %collective-permute-done.6.across), channel_id=1, source_target_pairs={{0,4},{1,5},{2,0},{3,1},{4,8},{5,9},{6,2},{7,3},{8,12},{9,13},{10,... | collective-permute-start | bytes 1572872 | tf_op jit(solution)/shard_map/ppermute | solution.py:180
  32.0 2.3 %shard_map.121 = (bf16[512,512]{1,0:T(8,128)(2,1)}, bf16[512,512]{1,0:T(8,128)(2,1)S(1)}, bf16[2,256,512]{2,1,0:T(8,128)(2,1)S(1)}, f32[2,256,512]{2,1,0:T(8,128)S(1)}) custom-call(s32[1]{0:T(128)} %bitcast.where_ref, f32[512,512]{1,0:T(8,128)S(1)} %get-tuple-element.41.acc_in, bf16[256,512]{1,0:T(8,128)(2,1)S(1)} %collective-permute-done.2.across_0, ...), custom_call_target="tpu_custom_call" | custom-call | flops 1342177280 | bytes 7864324 | tf_op jit(solution)/shard_map/pallas_call | solution.py:16
  34.5 10.0 %collective-permute-done.8.far = bf16[512,512]{1,0:T(8,128)(2,1)S(1)} collective-permute-done((bf16[512,512]{1,0:T(8,128)(2,1)S(1)}, bf16[512,512]{1,0:T(8,128)(2,1)S(1)}, u32[]{:S(2)}, u32[]{:S(2)}) %collective-permute-start.8) | collective-permute-done | bytes 524320 | tf_op jit(solution)/shard_map/ppermute | solution.py:180
  45.4 0.7 shard_map.122.acc_in
  46.5 1.6 %shard_map.123 = (bf16[512,512]{1,0:T(8,128)(2,1)}, bf16[1,256,512]{2,1,0:T(8,128)(2,1)S(1)}, f32[1,256,512]{2,1,0:T(8,128)S(1)}) custom-call(s32[1]{0:T(128)} %bitcast.where_ref, f32[512,512]{1,0:T(8,128)S(1)} %shard_map.122.acc_in, bf16[512,512]{1,0:T(8,128)(2,1)S(1)} %collective-permute-done.8.far, bf16[512,512]{1,0:T(8,128)(2,1)S(1)} %collective-permute-done.9.rest, ...), custom_call_target="tpu_custom_call" | custom-call | flops 805306368 | bytes 6029316 | tf_op jit(solution)/shard_map/pallas_call | solution.py:16
  48.0 5.6 %collective-permute-done.11 = bf16[2,128,512]{2,1,0:T(8,128)(2,1)S(1)} collective-permute-done((bf16[2,128,512]{2,1,0:T(8,128)(2,1)S(1)}, bf16[2,128,512]{2,1,0:T(8,128)(2,1)S(1)}, u32[]{:S(2)}, u32[]{:S(2)}) %collective-permute-start.11) | collective-permute-done | bytes 262176 | tf_op jit(solution)/shard_map/ppermute | solution.py:172
  53.8 1.6 %collective-permute-start.12 = (bf16[2,64,512]{2,1,0:T(8,128)(2,1)S(1)}, bf16[2,64,512]{2,1,0:T(8,128)(2,1)S(1)}, u32[]{:S(2)}, u32[]{:S(2)}) collective-permute-start(bf16[2,64,512]{2,1,0:T(8,128)(2,1)S(1)} %select_convert_fusion.2), channel_id=1, source_target_pairs={{0,4},{1,5},{2,6},{3,7},{4,0},{5,1},{6,2},{7,3},{8,12},{9,13},{10,... | collective-permute-start | bytes 393224 | tf_op jit(solution)/shard_map/ppermute | solution.py:172
  56.2 3.6 %collective-permute-done.12 = bf16[2,64,512]{2,1,0:T(8,128)(2,1)S(1)} collective-permute-done((bf16[2,64,512]{2,1,0:T(8,128)(2,1)S(1)}, bf16[2,64,512]{2,1,0:T(8,128)(2,1)S(1)}, u32[]{:S(2)}, u32[]{:S(2)}) %collective-permute-start.12) | collective-permute-done | bytes 131104 | tf_op jit(solution)/shard_map/ppermute | solution.py:172
  59.9 2.5 %collective-permute-start.13 = (bf16[2,64,512]{2,1,0:T(8,128)(2,1)S(1)}, bf16[2,64,512]{2,1,0:T(8,128)(2,1)S(1)}, u32[]{:S(2)}, u32[]{:S(2)}) collective-permute-start(bf16[2,64,512]{2,1,0:T(8,128)(2,1)S(1)} %add_convert_fusion.1), channel_id=1, source_target_pairs={{0,8},{1,9},{2,10},{3,11},{4,12},{5,13},{6,14},{7,15},{8,0},{9,1},... | collective-permute-start | bytes 393224 | tf_op jit(solution)/shard_map/ppermute | solution.py:172
  62.5 0.8 collective-permute-start.19
  63.3 5.5 %collective-permute-done.13 = bf16[2,64,512]{2,1,0:T(8,128)(2,1)S(1)} collective-permute-done((bf16[2,64,512]{2,1,0:T(8,128)(2,1)S(1)}, bf16[2,64,512]{2,1,0:T(8,128)(2,1)S(1)}, u32[]{:S(2)}, u32[]{:S(2)}) %collective-permute-start.13) | collective-permute-done | bytes 131104 | tf_op jit(solution)/shard_map/ppermute | solution.py:172
  68.9 3.3 %collective-permute-start.20 = (bf16[1,64,512]{2,1,0:T(8,128)(2,1)S(1)}, bf16[1,64,512]{2,1,0:T(8,128)(2,1)S(1)}, u32[]{:S(2)}, u32[]{:S(2)}) collective-permute-start(bf16[1,64,512]{2,1,0:T(8,128)(2,1)S(1)} %add_convert_fusion.3), channel_id=1, source_target_pairs={{0,8},{1,9},{2,10},{3,11},{4,12},{5,13},{6,14},{7,15},{8,0},{9,1},... | collective-permute-start | bytes 196616 | tf_op jit(solution)/shard_map/ppermute | solution.py:172
  72.2 2.3 %collective-permute-done.14 = bf16[2,64,512]{2,1,0:T(8,128)(2,1)S(1)} collective-permute-done((bf16[2,64,512]{2,1,0:T(8,128)(2,1)S(1)}, bf16[2,64,512]{2,1,0:T(8,128)(2,1)S(1)}, u32[]{:S(2)}, u32[]{:S(2)}) %collective-permute-start.14) | collective-permute-done | bytes 131104 | tf_op jit(solution)/shard_map/ppermute | solution.py:172
  74.9 1.7 %collective-permute-start.21 = (bf16[1,64,512]{2,1,0:T(8,128)(2,1)S(1)}, bf16[1,64,512]{2,1,0:T(8,128)(2,1)S(1)}, u32[]{:S(2)}, u32[]{:S(2)}) collective-permute-start(bf16[1,64,512]{2,1,0:T(8,128)(2,1)S(1)} %add_convert_fusion.2), channel_id=1, source_target_pairs={{0,4},{1,5},{2,6},{3,7},{4,0},{5,1},{6,2},{7,3},{8,12},{9,13},{10,... | collective-permute-start | bytes 196616 | tf_op jit(solution)/shard_map/ppermute | solution.py:172
  76.6 2.2 %collective-permute-start.15 = (bf16[2,128,512]{2,1,0:T(8,128)(2,1)S(1)}, bf16[2,128,512]{2,1,0:T(8,128)(2,1)S(1)}, u32[]{:S(2)}, u32[]{:S(2)}) collective-permute-start(bf16[2,128,512]{2,1,0:T(8,128)(2,1)S(1)} %pad_maximum_fusion.2), channel_id=1, source_target_pairs={{0,2},{1,3},{2,0},{3,1},{4,6},{5,7},{6,4},{7,5},{8,10},{9,11},{10,... | collective-permute-start | bytes 786440 | tf_op jit(solution)/shard_map/ppermute | solution.py:172
  79.2 1.7 %collective-permute-start.22 = (bf16[1,128,512]{2,1,0:T(8,128)(2,1)S(1)}, bf16[1,128,512]{2,1,0:T(8,128)(2,1)S(1)}, u32[]{:S(2)}, u32[]{:S(2)}) collective-permute-start(bf16[1,128,512]{2,1,0:T(8,128)(2,1)S(1)} %pad_maximum_fusion.4), channel_id=1, source_target_pairs={{0,2},{1,3},{2,0},{3,1},{4,6},{5,7},{6,4},{7,5},{8,10},{9,11},{10,... | collective-permute-start | bytes 393224 | tf_op jit(solution)/shard_map/ppermute | solution.py:172
  81.0 4.8 %collective-permute-done.15 = bf16[2,128,512]{2,1,0:T(8,128)(2,1)S(1)} collective-permute-done((bf16[2,128,512]{2,1,0:T(8,128)(2,1)S(1)}, bf16[2,128,512]{2,1,0:T(8,128)(2,1)S(1)}, u32[]{:S(2)}, u32[]{:S(2)}) %collective-permute-start.15) | collective-permute-done | bytes 262176 | tf_op jit(solution)/shard_map/ppermute | solution.py:172
  86.0 1.2 %collective-permute-done.22 = bf16[1,128,512]{2,1,0:T(8,128)(2,1)S(1)} collective-permute-done((bf16[1,128,512]{2,1,0:T(8,128)(2,1)S(1)}, bf16[1,128,512]{2,1,0:T(8,128)(2,1)S(1)}, u32[]{:S(2)}, u32[]{:S(2)}) %collective-permute-start.22) | collective-permute-done | bytes 131104 | tf_op jit(solution)/shard_map/ppermute | solution.py:172
  87.9 2.2 %shard_map.124 = (f32[512,512]{1,0:T(8,128)}, f32[512,512]{1,0:T(8,128)}, f32[512,512]{1,0:T(8,128)S(1)}) custom-call(s32[1]{0:T(128)} %bitcast.where_ref, bf16[2,256,512]{2,1,0:T(8,128)(2,1)S(1)} %pad_maximum_fusion.1.mine_ref, bf16[2,256,512]{2,1,0:T(8,128)(2,1)S(1)} %collective-permute-done.16.other_ref, ...), custom_call_target="tpu_custom_call" | custom-call | flops 1073741824 | bytes 6815748 | tf_op jit(solution)/shard_map/pallas_call | solution.py:16
  90.2 1.2 %shard_map.125 = f32[512,512]{1,0:T(8,128)} custom-call(s32[1]{0:T(128)} %bitcast.where_ref, bf16[1,256,512]{2,1,0:T(8,128)(2,1)S(1)} %pad_maximum_fusion.3.mine_ref, bf16[1,256,512]{2,1,0:T(8,128)(2,1)S(1)} %collective-permute-done.23.other_ref, f32[512,512]{1,0:T(8,128)S(1)} %get-tuple-element.66.base_ref), custom_call_target="tpu_custom_call" | custom-call | flops 262144 | bytes 2621444 | tf_op jit(solution)/shard_map/pallas_call | solution.py:16
  (60 shorter events, 5.7 us)
Async XLA Ops:
  0.6 22.1 %collective-permute-start.1 = (bf16[512,512]{1,0:T(8,128)(2,1)}, bf16[512,512]{1,0:T(8,128)(2,1)S(1)}, u32[]{:S(2)}, u32[]{:S(2)}) collective-permute-start(bf16[512,512]{1,0:T(8,128)(2,1)} %bitcast.10), channel_id=1, source_target_pairs={{0,1},{1,0},{2,3},{3,2},{4,5},{5,4},{6,7},{7,6},{8,9},{9,8},{10,11... | collective-permute-start | bytes 1572872 | tf_op jit(solution)/shard_map/ppermute | solution.py:172
  1.2 21.6 %collective-permute-start = (bf16[512,512]{1,0:T(8,128)(2,1)}, bf16[512,512]{1,0:T(8,128)(2,1)S(1)}, u32[]{:S(2)}, u32[]{:S(2)}) collective-permute-start(bf16[512,512]{1,0:T(8,128)(2,1)} %bitcast.13), channel_id=1, source_target_pairs={{0,1},{1,0},{2,3},{3,2},{4,5},{5,4},{6,7},{7,6},{8,9},{9,8},{10,11... | collective-permute-start | bytes 1572872 | tf_op jit(solution)/shard_map/ppermute | solution.py:172
  1.2 1.0 %copy-start.3 = (bf16[1,1,512,512]{3,2,1,0:T(8,128)(2,1)S(1)}, bf16[1,1,512,512]{3,2,1,0:T(8,128)(2,1)}, u32[]{:S(2)}) copy-start(bf16[1,1,512,512]{3,2,1,0:T(8,128)(2,1)} %param.9) | copy-start | bytes 1572868
  2.3 10.1 %collective-permute-start.2 = (bf16[256,512]{1,0:T(8,128)(2,1)S(1)}, bf16[256,512]{1,0:T(8,128)(2,1)S(1)}, u32[]{:S(2)}, u32[]{:S(2)}) collective-permute-start(bf16[256,512]{1,0:T(8,128)(2,1)S(1)} %get-tuple-element.38.first_0), channel_id=1, source_target_pairs={{0,2},{1,3},{2,0},{3,1},{4,6},{5,7},{6,4},{7,5},{8,10},{9,11},{10,... | collective-permute-start | bytes 786440 | tf_op jit(solution)/shard_map/ppermute | solution.py:172
  5.3 12.7 %collective-permute-start.3 = (bf16[256,512]{1,0:T(8,128)(2,1)S(1)}, bf16[256,512]{1,0:T(8,128)(2,1)S(1)}, u32[]{:S(2)}, u32[]{:S(2)}) collective-permute-start(bf16[256,512]{1,0:T(8,128)(2,1)S(1)} %get-tuple-element.39.first_1), channel_id=1, source_target_pairs={{0,2},{1,3},{2,0},{3,1},{4,6},{5,7},{6,4},{7,5},{8,10},{9,11},{10,... | collective-permute-start | bytes 786440 | tf_op jit(solution)/shard_map/ppermute | solution.py:172
  5.4 24.5 %collective-permute-start.6 = (bf16[512,512]{1,0:T(8,128)(2,1)}, bf16[512,512]{1,0:T(8,128)(2,1)S(1)}, u32[]{:S(2)}, u32[]{:S(2)}) collective-permute-start(bf16[512,512]{1,0:T(8,128)(2,1)} %bitcast.11), channel_id=1, source_target_pairs={{0,2},{1,3},{2,0},{3,1},{4,6},{5,7},{6,4},{7,5},{8,10},{9,11},{10,... | collective-permute-start | bytes 1572872 | tf_op jit(solution)/shard_map/ppermute | solution.py:172
  12.4 17.5 %collective-permute-start.4 = (bf16[256,512]{1,0:T(8,128)(2,1)S(1)}, bf16[256,512]{1,0:T(8,128)(2,1)S(1)}, u32[]{:S(2)}, u32[]{:S(2)}) collective-permute-start(bf16[256,512]{1,0:T(8,128)(2,1)S(1)} %collective-permute-done.2.across_0), channel_id=1, source_target_pairs={{0,4},{1,5},{4,8},{5,9},{6,2},{7,3},{8,12},{9,13},{10,6},{11,7},{1... | collective-permute-start | bytes 786440 | tf_op jit(solution)/shard_map/ppermute | solution.py:180
  18.1 11.9 %collective-permute-start.5 = (bf16[256,512]{1,0:T(8,128)(2,1)S(1)}, bf16[256,512]{1,0:T(8,128)(2,1)S(1)}, u32[]{:S(2)}, u32[]{:S(2)}) collective-permute-start(bf16[256,512]{1,0:T(8,128)(2,1)S(1)} %collective-permute-done.3.across_1), channel_id=1, source_target_pairs={{0,4},{1,5},{4,8},{5,9},{6,2},{7,3},{8,12},{9,13},{10,6},{11,7},{1... | collective-permute-start | bytes 786440 | tf_op jit(solution)/shard_map/ppermute | solution.py:180
  22.8 1.7 %copy-start = (bf16[1,1,5,512,512]{4,3,2,1,0:T(8,128)(2,1)S(1)}, bf16[1,1,5,512,512]{4,3,2,1,0:T(8,128)(2,1)}, u32[]{:S(2)}) copy-start(bf16[1,1,5,512,512]{4,3,2,1,0:T(8,128)(2,1)} %param.8) | copy-start | bytes 7864324
  24.5 1.0 %copy-start.1 = (bf16[512,512]{1,0:T(8,128)(2,1)S(1)}, bf16[512,512]{1,0:T(8,128)(2,1)}, u32[]{:S(2)}) copy-start(bf16[512,512]{1,0:T(8,128)(2,1)} %lower_hbm.1) | copy-start | bytes 1572868
  25.6 1.0 %copy-start.2 = (bf16[1,1,512,512]{3,2,1,0:T(8,128)(2,1)S(1)}, bf16[1,1,512,512]{3,2,1,0:T(8,128)(2,1)}, u32[]{:S(2)}) copy-start(bf16[1,1,512,512]{3,2,1,0:T(8,128)(2,1)} %param.10) | copy-start | bytes 1572868
  26.6 0.7 copy-start.4
  30.0 2.0 %collective-permute-start.7 = (bf16[512,512]{1,0:T(8,128)(2,1)S(1)}, bf16[512,512]{1,0:T(8,128)(2,1)S(1)}, u32[]{:S(2)}, u32[]{:S(2)}) collective-permute-start(bf16[512,512]{1,0:T(8,128)(2,1)S(1)} %pad_maximum_fusion), channel_id=1, source_target_pairs={{0,1},{1,0},{2,3},{3,2},{4,5},{5,4},{6,7},{7,6},{8,9},{9,8},{10,11... | collective-permute-start | bytes 1572872 | tf_op jit(solution)/shard_map/ppermute | solution.py:172
  30.1 14.3 %collective-permute-start.8 = (bf16[512,512]{1,0:T(8,128)(2,1)S(1)}, bf16[512,512]{1,0:T(8,128)(2,1)S(1)}, u32[]{:S(2)}, u32[]{:S(2)}) collective-permute-start(bf16[512,512]{1,0:T(8,128)(2,1)S(1)} %collective-permute-done.6.across), channel_id=1, source_target_pairs={{0,4},{1,5},{2,0},{3,1},{4,8},{5,9},{6,2},{7,3},{8,12},{9,13},{10,... | collective-permute-start | bytes 1572872 | tf_op jit(solution)/shard_map/ppermute | solution.py:180
  34.3 10.3 %collective-permute-start.10 = (bf16[2,256,512]{2,1,0:T(8,128)(2,1)S(1)}, bf16[2,256,512]{2,1,0:T(8,128)(2,1)S(1)}, u32[]{:S(2)}, u32[]{:S(2)}) collective-permute-start(bf16[2,256,512]{2,1,0:T(8,128)(2,1)S(1)} %get-tuple-element.59), channel_id=1, source_target_pairs={{0,1},{1,0},{2,3},{3,2},{4,5},{5,4},{6,7},{7,6},{8,9},{9,8},{10,11... | collective-permute-start | bytes 1572872 | tf_op jit(solution)/shard_map/ppermute | solution.py:172
  44.5 2.0 %collective-permute-start.9 = (bf16[512,512]{1,0:T(8,128)(2,1)S(1)}, bf16[512,512]{1,0:T(8,128)(2,1)S(1)}, u32[]{:S(2)}, u32[]{:S(2)}) collective-permute-start(bf16[512,512]{1,0:T(8,128)(2,1)S(1)} %broadcast_select_fusion), channel_id=1, source_target_pairs={{0,1},{1,0},{2,3},{3,2},{4,5},{5,4},{6,7},{7,6},{8,9},{9,8},{10,11... | collective-permute-start | bytes 1572872 | tf_op jit(solution)/shard_map/ppermute | solution.py:172
  44.8 8.8 %collective-permute-start.11 = (bf16[2,128,512]{2,1,0:T(8,128)(2,1)S(1)}, bf16[2,128,512]{2,1,0:T(8,128)(2,1)S(1)}, u32[]{:S(2)}, u32[]{:S(2)}) collective-permute-start(bf16[2,128,512]{2,1,0:T(8,128)(2,1)S(1)} %select_convert_fusion), channel_id=1, source_target_pairs={{0,2},{1,3},{2,0},{3,1},{4,6},{5,7},{6,4},{7,5},{8,10},{9,11},{10,... | collective-permute-start | bytes 786440 | tf_op jit(solution)/shard_map/ppermute | solution.py:172
  53.7 1.7 %collective-permute-start.17 = (bf16[1,256,512]{2,1,0:T(8,128)(2,1)S(1)}, bf16[1,256,512]{2,1,0:T(8,128)(2,1)S(1)}, u32[]{:S(2)}, u32[]{:S(2)}) collective-permute-start(bf16[1,256,512]{2,1,0:T(8,128)(2,1)S(1)} %get-tuple-element.65), channel_id=1, source_target_pairs={{0,1},{1,0},{2,3},{3,2},{4,5},{5,4},{6,7},{7,6},{8,9},{9,8},{10,11... | collective-permute-start | bytes 786440 | tf_op jit(solution)/shard_map/ppermute | solution.py:172
  53.8 6.0 %collective-permute-start.12 = (bf16[2,64,512]{2,1,0:T(8,128)(2,1)S(1)}, bf16[2,64,512]{2,1,0:T(8,128)(2,1)S(1)}, u32[]{:S(2)}, u32[]{:S(2)}) collective-permute-start(bf16[2,64,512]{2,1,0:T(8,128)(2,1)S(1)} %select_convert_fusion.2), channel_id=1, source_target_pairs={{0,4},{1,5},{2,6},{3,7},{4,0},{5,1},{6,2},{7,3},{8,12},{9,13},{10,... | collective-permute-start | bytes 393224 | tf_op jit(solution)/shard_map/ppermute | solution.py:172
  55.6 6.8 %collective-permute-start.18 = (bf16[1,128,512]{2,1,0:T(8,128)(2,1)S(1)}, bf16[1,128,512]{2,1,0:T(8,128)(2,1)S(1)}, u32[]{:S(2)}, u32[]{:S(2)}) collective-permute-start(bf16[1,128,512]{2,1,0:T(8,128)(2,1)S(1)} %select_convert_fusion.1), channel_id=1, source_target_pairs={{0,2},{1,3},{2,0},{3,1},{4,6},{5,7},{6,4},{7,5},{8,10},{9,11},{10,... | collective-permute-start | bytes 393224 | tf_op jit(solution)/shard_map/ppermute | solution.py:172
  59.9 8.9 %collective-permute-start.13 = (bf16[2,64,512]{2,1,0:T(8,128)(2,1)S(1)}, bf16[2,64,512]{2,1,0:T(8,128)(2,1)S(1)}, u32[]{:S(2)}, u32[]{:S(2)}) collective-permute-start(bf16[2,64,512]{2,1,0:T(8,128)(2,1)S(1)} %add_convert_fusion.1), channel_id=1, source_target_pairs={{0,8},{1,9},{2,10},{3,11},{4,12},{5,13},{6,14},{7,15},{8,0},{9,1},... | collective-permute-start | bytes 393224 | tf_op jit(solution)/shard_map/ppermute | solution.py:172
  62.5 6.4 %collective-permute-start.19 = (bf16[1,64,512]{2,1,0:T(8,128)(2,1)S(1)}, bf16[1,64,512]{2,1,0:T(8,128)(2,1)S(1)}, u32[]{:S(2)}, u32[]{:S(2)}) collective-permute-start(bf16[1,64,512]{2,1,0:T(8,128)(2,1)S(1)} %select_convert_fusion.3), channel_id=1, source_target_pairs={{0,4},{1,5},{2,6},{3,7},{4,0},{5,1},{6,2},{7,3},{8,12},{9,13},{10,... | collective-permute-start | bytes 196616 | tf_op jit(solution)/shard_map/ppermute | solution.py:172
  68.8 19.1 %copy-start.5 = (f32[512,512]{1,0:T(8,128)S(1)}, f32[512,512]{1,0:T(8,128)}, u32[]{:S(2)}) copy-start(f32[512,512]{1,0:T(8,128)} %first_diag_ref.1) | copy-start | bytes 3145732
  68.8 19.1 %copy-start.6 = (f32[512,512]{1,0:T(8,128)S(1)}, f32[512,512]{1,0:T(8,128)}, u32[]{:S(2)}) copy-start(f32[512,512]{1,0:T(8,128)} %second_diag_ref.1) | copy-start | bytes 3145732
  68.8 5.7 %collective-permute-start.14 = (bf16[2,64,512]{2,1,0:T(8,128)(2,1)S(1)}, bf16[2,64,512]{2,1,0:T(8,128)(2,1)S(1)}, u32[]{:S(2)}, u32[]{:S(2)}) collective-permute-start(bf16[2,64,512]{2,1,0:T(8,128)(2,1)S(1)} %add_convert_fusion), channel_id=1, source_target_pairs={{0,4},{1,5},{2,6},{3,7},{4,0},{5,1},{6,2},{7,3},{8,12},{9,13},{10,... | collective-permute-start | bytes 393224 | tf_op jit(solution)/shard_map/ppermute | solution.py:172
  68.9 5.9 %collective-permute-start.20 = (bf16[1,64,512]{2,1,0:T(8,128)(2,1)S(1)}, bf16[1,64,512]{2,1,0:T(8,128)(2,1)S(1)}, u32[]{:S(2)}, u32[]{:S(2)}) collective-permute-start(bf16[1,64,512]{2,1,0:T(8,128)(2,1)S(1)} %add_convert_fusion.3), channel_id=1, source_target_pairs={{0,8},{1,9},{2,10},{3,11},{4,12},{5,13},{6,14},{7,15},{8,0},{9,1},... | collective-permute-start | bytes 196616 | tf_op jit(solution)/shard_map/ppermute | solution.py:172
  74.9 4.3 %collective-permute-start.21 = (bf16[1,64,512]{2,1,0:T(8,128)(2,1)S(1)}, bf16[1,64,512]{2,1,0:T(8,128)(2,1)S(1)}, u32[]{:S(2)}, u32[]{:S(2)}) collective-permute-start(bf16[1,64,512]{2,1,0:T(8,128)(2,1)S(1)} %add_convert_fusion.2), channel_id=1, source_target_pairs={{0,4},{1,5},{2,6},{3,7},{4,0},{5,1},{6,2},{7,3},{8,12},{9,13},{10,... | collective-permute-start | bytes 196616 | tf_op jit(solution)/shard_map/ppermute | solution.py:172
  76.6 9.3 %collective-permute-start.15 = (bf16[2,128,512]{2,1,0:T(8,128)(2,1)S(1)}, bf16[2,128,512]{2,1,0:T(8,128)(2,1)S(1)}, u32[]{:S(2)}, u32[]{:S(2)}) collective-permute-start(bf16[2,128,512]{2,1,0:T(8,128)(2,1)S(1)} %pad_maximum_fusion.2), channel_id=1, source_target_pairs={{0,2},{1,3},{2,0},{3,1},{4,6},{5,7},{6,4},{7,5},{8,10},{9,11},{10,... | collective-permute-start | bytes 786440 | tf_op jit(solution)/shard_map/ppermute | solution.py:172
  79.2 8.0 %collective-permute-start.22 = (bf16[1,128,512]{2,1,0:T(8,128)(2,1)S(1)}, bf16[1,128,512]{2,1,0:T(8,128)(2,1)S(1)}, u32[]{:S(2)}, u32[]{:S(2)}) collective-permute-start(bf16[1,128,512]{2,1,0:T(8,128)(2,1)S(1)} %pad_maximum_fusion.4), channel_id=1, source_target_pairs={{0,2},{1,3},{2,0},{3,1},{4,6},{5,7},{6,4},{7,5},{8,10},{9,11},{10,... | collective-permute-start | bytes 393224 | tf_op jit(solution)/shard_map/ppermute | solution.py:172
  86.0 2.0 %collective-permute-start.16 = (bf16[2,256,512]{2,1,0:T(8,128)(2,1)S(1)}, bf16[2,256,512]{2,1,0:T(8,128)(2,1)S(1)}, u32[]{:S(2)}, u32[]{:S(2)}) collective-permute-start(bf16[2,256,512]{2,1,0:T(8,128)(2,1)S(1)} %pad_maximum_fusion.1.mine_ref), channel_id=1, source_target_pairs={{0,1},{1,0},{2,3},{3,2},{4,5},{5,4},{6,7},{7,6},{8,9},{9,8},{10,11... | collective-permute-start | bytes 1572872 | tf_op jit(solution)/shard_map/ppermute | solution.py:172
  87.3 2.9 %collective-permute-start.23 = (bf16[1,256,512]{2,1,0:T(8,128)(2,1)S(1)}, bf16[1,256,512]{2,1,0:T(8,128)(2,1)S(1)}, u32[]{:S(2)}, u32[]{:S(2)}) collective-permute-start(bf16[1,256,512]{2,1,0:T(8,128)(2,1)S(1)} %pad_maximum_fusion.3.mine_ref), channel_id=1, source_target_pairs={{0,1},{1,0},{2,3},{3,2},{4,5},{5,4},{6,7},{7,6},{8,9},{9,8},{10,11... | collective-permute-start | bytes 786440 | tf_op jit(solution)/shard_map/ppermute | solution.py:172

commit v12 on v11

--- a/solution.py
+++ b/solution.py
@@ -125,10 +125,12 @@
     acc_ref[...] += dot(sigma_ref[0], across[...])
 
 
-def second_kernel(where_ref, acc_in, far, rest, sigma_ref, turned_ref,
+def second_kernel(where_ref, acc_in, far_0, far_1, rest, sigma_ref, turned_ref,
                   column_ref, give_ref, keep_ref, acc_ref):
+    rows = far_0.shape[0]
     acc_ref[...] = acc_in[...]
-    acc_ref[...] += dot(sigma_ref[1], far[...])
+    acc_ref[...] += dot(sigma_ref[1, :, :rows], far_0[...])
+    acc_ref[...] += dot(sigma_ref[1, :, rows:], far_1[...])
     acc_ref[...] += dot(sigma_ref[2], rest[...])
     column = (-acc_ref[...]).astype(jnp.bfloat16)
     column_ref[...] = column
@@ -254,7 +256,8 @@
         [pltpu.VMEM((2, size, width), jnp.bfloat16), pltpu.SemaphoreType.DMA((6,))],
     )
     far = [far_of(part, devices) for part in across]
-    second_far = far_of(second_across, devices, closed=True)
+    second_parts = [second_across[: half // 2], second_across[half // 2 :]]
+    second_far = [far_of(second_parts[0], devices, closed=True), far_of(second_parts[1], devices)]
     far, second_across, turned = barrier((far, second_across, turned))
     rest = rest_of(across, far, give_across, devices)
     column_first, column_again, give, keep = call(
@@ -265,22 +268,22 @@
         5 * one,
         scratch,
     )
-    give, second_across = barrier((give, second_across))
+    give, second_far[0] = barrier((give, second_far[0]))
     give, keep = core_summed(give, keep, uppers, devices)
-    second_rest = rest_of([second_across], [second_far], give_across, devices)
     total = chip_summed(give, keep, devices)
+    second_parts, total = barrier((second_parts, total))
+    second_rest = rest_of(second_parts, second_far, give_across, devices)
     (second_acc,) = call(
         across_kernel, [wide], [second_acc, column_again, lower, second_across, sorted_sigma], "vvvvv", 2 * one
     )
     column_second, second_give, second_keep = call(
         second_kernel,
         [narrow] + parts(1),
-        [where, second_acc, second_far, second_rest, sorted_sigma, turned],
-        "svvvvv",
+        [where, second_acc, *second_far, second_rest, sorted_sigma, turned],
+        "svvvvvv",
         3 * one,
         scratch,
     )
-    second_give, total = barrier((second_give, total))
     second_give, second_keep = core_summed(second_give, second_keep, uppers, devices)
     mine, other = summed(total, uppers, devices)
     second_total = chip_summed(second_give, second_keep, devices)

time: 91.7 us -> 92.8 us (1.012)
  starting transfers between devices: 30.9 us -> 34.4 us
  waiting for transfers between devices: 41.6 us -> 38.8 us
    ppermute x3 -> x4, waiting for transfers between devices: 9.99 us -> 5.69 us  [far_of(): return lax.ppermute(across, 'row', pairs)]
    ppermute x3 -> x4, starting transfers between devices: 9.69 us -> 13.1 us  [far_of(): return lax.ppermute(across, 'row', pairs)]
    ppermute x21, waiting for transfers between devices: 31.6 us -> 33.1 us  [swapped(): return lax.ppermute(value, 'row', [(i, i ^ bit) for i in range(devices)])]
  transfers between devices with their start and end apart: 24 -> 25, of which waited for: 14 -> 14; matrix products, arithmetic and copies ran while one was open for 1% -> 1% of each run, Pallas kernels for 10% -> 10%
where the time goes in v12:
time: 92.8 us; the launch traced here: 92.4 us
  waiting for transfers between devices  38.8 us (42%)
  starting transfers between devices  34.4 us (37%)
  Pallas kernels  10.8 us (12%)
  local copies, waits for them, and re-layouts  5.56 us (6%)
  between operations  1.66 us (2%)
  other arithmetic  1.13 us (1%)
    ppermute x21, waiting for transfers between devices, swapped(): return lax.ppermute(value, 'row', [(i, i ^ bit) for i in range(devices)])  33.1 us
    ppermute x21, starting transfers between devices, swapped(): return lax.ppermute(value, 'row', [(i, i ^ bit) for i in range(devices)])  21.3 us
    ppermute x4, starting transfers between devices, far_of(): return lax.ppermute(across, 'row', pairs)  13.1 us
    pallas_call x7, Pallas kernels, call(): pl.pallas_call(body, out_shape=outs, in_specs=[pl.BlockSpec(memory_space=...  10.8 us
    ppermute x4, waiting for transfers between devices, far_of(): return lax.ppermute(across, 'row', pairs)  5.69 us
    unnamed x14, local copies, waits for them, and re-layouts  5.53 us
  transfers between devices with their start and end apart: 25, of which 14 were waited for; matrix products, arithmetic and copies ran while one was open for 1% of the time, Pallas kernels for 10%

profile of v12, /device:TPU:0, one launch (start us, length us, event | category | flops | bytes accessed | tf_op | source)
XLA Modules:
  0.0 92.4 jit_solution(16172942218692159208)
XLA Ops:
  1.2 1.0 %copy-done.3 = bf16[1,1,512,512]{3,2,1,0:T(8,128)(2,1)S(1)} copy-done((bf16[1,1,512,512]{3,2,1,0:T(8,128)(2,1)S(1)}, bf16[1,1,512,512]{3,2,1,0:T(8,128)(2,1)}, u32[]{:S(2)}) %copy-start.3) | copy-done | bytes 524312
  2.3 3.0 %collective-permute-start.2 = (bf16[256,512]{1,0:T(8,128)(2,1)S(1)}, bf16[256,512]{1,0:T(8,128)(2,1)S(1)}, u32[]{:S(2)}, u32[]{:S(2)}) collective-permute-start(bf16[256,512]{1,0:T(8,128)(2,1)S(1)} %get-tuple-element.39.first_0), channel_id=1, source_target_pairs={{0,2},{1,3},{2,0},{3,1},{4,6},{5,7},{6,4},{7,5},{8,10},{9,11},{10,... | collective-permute-start | bytes 786440 | tf_op jit(solution)/shard_map/ppermute | solution.py:174
  5.4 1.9 %collective-permute-start.6 = (bf16[512,512]{1,0:T(8,128)(2,1)}, bf16[512,512]{1,0:T(8,128)(2,1)S(1)}, u32[]{:S(2)}, u32[]{:S(2)}) collective-permute-start(bf16[512,512]{1,0:T(8,128)(2,1)} %bitcast.11), channel_id=1, source_target_pairs={{0,2},{1,3},{2,0},{3,1},{4,6},{5,7},{6,4},{7,5},{8,10},{9,11},{10,... | collective-permute-start | bytes 1572872 | tf_op jit(solution)/shard_map/ppermute | solution.py:174
  7.4 5.1 %collective-permute-done.2.across_0 = bf16[256,512]{1,0:T(8,128)(2,1)S(1)} collective-permute-done((bf16[256,512]{1,0:T(8,128)(2,1)S(1)}, bf16[256,512]{1,0:T(8,128)(2,1)S(1)}, u32[]{:S(2)}, u32[]{:S(2)}) %collective-permute-start.2) | collective-permute-done | bytes 262176 | tf_op jit(solution)/shard_map/ppermute | solution.py:174
  12.4 4.1 %collective-permute-start.4 = (bf16[256,512]{1,0:T(8,128)(2,1)S(1)}, bf16[256,512]{1,0:T(8,128)(2,1)S(1)}, u32[]{:S(2)}, u32[]{:S(2)}) collective-permute-start(bf16[256,512]{1,0:T(8,128)(2,1)S(1)} %collective-permute-done.2.across_0), channel_id=1, source_target_pairs={{0,4},{1,5},{4,8},{5,9},{6,2},{7,3},{8,12},{9,13},{10,6},{11,7},{1... | collective-permute-start | bytes 786440 | tf_op jit(solution)/shard_map/ppermute | solution.py:182
  16.5 1.6 %collective-permute-done.3.across_1 = bf16[256,512]{1,0:T(8,128)(2,1)S(1)} collective-permute-done((bf16[256,512]{1,0:T(8,128)(2,1)S(1)}, bf16[256,512]{1,0:T(8,128)(2,1)S(1)}, u32[]{:S(2)}, u32[]{:S(2)}) %collective-permute-start.3) | collective-permute-done | bytes 262176 | tf_op jit(solution)/shard_map/ppermute | solution.py:174
  18.1 4.1 %collective-permute-start.5 = (bf16[256,512]{1,0:T(8,128)(2,1)S(1)}, bf16[256,512]{1,0:T(8,128)(2,1)S(1)}, u32[]{:S(2)}, u32[]{:S(2)}) collective-permute-start(bf16[256,512]{1,0:T(8,128)(2,1)S(1)} %collective-permute-done.3.across_1), channel_id=1, source_target_pairs={{0,4},{1,5},{4,8},{5,9},{6,2},{7,3},{8,12},{9,13},{10,6},{11,7},{1... | collective-permute-start | bytes 786440 | tf_op jit(solution)/shard_map/ppermute | solution.py:182
  22.8 1.7 %copy-done = bf16[1,1,5,512,512]{4,3,2,1,0:T(8,128)(2,1)S(1)} copy-done((bf16[1,1,5,512,512]{4,3,2,1,0:T(8,128)(2,1)S(1)}, bf16[1,1,5,512,512]{4,3,2,1,0:T(8,128)(2,1)}, u32[]{:S(2)}) %copy-start) | copy-done | bytes 2621464
  24.5 1.0 %copy-done.1 = bf16[512,512]{1,0:T(8,128)(2,1)S(1)} copy-done((bf16[512,512]{1,0:T(8,128)(2,1)S(1)}, bf16[512,512]{1,0:T(8,128)(2,1)}, u32[]{:S(2)}) %copy-start.1) | copy-done | bytes 524312
  27.3 2.6 %shard_map.120 = (f32[512,512]{1,0:T(8,128)S(1)}, f32[512,512]{1,0:T(8,128)S(1)}, bf16[1024,512]{1,0:T(8,128)(2,1)S(1)}, bf16[3,512,512]{2,1,0:T(8,128)(2,1)S(1)}, bf16[512,512]{1,0:T(8,128)(2,1)S(1)}) custom-call(s32[1]{0:T(128)} %bitcast.where_ref, s32[5]{0:T(128)S(1)} %bitcast.15, s32[1]{0:T(128)} %bitcast.8.count_ref, bf16[5,512,512]{2,1,0:T(8,128)(2,1)S(1)} %bitcast.9, ...), custom_call_target="tpu_custom_call" | custom-call | flops 1073741824 | bytes 10485788 | tf_op jit(solution)/shard_map/pallas_call | solution.py:16
  30.1 1.5 %collective-permute-start.8 = (bf16[128,512]{1,0:T(8,128)(2,1)S(1)}, bf16[128,512]{1,0:T(8,128)(2,1)S(1)}, u32[]{:S(2)}, u32[]{:S(2)}) collective-permute-start(bf16[128,512]{1,0:T(8,128)(2,1)S(1)} %slice.40), channel_id=1, source_target_pairs={{0,4},{1,5},{2,0},{3,1},{4,8},{5,9},{6,2},{7,3},{8,12},{9,13},{10,... | collective-permute-start | bytes 393224 | tf_op jit(solution)/shard_map/ppermute | solution.py:182
  32.0 2.3 %shard_map.121 = (bf16[512,512]{1,0:T(8,128)(2,1)}, bf16[512,512]{1,0:T(8,128)(2,1)S(1)}, bf16[2,256,512]{2,1,0:T(8,128)(2,1)S(1)}, f32[2,256,512]{2,1,0:T(8,128)S(1)}) custom-call(s32[1]{0:T(128)} %bitcast.where_ref, f32[512,512]{1,0:T(8,128)S(1)} %get-tuple-element.42.acc_in, bf16[256,512]{1,0:T(8,128)(2,1)S(1)} %collective-permute-done.2.across_0, ...), custom_call_target="tpu_custom_call" | custom-call | flops 1342177280 | bytes 7864324 | tf_op jit(solution)/shard_map/pallas_call | solution.py:16
  34.3 1.8 %collective-permute-done.8.far_0 = bf16[128,512]{1,0:T(8,128)(2,1)S(1)} collective-permute-done((bf16[128,512]{1,0:T(8,128)(2,1)S(1)}, bf16[128,512]{1,0:T(8,128)(2,1)S(1)}, u32[]{:S(2)}, u32[]{:S(2)}) %collective-permute-start.8) | collective-permute-done | bytes 131104 | tf_op jit(solution)/shard_map/ppermute | solution.py:182
  36.1 1.9 %collective-permute-done.9 = bf16[2,256,512]{2,1,0:T(8,128)(2,1)S(1)} collective-permute-done((bf16[2,256,512]{2,1,0:T(8,128)(2,1)S(1)}, bf16[2,256,512]{2,1,0:T(8,128)(2,1)S(1)}, u32[]{:S(2)}, u32[]{:S(2)}) %collective-permute-start.9) | collective-permute-done | bytes 524320 | tf_op jit(solution)/shard_map/ppermute | solution.py:174
  38.9 3.5 %collective-permute-start.16 = (bf16[384,512]{1,0:T(8,128)(2,1)S(1)}, bf16[384,512]{1,0:T(8,128)(2,1)S(1)}, u32[]{:S(2)}, u32[]{:S(2)}) collective-permute-start(bf16[384,512]{1,0:T(8,128)(2,1)S(1)} %slice.41), channel_id=1, source_target_pairs={{0,4},{1,5},{4,8},{5,9},{6,2},{7,3},{8,12},{9,13},{10,6},{11,7},{1... | collective-permute-start | bytes 1179656 | tf_op jit(solution)/shard_map/ppermute | solution.py:182
  42.4 4.3 %collective-permute-done.10 = bf16[2,128,512]{2,1,0:T(8,128)(2,1)S(1)} collective-permute-done((bf16[2,128,512]{2,1,0:T(8,128)(2,1)S(1)}, bf16[2,128,512]{2,1,0:T(8,128)(2,1)S(1)}, u32[]{:S(2)}, u32[]{:S(2)}) %collective-permute-start.10) | collective-permute-done | bytes 262176 | tf_op jit(solution)/shard_map/ppermute | solution.py:174
  46.8 3.9 %collective-permute-done.16.far_1 = bf16[384,512]{1,0:T(8,128)(2,1)S(1)} collective-permute-done((bf16[384,512]{1,0:T(8,128)(2,1)S(1)}, bf16[384,512]{1,0:T(8,128)(2,1)S(1)}, u32[]{:S(2)}, u32[]{:S(2)}) %collective-permute-start.16) | collective-permute-done | bytes 393248 | tf_op jit(solution)/shard_map/ppermute | solution.py:182
  51.0 2.5 %collective-permute-start.11 = (bf16[2,64,512]{2,1,0:T(8,128)(2,1)S(1)}, bf16[2,64,512]{2,1,0:T(8,128)(2,1)S(1)}, u32[]{:S(2)}, u32[]{:S(2)}) collective-permute-start(bf16[2,64,512]{2,1,0:T(8,128)(2,1)S(1)} %select_convert_fusion.2), channel_id=1, source_target_pairs={{0,4},{1,5},{2,6},{3,7},{4,0},{5,1},{6,2},{7,3},{8,12},{9,13},{10,... | collective-permute-start | bytes 393224 | tf_op jit(solution)/shard_map/ppermute | solution.py:174
  54.2 1.7 %shard_map.124 = (bf16[512,512]{1,0:T(8,128)(2,1)}, bf16[1,256,512]{2,1,0:T(8,128)(2,1)S(1)}, f32[1,256,512]{2,1,0:T(8,128)S(1)}) custom-call(s32[1]{0:T(128)} %bitcast.where_ref, f32[512,512]{1,0:T(8,128)S(1)} %shard_map.123.acc_in, bf16[128,512]{1,0:T(8,128)(2,1)S(1)} %collective-permute-done.8.far_0, bf16[384,512]{1,0:T(8,128)(2,1)S(1)} %collective-permute-done.16.far_1, ...), custom_call_target="tpu_custom_call" | custom-call | flops 805306368 | bytes 6029316 | tf_op jit(solution)/shard_map/pallas_call | solution.py:16
  56.1 1.5 %collective-permute-done.11 = bf16[2,64,512]{2,1,0:T(8,128)(2,1)S(1)} collective-permute-done((bf16[2,64,512]{2,1,0:T(8,128)(2,1)S(1)}, bf16[2,64,512]{2,1,0:T(8,128)(2,1)S(1)}, u32[]{:S(2)}, u32[]{:S(2)}) %collective-permute-start.11) | collective-permute-done | bytes 131104 | tf_op jit(solution)/shard_map/ppermute | solution.py:174
  57.7 2.8 %collective-permute-start.12 = (bf16[2,64,512]{2,1,0:T(8,128)(2,1)S(1)}, bf16[2,64,512]{2,1,0:T(8,128)(2,1)S(1)}, u32[]{:S(2)}, u32[]{:S(2)}) collective-permute-start(bf16[2,64,512]{2,1,0:T(8,128)(2,1)S(1)} %add_convert_fusion.1), channel_id=1, source_target_pairs={{0,8},{1,9},{2,10},{3,11},{4,12},{5,13},{6,14},{7,15},{8,0},{9,1},... | collective-permute-start | bytes 393224 | tf_op jit(solution)/shard_map/ppermute | solution.py:174
  60.6 1.4 %collective-permute-start.19 = (bf16[1,128,512]{2,1,0:T(8,128)(2,1)S(1)}, bf16[1,128,512]{2,1,0:T(8,128)(2,1)S(1)}, u32[]{:S(2)}, u32[]{:S(2)}) collective-permute-start(bf16[1,128,512]{2,1,0:T(8,128)(2,1)S(1)} %select_convert_fusion.1), channel_id=1, source_target_pairs={{0,2},{1,3},{2,0},{3,1},{4,6},{5,7},{6,4},{7,5},{8,10},{9,11},{10,... | collective-permute-start | bytes 393224 | tf_op jit(solution)/shard_map/ppermute | solution.py:174
  62.1 4.7 %collective-permute-done.12 = bf16[2,64,512]{2,1,0:T(8,128)(2,1)S(1)} collective-permute-done((bf16[2,64,512]{2,1,0:T(8,128)(2,1)S(1)}, bf16[2,64,512]{2,1,0:T(8,128)(2,1)S(1)}, u32[]{:S(2)}, u32[]{:S(2)}) %collective-permute-start.12) | collective-permute-done | bytes 131104 | tf_op jit(solution)/shard_map/ppermute | solution.py:174
  67.6 1.5 %collective-permute-start.20 = (bf16[1,64,512]{2,1,0:T(8,128)(2,1)S(1)}, bf16[1,64,512]{2,1,0:T(8,128)(2,1)S(1)}, u32[]{:S(2)}, u32[]{:S(2)}) collective-permute-start(bf16[1,64,512]{2,1,0:T(8,128)(2,1)S(1)} %select_convert_fusion.3), channel_id=1, source_target_pairs={{0,4},{1,5},{2,6},{3,7},{4,0},{5,1},{6,2},{7,3},{8,12},{9,13},{10,... | collective-permute-start | bytes 196616 | tf_op jit(solution)/shard_map/ppermute | solution.py:174
  69.1 3.0 %collective-permute-done.13 = bf16[2,64,512]{2,1,0:T(8,128)(2,1)S(1)} collective-permute-done((bf16[2,64,512]{2,1,0:T(8,128)(2,1)S(1)}, bf16[2,64,512]{2,1,0:T(8,128)(2,1)S(1)}, u32[]{:S(2)}, u32[]{:S(2)}) %collective-permute-start.13) | collective-permute-done | bytes 131104 | tf_op jit(solution)/shard_map/ppermute | solution.py:174
  72.9 3.2 %collective-permute-start.21 = (bf16[1,64,512]{2,1,0:T(8,128)(2,1)S(1)}, bf16[1,64,512]{2,1,0:T(8,128)(2,1)S(1)}, u32[]{:S(2)}, u32[]{:S(2)}) collective-permute-start(bf16[1,64,512]{2,1,0:T(8,128)(2,1)S(1)} %add_convert_fusion.3), channel_id=1, source_target_pairs={{0,8},{1,9},{2,10},{3,11},{4,12},{5,13},{6,14},{7,15},{8,0},{9,1},... | collective-permute-start | bytes 196616 | tf_op jit(solution)/shard_map/ppermute | solution.py:174
  76.2 2.5 %collective-permute-done.21 = bf16[1,64,512]{2,1,0:T(8,128)(2,1)S(1)} collective-permute-done((bf16[1,64,512]{2,1,0:T(8,128)(2,1)S(1)}, bf16[1,64,512]{2,1,0:T(8,128)(2,1)S(1)}, u32[]{:S(2)}, u32[]{:S(2)}) %collective-permute-start.21) | collective-permute-done | bytes 65568 | tf_op jit(solution)/shard_map/ppermute | solution.py:174
  78.7 1.4 %collective-permute-start.22 = (bf16[1,64,512]{2,1,0:T(8,128)(2,1)S(1)}, bf16[1,64,512]{2,1,0:T(8,128)(2,1)S(1)}, u32[]{:S(2)}, u32[]{:S(2)}) collective-permute-start(bf16[1,64,512]{2,1,0:T(8,128)(2,1)S(1)} %add_convert_fusion.2), channel_id=1, source_target_pairs={{0,4},{1,5},{2,6},{3,7},{4,0},{5,1},{6,2},{7,3},{8,12},{9,13},{10,... | collective-permute-start | bytes 196616 | tf_op jit(solution)/shard_map/ppermute | solution.py:174
  80.2 3.4 %collective-permute-done.14 = bf16[2,128,512]{2,1,0:T(8,128)(2,1)S(1)} collective-permute-done((bf16[2,128,512]{2,1,0:T(8,128)(2,1)S(1)}, bf16[2,128,512]{2,1,0:T(8,128)(2,1)S(1)}, u32[]{:S(2)}, u32[]{:S(2)}) %collective-permute-start.14) | collective-permute-done | bytes 262176 | tf_op jit(solution)/shard_map/ppermute | solution.py:174
  84.8 4.0 %collective-permute-done.23 = bf16[1,128,512]{2,1,0:T(8,128)(2,1)S(1)} collective-permute-done((bf16[1,128,512]{2,1,0:T(8,128)(2,1)S(1)}, bf16[1,128,512]{2,1,0:T(8,128)(2,1)S(1)}, u32[]{:S(2)}, u32[]{:S(2)}) %collective-permute-start.23) | collective-permute-done | bytes 131104 | tf_op jit(solution)/shard_map/ppermute | solution.py:174
  89.0 2.2 %shard_map.122 = (f32[512,512]{1,0:T(8,128)}, f32[512,512]{1,0:T(8,128)}, f32[512,512]{1,0:T(8,128)S(1)}) custom-call(s32[1]{0:T(128)} %bitcast.where_ref, bf16[2,256,512]{2,1,0:T(8,128)(2,1)S(1)} %pad_maximum_fusion.1.mine_ref, bf16[2,256,512]{2,1,0:T(8,128)(2,1)S(1)} %collective-permute-done.15.other_ref, ...), custom_call_target="tpu_custom_call" | custom-call | flops 1073741824 | bytes 6815748 | tf_op jit(solution)/shard_map/pallas_call | solution.py:16
  91.2 1.2 %shard_map.125 = f32[512,512]{1,0:T(8,128)} custom-call(s32[1]{0:T(128)} %bitcast.where_ref, bf16[1,256,512]{2,1,0:T(8,128)(2,1)S(1)} %pad_maximum_fusion.4.mine_ref, bf16[1,256,512]{2,1,0:T(8,128)(2,1)S(1)} %collective-permute-done.24.other_ref, f32[512,512]{1,0:T(8,128)S(1)} %get-tuple-element.68.base_ref), custom_call_target="tpu_custom_call" | custom-call | flops 262144 | bytes 2621444 | tf_op jit(solution)/shard_map/pallas_call | solution.py:16
  (66 shorter events, 8.2 us)
Async XLA Ops:
  0.6 22.1 %collective-permute-start.1 = (bf16[512,512]{1,0:T(8,128)(2,1)}, bf16[512,512]{1,0:T(8,128)(2,1)S(1)}, u32[]{:S(2)}, u32[]{:S(2)}) collective-permute-start(bf16[512,512]{1,0:T(8,128)(2,1)} %bitcast.10), channel_id=1, source_target_pairs={{0,1},{1,0},{2,3},{3,2},{4,5},{5,4},{6,7},{7,6},{8,9},{9,8},{10,11... | collective-permute-start | bytes 1572872 | tf_op jit(solution)/shard_map/ppermute | solution.py:174
  1.2 21.6 %collective-permute-start = (bf16[512,512]{1,0:T(8,128)(2,1)}, bf16[512,512]{1,0:T(8,128)(2,1)S(1)}, u32[]{:S(2)}, u32[]{:S(2)}) collective-permute-start(bf16[512,512]{1,0:T(8,128)(2,1)} %bitcast.13), channel_id=1, source_target_pairs={{0,1},{1,0},{2,3},{3,2},{4,5},{5,4},{6,7},{7,6},{8,9},{9,8},{10,11... | collective-permute-start | bytes 1572872 | tf_op jit(solution)/shard_map/ppermute | solution.py:174
  1.2 1.0 %copy-start.3 = (bf16[1,1,512,512]{3,2,1,0:T(8,128)(2,1)S(1)}, bf16[1,1,512,512]{3,2,1,0:T(8,128)(2,1)}, u32[]{:S(2)}) copy-start(bf16[1,1,512,512]{3,2,1,0:T(8,128)(2,1)} %param.9) | copy-start | bytes 1572868
  2.3 10.1 %collective-permute-start.2 = (bf16[256,512]{1,0:T(8,128)(2,1)S(1)}, bf16[256,512]{1,0:T(8,128)(2,1)S(1)}, u32[]{:S(2)}, u32[]{:S(2)}) collective-permute-start(bf16[256,512]{1,0:T(8,128)(2,1)S(1)} %get-tuple-element.39.first_0), channel_id=1, source_target_pairs={{0,2},{1,3},{2,0},{3,1},{4,6},{5,7},{6,4},{7,5},{8,10},{9,11},{10,... | collective-permute-start | bytes 786440 | tf_op jit(solution)/shard_map/ppermute | solution.py:174
  5.3 12.7 %collective-permute-start.3 = (bf16[256,512]{1,0:T(8,128)(2,1)S(1)}, bf16[256,512]{1,0:T(8,128)(2,1)S(1)}, u32[]{:S(2)}, u32[]{:S(2)}) collective-permute-start(bf16[256,512]{1,0:T(8,128)(2,1)S(1)} %get-tuple-element.40.first_1), channel_id=1, source_target_pairs={{0,2},{1,3},{2,0},{3,1},{4,6},{5,7},{6,4},{7,5},{8,10},{9,11},{10,... | collective-permute-start | bytes 786440 | tf_op jit(solution)/shard_map/ppermute | solution.py:174
  5.4 24.5 %collective-permute-start.6 = (bf16[512,512]{1,0:T(8,128)(2,1)}, bf16[512,512]{1,0:T(8,128)(2,1)S(1)}, u32[]{:S(2)}, u32[]{:S(2)}) collective-permute-start(bf16[512,512]{1,0:T(8,128)(2,1)} %bitcast.11), channel_id=1, source_target_pairs={{0,2},{1,3},{2,0},{3,1},{4,6},{5,7},{6,4},{7,5},{8,10},{9,11},{10,... | collective-permute-start | bytes 1572872 | tf_op jit(solution)/shard_map/ppermute | solution.py:174
  12.4 17.5 %collective-permute-start.4 = (bf16[256,512]{1,0:T(8,128)(2,1)S(1)}, bf16[256,512]{1,0:T(8,128)(2,1)S(1)}, u32[]{:S(2)}, u32[]{:S(2)}) collective-permute-start(bf16[256,512]{1,0:T(8,128)(2,1)S(1)} %collective-permute-done.2.across_0), channel_id=1, source_target_pairs={{0,4},{1,5},{4,8},{5,9},{6,2},{7,3},{8,12},{9,13},{10,6},{11,7},{1... | collective-permute-start | bytes 786440 | tf_op jit(solution)/shard_map/ppermute | solution.py:182
  18.1 11.9 %collective-permute-start.5 = (bf16[256,512]{1,0:T(8,128)(2,1)S(1)}, bf16[256,512]{1,0:T(8,128)(2,1)S(1)}, u32[]{:S(2)}, u32[]{:S(2)}) collective-permute-start(bf16[256,512]{1,0:T(8,128)(2,1)S(1)} %collective-permute-done.3.across_1), channel_id=1, source_target_pairs={{0,4},{1,5},{4,8},{5,9},{6,2},{7,3},{8,12},{9,13},{10,6},{11,7},{1... | collective-permute-start | bytes 786440 | tf_op jit(solution)/shard_map/ppermute | solution.py:182
  22.8 1.7 %copy-start = (bf16[1,1,5,512,512]{4,3,2,1,0:T(8,128)(2,1)S(1)}, bf16[1,1,5,512,512]{4,3,2,1,0:T(8,128)(2,1)}, u32[]{:S(2)}) copy-start(bf16[1,1,5,512,512]{4,3,2,1,0:T(8,128)(2,1)} %param.8) | copy-start | bytes 7864324
  24.5 1.0 %copy-start.1 = (bf16[512,512]{1,0:T(8,128)(2,1)S(1)}, bf16[512,512]{1,0:T(8,128)(2,1)}, u32[]{:S(2)}) copy-start(bf16[512,512]{1,0:T(8,128)(2,1)} %lower_hbm.1) | copy-start | bytes 1572868
  25.6 1.0 %copy-start.2 = (bf16[1,1,512,512]{3,2,1,0:T(8,128)(2,1)S(1)}, bf16[1,1,512,512]{3,2,1,0:T(8,128)(2,1)}, u32[]{:S(2)}) copy-start(bf16[1,1,512,512]{3,2,1,0:T(8,128)(2,1)} %param.10) | copy-start | bytes 1572868
  26.6 0.7 copy-start.4
  30.0 2.0 %collective-permute-start.7 = (bf16[512,512]{1,0:T(8,128)(2,1)S(1)}, bf16[512,512]{1,0:T(8,128)(2,1)S(1)}, u32[]{:S(2)}, u32[]{:S(2)}) collective-permute-start(bf16[512,512]{1,0:T(8,128)(2,1)S(1)} %pad_maximum_fusion), channel_id=1, source_target_pairs={{0,1},{1,0},{2,3},{3,2},{4,5},{5,4},{6,7},{7,6},{8,9},{9,8},{10,11... | collective-permute-start | bytes 1572872 | tf_op jit(solution)/shard_map/ppermute | solution.py:174
  30.1 5.9 %collective-permute-start.8 = (bf16[128,512]{1,0:T(8,128)(2,1)S(1)}, bf16[128,512]{1,0:T(8,128)(2,1)S(1)}, u32[]{:S(2)}, u32[]{:S(2)}) collective-permute-start(bf16[128,512]{1,0:T(8,128)(2,1)S(1)} %slice.40), channel_id=1, source_target_pairs={{0,4},{1,5},{2,0},{3,1},{4,8},{5,9},{6,2},{7,3},{8,12},{9,13},{10,... | collective-permute-start | bytes 393224 | tf_op jit(solution)/shard_map/ppermute | solution.py:182
  36.1 1.9 %collective-permute-start.9 = (bf16[2,256,512]{2,1,0:T(8,128)(2,1)S(1)}, bf16[2,256,512]{2,1,0:T(8,128)(2,1)S(1)}, u32[]{:S(2)}, u32[]{:S(2)}) collective-permute-start(bf16[2,256,512]{2,1,0:T(8,128)(2,1)S(1)} %get-tuple-element.54), channel_id=1, source_target_pairs={{0,1},{1,0},{2,3},{3,2},{4,5},{5,4},{6,7},{7,6},{8,9},{9,8},{10,11... | collective-permute-start | bytes 1572872 | tf_op jit(solution)/shard_map/ppermute | solution.py:174
  38.2 8.4 %collective-permute-start.10 = (bf16[2,128,512]{2,1,0:T(8,128)(2,1)S(1)}, bf16[2,128,512]{2,1,0:T(8,128)(2,1)S(1)}, u32[]{:S(2)}, u32[]{:S(2)}) collective-permute-start(bf16[2,128,512]{2,1,0:T(8,128)(2,1)S(1)} %select_convert_fusion), channel_id=1, source_target_pairs={{0,2},{1,3},{2,0},{3,1},{4,6},{5,7},{6,4},{7,5},{8,10},{9,11},{10,... | collective-permute-start | bytes 786440 | tf_op jit(solution)/shard_map/ppermute | solution.py:174
  38.9 11.9 %collective-permute-start.16 = (bf16[384,512]{1,0:T(8,128)(2,1)S(1)}, bf16[384,512]{1,0:T(8,128)(2,1)S(1)}, u32[]{:S(2)}, u32[]{:S(2)}) collective-permute-start(bf16[384,512]{1,0:T(8,128)(2,1)S(1)} %slice.41), channel_id=1, source_target_pairs={{0,4},{1,5},{4,8},{5,9},{6,2},{7,3},{8,12},{9,13},{10,6},{11,7},{1... | collective-permute-start | bytes 1179656 | tf_op jit(solution)/shard_map/ppermute | solution.py:182
  50.8 3.4 %collective-permute-start.17 = (bf16[512,512]{1,0:T(8,128)(2,1)S(1)}, bf16[512,512]{1,0:T(8,128)(2,1)S(1)}, u32[]{:S(2)}, u32[]{:S(2)}) collective-permute-start(bf16[512,512]{1,0:T(8,128)(2,1)S(1)} %pad_maximum_fusion.2), channel_id=1, source_target_pairs={{0,1},{1,0},{2,3},{3,2},{4,5},{5,4},{6,7},{7,6},{8,9},{9,8},{10,11... | collective-permute-start | bytes 1572872 | tf_op jit(solution)/shard_map/ppermute | solution.py:174
  51.0 6.7 %collective-permute-start.11 = (bf16[2,64,512]{2,1,0:T(8,128)(2,1)S(1)}, bf16[2,64,512]{2,1,0:T(8,128)(2,1)S(1)}, u32[]{:S(2)}, u32[]{:S(2)}) collective-permute-start(bf16[2,64,512]{2,1,0:T(8,128)(2,1)S(1)} %select_convert_fusion.2), channel_id=1, source_target_pairs={{0,4},{1,5},{2,6},{3,7},{4,0},{5,1},{6,2},{7,3},{8,12},{9,13},{10,... | collective-permute-start | bytes 393224 | tf_op jit(solution)/shard_map/ppermute | solution.py:174
  55.9 4.6 %collective-permute-start.18 = (bf16[1,256,512]{2,1,0:T(8,128)(2,1)S(1)}, bf16[1,256,512]{2,1,0:T(8,128)(2,1)S(1)}, u32[]{:S(2)}, u32[]{:S(2)}) collective-permute-start(bf16[1,256,512]{2,1,0:T(8,128)(2,1)S(1)} %get-tuple-element.67), channel_id=1, source_target_pairs={{0,1},{1,0},{2,3},{3,2},{4,5},{5,4},{6,7},{7,6},{8,9},{9,8},{10,11... | collective-permute-start | bytes 786440 | tf_op jit(solution)/shard_map/ppermute | solution.py:174
  57.7 9.1 %collective-permute-start.12 = (bf16[2,64,512]{2,1,0:T(8,128)(2,1)S(1)}, bf16[2,64,512]{2,1,0:T(8,128)(2,1)S(1)}, u32[]{:S(2)}, u32[]{:S(2)}) collective-permute-start(bf16[2,64,512]{2,1,0:T(8,128)(2,1)S(1)} %add_convert_fusion.1), channel_id=1, source_target_pairs={{0,8},{1,9},{2,10},{3,11},{4,12},{5,13},{6,14},{7,15},{8,0},{9,1},... | collective-permute-start | bytes 393224 | tf_op jit(solution)/shard_map/ppermute | solution.py:174
  60.6 6.9 %collective-permute-start.19 = (bf16[1,128,512]{2,1,0:T(8,128)(2,1)S(1)}, bf16[1,128,512]{2,1,0:T(8,128)(2,1)S(1)}, u32[]{:S(2)}, u32[]{:S(2)}) collective-permute-start(bf16[1,128,512]{2,1,0:T(8,128)(2,1)S(1)} %select_convert_fusion.1), channel_id=1, source_target_pairs={{0,2},{1,3},{2,0},{3,1},{4,6},{5,7},{6,4},{7,5},{8,10},{9,11},{10,... | collective-permute-start | bytes 393224 | tf_op jit(solution)/shard_map/ppermute | solution.py:174
  66.8 5.3 %collective-permute-start.13 = (bf16[2,64,512]{2,1,0:T(8,128)(2,1)S(1)}, bf16[2,64,512]{2,1,0:T(8,128)(2,1)S(1)}, u32[]{:S(2)}, u32[]{:S(2)}) collective-permute-start(bf16[2,64,512]{2,1,0:T(8,128)(2,1)S(1)} %add_convert_fusion), channel_id=1, source_target_pairs={{0,4},{1,5},{2,6},{3,7},{4,0},{5,1},{6,2},{7,3},{8,12},{9,13},{10,... | collective-permute-start | bytes 393224 | tf_op jit(solution)/shard_map/ppermute | solution.py:174
  67.6 21.3 %copy-start.5 = (f32[512,512]{1,0:T(8,128)S(1)}, f32[512,512]{1,0:T(8,128)}, u32[]{:S(2)}) copy-start(f32[512,512]{1,0:T(8,128)} %first_diag_ref.1) | copy-start | bytes 3145732
  67.6 21.3 %copy-start.6 = (f32[512,512]{1,0:T(8,128)S(1)}, f32[512,512]{1,0:T(8,128)}, u32[]{:S(2)}) copy-start(f32[512,512]{1,0:T(8,128)} %second_diag_ref.1) | copy-start | bytes 3145732
  67.6 5.2 %collective-permute-start.20 = (bf16[1,64,512]{2,1,0:T(8,128)(2,1)S(1)}, bf16[1,64,512]{2,1,0:T(8,128)(2,1)S(1)}, u32[]{:S(2)}, u32[]{:S(2)}) collective-permute-start(bf16[1,64,512]{2,1,0:T(8,128)(2,1)S(1)} %select_convert_fusion.3), channel_id=1, source_target_pairs={{0,4},{1,5},{2,6},{3,7},{4,0},{5,1},{6,2},{7,3},{8,12},{9,13},{10,... | collective-permute-start | bytes 196616 | tf_op jit(solution)/shard_map/ppermute | solution.py:174
  72.9 5.8 %collective-permute-start.21 = (bf16[1,64,512]{2,1,0:T(8,128)(2,1)S(1)}, bf16[1,64,512]{2,1,0:T(8,128)(2,1)S(1)}, u32[]{:S(2)}, u32[]{:S(2)}) collective-permute-start(bf16[1,64,512]{2,1,0:T(8,128)(2,1)S(1)} %add_convert_fusion.3), channel_id=1, source_target_pairs={{0,8},{1,9},{2,10},{3,11},{4,12},{5,13},{6,14},{7,15},{8,0},{9,1},... | collective-permute-start | bytes 196616 | tf_op jit(solution)/shard_map/ppermute | solution.py:174
  76.1 7.5 %collective-permute-start.14 = (bf16[2,128,512]{2,1,0:T(8,128)(2,1)S(1)}, bf16[2,128,512]{2,1,0:T(8,128)(2,1)S(1)}, u32[]{:S(2)}, u32[]{:S(2)}) collective-permute-start(bf16[2,128,512]{2,1,0:T(8,128)(2,1)S(1)} %pad_maximum_fusion.3), channel_id=1, source_target_pairs={{0,2},{1,3},{2,0},{3,1},{4,6},{5,7},{6,4},{7,5},{8,10},{9,11},{10,... | collective-permute-start | bytes 786440 | tf_op jit(solution)/shard_map/ppermute | solution.py:174
  78.7 5.0 %collective-permute-start.22 = (bf16[1,64,512]{2,1,0:T(8,128)(2,1)S(1)}, bf16[1,64,512]{2,1,0:T(8,128)(2,1)S(1)}, u32[]{:S(2)}, u32[]{:S(2)}) collective-permute-start(bf16[1,64,512]{2,1,0:T(8,128)(2,1)S(1)} %add_convert_fusion.2), channel_id=1, source_target_pairs={{0,4},{1,5},{2,6},{3,7},{4,0},{5,1},{6,2},{7,3},{8,12},{9,13},{10,... | collective-permute-start | bytes 196616 | tf_op jit(solution)/shard_map/ppermute | solution.py:174
  83.7 5.0 %collective-permute-start.23 = (bf16[1,128,512]{2,1,0:T(8,128)(2,1)S(1)}, bf16[1,128,512]{2,1,0:T(8,128)(2,1)S(1)}, u32[]{:S(2)}, u32[]{:S(2)}) collective-permute-start(bf16[1,128,512]{2,1,0:T(8,128)(2,1)S(1)} %pad_maximum_fusion.5), channel_id=1, source_target_pairs={{0,2},{1,3},{2,0},{3,1},{4,6},{5,7},{6,4},{7,5},{8,10},{9,11},{10,... | collective-permute-start | bytes 393224 | tf_op jit(solution)/shard_map/ppermute | solution.py:174
  84.7 4.2 %collective-permute-start.15 = (bf16[2,256,512]{2,1,0:T(8,128)(2,1)S(1)}, bf16[2,256,512]{2,1,0:T(8,128)(2,1)S(1)}, u32[]{:S(2)}, u32[]{:S(2)}) collective-permute-start(bf16[2,256,512]{2,1,0:T(8,128)(2,1)S(1)} %pad_maximum_fusion.1.mine_ref), channel_id=1, source_target_pairs={{0,1},{1,0},{2,3},{3,2},{4,5},{5,4},{6,7},{7,6},{8,9},{9,8},{10,11... | collective-permute-start | bytes 1572872 | tf_op jit(solution)/shard_map/ppermute | solution.py:174
  88.9 2.3 %collective-permute-start.24 = (bf16[1,256,512]{2,1,0:T(8,128)(2,1)S(1)}, bf16[1,256,512]{2,1,0:T(8,128)(2,1)S(1)}, u32[]{:S(2)}, u32[]{:S(2)}) collective-permute-start(bf16[1,256,512]{2,1,0:T(8,128)(2,1)S(1)} %pad_maximum_fusion.4.mine_ref), channel_id=1, source_target_pairs={{0,1},{1,0},{2,3},{3,2},{4,5},{5,4},{6,7},{7,6},{8,9},{9,8},{10,11... | collective-permute-start | bytes 786440 | tf_op jit(solution)/shard_map/ppermute | solution.py:174

commit v13 on v11

--- a/solution.py
+++ b/solution.py
@@ -10,14 +10,14 @@
 VMEM_BYTES = 14 * 1024 * 1024
 
 
-def call(body, outs, args, spaces, flops, scratch=()):
+def call(body, outs, args, spaces, flops, scratch=(), out_space="v"):
     kinds = {"s": pltpu.SMEM, "v": pltpu.VMEM, "h": pltpu.HBM}
     moved = sum(a.size * a.dtype.itemsize for a in args) + sum(o.size * o.dtype.itemsize for o in outs)
     return pl.pallas_call(
         body,
         out_shape=outs,
         in_specs=[pl.BlockSpec(memory_space=kinds[c]) for c in spaces],
-        out_specs=[pl.BlockSpec(memory_space=pltpu.VMEM)] * len(outs),
+        out_specs=[pl.BlockSpec(memory_space=kinds[out_space])] * len(outs),
         scratch_shapes=list(scratch),
         compiler_params=pltpu.CompilerParams(vmem_limit_bytes=VMEM_BYTES),
         cost_estimate=pl.CostEstimate(flops=flops, bytes_accessed=moved, transcendentals=0),
@@ -53,7 +53,7 @@
 
 def near_kernel(where_ref, list_ref, count_ref, sigma_hbm, lower_hbm, first_0, first_1, second,
                 first_beside, second_beside,
-                first_acc, second_acc, turned_ref, sigma_ref, lower_ref, near_ref, sems):
+                first_acc, second_acc, turned_ref, sigma_ref, lower_ref, lower_turned_ref, near_ref, sems):
     lives = []
     copies = []
     for index, offset in enumerate(offsets_of(where_ref)):
@@ -93,6 +93,7 @@
     for index in (2, 3, 4):
         arrived(index)
     copies[5].wait()
+    lower_turned_ref[...] = lower_ref[...].T
 
 
 def halves(value, where_ref, scratch_ref, give_ref, keep_ref, index):
@@ -149,23 +150,30 @@
     out_ref[pl.ds(pl.multiple_of((1 - core) * half, half), half)] = other_ref[index].astype(jnp.float32)
 
 
-def link_kernel(where_ref, mine_ref, other_ref, lower_ref, first_diag_ref, second_diag_ref,
-                first_ref, link_ref, base_ref, sum_ref):
+def final_kernel(where_ref, mine_ref, other_ref, second_mine_ref, second_other_ref, lower_ref, lower_turned_ref,
+                 first_diag_ref, second_diag_ref, first_hbm, link_hbm, second_hbm,
+                 sum_ref, first_ref, link_ref, second_ref, sems):
+    copies = [
+        pltpu.make_async_copy(source, target, sems.at[index])
+        for index, (source, target) in enumerate(((first_ref, first_hbm), (link_ref, link_hbm), (second_ref, second_hbm)))
+    ]
     lower = lower_ref[...]
+    turned = lower_turned_ref[...]
     place(where_ref, mine_ref, other_ref, 0, sum_ref)
     block_first = first_diag_ref[...] + sum_ref[...]
     first_ref[...] = block_first
+    copies[0].start()
     place(where_ref, mine_ref, other_ref, 1, sum_ref)
+    place(where_ref, second_mine_ref, second_other_ref, 0, second_ref)
     high, low = split(block_first)
     link = dot(high, lower) + dot(low, lower) + sum_ref[...].T
     link_ref[...] = -link
+    copies[1].start()
     high, low = split(link)
-    base_ref[...] = second_diag_ref[...] + dot_t(lower, high) + dot_t(lower, low)
-
-
-def last_kernel(where_ref, mine_ref, other_ref, base_ref, second_ref):
-    place(where_ref, mine_ref, other_ref, 0, second_ref)
-    second_ref[...] += base_ref[...]
+    second_ref[...] += second_diag_ref[...] + dot(turned, high) + dot(turned, low)
+    copies[2].start()
+    for copy in copies:
+        copy.wait()
 
 
 def swapped(value, bit, devices):
@@ -244,10 +252,10 @@
     second_across = swapped(second, 2, devices)
     beside = swapped(first, 1, devices)
     second_beside = swapped(second, 1, devices)
-    first_acc, second_acc, turned, sorted_sigma, lower = call(
+    first_acc, second_acc, turned, sorted_sigma, lower, lower_turned = call(
         near_kernel,
         [wide, wide, jax.ShapeDtypeStruct((2 * size, width), jnp.bfloat16),
-         jax.ShapeDtypeStruct((3, size, width), jnp.bfloat16), narrow],
+         jax.ShapeDtypeStruct((3, size, width), jnp.bfloat16), narrow, narrow],
         [where, listed, count, sigma, lower_panel, *pieces, second, beside, second_beside],
         "ssshhvvvvv",
         4 * one,
@@ -285,10 +293,15 @@
     mine, other = summed(total, uppers, devices)
     second_total = chip_summed(second_give, second_keep, devices)
     second_mine, second_other = summed(second_total, uppers, devices)
-    block_first, block_link, base = call(
-        link_kernel, [wide] * 3, [where, mine, other, lower, first_diag, second_diag], "svvvvv", 4 * one, scratch
-    )
-    (block_second,) = call(last_kernel, [wide], [where, second_mine, second_other, base], "svvv", size * width)
+    block_first, block_link, block_second = call(
+        final_kernel,
+        [wide] * 3,
+        [where, mine, other, second_mine, second_other, lower, lower_turned, first_diag, second_diag],
+        "svvvvvvvv",
+        4 * one,
+        scratch * 4 + [pltpu.SemaphoreType.DMA((3,))],
+        "h",
+    )
     shape = first_panel.shape
     return column_first.reshape(shape), block_first, block_link, column_second.reshape(shape), block_second
 

time: 91.7 us -> 92.3 us (level)
  waiting for transfers between devices: 41.6 us -> 43.4 us
  starting transfers between devices: 30.9 us -> 29.8 us
    ppermute x21, waiting for transfers between devices: 31.6 us -> 33.4 us  [swapped(): return lax.ppermute(value, 'row', [(i, i ^ bit) for i in range(devices)])]
    ppermute x21, starting transfers between devices: 21.2 us -> 20.2 us  [swapped(): return lax.ppermute(value, 'row', [(i, i ^ bit) for i in range(devices)])]
    pallas_call x7 -> x6, Pallas kernels: 10.6 us -> 10.4 us  [call(): pl.pallas_call(body, out_shape=outs, in_specs=[pl.BlockSpec(memory_space=...]
  transfers between devices with their start and end apart: 24 -> 24, of which waited for: 14 -> 13; matrix products, arithmetic and copies ran while one was open for 1% -> 1% of each run, Pallas kernels for 10% -> 8%
where the time goes in v13:
time: 92.3 us; the launch traced here: 91.9 us
  waiting for transfers between devices  43.4 us (47%)
  starting transfers between devices  29.8 us (32%)
  Pallas kernels  10.4 us (11%)
  local copies, waits for them, and re-layouts  5.53 us (6%)
  between operations  1.62 us (2%)
  other arithmetic  1.1 us (1%)
    ppermute x21, waiting for transfers between devices, swapped(): return lax.ppermute(value, 'row', [(i, i ^ bit) for i in range(devices)])  33.4 us
    ppermute x21, starting transfers between devices, swapped(): return lax.ppermute(value, 'row', [(i, i ^ bit) for i in range(devices)])  20.2 us
    pallas_call x6, Pallas kernels, call(): pl.pallas_call(body, out_shape=outs, in_specs=[pl.BlockSpec(memory_space=...  10.4 us
    ppermute x3, waiting for transfers between devices, far_of(): return lax.ppermute(across, 'row', pairs)  9.99 us
    ppermute x3, starting transfers between devices, far_of(): return lax.ppermute(across, 'row', pairs)  9.63 us
    unnamed x14, local copies, waits for them, and re-layouts  5.53 us
  transfers between devices with their start and end apart: 24, of which 13 were waited for; matrix products, arithmetic and copies ran while one was open for 1% of the time, Pallas kernels for 8%

profile of v13, /device:TPU:0, one launch (start us, length us, event | category | flops | bytes accessed | tf_op | source)
XLA Modules:
  0.0 91.9 jit_solution(13890172214864776010)
XLA Ops:
  1.2 1.0 %copy-done.5 = bf16[1,1,512,512]{3,2,1,0:T(8,128)(2,1)S(1)} copy-done((bf16[1,1,512,512]{3,2,1,0:T(8,128)(2,1)S(1)}, bf16[1,1,512,512]{3,2,1,0:T(8,128)(2,1)}, u32[]{:S(2)}) %copy-start.5) | copy-done | bytes 524312
  2.3 3.0 %collective-permute-start.2 = (bf16[256,512]{1,0:T(8,128)(2,1)S(1)}, bf16[256,512]{1,0:T(8,128)(2,1)S(1)}, u32[]{:S(2)}, u32[]{:S(2)}) collective-permute-start(bf16[256,512]{1,0:T(8,128)(2,1)S(1)} %get-tuple-element.39.first_0), channel_id=1, source_target_pairs={{0,2},{1,3},{2,0},{3,1},{4,6},{5,7},{6,4},{7,5},{8,10},{9,11},{10,... | collective-permute-start | bytes 786440 | tf_op jit(solution)/shard_map/ppermute | solution.py:180
  5.4 1.9 %collective-permute-start.6 = (bf16[512,512]{1,0:T(8,128)(2,1)}, bf16[512,512]{1,0:T(8,128)(2,1)S(1)}, u32[]{:S(2)}, u32[]{:S(2)}) collective-permute-start(bf16[512,512]{1,0:T(8,128)(2,1)} %bitcast.11), channel_id=1, source_target_pairs={{0,2},{1,3},{2,0},{3,1},{4,6},{5,7},{6,4},{7,5},{8,10},{9,11},{10,... | collective-permute-start | bytes 1572872 | tf_op jit(solution)/shard_map/ppermute | solution.py:180
  7.4 5.1 %collective-permute-done.2.across_0 = bf16[256,512]{1,0:T(8,128)(2,1)S(1)} collective-permute-done((bf16[256,512]{1,0:T(8,128)(2,1)S(1)}, bf16[256,512]{1,0:T(8,128)(2,1)S(1)}, u32[]{:S(2)}, u32[]{:S(2)}) %collective-permute-start.2) | collective-permute-done | bytes 262176 | tf_op jit(solution)/shard_map/ppermute | solution.py:180
  12.4 4.1 %collective-permute-start.4 = (bf16[256,512]{1,0:T(8,128)(2,1)S(1)}, bf16[256,512]{1,0:T(8,128)(2,1)S(1)}, u32[]{:S(2)}, u32[]{:S(2)}) collective-permute-start(bf16[256,512]{1,0:T(8,128)(2,1)S(1)} %collective-permute-done.2.across_0), channel_id=1, source_target_pairs={{0,4},{1,5},{4,8},{5,9},{6,2},{7,3},{8,12},{9,13},{10,6},{11,7},{1... | collective-permute-start | bytes 786440 | tf_op jit(solution)/shard_map/ppermute | solution.py:188
  16.5 1.6 %collective-permute-done.3.across_1 = bf16[256,512]{1,0:T(8,128)(2,1)S(1)} collective-permute-done((bf16[256,512]{1,0:T(8,128)(2,1)S(1)}, bf16[256,512]{1,0:T(8,128)(2,1)S(1)}, u32[]{:S(2)}, u32[]{:S(2)}) %collective-permute-start.3) | collective-permute-done | bytes 262176 | tf_op jit(solution)/shard_map/ppermute | solution.py:180
  18.1 4.1 %collective-permute-start.5 = (bf16[256,512]{1,0:T(8,128)(2,1)S(1)}, bf16[256,512]{1,0:T(8,128)(2,1)S(1)}, u32[]{:S(2)}, u32[]{:S(2)}) collective-permute-start(bf16[256,512]{1,0:T(8,128)(2,1)S(1)} %collective-permute-done.3.across_1), channel_id=1, source_target_pairs={{0,4},{1,5},{4,8},{5,9},{6,2},{7,3},{8,12},{9,13},{10,6},{11,7},{1... | collective-permute-start | bytes 786440 | tf_op jit(solution)/shard_map/ppermute | solution.py:188
  22.8 1.7 %copy-done = bf16[1,1,5,512,512]{4,3,2,1,0:T(8,128)(2,1)S(1)} copy-done((bf16[1,1,5,512,512]{4,3,2,1,0:T(8,128)(2,1)S(1)}, bf16[1,1,5,512,512]{4,3,2,1,0:T(8,128)(2,1)}, u32[]{:S(2)}) %copy-start) | copy-done | bytes 2621464
  24.5 1.0 %copy-done.3 = bf16[512,512]{1,0:T(8,128)(2,1)S(1)} copy-done((bf16[512,512]{1,0:T(8,128)(2,1)S(1)}, bf16[512,512]{1,0:T(8,128)(2,1)}, u32[]{:S(2)}) %copy-start.3) | copy-done | bytes 524312
  25.6 1.0 %copy-done.4 = bf16[1,1,512,512]{3,2,1,0:T(8,128)(2,1)S(1)} copy-done((bf16[1,1,512,512]{3,2,1,0:T(8,128)(2,1)S(1)}, bf16[1,1,512,512]{3,2,1,0:T(8,128)(2,1)}, u32[]{:S(2)}) %copy-start.4) | copy-done | bytes 524312
  26.6 0.7 copy-done.6
  27.3 2.8 %shard_map.120 = (f32[512,512]{1,0:T(8,128)S(1)}, f32[512,512]{1,0:T(8,128)S(1)}, bf16[1024,512]{1,0:T(8,128)(2,1)S(1)}, bf16[3,512,512]{2,1,0:T(8,128)(2,1)S(1)...) custom-call(s32[1]{0:T(128)} %bitcast.where_ref, s32[5]{0:T(128)S(1)} %bitcast.15, s32[1]{0:T(128)} %bitcast.8.count_ref, ...), custom_call_target="tpu_custom_call" | custom-call | flops 1073741824 | bytes 11010076 | tf_op jit(solution)/shard_map/pallas_call | solution.py:16
  30.3 1.5 %collective-permute-start.8 = (bf16[512,512]{1,0:T(8,128)(2,1)S(1)}, bf16[512,512]{1,0:T(8,128)(2,1)S(1)}, u32[]{:S(2)}, u32[]{:S(2)}) collective-permute-start(bf16[512,512]{1,0:T(8,128)(2,1)S(1)} %collective-permute-done.6.across), channel_id=1, source_target_pairs={{0,4},{1,5},{2,0},{3,1},{4,8},{5,9},{6,2},{7,3},{8,12},{9,13},{10,... | collective-permute-start | bytes 1572872 | tf_op jit(solution)/shard_map/ppermute | solution.py:188
  32.2 2.3 %shard_map.121 = (bf16[512,512]{1,0:T(8,128)(2,1)}, bf16[512,512]{1,0:T(8,128)(2,1)S(1)}, bf16[2,256,512]{2,1,0:T(8,128)(2,1)S(1)}, f32[2,256,512]{2,1,0:T(8,128)S(1)}) custom-call(s32[1]{0:T(128)} %bitcast.where_ref, f32[512,512]{1,0:T(8,128)S(1)} %get-tuple-element.42.acc_in, bf16[256,512]{1,0:T(8,128)(2,1)S(1)} %collective-permute-done.2.across_0, ...), custom_call_target="tpu_custom_call" | custom-call | flops 1342177280 | bytes 7864324 | tf_op jit(solution)/shard_map/pallas_call | solution.py:16
  34.6 10.0 %collective-permute-done.8.far = bf16[512,512]{1,0:T(8,128)(2,1)S(1)} collective-permute-done((bf16[512,512]{1,0:T(8,128)(2,1)S(1)}, bf16[512,512]{1,0:T(8,128)(2,1)S(1)}, u32[]{:S(2)}, u32[]{:S(2)}) %collective-permute-start.8) | collective-permute-done | bytes 524320 | tf_op jit(solution)/shard_map/ppermute | solution.py:188
  45.4 0.7 shard_map.122.acc_in
  46.7 1.6 %shard_map.123 = (bf16[512,512]{1,0:T(8,128)(2,1)}, bf16[1,256,512]{2,1,0:T(8,128)(2,1)S(1)}, f32[1,256,512]{2,1,0:T(8,128)S(1)}) custom-call(s32[1]{0:T(128)} %bitcast.where_ref, f32[512,512]{1,0:T(8,128)S(1)} %shard_map.122.acc_in, bf16[512,512]{1,0:T(8,128)(2,1)S(1)} %collective-permute-done.8.far, bf16[512,512]{1,0:T(8,128)(2,1)S(1)} %collective-permute-done.9.rest, ...), custom_call_target="tpu_custom_call" | custom-call | flops 805306368 | bytes 6029316 | tf_op jit(solution)/shard_map/pallas_call | solution.py:16
  48.2 5.6 %collective-permute-done.11 = bf16[2,128,512]{2,1,0:T(8,128)(2,1)S(1)} collective-permute-done((bf16[2,128,512]{2,1,0:T(8,128)(2,1)S(1)}, bf16[2,128,512]{2,1,0:T(8,128)(2,1)S(1)}, u32[]{:S(2)}, u32[]{:S(2)}) %collective-permute-start.11) | collective-permute-done | bytes 262176 | tf_op jit(solution)/shard_map/ppermute | solution.py:180
  54.0 1.5 %collective-permute-start.12 = (bf16[2,64,512]{2,1,0:T(8,128)(2,1)S(1)}, bf16[2,64,512]{2,1,0:T(8,128)(2,1)S(1)}, u32[]{:S(2)}, u32[]{:S(2)}) collective-permute-start(bf16[2,64,512]{2,1,0:T(8,128)(2,1)S(1)} %select_convert_fusion.2), channel_id=1, source_target_pairs={{0,4},{1,5},{2,6},{3,7},{4,0},{5,1},{6,2},{7,3},{8,12},{9,13},{10,... | collective-permute-start | bytes 393224 | tf_op jit(solution)/shard_map/ppermute | solution.py:180
  56.2 3.8 %collective-permute-done.12 = bf16[2,64,512]{2,1,0:T(8,128)(2,1)S(1)} collective-permute-done((bf16[2,64,512]{2,1,0:T(8,128)(2,1)S(1)}, bf16[2,64,512]{2,1,0:T(8,128)(2,1)S(1)}, u32[]{:S(2)}, u32[]{:S(2)}) %collective-permute-start.12) | collective-permute-done | bytes 131104 | tf_op jit(solution)/shard_map/ppermute | solution.py:180
  60.0 2.5 %collective-permute-start.13 = (bf16[2,64,512]{2,1,0:T(8,128)(2,1)S(1)}, bf16[2,64,512]{2,1,0:T(8,128)(2,1)S(1)}, u32[]{:S(2)}, u32[]{:S(2)}) collective-permute-start(bf16[2,64,512]{2,1,0:T(8,128)(2,1)S(1)} %add_convert_fusion.1), channel_id=1, source_target_pairs={{0,8},{1,9},{2,10},{3,11},{4,12},{5,13},{6,14},{7,15},{8,0},{9,1},... | collective-permute-start | bytes 393224 | tf_op jit(solution)/shard_map/ppermute | solution.py:180
  62.6 0.6 collective-permute-start.19
  63.3 5.6 %collective-permute-done.13 = bf16[2,64,512]{2,1,0:T(8,128)(2,1)S(1)} collective-permute-done((bf16[2,64,512]{2,1,0:T(8,128)(2,1)S(1)}, bf16[2,64,512]{2,1,0:T(8,128)(2,1)S(1)}, u32[]{:S(2)}, u32[]{:S(2)}) %collective-permute-start.13) | collective-permute-done | bytes 131104 | tf_op jit(solution)/shard_map/ppermute | solution.py:180
  69.1 3.1 %collective-permute-start.20 = (bf16[1,64,512]{2,1,0:T(8,128)(2,1)S(1)}, bf16[1,64,512]{2,1,0:T(8,128)(2,1)S(1)}, u32[]{:S(2)}, u32[]{:S(2)}) collective-permute-start(bf16[1,64,512]{2,1,0:T(8,128)(2,1)S(1)} %add_convert_fusion.3), channel_id=1, source_target_pairs={{0,8},{1,9},{2,10},{3,11},{4,12},{5,13},{6,14},{7,15},{8,0},{9,1},... | collective-permute-start | bytes 196616 | tf_op jit(solution)/shard_map/ppermute | solution.py:180
  72.2 2.8 %collective-permute-done.14 = bf16[2,64,512]{2,1,0:T(8,128)(2,1)S(1)} collective-permute-done((bf16[2,64,512]{2,1,0:T(8,128)(2,1)S(1)}, bf16[2,64,512]{2,1,0:T(8,128)(2,1)S(1)}, u32[]{:S(2)}, u32[]{:S(2)}) %collective-permute-start.14) | collective-permute-done | bytes 131104 | tf_op jit(solution)/shard_map/ppermute | solution.py:180
  75.0 1.4 %collective-permute-start.21 = (bf16[1,64,512]{2,1,0:T(8,128)(2,1)S(1)}, bf16[1,64,512]{2,1,0:T(8,128)(2,1)S(1)}, u32[]{:S(2)}, u32[]{:S(2)}) collective-permute-start(bf16[1,64,512]{2,1,0:T(8,128)(2,1)S(1)} %add_convert_fusion.2), channel_id=1, source_target_pairs={{0,4},{1,5},{2,6},{3,7},{4,0},{5,1},{6,2},{7,3},{8,12},{9,13},{10,... | collective-permute-start | bytes 196616 | tf_op jit(solution)/shard_map/ppermute | solution.py:180
  76.5 2.3 %collective-permute-start.15 = (bf16[2,128,512]{2,1,0:T(8,128)(2,1)S(1)}, bf16[2,128,512]{2,1,0:T(8,128)(2,1)S(1)}, u32[]{:S(2)}, u32[]{:S(2)}) collective-permute-start(bf16[2,128,512]{2,1,0:T(8,128)(2,1)S(1)} %pad_maximum_fusion.2), channel_id=1, source_target_pairs={{0,2},{1,3},{2,0},{3,1},{4,6},{5,7},{6,4},{7,5},{8,10},{9,11},{10,... | collective-permute-start | bytes 786440 | tf_op jit(solution)/shard_map/ppermute | solution.py:180
  79.4 1.6 %collective-permute-start.22 = (bf16[1,128,512]{2,1,0:T(8,128)(2,1)S(1)}, bf16[1,128,512]{2,1,0:T(8,128)(2,1)S(1)}, u32[]{:S(2)}, u32[]{:S(2)}) collective-permute-start(bf16[1,128,512]{2,1,0:T(8,128)(2,1)S(1)} %pad_maximum_fusion.4), channel_id=1, source_target_pairs={{0,2},{1,3},{2,0},{3,1},{4,6},{5,7},{6,4},{7,5},{8,10},{9,11},{10,... | collective-permute-start | bytes 393224 | tf_op jit(solution)/shard_map/ppermute | solution.py:180
  81.0 4.8 %collective-permute-done.15 = bf16[2,128,512]{2,1,0:T(8,128)(2,1)S(1)} collective-permute-done((bf16[2,128,512]{2,1,0:T(8,128)(2,1)S(1)}, bf16[2,128,512]{2,1,0:T(8,128)(2,1)S(1)}, u32[]{:S(2)}, u32[]{:S(2)}) %collective-permute-start.15) | collective-permute-done | bytes 262176 | tf_op jit(solution)/shard_map/ppermute | solution.py:180
  86.0 1.2 %collective-permute-done.22 = bf16[1,128,512]{2,1,0:T(8,128)(2,1)S(1)} collective-permute-done((bf16[1,128,512]{2,1,0:T(8,128)(2,1)S(1)}, bf16[1,128,512]{2,1,0:T(8,128)(2,1)S(1)}, u32[]{:S(2)}, u32[]{:S(2)}) %collective-permute-start.22) | collective-permute-done | bytes 131104 | tf_op jit(solution)/shard_map/ppermute | solution.py:180
  87.4 1.5 %collective-permute-done.23.second_other_ref = bf16[1,256,512]{2,1,0:T(8,128)(2,1)S(1)} collective-permute-done((bf16[1,256,512]{2,1,0:T(8,128)(2,1)S(1)}, bf16[1,256,512]{2,1,0:T(8,128)(2,1)S(1)}, u32[]{:S(2)}, u32[]{:S(2)}) %collective-permute-start.23) | collective-permute-done | bytes 262176 | tf_op jit(solution)/shard_map/ppermute | solution.py:180
  88.9 3.0 %shard_map.124 = (f32[512,512]{1,0:T(8,128)}, f32[512,512]{1,0:T(8,128)}, f32[512,512]{1,0:T(8,128)}) custom-call(s32[1]{0:T(128)} %bitcast.where_ref, bf16[2,256,512]{2,1,0:T(8,128)(2,1)S(1)} %pad_maximum_fusion.1.mine_ref, bf16[2,256,512]{2,1,0:T(8,128)(2,1)S(1)} %collective-permute-done.16.other_ref, ...), custom_call_target="tpu_custom_call" | custom-call | flops 1073741824 | bytes 7864324 | tf_op jit(solution)/shard_map/pallas_call | solution.py:16
  (59 shorter events, 4.9 us)
Async XLA Ops:
  0.6 22.1 %collective-permute-start.1 = (bf16[512,512]{1,0:T(8,128)(2,1)}, bf16[512,512]{1,0:T(8,128)(2,1)S(1)}, u32[]{:S(2)}, u32[]{:S(2)}) collective-permute-start(bf16[512,512]{1,0:T(8,128)(2,1)} %bitcast.10), channel_id=1, source_target_pairs={{0,1},{1,0},{2,3},{3,2},{4,5},{5,4},{6,7},{7,6},{8,9},{9,8},{10,11... | collective-permute-start | bytes 1572872 | tf_op jit(solution)/shard_map/ppermute | solution.py:180
  1.2 21.6 %collective-permute-start = (bf16[512,512]{1,0:T(8,128)(2,1)}, bf16[512,512]{1,0:T(8,128)(2,1)S(1)}, u32[]{:S(2)}, u32[]{:S(2)}) collective-permute-start(bf16[512,512]{1,0:T(8,128)(2,1)} %bitcast.13), channel_id=1, source_target_pairs={{0,1},{1,0},{2,3},{3,2},{4,5},{5,4},{6,7},{7,6},{8,9},{9,8},{10,11... | collective-permute-start | bytes 1572872 | tf_op jit(solution)/shard_map/ppermute | solution.py:180
  1.2 1.0 %copy-start.5 = (bf16[1,1,512,512]{3,2,1,0:T(8,128)(2,1)S(1)}, bf16[1,1,512,512]{3,2,1,0:T(8,128)(2,1)}, u32[]{:S(2)}) copy-start(bf16[1,1,512,512]{3,2,1,0:T(8,128)(2,1)} %param.9) | copy-start | bytes 1572868
  2.3 10.1 %collective-permute-start.2 = (bf16[256,512]{1,0:T(8,128)(2,1)S(1)}, bf16[256,512]{1,0:T(8,128)(2,1)S(1)}, u32[]{:S(2)}, u32[]{:S(2)}) collective-permute-start(bf16[256,512]{1,0:T(8,128)(2,1)S(1)} %get-tuple-element.39.first_0), channel_id=1, source_target_pairs={{0,2},{1,3},{2,0},{3,1},{4,6},{5,7},{6,4},{7,5},{8,10},{9,11},{10,... | collective-permute-start | bytes 786440 | tf_op jit(solution)/shard_map/ppermute | solution.py:180
  5.3 12.7 %collective-permute-start.3 = (bf16[256,512]{1,0:T(8,128)(2,1)S(1)}, bf16[256,512]{1,0:T(8,128)(2,1)S(1)}, u32[]{:S(2)}, u32[]{:S(2)}) collective-permute-start(bf16[256,512]{1,0:T(8,128)(2,1)S(1)} %get-tuple-element.40.first_1), channel_id=1, source_target_pairs={{0,2},{1,3},{2,0},{3,1},{4,6},{5,7},{6,4},{7,5},{8,10},{9,11},{10,... | collective-permute-start | bytes 786440 | tf_op jit(solution)/shard_map/ppermute | solution.py:180
  5.4 24.7 %collective-permute-start.6 = (bf16[512,512]{1,0:T(8,128)(2,1)}, bf16[512,512]{1,0:T(8,128)(2,1)S(1)}, u32[]{:S(2)}, u32[]{:S(2)}) collective-permute-start(bf16[512,512]{1,0:T(8,128)(2,1)} %bitcast.11), channel_id=1, source_target_pairs={{0,2},{1,3},{2,0},{3,1},{4,6},{5,7},{6,4},{7,5},{8,10},{9,11},{10,... | collective-permute-start | bytes 1572872 | tf_op jit(solution)/shard_map/ppermute | solution.py:180
  12.4 17.7 %collective-permute-start.4 = (bf16[256,512]{1,0:T(8,128)(2,1)S(1)}, bf16[256,512]{1,0:T(8,128)(2,1)S(1)}, u32[]{:S(2)}, u32[]{:S(2)}) collective-permute-start(bf16[256,512]{1,0:T(8,128)(2,1)S(1)} %collective-permute-done.2.across_0), channel_id=1, source_target_pairs={{0,4},{1,5},{4,8},{5,9},{6,2},{7,3},{8,12},{9,13},{10,6},{11,7},{1... | collective-permute-start | bytes 786440 | tf_op jit(solution)/shard_map/ppermute | solution.py:188
  18.1 12.0 %collective-permute-start.5 = (bf16[256,512]{1,0:T(8,128)(2,1)S(1)}, bf16[256,512]{1,0:T(8,128)(2,1)S(1)}, u32[]{:S(2)}, u32[]{:S(2)}) collective-permute-start(bf16[256,512]{1,0:T(8,128)(2,1)S(1)} %collective-permute-done.3.across_1), channel_id=1, source_target_pairs={{0,4},{1,5},{4,8},{5,9},{6,2},{7,3},{8,12},{9,13},{10,6},{11,7},{1... | collective-permute-start | bytes 786440 | tf_op jit(solution)/shard_map/ppermute | solution.py:188
  22.8 1.7 %copy-start = (bf16[1,1,5,512,512]{4,3,2,1,0:T(8,128)(2,1)S(1)}, bf16[1,1,5,512,512]{4,3,2,1,0:T(8,128)(2,1)}, u32[]{:S(2)}) copy-start(bf16[1,1,5,512,512]{4,3,2,1,0:T(8,128)(2,1)} %param.8) | copy-start | bytes 7864324
  24.5 1.0 %copy-start.3 = (bf16[512,512]{1,0:T(8,128)(2,1)S(1)}, bf16[512,512]{1,0:T(8,128)(2,1)}, u32[]{:S(2)}) copy-start(bf16[512,512]{1,0:T(8,128)(2,1)} %lower_hbm.1) | copy-start | bytes 1572868
  25.6 1.0 %copy-start.4 = (bf16[1,1,512,512]{3,2,1,0:T(8,128)(2,1)S(1)}, bf16[1,1,512,512]{3,2,1,0:T(8,128)(2,1)}, u32[]{:S(2)}) copy-start(bf16[1,1,512,512]{3,2,1,0:T(8,128)(2,1)} %param.10) | copy-start | bytes 1572868
  26.6 0.7 copy-start.6
  30.2 2.0 %collective-permute-start.7 = (bf16[512,512]{1,0:T(8,128)(2,1)S(1)}, bf16[512,512]{1,0:T(8,128)(2,1)S(1)}, u32[]{:S(2)}, u32[]{:S(2)}) collective-permute-start(bf16[512,512]{1,0:T(8,128)(2,1)S(1)} %pad_maximum_fusion), channel_id=1, source_target_pairs={{0,1},{1,0},{2,3},{3,2},{4,5},{5,4},{6,7},{7,6},{8,9},{9,8},{10,11... | collective-permute-start | bytes 1572872 | tf_op jit(solution)/shard_map/ppermute | solution.py:180
  30.3 14.3 %collective-permute-start.8 = (bf16[512,512]{1,0:T(8,128)(2,1)S(1)}, bf16[512,512]{1,0:T(8,128)(2,1)S(1)}, u32[]{:S(2)}, u32[]{:S(2)}) collective-permute-start(bf16[512,512]{1,0:T(8,128)(2,1)S(1)} %collective-permute-done.6.across), channel_id=1, source_target_pairs={{0,4},{1,5},{2,0},{3,1},{4,8},{5,9},{6,2},{7,3},{8,12},{9,13},{10,... | collective-permute-start | bytes 1572872 | tf_op jit(solution)/shard_map/ppermute | solution.py:188
  34.5 10.3 %collective-permute-start.10 = (bf16[2,256,512]{2,1,0:T(8,128)(2,1)S(1)}, bf16[2,256,512]{2,1,0:T(8,128)(2,1)S(1)}, u32[]{:S(2)}, u32[]{:S(2)}) collective-permute-start(bf16[2,256,512]{2,1,0:T(8,128)(2,1)S(1)} %get-tuple-element.60), channel_id=1, source_target_pairs={{0,1},{1,0},{2,3},{3,2},{4,5},{5,4},{6,7},{7,6},{8,9},{9,8},{10,11... | collective-permute-start | bytes 1572872 | tf_op jit(solution)/shard_map/ppermute | solution.py:180
  44.7 2.0 %collective-permute-start.9 = (bf16[512,512]{1,0:T(8,128)(2,1)S(1)}, bf16[512,512]{1,0:T(8,128)(2,1)S(1)}, u32[]{:S(2)}, u32[]{:S(2)}) collective-permute-start(bf16[512,512]{1,0:T(8,128)(2,1)S(1)} %broadcast_select_fusion), channel_id=1, source_target_pairs={{0,1},{1,0},{2,3},{3,2},{4,5},{5,4},{6,7},{7,6},{8,9},{9,8},{10,11... | collective-permute-start | bytes 1572872 | tf_op jit(solution)/shard_map/ppermute | solution.py:180
  45.0 8.8 %collective-permute-start.11 = (bf16[2,128,512]{2,1,0:T(8,128)(2,1)S(1)}, bf16[2,128,512]{2,1,0:T(8,128)(2,1)S(1)}, u32[]{:S(2)}, u32[]{:S(2)}) collective-permute-start(bf16[2,128,512]{2,1,0:T(8,128)(2,1)S(1)} %select_convert_fusion), channel_id=1, source_target_pairs={{0,2},{1,3},{2,0},{3,1},{4,6},{5,7},{6,4},{7,5},{8,10},{9,11},{10,... | collective-permute-start | bytes 786440 | tf_op jit(solution)/shard_map/ppermute | solution.py:180
  53.9 1.7 %collective-permute-start.17 = (bf16[1,256,512]{2,1,0:T(8,128)(2,1)S(1)}, bf16[1,256,512]{2,1,0:T(8,128)(2,1)S(1)}, u32[]{:S(2)}, u32[]{:S(2)}) collective-permute-start(bf16[1,256,512]{2,1,0:T(8,128)(2,1)S(1)} %get-tuple-element.63), channel_id=1, source_target_pairs={{0,1},{1,0},{2,3},{3,2},{4,5},{5,4},{6,7},{7,6},{8,9},{9,8},{10,11... | collective-permute-start | bytes 786440 | tf_op jit(solution)/shard_map/ppermute | solution.py:180
  54.0 6.0 %collective-permute-start.12 = (bf16[2,64,512]{2,1,0:T(8,128)(2,1)S(1)}, bf16[2,64,512]{2,1,0:T(8,128)(2,1)S(1)}, u32[]{:S(2)}, u32[]{:S(2)}) collective-permute-start(bf16[2,64,512]{2,1,0:T(8,128)(2,1)S(1)} %select_convert_fusion.2), channel_id=1, source_target_pairs={{0,4},{1,5},{2,6},{3,7},{4,0},{5,1},{6,2},{7,3},{8,12},{9,13},{10,... | collective-permute-start | bytes 393224 | tf_op jit(solution)/shard_map/ppermute | solution.py:180
  55.7 6.9 %collective-permute-start.18 = (bf16[1,128,512]{2,1,0:T(8,128)(2,1)S(1)}, bf16[1,128,512]{2,1,0:T(8,128)(2,1)S(1)}, u32[]{:S(2)}, u32[]{:S(2)}) collective-permute-start(bf16[1,128,512]{2,1,0:T(8,128)(2,1)S(1)} %select_convert_fusion.1), channel_id=1, source_target_pairs={{0,2},{1,3},{2,0},{3,1},{4,6},{5,7},{6,4},{7,5},{8,10},{9,11},{10,... | collective-permute-start | bytes 393224 | tf_op jit(solution)/shard_map/ppermute | solution.py:180
  60.0 8.9 %collective-permute-start.13 = (bf16[2,64,512]{2,1,0:T(8,128)(2,1)S(1)}, bf16[2,64,512]{2,1,0:T(8,128)(2,1)S(1)}, u32[]{:S(2)}, u32[]{:S(2)}) collective-permute-start(bf16[2,64,512]{2,1,0:T(8,128)(2,1)S(1)} %add_convert_fusion.1), channel_id=1, source_target_pairs={{0,8},{1,9},{2,10},{3,11},{4,12},{5,13},{6,14},{7,15},{8,0},{9,1},... | collective-permute-start | bytes 393224 | tf_op jit(solution)/shard_map/ppermute | solution.py:180
  62.6 6.4 %collective-permute-start.19 = (bf16[1,64,512]{2,1,0:T(8,128)(2,1)S(1)}, bf16[1,64,512]{2,1,0:T(8,128)(2,1)S(1)}, u32[]{:S(2)}, u32[]{:S(2)}) collective-permute-start(bf16[1,64,512]{2,1,0:T(8,128)(2,1)S(1)} %select_convert_fusion.3), channel_id=1, source_target_pairs={{0,4},{1,5},{2,6},{3,7},{4,0},{5,1},{6,2},{7,3},{8,12},{9,13},{10,... | collective-permute-start | bytes 196616 | tf_op jit(solution)/shard_map/ppermute | solution.py:180
  69.0 19.9 %copy-start.1 = (f32[512,512]{1,0:T(8,128)S(1)}, f32[512,512]{1,0:T(8,128)}, u32[]{:S(2)}) copy-start(f32[512,512]{1,0:T(8,128)} %first_diag_ref.1) | copy-start | bytes 3145732
  69.0 19.9 %copy-start.2 = (f32[512,512]{1,0:T(8,128)S(1)}, f32[512,512]{1,0:T(8,128)}, u32[]{:S(2)}) copy-start(f32[512,512]{1,0:T(8,128)} %second_diag_ref.1) | copy-start | bytes 3145732
  69.0 5.9 %collective-permute-start.14 = (bf16[2,64,512]{2,1,0:T(8,128)(2,1)S(1)}, bf16[2,64,512]{2,1,0:T(8,128)(2,1)S(1)}, u32[]{:S(2)}, u32[]{:S(2)}) collective-permute-start(bf16[2,64,512]{2,1,0:T(8,128)(2,1)S(1)} %add_convert_fusion), channel_id=1, source_target_pairs={{0,4},{1,5},{2,6},{3,7},{4,0},{5,1},{6,2},{7,3},{8,12},{9,13},{10,... | collective-permute-start | bytes 393224 | tf_op jit(solution)/shard_map/ppermute | solution.py:180
  69.1 5.9 %collective-permute-start.20 = (bf16[1,64,512]{2,1,0:T(8,128)(2,1)S(1)}, bf16[1,64,512]{2,1,0:T(8,128)(2,1)S(1)}, u32[]{:S(2)}, u32[]{:S(2)}) collective-permute-start(bf16[1,64,512]{2,1,0:T(8,128)(2,1)S(1)} %add_convert_fusion.3), channel_id=1, source_target_pairs={{0,8},{1,9},{2,10},{3,11},{4,12},{5,13},{6,14},{7,15},{8,0},{9,1},... | collective-permute-start | bytes 196616 | tf_op jit(solution)/shard_map/ppermute | solution.py:180
  75.0 4.3 %collective-permute-start.21 = (bf16[1,64,512]{2,1,0:T(8,128)(2,1)S(1)}, bf16[1,64,512]{2,1,0:T(8,128)(2,1)S(1)}, u32[]{:S(2)}, u32[]{:S(2)}) collective-permute-start(bf16[1,64,512]{2,1,0:T(8,128)(2,1)S(1)} %add_convert_fusion.2), channel_id=1, source_target_pairs={{0,4},{1,5},{2,6},{3,7},{4,0},{5,1},{6,2},{7,3},{8,12},{9,13},{10,... | collective-permute-start | bytes 196616 | tf_op jit(solution)/shard_map/ppermute | solution.py:180
  76.5 9.4 %collective-permute-start.15 = (bf16[2,128,512]{2,1,0:T(8,128)(2,1)S(1)}, bf16[2,128,512]{2,1,0:T(8,128)(2,1)S(1)}, u32[]{:S(2)}, u32[]{:S(2)}) collective-permute-start(bf16[2,128,512]{2,1,0:T(8,128)(2,1)S(1)} %pad_maximum_fusion.2), channel_id=1, source_target_pairs={{0,2},{1,3},{2,0},{3,1},{4,6},{5,7},{6,4},{7,5},{8,10},{9,11},{10,... | collective-permute-start | bytes 786440 | tf_op jit(solution)/shard_map/ppermute | solution.py:180
  79.4 7.8 %collective-permute-start.22 = (bf16[1,128,512]{2,1,0:T(8,128)(2,1)S(1)}, bf16[1,128,512]{2,1,0:T(8,128)(2,1)S(1)}, u32[]{:S(2)}, u32[]{:S(2)}) collective-permute-start(bf16[1,128,512]{2,1,0:T(8,128)(2,1)S(1)} %pad_maximum_fusion.4), channel_id=1, source_target_pairs={{0,2},{1,3},{2,0},{3,1},{4,6},{5,7},{6,4},{7,5},{8,10},{9,11},{10,... | collective-permute-start | bytes 393224 | tf_op jit(solution)/shard_map/ppermute | solution.py:180
  86.0 2.9 %collective-permute-start.16 = (bf16[2,256,512]{2,1,0:T(8,128)(2,1)S(1)}, bf16[2,256,512]{2,1,0:T(8,128)(2,1)S(1)}, u32[]{:S(2)}, u32[]{:S(2)}) collective-permute-start(bf16[2,256,512]{2,1,0:T(8,128)(2,1)S(1)} %pad_maximum_fusion.1.mine_ref), channel_id=1, source_target_pairs={{0,1},{1,0},{2,3},{3,2},{4,5},{5,4},{6,7},{7,6},{8,9},{9,8},{10,11... | collective-permute-start | bytes 1572872 | tf_op jit(solution)/shard_map/ppermute | solution.py:180
  87.3 1.6 %collective-permute-start.23 = (bf16[1,256,512]{2,1,0:T(8,128)(2,1)S(1)}, bf16[1,256,512]{2,1,0:T(8,128)(2,1)S(1)}, u32[]{:S(2)}, u32[]{:S(2)}) collective-permute-start(bf16[1,256,512]{2,1,0:T(8,128)(2,1)S(1)} %pad_maximum_fusion.3.second_mine_ref), channel_id=1, source_target_pairs={{0,1},{1,0},{2,3},{3,2},{4,5},{5,4},{6,7},{7,6},{8,9},{9,8},{10,11... | collective-permute-start | bytes 786440 | tf_op jit(solution)/shard_map/ppermute | solution.py:180

commit v14 on v13

--- a/solution.py
+++ b/solution.py
@@ -193,12 +193,13 @@
     return swapped(jnp.concatenate(pieces, axis=0), 1, devices)
 
 
-def core_summed(give, keep, uppers, devices):
-    return halved(keep + swapped(give, 1, devices).astype(jnp.float32), uppers[1])
-
-
-def chip_summed(give, keep, devices):
-    return keep + swapped(give, 2, devices).astype(jnp.float32)
+def core_summed(give, keep, devices):
+    return keep + swapped(give, 1, devices).astype(jnp.float32)
+
+
+def step_summed(total, b, uppers, devices):
+    give, keep = halved(total, uppers[b])
+    return keep + swapped(give, 2 ** b, devices).astype(jnp.float32)
 
 
 def halved(total, upper):
@@ -207,14 +208,13 @@
     return jnp.where(upper, low, high).astype(jnp.bfloat16), jnp.where(upper, high, low)
 
 
-def summed(total, uppers, devices):
-    last = len(uppers) - 1
-    for b in range(2, last):
-        give, keep = halved(total, uppers[b])
-        total = keep + swapped(give, 2 ** b, devices).astype(jnp.float32)
+def summed(total, order, uppers, devices):
+    halve, swap, double = order
+    for b in halve:
+        total = step_summed(total, b, uppers, devices)
     own = total.astype(jnp.bfloat16)
-    gathered = (own.astype(jnp.float32) + swapped(own, 2 ** last, devices).astype(jnp.float32)).astype(jnp.bfloat16)
-    for b in range(last - 1, 0, -1):
+    gathered = (own.astype(jnp.float32) + swapped(own, 2 ** swap, devices).astype(jnp.float32)).astype(jnp.bfloat16)
+    for b in double:
         other = swapped(gathered, 2 ** b, devices)
         low = jnp.where(uppers[b], other, gathered)
         high = jnp.where(uppers[b], gathered, other)
@@ -274,9 +274,9 @@
         scratch,
     )
     give, second_across = barrier((give, second_across))
-    give, keep = core_summed(give, keep, uppers, devices)
+    total = core_summed(give, keep, devices)
     second_rest = rest_of([second_across], [second_far], give_across, devices)
-    total = chip_summed(give, keep, devices)
+    total = step_summed(total, 1, uppers, devices)
     (second_acc,) = call(
         across_kernel, [wide], [second_acc, column_again, lower, second_across, sorted_sigma], "vvvvv", 2 * one
     )
@@ -288,11 +288,12 @@
         3 * one,
         scratch,
     )
-    second_give, total = barrier((second_give, total))
-    second_give, second_keep = core_summed(second_give, second_keep, uppers, devices)
-    mine, other = summed(total, uppers, devices)
-    second_total = chip_summed(second_give, second_keep, devices)
-    second_mine, second_other = summed(second_total, uppers, devices)
+    last = len(uppers) - 1
+    second_total = core_summed(second_give, second_keep, devices)
+    mine, other = summed(total, (range(2, last), last, range(last - 1, 0, -1)), uppers, devices)
+    second_mine, second_other = summed(
+        second_total, (range(2, last + 1), 1, range(last, 1, -1)), uppers, devices
+    )
     block_first, block_link, block_second = call(
         final_kernel,
         [wide] * 3,

time: 92.3 us -> 89.3 us (0.967)
  waiting for transfers between devices: 43.4 us -> 40.6 us
    ppermute x21, waiting for transfers between devices: 33.4 us -> 30.5 us  [swapped(): return lax.ppermute(value, 'row', [(i, i ^ bit) for i in range(devices)])]
  transfers between devices with their start and end apart: 24 -> 24, of which waited for: 13 -> 12; matrix products, arithmetic and copies ran while one was open for 1% -> 1% of each run, Pallas kernels for 8% -> 8%
where the time goes in v14:
time: 89.3 us; the launch traced here: 89 us
  waiting for transfers between devices  40.6 us (45%)
  starting transfers between devices  29.7 us (33%)
  Pallas kernels  10.4 us (12%)
  local copies, waits for them, and re-layouts  5.53 us (6%)
  between operations  1.63 us (2%)
  other arithmetic  1.12 us (1%)
    ppermute x21, waiting for transfers between devices, swapped(): return lax.ppermute(value, 'row', [(i, i ^ bit) for i in range(devices)])  30.5 us
    ppermute x21, starting transfers between devices, swapped(): return lax.ppermute(value, 'row', [(i, i ^ bit) for i in range(devices)])  20 us
    pallas_call x6, Pallas kernels, call(): pl.pallas_call(body, out_shape=outs, in_specs=[pl.BlockSpec(memory_space=...  10.4 us
    ppermute x3, waiting for transfers between devices, far_of(): return lax.ppermute(across, 'row', pairs)  10.1 us
    ppermute x3, starting transfers between devices, far_of(): return lax.ppermute(across, 'row', pairs)  9.66 us
    unnamed x14, local copies, waits for them, and re-layouts  5.53 us
  transfers between devices with their start and end apart: 24, of which 12 were waited for; matrix products, arithmetic and copies ran while one was open for 1% of the time, Pallas kernels for 8%

profile of v14, /device:TPU:0, one launch (start us, length us, event | category | flops | bytes accessed | tf_op | source)
XLA Modules:
  0.0 89.0 jit_solution(11865099674016140656)
XLA Ops:
  1.2 1.0 %copy-done.5 = bf16[1,1,512,512]{3,2,1,0:T(8,128)(2,1)S(1)} copy-done((bf16[1,1,512,512]{3,2,1,0:T(8,128)(2,1)S(1)}, bf16[1,1,512,512]{3,2,1,0:T(8,128)(2,1)}, u32[]{:S(2)}) %copy-start.5) | copy-done | bytes 524312
  2.3 3.0 %collective-permute-start.2 = (bf16[256,512]{1,0:T(8,128)(2,1)S(1)}, bf16[256,512]{1,0:T(8,128)(2,1)S(1)}, u32[]{:S(2)}, u32[]{:S(2)}) collective-permute-start(bf16[256,512]{1,0:T(8,128)(2,1)S(1)} %get-tuple-element.38.first_0), channel_id=1, source_target_pairs={{0,2},{1,3},{2,0},{3,1},{4,6},{5,7},{6,4},{7,5},{8,10},{9,11},{10,... | collective-permute-start | bytes 786440 | tf_op jit(solution)/shard_map/ppermute | solution.py:180
  5.4 1.9 %collective-permute-start.6 = (bf16[512,512]{1,0:T(8,128)(2,1)}, bf16[512,512]{1,0:T(8,128)(2,1)S(1)}, u32[]{:S(2)}, u32[]{:S(2)}) collective-permute-start(bf16[512,512]{1,0:T(8,128)(2,1)} %bitcast.11), channel_id=1, source_target_pairs={{0,2},{1,3},{2,0},{3,1},{4,6},{5,7},{6,4},{7,5},{8,10},{9,11},{10,... | collective-permute-start | bytes 1572872 | tf_op jit(solution)/shard_map/ppermute | solution.py:180
  7.4 5.1 %collective-permute-done.2.across_0 = bf16[256,512]{1,0:T(8,128)(2,1)S(1)} collective-permute-done((bf16[256,512]{1,0:T(8,128)(2,1)S(1)}, bf16[256,512]{1,0:T(8,128)(2,1)S(1)}, u32[]{:S(2)}, u32[]{:S(2)}) %collective-permute-start.2) | collective-permute-done | bytes 262176 | tf_op jit(solution)/shard_map/ppermute | solution.py:180
  12.4 4.1 %collective-permute-start.4 = (bf16[256,512]{1,0:T(8,128)(2,1)S(1)}, bf16[256,512]{1,0:T(8,128)(2,1)S(1)}, u32[]{:S(2)}, u32[]{:S(2)}) collective-permute-start(bf16[256,512]{1,0:T(8,128)(2,1)S(1)} %collective-permute-done.2.across_0), channel_id=1, source_target_pairs={{0,4},{1,5},{4,8},{5,9},{6,2},{7,3},{8,12},{9,13},{10,6},{11,7},{1... | collective-permute-start | bytes 786440 | tf_op jit(solution)/shard_map/ppermute | solution.py:188
  16.5 1.6 %collective-permute-done.3.across_1 = bf16[256,512]{1,0:T(8,128)(2,1)S(1)} collective-permute-done((bf16[256,512]{1,0:T(8,128)(2,1)S(1)}, bf16[256,512]{1,0:T(8,128)(2,1)S(1)}, u32[]{:S(2)}, u32[]{:S(2)}) %collective-permute-start.3) | collective-permute-done | bytes 262176 | tf_op jit(solution)/shard_map/ppermute | solution.py:180
  18.1 4.1 %collective-permute-start.5 = (bf16[256,512]{1,0:T(8,128)(2,1)S(1)}, bf16[256,512]{1,0:T(8,128)(2,1)S(1)}, u32[]{:S(2)}, u32[]{:S(2)}) collective-permute-start(bf16[256,512]{1,0:T(8,128)(2,1)S(1)} %collective-permute-done.3.across_1), channel_id=1, source_target_pairs={{0,4},{1,5},{4,8},{5,9},{6,2},{7,3},{8,12},{9,13},{10,6},{11,7},{1... | collective-permute-start | bytes 786440 | tf_op jit(solution)/shard_map/ppermute | solution.py:188
  22.8 1.7 %copy-done = bf16[1,1,5,512,512]{4,3,2,1,0:T(8,128)(2,1)S(1)} copy-done((bf16[1,1,5,512,512]{4,3,2,1,0:T(8,128)(2,1)S(1)}, bf16[1,1,5,512,512]{4,3,2,1,0:T(8,128)(2,1)}, u32[]{:S(2)}) %copy-start) | copy-done | bytes 2621464
  24.5 1.0 %copy-done.3 = bf16[512,512]{1,0:T(8,128)(2,1)S(1)} copy-done((bf16[512,512]{1,0:T(8,128)(2,1)S(1)}, bf16[512,512]{1,0:T(8,128)(2,1)}, u32[]{:S(2)}) %copy-start.3) | copy-done | bytes 524312
  25.6 1.0 %copy-done.4 = bf16[1,1,512,512]{3,2,1,0:T(8,128)(2,1)S(1)} copy-done((bf16[1,1,512,512]{3,2,1,0:T(8,128)(2,1)S(1)}, bf16[1,1,512,512]{3,2,1,0:T(8,128)(2,1)}, u32[]{:S(2)}) %copy-start.4) | copy-done | bytes 524312
  26.6 0.7 copy-done.6
  27.3 2.8 %shard_map.120 = (f32[512,512]{1,0:T(8,128)S(1)}, f32[512,512]{1,0:T(8,128)S(1)}, bf16[1024,512]{1,0:T(8,128)(2,1)S(1)}, bf16[3,512,512]{2,1,0:T(8,128)(2,1)S(1)...) custom-call(s32[1]{0:T(128)} %bitcast.where_ref, s32[5]{0:T(128)S(1)} %bitcast.15, s32[1]{0:T(128)} %bitcast.8.count_ref, ...), custom_call_target="tpu_custom_call" | custom-call | flops 1073741824 | bytes 11010076 | tf_op jit(solution)/shard_map/pallas_call | solution.py:16
  30.3 1.6 %collective-permute-start.15 = (bf16[512,512]{1,0:T(8,128)(2,1)S(1)}, bf16[512,512]{1,0:T(8,128)(2,1)S(1)}, u32[]{:S(2)}, u32[]{:S(2)}) collective-permute-start(bf16[512,512]{1,0:T(8,128)(2,1)S(1)} %collective-permute-done.6.across), channel_id=1, source_target_pairs={{0,4},{1,5},{2,0},{3,1},{4,8},{5,9},{6,2},{7,3},{8,12},{9,13},{10,... | collective-permute-start | bytes 1572872 | tf_op jit(solution)/shard_map/ppermute | solution.py:188
  32.2 2.3 %shard_map.121 = (bf16[512,512]{1,0:T(8,128)(2,1)}, bf16[512,512]{1,0:T(8,128)(2,1)S(1)}, bf16[2,256,512]{2,1,0:T(8,128)(2,1)S(1)}, f32[2,256,512]{2,1,0:T(8,128)S(1)}) custom-call(s32[1]{0:T(128)} %bitcast.where_ref, f32[512,512]{1,0:T(8,128)S(1)} %get-tuple-element.41.acc_in, bf16[256,512]{1,0:T(8,128)(2,1)S(1)} %collective-permute-done.2.across_0, ...), custom_call_target="tpu_custom_call" | custom-call | flops 1342177280 | bytes 7864324 | tf_op jit(solution)/shard_map/pallas_call | solution.py:16
  34.5 10.1 %collective-permute-done.15.far = bf16[512,512]{1,0:T(8,128)(2,1)S(1)} collective-permute-done((bf16[512,512]{1,0:T(8,128)(2,1)S(1)}, bf16[512,512]{1,0:T(8,128)(2,1)S(1)}, u32[]{:S(2)}, u32[]{:S(2)}) %collective-permute-start.15) | collective-permute-done | bytes 524320 | tf_op jit(solution)/shard_map/ppermute | solution.py:188
  45.3 0.7 shard_map.122.acc_in
  46.0 0.7 collective-permute-done.16.rest
  46.7 1.6 %shard_map.123 = (bf16[512,512]{1,0:T(8,128)(2,1)}, bf16[1,256,512]{2,1,0:T(8,128)(2,1)S(1)}, f32[1,256,512]{2,1,0:T(8,128)S(1)}) custom-call(s32[1]{0:T(128)} %bitcast.where_ref, f32[512,512]{1,0:T(8,128)S(1)} %shard_map.122.acc_in, bf16[512,512]{1,0:T(8,128)(2,1)S(1)} %collective-permute-done.15.far, bf16[512,512]{1,0:T(8,128)(2,1)S(1)} %collective-permute-done.16.rest, ...), custom_call_target="tpu_custom_call" | custom-call | flops 805306368 | bytes 6029316 | tf_op jit(solution)/shard_map/pallas_call | solution.py:16
  49.0 0.7 collective-permute-done.17
  49.9 1.6 %collective-permute-start.18 = (bf16[1,128,512]{2,1,0:T(8,128)(2,1)S(1)}, bf16[1,128,512]{2,1,0:T(8,128)(2,1)S(1)}, u32[]{:S(2)}, u32[]{:S(2)}) collective-permute-start(bf16[1,128,512]{2,1,0:T(8,128)(2,1)S(1)} %select_convert_fusion.1), channel_id=1, source_target_pairs={{0,4},{1,5},{2,6},{3,7},{4,0},{5,1},{6,2},{7,3},{8,12},{9,13},{10,... | collective-permute-start | bytes 393224 | tf_op jit(solution)/shard_map/ppermute | solution.py:180
  51.4 5.8 %collective-permute-done.9 = bf16[2,128,512]{2,1,0:T(8,128)(2,1)S(1)} collective-permute-done((bf16[2,128,512]{2,1,0:T(8,128)(2,1)S(1)}, bf16[2,128,512]{2,1,0:T(8,128)(2,1)S(1)}, u32[]{:S(2)}, u32[]{:S(2)}) %collective-permute-start.9) | collective-permute-done | bytes 262176 | tf_op jit(solution)/shard_map/ppermute | solution.py:180
  57.4 1.6 %collective-permute-start.10 = (bf16[2,64,512]{2,1,0:T(8,128)(2,1)S(1)}, bf16[2,64,512]{2,1,0:T(8,128)(2,1)S(1)}, u32[]{:S(2)}, u32[]{:S(2)}) collective-permute-start(bf16[2,64,512]{2,1,0:T(8,128)(2,1)S(1)} %select_convert_fusion.2), channel_id=1, source_target_pairs={{0,4},{1,5},{2,6},{3,7},{4,0},{5,1},{6,2},{7,3},{8,12},{9,13},{10,... | collective-permute-start | bytes 393224 | tf_op jit(solution)/shard_map/ppermute | solution.py:180
  59.1 1.6 %collective-permute-start.19 = (bf16[1,64,512]{2,1,0:T(8,128)(2,1)S(1)}, bf16[1,64,512]{2,1,0:T(8,128)(2,1)S(1)}, u32[]{:S(2)}, u32[]{:S(2)}) collective-permute-start(bf16[1,64,512]{2,1,0:T(8,128)(2,1)S(1)} %select_convert_fusion.3), channel_id=1, source_target_pairs={{0,8},{1,9},{2,10},{3,11},{4,12},{5,13},{6,14},{7,15},{8,0},{9,1},... | collective-permute-start | bytes 196616 | tf_op jit(solution)/shard_map/ppermute | solution.py:180
  60.7 2.5 %collective-permute-done.10 = bf16[2,64,512]{2,1,0:T(8,128)(2,1)S(1)} collective-permute-done((bf16[2,64,512]{2,1,0:T(8,128)(2,1)S(1)}, bf16[2,64,512]{2,1,0:T(8,128)(2,1)S(1)}, u32[]{:S(2)}, u32[]{:S(2)}) %collective-permute-start.10) | collective-permute-done | bytes 131104 | tf_op jit(solution)/shard_map/ppermute | solution.py:180
  63.2 2.5 %collective-permute-start.11 = (bf16[2,64,512]{2,1,0:T(8,128)(2,1)S(1)}, bf16[2,64,512]{2,1,0:T(8,128)(2,1)S(1)}, u32[]{:S(2)}, u32[]{:S(2)}) collective-permute-start(bf16[2,64,512]{2,1,0:T(8,128)(2,1)S(1)} %add_convert_fusion.1), channel_id=1, source_target_pairs={{0,8},{1,9},{2,10},{3,11},{4,12},{5,13},{6,14},{7,15},{8,0},{9,1},... | collective-permute-start | bytes 393224 | tf_op jit(solution)/shard_map/ppermute | solution.py:180
  66.3 4.6 %collective-permute-done.11 = bf16[2,64,512]{2,1,0:T(8,128)(2,1)S(1)} collective-permute-done((bf16[2,64,512]{2,1,0:T(8,128)(2,1)S(1)}, bf16[2,64,512]{2,1,0:T(8,128)(2,1)S(1)}, u32[]{:S(2)}, u32[]{:S(2)}) %collective-permute-start.11) | collective-permute-done | bytes 131104 | tf_op jit(solution)/shard_map/ppermute | solution.py:180
  71.1 2.7 %collective-permute-start.21 = (bf16[1,64,512]{2,1,0:T(8,128)(2,1)S(1)}, bf16[1,64,512]{2,1,0:T(8,128)(2,1)S(1)}, u32[]{:S(2)}, u32[]{:S(2)}) collective-permute-start(bf16[1,64,512]{2,1,0:T(8,128)(2,1)S(1)} %add_convert_fusion.2), channel_id=1, source_target_pairs={{0,8},{1,9},{2,10},{3,11},{4,12},{5,13},{6,14},{7,15},{8,0},{9,1},... | collective-permute-start | bytes 196616 | tf_op jit(solution)/shard_map/ppermute | solution.py:180
  73.8 3.2 %collective-permute-done.12 = bf16[2,64,512]{2,1,0:T(8,128)(2,1)S(1)} collective-permute-done((bf16[2,64,512]{2,1,0:T(8,128)(2,1)S(1)}, bf16[2,64,512]{2,1,0:T(8,128)(2,1)S(1)}, u32[]{:S(2)}, u32[]{:S(2)}) %collective-permute-start.12) | collective-permute-done | bytes 131104 | tf_op jit(solution)/shard_map/ppermute | solution.py:180
  77.2 2.0 %collective-permute-start.22 = (bf16[1,128,512]{2,1,0:T(8,128)(2,1)S(1)}, bf16[1,128,512]{2,1,0:T(8,128)(2,1)S(1)}, u32[]{:S(2)}, u32[]{:S(2)}) collective-permute-start(bf16[1,128,512]{2,1,0:T(8,128)(2,1)S(1)} %pad_maximum_fusion.4), channel_id=1, source_target_pairs={{0,4},{1,5},{2,6},{3,7},{4,0},{5,1},{6,2},{7,3},{8,12},{9,13},{10,... | collective-permute-start | bytes 393224 | tf_op jit(solution)/shard_map/ppermute | solution.py:180
  79.1 4.3 %collective-permute-done.13 = bf16[2,128,512]{2,1,0:T(8,128)(2,1)S(1)} collective-permute-done((bf16[2,128,512]{2,1,0:T(8,128)(2,1)S(1)}, bf16[2,128,512]{2,1,0:T(8,128)(2,1)S(1)}, u32[]{:S(2)}, u32[]{:S(2)}) %collective-permute-start.13) | collective-permute-done | bytes 262176 | tf_op jit(solution)/shard_map/ppermute | solution.py:180
  84.3 1.6 %collective-permute-done.23.second_other_ref = bf16[1,256,512]{2,1,0:T(8,128)(2,1)S(1)} collective-permute-done((bf16[1,256,512]{2,1,0:T(8,128)(2,1)S(1)}, bf16[1,256,512]{2,1,0:T(8,128)(2,1)S(1)}, u32[]{:S(2)}, u32[]{:S(2)}) %collective-permute-start.23) | collective-permute-done | bytes 262176 | tf_op jit(solution)/shard_map/ppermute | solution.py:180
  86.0 3.0 %shard_map.124 = (f32[512,512]{1,0:T(8,128)}, f32[512,512]{1,0:T(8,128)}, f32[512,512]{1,0:T(8,128)}) custom-call(s32[1]{0:T(128)} %bitcast.where_ref, bf16[2,256,512]{2,1,0:T(8,128)(2,1)S(1)} %pad_maximum_fusion.1.mine_ref, bf16[2,256,512]{2,1,0:T(8,128)(2,1)S(1)} %collective-permute-done.14.other_ref, ...), custom_call_target="tpu_custom_call" | custom-call | flops 1073741824 | bytes 7864324 | tf_op jit(solution)/shard_map/pallas_call | solution.py:16
  (59 shorter events, 4.8 us)
Async XLA Ops:
  0.6 22.1 %collective-permute-start.1 = (bf16[512,512]{1,0:T(8,128)(2,1)}, bf16[512,512]{1,0:T(8,128)(2,1)S(1)}, u32[]{:S(2)}, u32[]{:S(2)}) collective-permute-start(bf16[512,512]{1,0:T(8,128)(2,1)} %bitcast.10), channel_id=1, source_target_pairs={{0,1},{1,0},{2,3},{3,2},{4,5},{5,4},{6,7},{7,6},{8,9},{9,8},{10,11... | collective-permute-start | bytes 1572872 | tf_op jit(solution)/shard_map/ppermute | solution.py:180
  1.2 21.6 %collective-permute-start = (bf16[512,512]{1,0:T(8,128)(2,1)}, bf16[512,512]{1,0:T(8,128)(2,1)S(1)}, u32[]{:S(2)}, u32[]{:S(2)}) collective-permute-start(bf16[512,512]{1,0:T(8,128)(2,1)} %bitcast.13), channel_id=1, source_target_pairs={{0,1},{1,0},{2,3},{3,2},{4,5},{5,4},{6,7},{7,6},{8,9},{9,8},{10,11... | collective-permute-start | bytes 1572872 | tf_op jit(solution)/shard_map/ppermute | solution.py:180
  1.2 1.0 %copy-start.5 = (bf16[1,1,512,512]{3,2,1,0:T(8,128)(2,1)S(1)}, bf16[1,1,512,512]{3,2,1,0:T(8,128)(2,1)}, u32[]{:S(2)}) copy-start(bf16[1,1,512,512]{3,2,1,0:T(8,128)(2,1)} %param.9) | copy-start | bytes 1572868
  2.3 10.1 %collective-permute-start.2 = (bf16[256,512]{1,0:T(8,128)(2,1)S(1)}, bf16[256,512]{1,0:T(8,128)(2,1)S(1)}, u32[]{:S(2)}, u32[]{:S(2)}) collective-permute-start(bf16[256,512]{1,0:T(8,128)(2,1)S(1)} %get-tuple-element.38.first_0), channel_id=1, source_target_pairs={{0,2},{1,3},{2,0},{3,1},{4,6},{5,7},{6,4},{7,5},{8,10},{9,11},{10,... | collective-permute-start | bytes 786440 | tf_op jit(solution)/shard_map/ppermute | solution.py:180
  5.3 12.7 %collective-permute-start.3 = (bf16[256,512]{1,0:T(8,128)(2,1)S(1)}, bf16[256,512]{1,0:T(8,128)(2,1)S(1)}, u32[]{:S(2)}, u32[]{:S(2)}) collective-permute-start(bf16[256,512]{1,0:T(8,128)(2,1)S(1)} %get-tuple-element.39.first_1), channel_id=1, source_target_pairs={{0,2},{1,3},{2,0},{3,1},{4,6},{5,7},{6,4},{7,5},{8,10},{9,11},{10,... | collective-permute-start | bytes 786440 | tf_op jit(solution)/shard_map/ppermute | solution.py:180
  5.4 24.7 %collective-permute-start.6 = (bf16[512,512]{1,0:T(8,128)(2,1)}, bf16[512,512]{1,0:T(8,128)(2,1)S(1)}, u32[]{:S(2)}, u32[]{:S(2)}) collective-permute-start(bf16[512,512]{1,0:T(8,128)(2,1)} %bitcast.11), channel_id=1, source_target_pairs={{0,2},{1,3},{2,0},{3,1},{4,6},{5,7},{6,4},{7,5},{8,10},{9,11},{10,... | collective-permute-start | bytes 1572872 | tf_op jit(solution)/shard_map/ppermute | solution.py:180
  12.4 17.7 %collective-permute-start.4 = (bf16[256,512]{1,0:T(8,128)(2,1)S(1)}, bf16[256,512]{1,0:T(8,128)(2,1)S(1)}, u32[]{:S(2)}, u32[]{:S(2)}) collective-permute-start(bf16[256,512]{1,0:T(8,128)(2,1)S(1)} %collective-permute-done.2.across_0), channel_id=1, source_target_pairs={{0,4},{1,5},{4,8},{5,9},{6,2},{7,3},{8,12},{9,13},{10,6},{11,7},{1... | collective-permute-start | bytes 786440 | tf_op jit(solution)/shard_map/ppermute | solution.py:188
  18.1 12.0 %collective-permute-start.5 = (bf16[256,512]{1,0:T(8,128)(2,1)S(1)}, bf16[256,512]{1,0:T(8,128)(2,1)S(1)}, u32[]{:S(2)}, u32[]{:S(2)}) collective-permute-start(bf16[256,512]{1,0:T(8,128)(2,1)S(1)} %collective-permute-done.3.across_1), channel_id=1, source_target_pairs={{0,4},{1,5},{4,8},{5,9},{6,2},{7,3},{8,12},{9,13},{10,6},{11,7},{1... | collective-permute-start | bytes 786440 | tf_op jit(solution)/shard_map/ppermute | solution.py:188
  22.8 1.7 %copy-start = (bf16[1,1,5,512,512]{4,3,2,1,0:T(8,128)(2,1)S(1)}, bf16[1,1,5,512,512]{4,3,2,1,0:T(8,128)(2,1)}, u32[]{:S(2)}) copy-start(bf16[1,1,5,512,512]{4,3,2,1,0:T(8,128)(2,1)} %param.8) | copy-start | bytes 7864324
  24.5 1.0 %copy-start.3 = (bf16[512,512]{1,0:T(8,128)(2,1)S(1)}, bf16[512,512]{1,0:T(8,128)(2,1)}, u32[]{:S(2)}) copy-start(bf16[512,512]{1,0:T(8,128)(2,1)} %lower_hbm.1) | copy-start | bytes 1572868
  25.6 1.0 %copy-start.4 = (bf16[1,1,512,512]{3,2,1,0:T(8,128)(2,1)S(1)}, bf16[1,1,512,512]{3,2,1,0:T(8,128)(2,1)}, u32[]{:S(2)}) copy-start(bf16[1,1,512,512]{3,2,1,0:T(8,128)(2,1)} %param.10) | copy-start | bytes 1572868
  26.6 0.7 copy-start.6
  30.2 2.0 %collective-permute-start.7 = (bf16[512,512]{1,0:T(8,128)(2,1)S(1)}, bf16[512,512]{1,0:T(8,128)(2,1)S(1)}, u32[]{:S(2)}, u32[]{:S(2)}) collective-permute-start(bf16[512,512]{1,0:T(8,128)(2,1)S(1)} %pad_maximum_fusion), channel_id=1, source_target_pairs={{0,1},{1,0},{2,3},{3,2},{4,5},{5,4},{6,7},{7,6},{8,9},{9,8},{10,11... | collective-permute-start | bytes 1572872 | tf_op jit(solution)/shard_map/ppermute | solution.py:180
  30.3 14.3 %collective-permute-start.15 = (bf16[512,512]{1,0:T(8,128)(2,1)S(1)}, bf16[512,512]{1,0:T(8,128)(2,1)S(1)}, u32[]{:S(2)}, u32[]{:S(2)}) collective-permute-start(bf16[512,512]{1,0:T(8,128)(2,1)S(1)} %collective-permute-done.6.across), channel_id=1, source_target_pairs={{0,4},{1,5},{2,0},{3,1},{4,8},{5,9},{6,2},{7,3},{8,12},{9,13},{10,... | collective-permute-start | bytes 1572872 | tf_op jit(solution)/shard_map/ppermute | solution.py:188
  44.7 2.0 %collective-permute-start.16 = (bf16[512,512]{1,0:T(8,128)(2,1)S(1)}, bf16[512,512]{1,0:T(8,128)(2,1)S(1)}, u32[]{:S(2)}, u32[]{:S(2)}) collective-permute-start(bf16[512,512]{1,0:T(8,128)(2,1)S(1)} %broadcast_select_fusion), channel_id=1, source_target_pairs={{0,1},{1,0},{2,3},{3,2},{4,5},{5,4},{6,7},{7,6},{8,9},{9,8},{10,11... | collective-permute-start | bytes 1572872 | tf_op jit(solution)/shard_map/ppermute | solution.py:180
  44.8 3.6 %collective-permute-start.8 = (bf16[2,256,512]{2,1,0:T(8,128)(2,1)S(1)}, bf16[2,256,512]{2,1,0:T(8,128)(2,1)S(1)}, u32[]{:S(2)}, u32[]{:S(2)}) collective-permute-start(bf16[2,256,512]{2,1,0:T(8,128)(2,1)S(1)} %get-tuple-element.54), channel_id=1, source_target_pairs={{0,1},{1,0},{2,3},{3,2},{4,5},{5,4},{6,7},{7,6},{8,9},{9,8},{10,11... | collective-permute-start | bytes 1572872 | tf_op jit(solution)/shard_map/ppermute | solution.py:180
  48.2 1.5 %collective-permute-start.17 = (bf16[1,256,512]{2,1,0:T(8,128)(2,1)S(1)}, bf16[1,256,512]{2,1,0:T(8,128)(2,1)S(1)}, u32[]{:S(2)}, u32[]{:S(2)}) collective-permute-start(bf16[1,256,512]{2,1,0:T(8,128)(2,1)S(1)} %get-tuple-element.61), channel_id=1, source_target_pairs={{0,1},{1,0},{2,3},{3,2},{4,5},{5,4},{6,7},{7,6},{8,9},{9,8},{10,11... | collective-permute-start | bytes 786440 | tf_op jit(solution)/shard_map/ppermute | solution.py:180
  48.6 8.6 %collective-permute-start.9 = (bf16[2,128,512]{2,1,0:T(8,128)(2,1)S(1)}, bf16[2,128,512]{2,1,0:T(8,128)(2,1)S(1)}, u32[]{:S(2)}, u32[]{:S(2)}) collective-permute-start(bf16[2,128,512]{2,1,0:T(8,128)(2,1)S(1)} %select_convert_fusion), channel_id=1, source_target_pairs={{0,2},{1,3},{2,0},{3,1},{4,6},{5,7},{6,4},{7,5},{8,10},{9,11},{10,... | collective-permute-start | bytes 786440 | tf_op jit(solution)/shard_map/ppermute | solution.py:180
  49.9 9.1 %collective-permute-start.18 = (bf16[1,128,512]{2,1,0:T(8,128)(2,1)S(1)}, bf16[1,128,512]{2,1,0:T(8,128)(2,1)S(1)}, u32[]{:S(2)}, u32[]{:S(2)}) collective-permute-start(bf16[1,128,512]{2,1,0:T(8,128)(2,1)S(1)} %select_convert_fusion.1), channel_id=1, source_target_pairs={{0,4},{1,5},{2,6},{3,7},{4,0},{5,1},{6,2},{7,3},{8,12},{9,13},{10,... | collective-permute-start | bytes 393224 | tf_op jit(solution)/shard_map/ppermute | solution.py:180
  57.4 5.7 %collective-permute-start.10 = (bf16[2,64,512]{2,1,0:T(8,128)(2,1)S(1)}, bf16[2,64,512]{2,1,0:T(8,128)(2,1)S(1)}, u32[]{:S(2)}, u32[]{:S(2)}) collective-permute-start(bf16[2,64,512]{2,1,0:T(8,128)(2,1)S(1)} %select_convert_fusion.2), channel_id=1, source_target_pairs={{0,4},{1,5},{2,6},{3,7},{4,0},{5,1},{6,2},{7,3},{8,12},{9,13},{10,... | collective-permute-start | bytes 393224 | tf_op jit(solution)/shard_map/ppermute | solution.py:180
  59.1 6.6 %collective-permute-start.19 = (bf16[1,64,512]{2,1,0:T(8,128)(2,1)S(1)}, bf16[1,64,512]{2,1,0:T(8,128)(2,1)S(1)}, u32[]{:S(2)}, u32[]{:S(2)}) collective-permute-start(bf16[1,64,512]{2,1,0:T(8,128)(2,1)S(1)} %select_convert_fusion.3), channel_id=1, source_target_pairs={{0,8},{1,9},{2,10},{3,11},{4,12},{5,13},{6,14},{7,15},{8,0},{9,1},... | collective-permute-start | bytes 196616 | tf_op jit(solution)/shard_map/ppermute | solution.py:180
  63.2 7.7 %collective-permute-start.11 = (bf16[2,64,512]{2,1,0:T(8,128)(2,1)S(1)}, bf16[2,64,512]{2,1,0:T(8,128)(2,1)S(1)}, u32[]{:S(2)}, u32[]{:S(2)}) collective-permute-start(bf16[2,64,512]{2,1,0:T(8,128)(2,1)S(1)} %add_convert_fusion.1), channel_id=1, source_target_pairs={{0,8},{1,9},{2,10},{3,11},{4,12},{5,13},{6,14},{7,15},{8,0},{9,1},... | collective-permute-start | bytes 393224 | tf_op jit(solution)/shard_map/ppermute | solution.py:180
  65.8 20.2 %copy-start.1 = (f32[512,512]{1,0:T(8,128)S(1)}, f32[512,512]{1,0:T(8,128)}, u32[]{:S(2)}) copy-start(f32[512,512]{1,0:T(8,128)} %first_diag_ref.1) | copy-start | bytes 3145732
  65.8 20.2 %copy-start.2 = (f32[512,512]{1,0:T(8,128)S(1)}, f32[512,512]{1,0:T(8,128)}, u32[]{:S(2)}) copy-start(f32[512,512]{1,0:T(8,128)} %second_diag_ref.1) | copy-start | bytes 3145732
  65.8 5.3 %collective-permute-start.20 = (bf16[1,64,512]{2,1,0:T(8,128)(2,1)S(1)}, bf16[1,64,512]{2,1,0:T(8,128)(2,1)S(1)}, u32[]{:S(2)}, u32[]{:S(2)}) collective-permute-start(bf16[1,64,512]{2,1,0:T(8,128)(2,1)S(1)} %add_convert_fusion.3), channel_id=1, source_target_pairs={{0,2},{1,3},{2,0},{3,1},{4,6},{5,7},{6,4},{7,5},{8,10},{9,11},{10,... | collective-permute-start | bytes 196616 | tf_op jit(solution)/shard_map/ppermute | solution.py:180
  71.0 6.0 %collective-permute-start.12 = (bf16[2,64,512]{2,1,0:T(8,128)(2,1)S(1)}, bf16[2,64,512]{2,1,0:T(8,128)(2,1)S(1)}, u32[]{:S(2)}, u32[]{:S(2)}) collective-permute-start(bf16[2,64,512]{2,1,0:T(8,128)(2,1)S(1)} %add_convert_fusion), channel_id=1, source_target_pairs={{0,4},{1,5},{2,6},{3,7},{4,0},{5,1},{6,2},{7,3},{8,12},{9,13},{10,... | collective-permute-start | bytes 393224 | tf_op jit(solution)/shard_map/ppermute | solution.py:180
  71.1 6.0 %collective-permute-start.21 = (bf16[1,64,512]{2,1,0:T(8,128)(2,1)S(1)}, bf16[1,64,512]{2,1,0:T(8,128)(2,1)S(1)}, u32[]{:S(2)}, u32[]{:S(2)}) collective-permute-start(bf16[1,64,512]{2,1,0:T(8,128)(2,1)S(1)} %add_convert_fusion.2), channel_id=1, source_target_pairs={{0,8},{1,9},{2,10},{3,11},{4,12},{5,13},{6,14},{7,15},{8,0},{9,1},... | collective-permute-start | bytes 196616 | tf_op jit(solution)/shard_map/ppermute | solution.py:180
  77.0 6.4 %collective-permute-start.13 = (bf16[2,128,512]{2,1,0:T(8,128)(2,1)S(1)}, bf16[2,128,512]{2,1,0:T(8,128)(2,1)S(1)}, u32[]{:S(2)}, u32[]{:S(2)}) collective-permute-start(bf16[2,128,512]{2,1,0:T(8,128)(2,1)S(1)} %pad_maximum_fusion.2), channel_id=1, source_target_pairs={{0,2},{1,3},{2,0},{3,1},{4,6},{5,7},{6,4},{7,5},{8,10},{9,11},{10,... | collective-permute-start | bytes 786440 | tf_op jit(solution)/shard_map/ppermute | solution.py:180
  77.2 6.5 %collective-permute-start.22 = (bf16[1,128,512]{2,1,0:T(8,128)(2,1)S(1)}, bf16[1,128,512]{2,1,0:T(8,128)(2,1)S(1)}, u32[]{:S(2)}, u32[]{:S(2)}) collective-permute-start(bf16[1,128,512]{2,1,0:T(8,128)(2,1)S(1)} %pad_maximum_fusion.4), channel_id=1, source_target_pairs={{0,4},{1,5},{2,6},{3,7},{4,0},{5,1},{6,2},{7,3},{8,12},{9,13},{10,... | collective-permute-start | bytes 393224 | tf_op jit(solution)/shard_map/ppermute | solution.py:180
  83.6 2.4 %collective-permute-start.14 = (bf16[2,256,512]{2,1,0:T(8,128)(2,1)S(1)}, bf16[2,256,512]{2,1,0:T(8,128)(2,1)S(1)}, u32[]{:S(2)}, u32[]{:S(2)}) collective-permute-start(bf16[2,256,512]{2,1,0:T(8,128)(2,1)S(1)} %pad_maximum_fusion.1.mine_ref), channel_id=1, source_target_pairs={{0,1},{1,0},{2,3},{3,2},{4,5},{5,4},{6,7},{7,6},{8,9},{9,8},{10,11... | collective-permute-start | bytes 1572872 | tf_op jit(solution)/shard_map/ppermute | solution.py:180
  83.8 2.2 %collective-permute-start.23 = (bf16[1,256,512]{2,1,0:T(8,128)(2,1)S(1)}, bf16[1,256,512]{2,1,0:T(8,128)(2,1)S(1)}, u32[]{:S(2)}, u32[]{:S(2)}) collective-permute-start(bf16[1,256,512]{2,1,0:T(8,128)(2,1)S(1)} %pad_maximum_fusion.3.second_mine_ref), channel_id=1, source_target_pairs={{0,1},{1,0},{2,3},{3,2},{4,5},{5,4},{6,7},{7,6},{8,9},{9,8},{10,11... | collective-permute-start | bytes 786440 | tf_op jit(solution)/shard_map/ppermute | solution.py:180

commit v15 on v14

--- a/solution.py
+++ b/solution.py
@@ -290,10 +290,10 @@
     )
     last = len(uppers) - 1
     second_total = core_summed(second_give, second_keep, devices)
-    mine, other = summed(total, (range(2, last), last, range(last - 1, 0, -1)), uppers, devices)
-    second_mine, second_other = summed(
-        second_total, (range(2, last + 1), 1, range(last, 1, -1)), uppers, devices
-    )
+    halve = [1, *range(2, last)]
+    second_halve = [2, 1, *range(3, last)]
+    mine, other = summed(total, (halve[1:], last, halve[::-1]), uppers, devices)
+    second_mine, second_other = summed(second_total, (second_halve, last, second_halve[::-1]), uppers, devices)
     block_first, block_link, block_second = call(
         final_kernel,
         [wide] * 3,

time: 89.3 us -> 89.6 us (level)
  waiting for transfers between devices: 40.6 us -> 44.2 us
  starting transfers between devices: 29.7 us -> 26.5 us
    ppermute x21, waiting for transfers between devices: 30.5 us -> 34 us  [swapped(): return lax.ppermute(value, 'row', [(i, i ^ bit) for i in range(devices)])]
    ppermute x21, starting transfers between devices: 20 us -> 16.7 us  [swapped(): return lax.ppermute(value, 'row', [(i, i ^ bit) for i in range(devices)])]
  transfers between devices with their start and end apart: 24 -> 24, of which waited for: 12 -> 13; matrix products, arithmetic and copies ran while one was open for 1% -> 1% of each run, Pallas kernels for 8% -> 8%
where the time goes in v15:
time: 89.6 us; the launch traced here: 89.3 us
  waiting for transfers between devices  44.2 us (49%)
  starting transfers between devices  26.5 us (30%)
  Pallas kernels  10.4 us (12%)
  local copies, waits for them, and re-layouts  5.53 us (6%)
  between operations  1.6 us (2%)
  other arithmetic  1.12 us (1%)
    ppermute x21, waiting for transfers between devices, swapped(): return lax.ppermute(value, 'row', [(i, i ^ bit) for i in range(devices)])  34 us
    ppermute x21, starting transfers between devices, swapped(): return lax.ppermute(value, 'row', [(i, i ^ bit) for i in range(devices)])  16.7 us
    pallas_call x6, Pallas kernels, call(): pl.pallas_call(body, out_shape=outs, in_specs=[pl.BlockSpec(memory_space=...  10.4 us
    ppermute x3, waiting for transfers between devices, far_of(): return lax.ppermute(across, 'row', pairs)  10.1 us
    ppermute x3, starting transfers between devices, far_of(): return lax.ppermute(across, 'row', pairs)  9.72 us
    unnamed x14, local copies, waits for them, and re-layouts  5.53 us
  transfers between devices with their start and end apart: 24, of which 13 were waited for; matrix products, arithmetic and copies ran while one was open for 1% of the time, Pallas kernels for 8%

profile of v15, /device:TPU:0, one launch (start us, length us, event | category | flops | bytes accessed | tf_op | source)
XLA Modules:
  0.0 89.3 jit_solution(9741427729511935487)
XLA Ops:
  1.2 1.0 %copy-done.5 = bf16[1,1,512,512]{3,2,1,0:T(8,128)(2,1)S(1)} copy-done((bf16[1,1,512,512]{3,2,1,0:T(8,128)(2,1)S(1)}, bf16[1,1,512,512]{3,2,1,0:T(8,128)(2,1)}, u32[]{:S(2)}) %copy-start.5) | copy-done | bytes 524312
  2.3 3.0 %collective-permute-start.2 = (bf16[256,512]{1,0:T(8,128)(2,1)S(1)}, bf16[256,512]{1,0:T(8,128)(2,1)S(1)}, u32[]{:S(2)}, u32[]{:S(2)}) collective-permute-start(bf16[256,512]{1,0:T(8,128)(2,1)S(1)} %get-tuple-element.37.first_0), channel_id=1, source_target_pairs={{0,2},{1,3},{2,0},{3,1},{4,6},{5,7},{6,4},{7,5},{8,10},{9,11},{10,... | collective-permute-start | bytes 786440 | tf_op jit(solution)/shard_map/ppermute | solution.py:180
  5.4 1.9 %collective-permute-start.6 = (bf16[512,512]{1,0:T(8,128)(2,1)}, bf16[512,512]{1,0:T(8,128)(2,1)S(1)}, u32[]{:S(2)}, u32[]{:S(2)}) collective-permute-start(bf16[512,512]{1,0:T(8,128)(2,1)} %bitcast.11), channel_id=1, source_target_pairs={{0,2},{1,3},{2,0},{3,1},{4,6},{5,7},{6,4},{7,5},{8,10},{9,11},{10,... | collective-permute-start | bytes 1572872 | tf_op jit(solution)/shard_map/ppermute | solution.py:180
  7.4 5.1 %collective-permute-done.2.across_0 = bf16[256,512]{1,0:T(8,128)(2,1)S(1)} collective-permute-done((bf16[256,512]{1,0:T(8,128)(2,1)S(1)}, bf16[256,512]{1,0:T(8,128)(2,1)S(1)}, u32[]{:S(2)}, u32[]{:S(2)}) %collective-permute-start.2) | collective-permute-done | bytes 262176 | tf_op jit(solution)/shard_map/ppermute | solution.py:180
  12.4 4.1 %collective-permute-start.4 = (bf16[256,512]{1,0:T(8,128)(2,1)S(1)}, bf16[256,512]{1,0:T(8,128)(2,1)S(1)}, u32[]{:S(2)}, u32[]{:S(2)}) collective-permute-start(bf16[256,512]{1,0:T(8,128)(2,1)S(1)} %collective-permute-done.2.across_0), channel_id=1, source_target_pairs={{0,4},{1,5},{4,8},{5,9},{6,2},{7,3},{8,12},{9,13},{10,6},{11,7},{1... | collective-permute-start | bytes 786440 | tf_op jit(solution)/shard_map/ppermute | solution.py:188
  16.5 1.6 %collective-permute-done.3.across_1 = bf16[256,512]{1,0:T(8,128)(2,1)S(1)} collective-permute-done((bf16[256,512]{1,0:T(8,128)(2,1)S(1)}, bf16[256,512]{1,0:T(8,128)(2,1)S(1)}, u32[]{:S(2)}, u32[]{:S(2)}) %collective-permute-start.3) | collective-permute-done | bytes 262176 | tf_op jit(solution)/shard_map/ppermute | solution.py:180
  18.1 4.1 %collective-permute-start.5 = (bf16[256,512]{1,0:T(8,128)(2,1)S(1)}, bf16[256,512]{1,0:T(8,128)(2,1)S(1)}, u32[]{:S(2)}, u32[]{:S(2)}) collective-permute-start(bf16[256,512]{1,0:T(8,128)(2,1)S(1)} %collective-permute-done.3.across_1), channel_id=1, source_target_pairs={{0,4},{1,5},{4,8},{5,9},{6,2},{7,3},{8,12},{9,13},{10,6},{11,7},{1... | collective-permute-start | bytes 786440 | tf_op jit(solution)/shard_map/ppermute | solution.py:188
  22.8 1.7 %copy-done = bf16[1,1,5,512,512]{4,3,2,1,0:T(8,128)(2,1)S(1)} copy-done((bf16[1,1,5,512,512]{4,3,2,1,0:T(8,128)(2,1)S(1)}, bf16[1,1,5,512,512]{4,3,2,1,0:T(8,128)(2,1)}, u32[]{:S(2)}) %copy-start) | copy-done | bytes 2621464
  24.5 1.0 %copy-done.3 = bf16[512,512]{1,0:T(8,128)(2,1)S(1)} copy-done((bf16[512,512]{1,0:T(8,128)(2,1)S(1)}, bf16[512,512]{1,0:T(8,128)(2,1)}, u32[]{:S(2)}) %copy-start.3) | copy-done | bytes 524312
  25.6 1.0 %copy-done.4 = bf16[1,1,512,512]{3,2,1,0:T(8,128)(2,1)S(1)} copy-done((bf16[1,1,512,512]{3,2,1,0:T(8,128)(2,1)S(1)}, bf16[1,1,512,512]{3,2,1,0:T(8,128)(2,1)}, u32[]{:S(2)}) %copy-start.4) | copy-done | bytes 524312
  26.6 0.7 copy-done.6
  27.3 2.8 %shard_map.120 = (f32[512,512]{1,0:T(8,128)S(1)}, f32[512,512]{1,0:T(8,128)S(1)}, bf16[1024,512]{1,0:T(8,128)(2,1)S(1)}, bf16[3,512,512]{2,1,0:T(8,128)(2,1)S(1)...) custom-call(s32[1]{0:T(128)} %bitcast.where_ref, s32[5]{0:T(128)S(1)} %bitcast.15, s32[1]{0:T(128)} %bitcast.8.count_ref, ...), custom_call_target="tpu_custom_call" | custom-call | flops 1073741824 | bytes 11010076 | tf_op jit(solution)/shard_map/pallas_call | solution.py:16
  30.3 1.6 %collective-permute-start.15 = (bf16[512,512]{1,0:T(8,128)(2,1)S(1)}, bf16[512,512]{1,0:T(8,128)(2,1)S(1)}, u32[]{:S(2)}, u32[]{:S(2)}) collective-permute-start(bf16[512,512]{1,0:T(8,128)(2,1)S(1)} %collective-permute-done.6.across), channel_id=1, source_target_pairs={{0,4},{1,5},{2,0},{3,1},{4,8},{5,9},{6,2},{7,3},{8,12},{9,13},{10,... | collective-permute-start | bytes 1572872 | tf_op jit(solution)/shard_map/ppermute | solution.py:188
  32.2 2.3 %shard_map.121 = (bf16[512,512]{1,0:T(8,128)(2,1)}, bf16[512,512]{1,0:T(8,128)(2,1)S(1)}, bf16[2,256,512]{2,1,0:T(8,128)(2,1)S(1)}, f32[2,256,512]{2,1,0:T(8,128)S(1)}) custom-call(s32[1]{0:T(128)} %bitcast.where_ref, f32[512,512]{1,0:T(8,128)S(1)} %get-tuple-element.40.acc_in, bf16[256,512]{1,0:T(8,128)(2,1)S(1)} %collective-permute-done.2.across_0, ...), custom_call_target="tpu_custom_call" | custom-call | flops 1342177280 | bytes 7864324 | tf_op jit(solution)/shard_map/pallas_call | solution.py:16
  34.5 10.1 %collective-permute-done.15.far = bf16[512,512]{1,0:T(8,128)(2,1)S(1)} collective-permute-done((bf16[512,512]{1,0:T(8,128)(2,1)S(1)}, bf16[512,512]{1,0:T(8,128)(2,1)S(1)}, u32[]{:S(2)}, u32[]{:S(2)}) %collective-permute-start.15) | collective-permute-done | bytes 524320 | tf_op jit(solution)/shard_map/ppermute | solution.py:188
  45.3 0.7 shard_map.122.acc_in
  46.0 0.7 collective-permute-done.16.rest
  46.7 1.6 %shard_map.123 = (bf16[512,512]{1,0:T(8,128)(2,1)}, bf16[1,256,512]{2,1,0:T(8,128)(2,1)S(1)}, f32[1,256,512]{2,1,0:T(8,128)S(1)}) custom-call(s32[1]{0:T(128)} %bitcast.where_ref, f32[512,512]{1,0:T(8,128)S(1)} %shard_map.122.acc_in, bf16[512,512]{1,0:T(8,128)(2,1)S(1)} %collective-permute-done.15.far, bf16[512,512]{1,0:T(8,128)(2,1)S(1)} %collective-permute-done.16.rest, ...), custom_call_target="tpu_custom_call" | custom-call | flops 805306368 | bytes 6029316 | tf_op jit(solution)/shard_map/pallas_call | solution.py:16
  49.0 0.7 collective-permute-done.17
  49.9 1.6 %collective-permute-start.18 = (bf16[1,128,512]{2,1,0:T(8,128)(2,1)S(1)}, bf16[1,128,512]{2,1,0:T(8,128)(2,1)S(1)}, u32[]{:S(2)}, u32[]{:S(2)}) collective-permute-start(bf16[1,128,512]{2,1,0:T(8,128)(2,1)S(1)} %select_convert_fusion.1), channel_id=1, source_target_pairs={{0,4},{1,5},{2,6},{3,7},{4,0},{5,1},{6,2},{7,3},{8,12},{9,13},{10,... | collective-permute-start | bytes 393224 | tf_op jit(solution)/shard_map/ppermute | solution.py:180
  51.5 5.8 %collective-permute-done.9 = bf16[2,128,512]{2,1,0:T(8,128)(2,1)S(1)} collective-permute-done((bf16[2,128,512]{2,1,0:T(8,128)(2,1)S(1)}, bf16[2,128,512]{2,1,0:T(8,128)(2,1)S(1)}, u32[]{:S(2)}, u32[]{:S(2)}) %collective-permute-start.9) | collective-permute-done | bytes 262176 | tf_op jit(solution)/shard_map/ppermute | solution.py:180
  57.4 1.6 %collective-permute-start.10 = (bf16[2,64,512]{2,1,0:T(8,128)(2,1)S(1)}, bf16[2,64,512]{2,1,0:T(8,128)(2,1)S(1)}, u32[]{:S(2)}, u32[]{:S(2)}) collective-permute-start(bf16[2,64,512]{2,1,0:T(8,128)(2,1)S(1)} %select_convert_fusion.2), channel_id=1, source_target_pairs={{0,4},{1,5},{2,6},{3,7},{4,0},{5,1},{6,2},{7,3},{8,12},{9,13},{10,... | collective-permute-start | bytes 393224 | tf_op jit(solution)/shard_map/ppermute | solution.py:180
  59.6 2.9 %collective-permute-done.10 = bf16[2,64,512]{2,1,0:T(8,128)(2,1)S(1)} collective-permute-done((bf16[2,64,512]{2,1,0:T(8,128)(2,1)S(1)}, bf16[2,64,512]{2,1,0:T(8,128)(2,1)S(1)}, u32[]{:S(2)}, u32[]{:S(2)}) %collective-permute-start.10) | collective-permute-done | bytes 131104 | tf_op jit(solution)/shard_map/ppermute | solution.py:180
  62.5 2.5 %collective-permute-start.11 = (bf16[2,64,512]{2,1,0:T(8,128)(2,1)S(1)}, bf16[2,64,512]{2,1,0:T(8,128)(2,1)S(1)}, u32[]{:S(2)}, u32[]{:S(2)}) collective-permute-start(bf16[2,64,512]{2,1,0:T(8,128)(2,1)S(1)} %add_convert_fusion.1), channel_id=1, source_target_pairs={{0,8},{1,9},{2,10},{3,11},{4,12},{5,13},{6,14},{7,15},{8,0},{9,1},... | collective-permute-start | bytes 393224 | tf_op jit(solution)/shard_map/ppermute | solution.py:180
  65.6 6.6 %collective-permute-done.11 = bf16[2,64,512]{2,1,0:T(8,128)(2,1)S(1)} collective-permute-done((bf16[2,64,512]{2,1,0:T(8,128)(2,1)S(1)}, bf16[2,64,512]{2,1,0:T(8,128)(2,1)S(1)}, u32[]{:S(2)}, u32[]{:S(2)}) %collective-permute-start.11) | collective-permute-done | bytes 131104 | tf_op jit(solution)/shard_map/ppermute | solution.py:180
  72.3 0.6 collective-permute-done.20
  73.4 3.9 %collective-permute-done.12 = bf16[2,64,512]{2,1,0:T(8,128)(2,1)S(1)} collective-permute-done((bf16[2,64,512]{2,1,0:T(8,128)(2,1)S(1)}, bf16[2,64,512]{2,1,0:T(8,128)(2,1)S(1)}, u32[]{:S(2)}, u32[]{:S(2)}) %collective-permute-start.12) | collective-permute-done | bytes 131104 | tf_op jit(solution)/shard_map/ppermute | solution.py:180
  77.8 1.7 %collective-permute-start.22 = (bf16[1,128,512]{2,1,0:T(8,128)(2,1)S(1)}, bf16[1,128,512]{2,1,0:T(8,128)(2,1)S(1)}, u32[]{:S(2)}, u32[]{:S(2)}) collective-permute-start(bf16[1,128,512]{2,1,0:T(8,128)(2,1)S(1)} %pad_maximum_fusion.4), channel_id=1, source_target_pairs={{0,4},{1,5},{2,6},{3,7},{4,0},{5,1},{6,2},{7,3},{8,12},{9,13},{10,... | collective-permute-start | bytes 393224 | tf_op jit(solution)/shard_map/ppermute | solution.py:180
  79.5 4.3 %collective-permute-done.13 = bf16[2,128,512]{2,1,0:T(8,128)(2,1)S(1)} collective-permute-done((bf16[2,128,512]{2,1,0:T(8,128)(2,1)S(1)}, bf16[2,128,512]{2,1,0:T(8,128)(2,1)S(1)}, u32[]{:S(2)}, u32[]{:S(2)}) %collective-permute-start.13) | collective-permute-done | bytes 262176 | tf_op jit(solution)/shard_map/ppermute | solution.py:180
  84.1 0.5 collective-permute-start.23
  84.6 1.6 %collective-permute-done.23.second_other_ref = bf16[1,256,512]{2,1,0:T(8,128)(2,1)S(1)} collective-permute-done((bf16[1,256,512]{2,1,0:T(8,128)(2,1)S(1)}, bf16[1,256,512]{2,1,0:T(8,128)(2,1)S(1)}, u32[]{:S(2)}, u32[]{:S(2)}) %collective-permute-start.23) | collective-permute-done | bytes 262176 | tf_op jit(solution)/shard_map/ppermute | solution.py:180
  86.3 3.0 %shard_map.124 = (f32[512,512]{1,0:T(8,128)}, f32[512,512]{1,0:T(8,128)}, f32[512,512]{1,0:T(8,128)}) custom-call(s32[1]{0:T(128)} %bitcast.where_ref, bf16[2,256,512]{2,1,0:T(8,128)(2,1)S(1)} %pad_maximum_fusion.1.mine_ref, bf16[2,256,512]{2,1,0:T(8,128)(2,1)S(1)} %collective-permute-done.14.other_ref, ...), custom_call_target="tpu_custom_call" | custom-call | flops 1073741824 | bytes 7864324 | tf_op jit(solution)/shard_map/pallas_call | solution.py:16
  (59 shorter events, 5.3 us)
Async XLA Ops:
  0.6 22.1 %collective-permute-start.1 = (bf16[512,512]{1,0:T(8,128)(2,1)}, bf16[512,512]{1,0:T(8,128)(2,1)S(1)}, u32[]{:S(2)}, u32[]{:S(2)}) collective-permute-start(bf16[512,512]{1,0:T(8,128)(2,1)} %bitcast.10), channel_id=1, source_target_pairs={{0,1},{1,0},{2,3},{3,2},{4,5},{5,4},{6,7},{7,6},{8,9},{9,8},{10,11... | collective-permute-start | bytes 1572872 | tf_op jit(solution)/shard_map/ppermute | solution.py:180
  1.2 21.6 %collective-permute-start = (bf16[512,512]{1,0:T(8,128)(2,1)}, bf16[512,512]{1,0:T(8,128)(2,1)S(1)}, u32[]{:S(2)}, u32[]{:S(2)}) collective-permute-start(bf16[512,512]{1,0:T(8,128)(2,1)} %bitcast.13), channel_id=1, source_target_pairs={{0,1},{1,0},{2,3},{3,2},{4,5},{5,4},{6,7},{7,6},{8,9},{9,8},{10,11... | collective-permute-start | bytes 1572872 | tf_op jit(solution)/shard_map/ppermute | solution.py:180
  1.2 1.0 %copy-start.5 = (bf16[1,1,512,512]{3,2,1,0:T(8,128)(2,1)S(1)}, bf16[1,1,512,512]{3,2,1,0:T(8,128)(2,1)}, u32[]{:S(2)}) copy-start(bf16[1,1,512,512]{3,2,1,0:T(8,128)(2,1)} %param.9) | copy-start | bytes 1572868
  2.3 10.1 %collective-permute-start.2 = (bf16[256,512]{1,0:T(8,128)(2,1)S(1)}, bf16[256,512]{1,0:T(8,128)(2,1)S(1)}, u32[]{:S(2)}, u32[]{:S(2)}) collective-permute-start(bf16[256,512]{1,0:T(8,128)(2,1)S(1)} %get-tuple-element.37.first_0), channel_id=1, source_target_pairs={{0,2},{1,3},{2,0},{3,1},{4,6},{5,7},{6,4},{7,5},{8,10},{9,11},{10,... | collective-permute-start | bytes 786440 | tf_op jit(solution)/shard_map/ppermute | solution.py:180
  5.3 12.7 %collective-permute-start.3 = (bf16[256,512]{1,0:T(8,128)(2,1)S(1)}, bf16[256,512]{1,0:T(8,128)(2,1)S(1)}, u32[]{:S(2)}, u32[]{:S(2)}) collective-permute-start(bf16[256,512]{1,0:T(8,128)(2,1)S(1)} %get-tuple-element.38.first_1), channel_id=1, source_target_pairs={{0,2},{1,3},{2,0},{3,1},{4,6},{5,7},{6,4},{7,5},{8,10},{9,11},{10,... | collective-permute-start | bytes 786440 | tf_op jit(solution)/shard_map/ppermute | solution.py:180
  5.4 24.7 %collective-permute-start.6 = (bf16[512,512]{1,0:T(8,128)(2,1)}, bf16[512,512]{1,0:T(8,128)(2,1)S(1)}, u32[]{:S(2)}, u32[]{:S(2)}) collective-permute-start(bf16[512,512]{1,0:T(8,128)(2,1)} %bitcast.11), channel_id=1, source_target_pairs={{0,2},{1,3},{2,0},{3,1},{4,6},{5,7},{6,4},{7,5},{8,10},{9,11},{10,... | collective-permute-start | bytes 1572872 | tf_op jit(solution)/shard_map/ppermute | solution.py:180
  12.4 17.7 %collective-permute-start.4 = (bf16[256,512]{1,0:T(8,128)(2,1)S(1)}, bf16[256,512]{1,0:T(8,128)(2,1)S(1)}, u32[]{:S(2)}, u32[]{:S(2)}) collective-permute-start(bf16[256,512]{1,0:T(8,128)(2,1)S(1)} %collective-permute-done.2.across_0), channel_id=1, source_target_pairs={{0,4},{1,5},{4,8},{5,9},{6,2},{7,3},{8,12},{9,13},{10,6},{11,7},{1... | collective-permute-start | bytes 786440 | tf_op jit(solution)/shard_map/ppermute | solution.py:188
  18.1 12.0 %collective-permute-start.5 = (bf16[256,512]{1,0:T(8,128)(2,1)S(1)}, bf16[256,512]{1,0:T(8,128)(2,1)S(1)}, u32[]{:S(2)}, u32[]{:S(2)}) collective-permute-start(bf16[256,512]{1,0:T(8,128)(2,1)S(1)} %collective-permute-done.3.across_1), channel_id=1, source_target_pairs={{0,4},{1,5},{4,8},{5,9},{6,2},{7,3},{8,12},{9,13},{10,6},{11,7},{1... | collective-permute-start | bytes 786440 | tf_op jit(solution)/shard_map/ppermute | solution.py:188
  22.8 1.7 %copy-start = (bf16[1,1,5,512,512]{4,3,2,1,0:T(8,128)(2,1)S(1)}, bf16[1,1,5,512,512]{4,3,2,1,0:T(8,128)(2,1)}, u32[]{:S(2)}) copy-start(bf16[1,1,5,512,512]{4,3,2,1,0:T(8,128)(2,1)} %param.8) | copy-start | bytes 7864324
  24.5 1.0 %copy-start.3 = (bf16[512,512]{1,0:T(8,128)(2,1)S(1)}, bf16[512,512]{1,0:T(8,128)(2,1)}, u32[]{:S(2)}) copy-start(bf16[512,512]{1,0:T(8,128)(2,1)} %lower_hbm.1) | copy-start | bytes 1572868
  25.6 1.0 %copy-start.4 = (bf16[1,1,512,512]{3,2,1,0:T(8,128)(2,1)S(1)}, bf16[1,1,512,512]{3,2,1,0:T(8,128)(2,1)}, u32[]{:S(2)}) copy-start(bf16[1,1,512,512]{3,2,1,0:T(8,128)(2,1)} %param.10) | copy-start | bytes 1572868
  26.6 0.7 copy-start.6
  30.2 2.0 %collective-permute-start.7 = (bf16[512,512]{1,0:T(8,128)(2,1)S(1)}, bf16[512,512]{1,0:T(8,128)(2,1)S(1)}, u32[]{:S(2)}, u32[]{:S(2)}) collective-permute-start(bf16[512,512]{1,0:T(8,128)(2,1)S(1)} %pad_maximum_fusion), channel_id=1, source_target_pairs={{0,1},{1,0},{2,3},{3,2},{4,5},{5,4},{6,7},{7,6},{8,9},{9,8},{10,11... | collective-permute-start | bytes 1572872 | tf_op jit(solution)/shard_map/ppermute | solution.py:180
  30.3 14.3 %collective-permute-start.15 = (bf16[512,512]{1,0:T(8,128)(2,1)S(1)}, bf16[512,512]{1,0:T(8,128)(2,1)S(1)}, u32[]{:S(2)}, u32[]{:S(2)}) collective-permute-start(bf16[512,512]{1,0:T(8,128)(2,1)S(1)} %collective-permute-done.6.across), channel_id=1, source_target_pairs={{0,4},{1,5},{2,0},{3,1},{4,8},{5,9},{6,2},{7,3},{8,12},{9,13},{10,... | collective-permute-start | bytes 1572872 | tf_op jit(solution)/shard_map/ppermute | solution.py:188
  44.7 2.0 %collective-permute-start.16 = (bf16[512,512]{1,0:T(8,128)(2,1)S(1)}, bf16[512,512]{1,0:T(8,128)(2,1)S(1)}, u32[]{:S(2)}, u32[]{:S(2)}) collective-permute-start(bf16[512,512]{1,0:T(8,128)(2,1)S(1)} %broadcast_select_fusion), channel_id=1, source_target_pairs={{0,1},{1,0},{2,3},{3,2},{4,5},{5,4},{6,7},{7,6},{8,9},{9,8},{10,11... | collective-permute-start | bytes 1572872 | tf_op jit(solution)/shard_map/ppermute | solution.py:180
  44.8 3.6 %collective-permute-start.8 = (bf16[2,256,512]{2,1,0:T(8,128)(2,1)S(1)}, bf16[2,256,512]{2,1,0:T(8,128)(2,1)S(1)}, u32[]{:S(2)}, u32[]{:S(2)}) collective-permute-start(bf16[2,256,512]{2,1,0:T(8,128)(2,1)S(1)} %get-tuple-element.53), channel_id=1, source_target_pairs={{0,1},{1,0},{2,3},{3,2},{4,5},{5,4},{6,7},{7,6},{8,9},{9,8},{10,11... | collective-permute-start | bytes 1572872 | tf_op jit(solution)/shard_map/ppermute | solution.py:180
  48.2 1.5 %collective-permute-start.17 = (bf16[1,256,512]{2,1,0:T(8,128)(2,1)S(1)}, bf16[1,256,512]{2,1,0:T(8,128)(2,1)S(1)}, u32[]{:S(2)}, u32[]{:S(2)}) collective-permute-start(bf16[1,256,512]{2,1,0:T(8,128)(2,1)S(1)} %get-tuple-element.59), channel_id=1, source_target_pairs={{0,1},{1,0},{2,3},{3,2},{4,5},{5,4},{6,7},{7,6},{8,9},{9,8},{10,11... | collective-permute-start | bytes 786440 | tf_op jit(solution)/shard_map/ppermute | solution.py:180
  48.6 8.7 %collective-permute-start.9 = (bf16[2,128,512]{2,1,0:T(8,128)(2,1)S(1)}, bf16[2,128,512]{2,1,0:T(8,128)(2,1)S(1)}, u32[]{:S(2)}, u32[]{:S(2)}) collective-permute-start(bf16[2,128,512]{2,1,0:T(8,128)(2,1)S(1)} %select_convert_fusion), channel_id=1, source_target_pairs={{0,2},{1,3},{2,0},{3,1},{4,6},{5,7},{6,4},{7,5},{8,10},{9,11},{10,... | collective-permute-start | bytes 786440 | tf_op jit(solution)/shard_map/ppermute | solution.py:180
  49.9 9.2 %collective-permute-start.18 = (bf16[1,128,512]{2,1,0:T(8,128)(2,1)S(1)}, bf16[1,128,512]{2,1,0:T(8,128)(2,1)S(1)}, u32[]{:S(2)}, u32[]{:S(2)}) collective-permute-start(bf16[1,128,512]{2,1,0:T(8,128)(2,1)S(1)} %select_convert_fusion.1), channel_id=1, source_target_pairs={{0,4},{1,5},{2,6},{3,7},{4,0},{5,1},{6,2},{7,3},{8,12},{9,13},{10,... | collective-permute-start | bytes 393224 | tf_op jit(solution)/shard_map/ppermute | solution.py:180
  57.4 5.0 %collective-permute-start.10 = (bf16[2,64,512]{2,1,0:T(8,128)(2,1)S(1)}, bf16[2,64,512]{2,1,0:T(8,128)(2,1)S(1)}, u32[]{:S(2)}, u32[]{:S(2)}) collective-permute-start(bf16[2,64,512]{2,1,0:T(8,128)(2,1)S(1)} %select_convert_fusion.2), channel_id=1, source_target_pairs={{0,4},{1,5},{2,6},{3,7},{4,0},{5,1},{6,2},{7,3},{8,12},{9,13},{10,... | collective-permute-start | bytes 393224 | tf_op jit(solution)/shard_map/ppermute | solution.py:180
  59.2 5.9 %collective-permute-start.19 = (bf16[1,64,512]{2,1,0:T(8,128)(2,1)S(1)}, bf16[1,64,512]{2,1,0:T(8,128)(2,1)S(1)}, u32[]{:S(2)}, u32[]{:S(2)}) collective-permute-start(bf16[1,64,512]{2,1,0:T(8,128)(2,1)S(1)} %select_convert_fusion.3), channel_id=1, source_target_pairs={{0,2},{1,3},{2,0},{3,1},{4,6},{5,7},{6,4},{7,5},{8,10},{9,11},{10,... | collective-permute-start | bytes 196616 | tf_op jit(solution)/shard_map/ppermute | solution.py:180
  62.5 9.7 %collective-permute-start.11 = (bf16[2,64,512]{2,1,0:T(8,128)(2,1)S(1)}, bf16[2,64,512]{2,1,0:T(8,128)(2,1)S(1)}, u32[]{:S(2)}, u32[]{:S(2)}) collective-permute-start(bf16[2,64,512]{2,1,0:T(8,128)(2,1)S(1)} %add_convert_fusion.1), channel_id=1, source_target_pairs={{0,8},{1,9},{2,10},{3,11},{4,12},{5,13},{6,14},{7,15},{8,0},{9,1},... | collective-permute-start | bytes 393224 | tf_op jit(solution)/shard_map/ppermute | solution.py:180
  65.1 21.2 %copy-start.1 = (f32[512,512]{1,0:T(8,128)S(1)}, f32[512,512]{1,0:T(8,128)}, u32[]{:S(2)}) copy-start(f32[512,512]{1,0:T(8,128)} %first_diag_ref.1) | copy-start | bytes 3145732
  65.1 21.2 %copy-start.2 = (f32[512,512]{1,0:T(8,128)S(1)}, f32[512,512]{1,0:T(8,128)}, u32[]{:S(2)}) copy-start(f32[512,512]{1,0:T(8,128)} %second_diag_ref.1) | copy-start | bytes 3145732
  65.1 7.9 %collective-permute-start.20 = (bf16[1,64,512]{2,1,0:T(8,128)(2,1)S(1)}, bf16[1,64,512]{2,1,0:T(8,128)(2,1)S(1)}, u32[]{:S(2)}, u32[]{:S(2)}) collective-permute-start(bf16[1,64,512]{2,1,0:T(8,128)(2,1)S(1)} %add_convert_fusion.3), channel_id=1, source_target_pairs={{0,8},{1,9},{2,10},{3,11},{4,12},{5,13},{6,14},{7,15},{8,0},{9,1},... | collective-permute-start | bytes 196616 | tf_op jit(solution)/shard_map/ppermute | solution.py:180
  72.2 5.0 %collective-permute-start.12 = (bf16[2,64,512]{2,1,0:T(8,128)(2,1)S(1)}, bf16[2,64,512]{2,1,0:T(8,128)(2,1)S(1)}, u32[]{:S(2)}, u32[]{:S(2)}) collective-permute-start(bf16[2,64,512]{2,1,0:T(8,128)(2,1)S(1)} %add_convert_fusion), channel_id=1, source_target_pairs={{0,4},{1,5},{2,6},{3,7},{4,0},{5,1},{6,2},{7,3},{8,12},{9,13},{10,... | collective-permute-start | bytes 393224 | tf_op jit(solution)/shard_map/ppermute | solution.py:180
  73.0 4.8 %collective-permute-start.21 = (bf16[1,64,512]{2,1,0:T(8,128)(2,1)S(1)}, bf16[1,64,512]{2,1,0:T(8,128)(2,1)S(1)}, u32[]{:S(2)}, u32[]{:S(2)}) collective-permute-start(bf16[1,64,512]{2,1,0:T(8,128)(2,1)S(1)} %add_convert_fusion.2), channel_id=1, source_target_pairs={{0,2},{1,3},{2,0},{3,1},{4,6},{5,7},{6,4},{7,5},{8,10},{9,11},{10,... | collective-permute-start | bytes 196616 | tf_op jit(solution)/shard_map/ppermute | solution.py:180
  77.3 6.4 %collective-permute-start.13 = (bf16[2,128,512]{2,1,0:T(8,128)(2,1)S(1)}, bf16[2,128,512]{2,1,0:T(8,128)(2,1)S(1)}, u32[]{:S(2)}, u32[]{:S(2)}) collective-permute-start(bf16[2,128,512]{2,1,0:T(8,128)(2,1)S(1)} %pad_maximum_fusion.2), channel_id=1, source_target_pairs={{0,2},{1,3},{2,0},{3,1},{4,6},{5,7},{6,4},{7,5},{8,10},{9,11},{10,... | collective-permute-start | bytes 786440 | tf_op jit(solution)/shard_map/ppermute | solution.py:180
  77.8 6.2 %collective-permute-start.22 = (bf16[1,128,512]{2,1,0:T(8,128)(2,1)S(1)}, bf16[1,128,512]{2,1,0:T(8,128)(2,1)S(1)}, u32[]{:S(2)}, u32[]{:S(2)}) collective-permute-start(bf16[1,128,512]{2,1,0:T(8,128)(2,1)S(1)} %pad_maximum_fusion.4), channel_id=1, source_target_pairs={{0,4},{1,5},{2,6},{3,7},{4,0},{5,1},{6,2},{7,3},{8,12},{9,13},{10,... | collective-permute-start | bytes 393224 | tf_op jit(solution)/shard_map/ppermute | solution.py:180
  83.9 2.4 %collective-permute-start.14 = (bf16[2,256,512]{2,1,0:T(8,128)(2,1)S(1)}, bf16[2,256,512]{2,1,0:T(8,128)(2,1)S(1)}, u32[]{:S(2)}, u32[]{:S(2)}) collective-permute-start(bf16[2,256,512]{2,1,0:T(8,128)(2,1)S(1)} %pad_maximum_fusion.1.mine_ref), channel_id=1, source_target_pairs={{0,1},{1,0},{2,3},{3,2},{4,5},{5,4},{6,7},{7,6},{8,9},{9,8},{10,11... | collective-permute-start | bytes 1572872 | tf_op jit(solution)/shard_map/ppermute | solution.py:180
  84.1 2.2 %collective-permute-start.23 = (bf16[1,256,512]{2,1,0:T(8,128)(2,1)S(1)}, bf16[1,256,512]{2,1,0:T(8,128)(2,1)S(1)}, u32[]{:S(2)}, u32[]{:S(2)}) collective-permute-start(bf16[1,256,512]{2,1,0:T(8,128)(2,1)S(1)} %pad_maximum_fusion.3.second_mine_ref), channel_id=1, source_target_pairs={{0,1},{1,0},{2,3},{3,2},{4,5},{5,4},{6,7},{7,6},{8,9},{9,8},{10,11... | collective-permute-start | bytes 786440 | tf_op jit(solution)/shard_map/ppermute | solution.py:180

commit v16 on v14

--- a/solution.py
+++ b/solution.py
@@ -10,14 +10,14 @@
 VMEM_BYTES = 14 * 1024 * 1024
 
 
-def call(body, outs, args, spaces, flops, scratch=(), out_space="v"):
+def call(body, outs, args, spaces, flops, scratch=(), out_spaces=None):
     kinds = {"s": pltpu.SMEM, "v": pltpu.VMEM, "h": pltpu.HBM}
     moved = sum(a.size * a.dtype.itemsize for a in args) + sum(o.size * o.dtype.itemsize for o in outs)
     return pl.pallas_call(
         body,
         out_shape=outs,
         in_specs=[pl.BlockSpec(memory_space=kinds[c]) for c in spaces],
-        out_specs=[pl.BlockSpec(memory_space=kinds[out_space])] * len(outs),
+        out_specs=[pl.BlockSpec(memory_space=kinds[c]) for c in out_spaces or "v" * len(outs)],
         scratch_shapes=list(scratch),
         compiler_params=pltpu.CompilerParams(vmem_limit_bytes=VMEM_BYTES),
         cost_estimate=pl.CostEstimate(flops=flops, bytes_accessed=moved, transcendentals=0),
@@ -150,12 +150,11 @@
     out_ref[pl.ds(pl.multiple_of((1 - core) * half, half), half)] = other_ref[index].astype(jnp.float32)
 
 
-def final_kernel(where_ref, mine_ref, other_ref, second_mine_ref, second_other_ref, lower_ref, lower_turned_ref,
-                 first_diag_ref, second_diag_ref, first_hbm, link_hbm, second_hbm,
-                 sum_ref, first_ref, link_ref, second_ref, sems):
+def link_kernel(where_ref, mine_ref, other_ref, lower_ref, lower_turned_ref, first_diag_ref, second_diag_ref,
+                first_hbm, link_hbm, base_ref, sum_ref, first_ref, link_ref, sems):
     copies = [
-        pltpu.make_async_copy(source, target, sems.at[index])
-        for index, (source, target) in enumerate(((first_ref, first_hbm), (link_ref, link_hbm), (second_ref, second_hbm)))
+        pltpu.make_async_copy(first_ref, first_hbm, sems.at[0]),
+        pltpu.make_async_copy(link_ref, link_hbm, sems.at[1]),
     ]
     lower = lower_ref[...]
     turned = lower_turned_ref[...]
@@ -164,16 +163,19 @@
     first_ref[...] = block_first
     copies[0].start()
     place(where_ref, mine_ref, other_ref, 1, sum_ref)
-    place(where_ref, second_mine_ref, second_other_ref, 0, second_ref)
     high, low = split(block_first)
     link = dot(high, lower) + dot(low, lower) + sum_ref[...].T
     link_ref[...] = -link
     copies[1].start()
     high, low = split(link)
-    second_ref[...] += second_diag_ref[...] + dot(turned, high) + dot(turned, low)
-    copies[2].start()
+    base_ref[...] = second_diag_ref[...] + dot(turned, high) + dot(turned, low)
     for copy in copies:
         copy.wait()
+
+
+def last_kernel(where_ref, mine_ref, other_ref, base_ref, second_ref):
+    place(where_ref, mine_ref, other_ref, 0, second_ref)
+    second_ref[...] += base_ref[...]
 
 
 def swapped(value, bit, devices):
@@ -294,15 +296,16 @@
     second_mine, second_other = summed(
         second_total, (range(2, last + 1), 1, range(last, 1, -1)), uppers, devices
     )
-    block_first, block_link, block_second = call(
-        final_kernel,
+    block_first, block_link, base = call(
+        link_kernel,
         [wide] * 3,
-        [where, mine, other, second_mine, second_other, lower, lower_turned, first_diag, second_diag],
-        "svvvvvvvv",
+        [where, mine, other, lower, lower_turned, first_diag, second_diag],
+        "svvvvvv",
         4 * one,
-        scratch * 4 + [pltpu.SemaphoreType.DMA((3,))],
-        "h",
-    )
+        scratch * 3 + [pltpu.SemaphoreType.DMA((2,))],
+        "hhv",
+    )
+    (block_second,) = call(last_kernel, [wide], [where, second_mine, second_other, base], "svvv", size * width)
     shape = first_panel.shape
     return column_first.reshape(shape), block_first, block_link, column_second.reshape(shape), block_second
 

time: 89.3 us -> 89.3 us (level)
    pallas_call x6 -> x7, Pallas kernels: 10.4 us -> 10.8 us  [call(): pl.pallas_call(body, out_shape=outs, in_specs=[pl.BlockSpec(memory_space=...]
  transfers between devices with their start and end apart: 24 -> 24, of which waited for: 12 -> 12; matrix products, arithmetic and copies ran while one was open for 1% -> 1% of each run, Pallas kernels for 8% -> 11%
where the time goes in v16:
time: 89.3 us; the launch traced here: 88.9 us
  waiting for transfers between devices  40.2 us (45%)
  starting transfers between devices  29.7 us (33%)
  Pallas kernels  10.8 us (12%)
  local copies, waits for them, and re-layouts  5.53 us (6%)
  between operations  1.64 us (2%)
  other arithmetic  1.11 us (1%)
    ppermute x21, waiting for transfers between devices, swapped(): return lax.ppermute(value, 'row', [(i, i ^ bit) for i in range(devices)])  30.1 us
    ppermute x21, starting transfers between devices, swapped(): return lax.ppermute(value, 'row', [(i, i ^ bit) for i in range(devices)])  20 us
    pallas_call x7, Pallas kernels, call(): pl.pallas_call(body, out_shape=outs, in_specs=[pl.BlockSpec(memory_space=...  10.8 us
    ppermute x3, waiting for transfers between devices, far_of(): return lax.ppermute(across, 'row', pairs)  10.1 us
    ppermute x3, starting transfers between devices, far_of(): return lax.ppermute(across, 'row', pairs)  9.66 us
    unnamed x14, local copies, waits for them, and re-layouts  5.53 us
  transfers between devices with their start and end apart: 24, of which 12 were waited for; matrix products, arithmetic and copies ran while one was open for 1% of the time, Pallas kernels for 11%

profile of v16, /device:TPU:0, one launch (start us, length us, event | category | flops | bytes accessed | tf_op | source)
XLA Modules:
  0.0 88.9 jit_solution(12563140213709637126)
XLA Ops:
  1.2 1.0 %copy-done.5 = bf16[1,1,512,512]{3,2,1,0:T(8,128)(2,1)S(1)} copy-done((bf16[1,1,512,512]{3,2,1,0:T(8,128)(2,1)S(1)}, bf16[1,1,512,512]{3,2,1,0:T(8,128)(2,1)}, u32[]{:S(2)}) %copy-start.5) | copy-done | bytes 524312
  2.3 3.0 %collective-permute-start.2 = (bf16[256,512]{1,0:T(8,128)(2,1)S(1)}, bf16[256,512]{1,0:T(8,128)(2,1)S(1)}, u32[]{:S(2)}, u32[]{:S(2)}) collective-permute-start(bf16[256,512]{1,0:T(8,128)(2,1)S(1)} %get-tuple-element.38.first_0), channel_id=1, source_target_pairs={{0,2},{1,3},{2,0},{3,1},{4,6},{5,7},{6,4},{7,5},{8,10},{9,11},{10,... | collective-permute-start | bytes 786440 | tf_op jit(solution)/shard_map/ppermute | solution.py:182
  5.4 1.9 %collective-permute-start.6 = (bf16[512,512]{1,0:T(8,128)(2,1)}, bf16[512,512]{1,0:T(8,128)(2,1)S(1)}, u32[]{:S(2)}, u32[]{:S(2)}) collective-permute-start(bf16[512,512]{1,0:T(8,128)(2,1)} %bitcast.11), channel_id=1, source_target_pairs={{0,2},{1,3},{2,0},{3,1},{4,6},{5,7},{6,4},{7,5},{8,10},{9,11},{10,... | collective-permute-start | bytes 1572872 | tf_op jit(solution)/shard_map/ppermute | solution.py:182
  7.4 5.1 %collective-permute-done.2.across_0 = bf16[256,512]{1,0:T(8,128)(2,1)S(1)} collective-permute-done((bf16[256,512]{1,0:T(8,128)(2,1)S(1)}, bf16[256,512]{1,0:T(8,128)(2,1)S(1)}, u32[]{:S(2)}, u32[]{:S(2)}) %collective-permute-start.2) | collective-permute-done | bytes 262176 | tf_op jit(solution)/shard_map/ppermute | solution.py:182
  12.4 4.1 %collective-permute-start.4 = (bf16[256,512]{1,0:T(8,128)(2,1)S(1)}, bf16[256,512]{1,0:T(8,128)(2,1)S(1)}, u32[]{:S(2)}, u32[]{:S(2)}) collective-permute-start(bf16[256,512]{1,0:T(8,128)(2,1)S(1)} %collective-permute-done.2.across_0), channel_id=1, source_target_pairs={{0,4},{1,5},{4,8},{5,9},{6,2},{7,3},{8,12},{9,13},{10,6},{11,7},{1... | collective-permute-start | bytes 786440 | tf_op jit(solution)/shard_map/ppermute | solution.py:190
  16.5 1.6 %collective-permute-done.3.across_1 = bf16[256,512]{1,0:T(8,128)(2,1)S(1)} collective-permute-done((bf16[256,512]{1,0:T(8,128)(2,1)S(1)}, bf16[256,512]{1,0:T(8,128)(2,1)S(1)}, u32[]{:S(2)}, u32[]{:S(2)}) %collective-permute-start.3) | collective-permute-done | bytes 262176 | tf_op jit(solution)/shard_map/ppermute | solution.py:182
  18.1 4.1 %collective-permute-start.5 = (bf16[256,512]{1,0:T(8,128)(2,1)S(1)}, bf16[256,512]{1,0:T(8,128)(2,1)S(1)}, u32[]{:S(2)}, u32[]{:S(2)}) collective-permute-start(bf16[256,512]{1,0:T(8,128)(2,1)S(1)} %collective-permute-done.3.across_1), channel_id=1, source_target_pairs={{0,4},{1,5},{4,8},{5,9},{6,2},{7,3},{8,12},{9,13},{10,6},{11,7},{1... | collective-permute-start | bytes 786440 | tf_op jit(solution)/shard_map/ppermute | solution.py:190
  22.8 1.7 %copy-done = bf16[1,1,5,512,512]{4,3,2,1,0:T(8,128)(2,1)S(1)} copy-done((bf16[1,1,5,512,512]{4,3,2,1,0:T(8,128)(2,1)S(1)}, bf16[1,1,5,512,512]{4,3,2,1,0:T(8,128)(2,1)}, u32[]{:S(2)}) %copy-start) | copy-done | bytes 2621464
  24.5 1.0 %copy-done.3 = bf16[512,512]{1,0:T(8,128)(2,1)S(1)} copy-done((bf16[512,512]{1,0:T(8,128)(2,1)S(1)}, bf16[512,512]{1,0:T(8,128)(2,1)}, u32[]{:S(2)}) %copy-start.3) | copy-done | bytes 524312
  25.6 1.0 %copy-done.4 = bf16[1,1,512,512]{3,2,1,0:T(8,128)(2,1)S(1)} copy-done((bf16[1,1,512,512]{3,2,1,0:T(8,128)(2,1)S(1)}, bf16[1,1,512,512]{3,2,1,0:T(8,128)(2,1)}, u32[]{:S(2)}) %copy-start.4) | copy-done | bytes 524312
  27.3 2.8 %shard_map.120 = (f32[512,512]{1,0:T(8,128)S(1)}, f32[512,512]{1,0:T(8,128)S(1)}, bf16[1024,512]{1,0:T(8,128)(2,1)S(1)}, bf16[3,512,512]{2,1,0:T(8,128)(2,1)S(1)...) custom-call(s32[1]{0:T(128)} %bitcast.where_ref, s32[5]{0:T(128)S(1)} %bitcast.15, s32[1]{0:T(128)} %bitcast.8.count_ref, ...), custom_call_target="tpu_custom_call" | custom-call | flops 1073741824 | bytes 11010076 | tf_op jit(solution)/shard_map/pallas_call | solution.py:16
  30.3 1.6 %collective-permute-start.15 = (bf16[512,512]{1,0:T(8,128)(2,1)S(1)}, bf16[512,512]{1,0:T(8,128)(2,1)S(1)}, u32[]{:S(2)}, u32[]{:S(2)}) collective-permute-start(bf16[512,512]{1,0:T(8,128)(2,1)S(1)} %collective-permute-done.6.across), channel_id=1, source_target_pairs={{0,4},{1,5},{2,0},{3,1},{4,8},{5,9},{6,2},{7,3},{8,12},{9,13},{10,... | collective-permute-start | bytes 1572872 | tf_op jit(solution)/shard_map/ppermute | solution.py:190
  32.2 2.3 %shard_map.121 = (bf16[512,512]{1,0:T(8,128)(2,1)}, bf16[512,512]{1,0:T(8,128)(2,1)S(1)}, bf16[2,256,512]{2,1,0:T(8,128)(2,1)S(1)}, f32[2,256,512]{2,1,0:T(8,128)S(1)}) custom-call(s32[1]{0:T(128)} %bitcast.where_ref, f32[512,512]{1,0:T(8,128)S(1)} %get-tuple-element.41.acc_in, bf16[256,512]{1,0:T(8,128)(2,1)S(1)} %collective-permute-done.2.across_0, ...), custom_call_target="tpu_custom_call" | custom-call | flops 1342177280 | bytes 7864324 | tf_op jit(solution)/shard_map/pallas_call | solution.py:16
  34.5 10.1 %collective-permute-done.15.far = bf16[512,512]{1,0:T(8,128)(2,1)S(1)} collective-permute-done((bf16[512,512]{1,0:T(8,128)(2,1)S(1)}, bf16[512,512]{1,0:T(8,128)(2,1)S(1)}, u32[]{:S(2)}, u32[]{:S(2)}) %collective-permute-start.15) | collective-permute-done | bytes 524320 | tf_op jit(solution)/shard_map/ppermute | solution.py:190
  45.3 0.7 shard_map.123.acc_in
  46.0 0.7 collective-permute-done.16.rest
  46.7 1.6 %shard_map.124 = (bf16[512,512]{1,0:T(8,128)(2,1)}, bf16[1,256,512]{2,1,0:T(8,128)(2,1)S(1)}, f32[1,256,512]{2,1,0:T(8,128)S(1)}) custom-call(s32[1]{0:T(128)} %bitcast.where_ref, f32[512,512]{1,0:T(8,128)S(1)} %shard_map.123.acc_in, bf16[512,512]{1,0:T(8,128)(2,1)S(1)} %collective-permute-done.15.far, bf16[512,512]{1,0:T(8,128)(2,1)S(1)} %collective-permute-done.16.rest, ...), custom_call_target="tpu_custom_call" | custom-call | flops 805306368 | bytes 6029316 | tf_op jit(solution)/shard_map/pallas_call | solution.py:16
  49.0 0.7 collective-permute-done.17
  49.9 1.6 %collective-permute-start.18 = (bf16[1,128,512]{2,1,0:T(8,128)(2,1)S(1)}, bf16[1,128,512]{2,1,0:T(8,128)(2,1)S(1)}, u32[]{:S(2)}, u32[]{:S(2)}) collective-permute-start(bf16[1,128,512]{2,1,0:T(8,128)(2,1)S(1)} %select_convert_fusion.1), channel_id=1, source_target_pairs={{0,4},{1,5},{2,6},{3,7},{4,0},{5,1},{6,2},{7,3},{8,12},{9,13},{10,... | collective-permute-start | bytes 393224 | tf_op jit(solution)/shard_map/ppermute | solution.py:182
  51.4 5.8 %collective-permute-done.9 = bf16[2,128,512]{2,1,0:T(8,128)(2,1)S(1)} collective-permute-done((bf16[2,128,512]{2,1,0:T(8,128)(2,1)S(1)}, bf16[2,128,512]{2,1,0:T(8,128)(2,1)S(1)}, u32[]{:S(2)}, u32[]{:S(2)}) %collective-permute-start.9) | collective-permute-done | bytes 262176 | tf_op jit(solution)/shard_map/ppermute | solution.py:182
  57.4 1.6 %collective-permute-start.10 = (bf16[2,64,512]{2,1,0:T(8,128)(2,1)S(1)}, bf16[2,64,512]{2,1,0:T(8,128)(2,1)S(1)}, u32[]{:S(2)}, u32[]{:S(2)}) collective-permute-start(bf16[2,64,512]{2,1,0:T(8,128)(2,1)S(1)} %select_convert_fusion.2), channel_id=1, source_target_pairs={{0,4},{1,5},{2,6},{3,7},{4,0},{5,1},{6,2},{7,3},{8,12},{9,13},{10,... | collective-permute-start | bytes 393224 | tf_op jit(solution)/shard_map/ppermute | solution.py:182
  59.1 1.6 %collective-permute-start.19 = (bf16[1,64,512]{2,1,0:T(8,128)(2,1)S(1)}, bf16[1,64,512]{2,1,0:T(8,128)(2,1)S(1)}, u32[]{:S(2)}, u32[]{:S(2)}) collective-permute-start(bf16[1,64,512]{2,1,0:T(8,128)(2,1)S(1)} %select_convert_fusion.3), channel_id=1, source_target_pairs={{0,8},{1,9},{2,10},{3,11},{4,12},{5,13},{6,14},{7,15},{8,0},{9,1},... | collective-permute-start | bytes 196616 | tf_op jit(solution)/shard_map/ppermute | solution.py:182
  60.7 2.5 %collective-permute-done.10 = bf16[2,64,512]{2,1,0:T(8,128)(2,1)S(1)} collective-permute-done((bf16[2,64,512]{2,1,0:T(8,128)(2,1)S(1)}, bf16[2,64,512]{2,1,0:T(8,128)(2,1)S(1)}, u32[]{:S(2)}, u32[]{:S(2)}) %collective-permute-start.10) | collective-permute-done | bytes 131104 | tf_op jit(solution)/shard_map/ppermute | solution.py:182
  63.2 2.5 %collective-permute-start.11 = (bf16[2,64,512]{2,1,0:T(8,128)(2,1)S(1)}, bf16[2,64,512]{2,1,0:T(8,128)(2,1)S(1)}, u32[]{:S(2)}, u32[]{:S(2)}) collective-permute-start(bf16[2,64,512]{2,1,0:T(8,128)(2,1)S(1)} %add_convert_fusion.1), channel_id=1, source_target_pairs={{0,8},{1,9},{2,10},{3,11},{4,12},{5,13},{6,14},{7,15},{8,0},{9,1},... | collective-permute-start | bytes 393224 | tf_op jit(solution)/shard_map/ppermute | solution.py:182
  66.3 4.6 %collective-permute-done.11 = bf16[2,64,512]{2,1,0:T(8,128)(2,1)S(1)} collective-permute-done((bf16[2,64,512]{2,1,0:T(8,128)(2,1)S(1)}, bf16[2,64,512]{2,1,0:T(8,128)(2,1)S(1)}, u32[]{:S(2)}, u32[]{:S(2)}) %collective-permute-start.11) | collective-permute-done | bytes 131104 | tf_op jit(solution)/shard_map/ppermute | solution.py:182
  71.1 2.7 %collective-permute-start.21 = (bf16[1,64,512]{2,1,0:T(8,128)(2,1)S(1)}, bf16[1,64,512]{2,1,0:T(8,128)(2,1)S(1)}, u32[]{:S(2)}, u32[]{:S(2)}) collective-permute-start(bf16[1,64,512]{2,1,0:T(8,128)(2,1)S(1)} %add_convert_fusion.2), channel_id=1, source_target_pairs={{0,8},{1,9},{2,10},{3,11},{4,12},{5,13},{6,14},{7,15},{8,0},{9,1},... | collective-permute-start | bytes 196616 | tf_op jit(solution)/shard_map/ppermute | solution.py:182
  73.8 3.2 %collective-permute-done.12 = bf16[2,64,512]{2,1,0:T(8,128)(2,1)S(1)} collective-permute-done((bf16[2,64,512]{2,1,0:T(8,128)(2,1)S(1)}, bf16[2,64,512]{2,1,0:T(8,128)(2,1)S(1)}, u32[]{:S(2)}, u32[]{:S(2)}) %collective-permute-start.12) | collective-permute-done | bytes 131104 | tf_op jit(solution)/shard_map/ppermute | solution.py:182
  77.1 2.0 %collective-permute-start.22 = (bf16[1,128,512]{2,1,0:T(8,128)(2,1)S(1)}, bf16[1,128,512]{2,1,0:T(8,128)(2,1)S(1)}, u32[]{:S(2)}, u32[]{:S(2)}) collective-permute-start(bf16[1,128,512]{2,1,0:T(8,128)(2,1)S(1)} %pad_maximum_fusion.4), channel_id=1, source_target_pairs={{0,4},{1,5},{2,6},{3,7},{4,0},{5,1},{6,2},{7,3},{8,12},{9,13},{10,... | collective-permute-start | bytes 393224 | tf_op jit(solution)/shard_map/ppermute | solution.py:182
  79.1 4.3 %collective-permute-done.13 = bf16[2,128,512]{2,1,0:T(8,128)(2,1)S(1)} collective-permute-done((bf16[2,128,512]{2,1,0:T(8,128)(2,1)S(1)}, bf16[2,128,512]{2,1,0:T(8,128)(2,1)S(1)}, u32[]{:S(2)}, u32[]{:S(2)}) %collective-permute-start.13) | collective-permute-done | bytes 262176 | tf_op jit(solution)/shard_map/ppermute | solution.py:182
  84.3 1.3 %collective-permute-done.14.other_ref = bf16[2,256,512]{2,1,0:T(8,128)(2,1)S(1)} collective-permute-done((bf16[2,256,512]{2,1,0:T(8,128)(2,1)S(1)}, bf16[2,256,512]{2,1,0:T(8,128)(2,1)S(1)}, u32[]{:S(2)}, u32[]{:S(2)}) %collective-permute-start.14) | collective-permute-done | bytes 524320 | tf_op jit(solution)/shard_map/ppermute | solution.py:182
  85.6 2.1 %shard_map.122 = (f32[512,512]{1,0:T(8,128)}, f32[512,512]{1,0:T(8,128)}, f32[512,512]{1,0:T(8,128)S(1)}) custom-call(s32[1]{0:T(128)} %bitcast.where_ref, bf16[2,256,512]{2,1,0:T(8,128)(2,1)S(1)} %pad_maximum_fusion.1.mine_ref, bf16[2,256,512]{2,1,0:T(8,128)(2,1)S(1)} %collective-permute-done.14.other_ref, ...), custom_call_target="tpu_custom_call" | custom-call | flops 1073741824 | bytes 7340036 | tf_op jit(solution)/shard_map/pallas_call | solution.py:16
  87.7 1.2 %shard_map.125 = f32[512,512]{1,0:T(8,128)} custom-call(s32[1]{0:T(128)} %bitcast.where_ref, bf16[1,256,512]{2,1,0:T(8,128)(2,1)S(1)} %pad_maximum_fusion.3.mine_ref, bf16[1,256,512]{2,1,0:T(8,128)(2,1)S(1)} %collective-permute-done.23.other_ref, f32[512,512]{1,0:T(8,128)S(1)} %get-tuple-element.66.base_ref), custom_call_target="tpu_custom_call" | custom-call | flops 262144 | bytes 2621444 | tf_op jit(solution)/shard_map/pallas_call | solution.py:16
  (60 shorter events, 5.4 us)
Async XLA Ops:
  0.6 22.1 %collective-permute-start.1 = (bf16[512,512]{1,0:T(8,128)(2,1)}, bf16[512,512]{1,0:T(8,128)(2,1)S(1)}, u32[]{:S(2)}, u32[]{:S(2)}) collective-permute-start(bf16[512,512]{1,0:T(8,128)(2,1)} %bitcast.10), channel_id=1, source_target_pairs={{0,1},{1,0},{2,3},{3,2},{4,5},{5,4},{6,7},{7,6},{8,9},{9,8},{10,11... | collective-permute-start | bytes 1572872 | tf_op jit(solution)/shard_map/ppermute | solution.py:182
  1.2 21.6 %collective-permute-start = (bf16[512,512]{1,0:T(8,128)(2,1)}, bf16[512,512]{1,0:T(8,128)(2,1)S(1)}, u32[]{:S(2)}, u32[]{:S(2)}) collective-permute-start(bf16[512,512]{1,0:T(8,128)(2,1)} %bitcast.13), channel_id=1, source_target_pairs={{0,1},{1,0},{2,3},{3,2},{4,5},{5,4},{6,7},{7,6},{8,9},{9,8},{10,11... | collective-permute-start | bytes 1572872 | tf_op jit(solution)/shard_map/ppermute | solution.py:182
  1.2 1.0 %copy-start.5 = (bf16[1,1,512,512]{3,2,1,0:T(8,128)(2,1)S(1)}, bf16[1,1,512,512]{3,2,1,0:T(8,128)(2,1)}, u32[]{:S(2)}) copy-start(bf16[1,1,512,512]{3,2,1,0:T(8,128)(2,1)} %param.9) | copy-start | bytes 1572868
  2.3 10.1 %collective-permute-start.2 = (bf16[256,512]{1,0:T(8,128)(2,1)S(1)}, bf16[256,512]{1,0:T(8,128)(2,1)S(1)}, u32[]{:S(2)}, u32[]{:S(2)}) collective-permute-start(bf16[256,512]{1,0:T(8,128)(2,1)S(1)} %get-tuple-element.38.first_0), channel_id=1, source_target_pairs={{0,2},{1,3},{2,0},{3,1},{4,6},{5,7},{6,4},{7,5},{8,10},{9,11},{10,... | collective-permute-start | bytes 786440 | tf_op jit(solution)/shard_map/ppermute | solution.py:182
  5.3 12.7 %collective-permute-start.3 = (bf16[256,512]{1,0:T(8,128)(2,1)S(1)}, bf16[256,512]{1,0:T(8,128)(2,1)S(1)}, u32[]{:S(2)}, u32[]{:S(2)}) collective-permute-start(bf16[256,512]{1,0:T(8,128)(2,1)S(1)} %get-tuple-element.39.first_1), channel_id=1, source_target_pairs={{0,2},{1,3},{2,0},{3,1},{4,6},{5,7},{6,4},{7,5},{8,10},{9,11},{10,... | collective-permute-start | bytes 786440 | tf_op jit(solution)/shard_map/ppermute | solution.py:182
  5.4 24.7 %collective-permute-start.6 = (bf16[512,512]{1,0:T(8,128)(2,1)}, bf16[512,512]{1,0:T(8,128)(2,1)S(1)}, u32[]{:S(2)}, u32[]{:S(2)}) collective-permute-start(bf16[512,512]{1,0:T(8,128)(2,1)} %bitcast.11), channel_id=1, source_target_pairs={{0,2},{1,3},{2,0},{3,1},{4,6},{5,7},{6,4},{7,5},{8,10},{9,11},{10,... | collective-permute-start | bytes 1572872 | tf_op jit(solution)/shard_map/ppermute | solution.py:182
  12.4 17.7 %collective-permute-start.4 = (bf16[256,512]{1,0:T(8,128)(2,1)S(1)}, bf16[256,512]{1,0:T(8,128)(2,1)S(1)}, u32[]{:S(2)}, u32[]{:S(2)}) collective-permute-start(bf16[256,512]{1,0:T(8,128)(2,1)S(1)} %collective-permute-done.2.across_0), channel_id=1, source_target_pairs={{0,4},{1,5},{4,8},{5,9},{6,2},{7,3},{8,12},{9,13},{10,6},{11,7},{1... | collective-permute-start | bytes 786440 | tf_op jit(solution)/shard_map/ppermute | solution.py:190
  18.1 12.0 %collective-permute-start.5 = (bf16[256,512]{1,0:T(8,128)(2,1)S(1)}, bf16[256,512]{1,0:T(8,128)(2,1)S(1)}, u32[]{:S(2)}, u32[]{:S(2)}) collective-permute-start(bf16[256,512]{1,0:T(8,128)(2,1)S(1)} %collective-permute-done.3.across_1), channel_id=1, source_target_pairs={{0,4},{1,5},{4,8},{5,9},{6,2},{7,3},{8,12},{9,13},{10,6},{11,7},{1... | collective-permute-start | bytes 786440 | tf_op jit(solution)/shard_map/ppermute | solution.py:190
  22.8 1.7 %copy-start = (bf16[1,1,5,512,512]{4,3,2,1,0:T(8,128)(2,1)S(1)}, bf16[1,1,5,512,512]{4,3,2,1,0:T(8,128)(2,1)}, u32[]{:S(2)}) copy-start(bf16[1,1,5,512,512]{4,3,2,1,0:T(8,128)(2,1)} %param.8) | copy-start | bytes 7864324
  24.5 1.0 %copy-start.3 = (bf16[512,512]{1,0:T(8,128)(2,1)S(1)}, bf16[512,512]{1,0:T(8,128)(2,1)}, u32[]{:S(2)}) copy-start(bf16[512,512]{1,0:T(8,128)(2,1)} %lower_hbm.1) | copy-start | bytes 1572868
  25.6 1.0 %copy-start.4 = (bf16[1,1,512,512]{3,2,1,0:T(8,128)(2,1)S(1)}, bf16[1,1,512,512]{3,2,1,0:T(8,128)(2,1)}, u32[]{:S(2)}) copy-start(bf16[1,1,512,512]{3,2,1,0:T(8,128)(2,1)} %param.10) | copy-start | bytes 1572868
  26.6 0.7 copy-start.6
  30.2 2.0 %collective-permute-start.7 = (bf16[512,512]{1,0:T(8,128)(2,1)S(1)}, bf16[512,512]{1,0:T(8,128)(2,1)S(1)}, u32[]{:S(2)}, u32[]{:S(2)}) collective-permute-start(bf16[512,512]{1,0:T(8,128)(2,1)S(1)} %pad_maximum_fusion), channel_id=1, source_target_pairs={{0,1},{1,0},{2,3},{3,2},{4,5},{5,4},{6,7},{7,6},{8,9},{9,8},{10,11... | collective-permute-start | bytes 1572872 | tf_op jit(solution)/shard_map/ppermute | solution.py:182
  30.3 14.3 %collective-permute-start.15 = (bf16[512,512]{1,0:T(8,128)(2,1)S(1)}, bf16[512,512]{1,0:T(8,128)(2,1)S(1)}, u32[]{:S(2)}, u32[]{:S(2)}) collective-permute-start(bf16[512,512]{1,0:T(8,128)(2,1)S(1)} %collective-permute-done.6.across), channel_id=1, source_target_pairs={{0,4},{1,5},{2,0},{3,1},{4,8},{5,9},{6,2},{7,3},{8,12},{9,13},{10,... | collective-permute-start | bytes 1572872 | tf_op jit(solution)/shard_map/ppermute | solution.py:190
  44.7 2.0 %collective-permute-start.16 = (bf16[512,512]{1,0:T(8,128)(2,1)S(1)}, bf16[512,512]{1,0:T(8,128)(2,1)S(1)}, u32[]{:S(2)}, u32[]{:S(2)}) collective-permute-start(bf16[512,512]{1,0:T(8,128)(2,1)S(1)} %broadcast_select_fusion), channel_id=1, source_target_pairs={{0,1},{1,0},{2,3},{3,2},{4,5},{5,4},{6,7},{7,6},{8,9},{9,8},{10,11... | collective-permute-start | bytes 1572872 | tf_op jit(solution)/shard_map/ppermute | solution.py:182
  44.8 3.6 %collective-permute-start.8 = (bf16[2,256,512]{2,1,0:T(8,128)(2,1)S(1)}, bf16[2,256,512]{2,1,0:T(8,128)(2,1)S(1)}, u32[]{:S(2)}, u32[]{:S(2)}) collective-permute-start(bf16[2,256,512]{2,1,0:T(8,128)(2,1)S(1)} %get-tuple-element.54), channel_id=1, source_target_pairs={{0,1},{1,0},{2,3},{3,2},{4,5},{5,4},{6,7},{7,6},{8,9},{9,8},{10,11... | collective-permute-start | bytes 1572872 | tf_op jit(solution)/shard_map/ppermute | solution.py:182
  48.2 1.5 %collective-permute-start.17 = (bf16[1,256,512]{2,1,0:T(8,128)(2,1)S(1)}, bf16[1,256,512]{2,1,0:T(8,128)(2,1)S(1)}, u32[]{:S(2)}, u32[]{:S(2)}) collective-permute-start(bf16[1,256,512]{2,1,0:T(8,128)(2,1)S(1)} %get-tuple-element.65), channel_id=1, source_target_pairs={{0,1},{1,0},{2,3},{3,2},{4,5},{5,4},{6,7},{7,6},{8,9},{9,8},{10,11... | collective-permute-start | bytes 786440 | tf_op jit(solution)/shard_map/ppermute | solution.py:182
  48.6 8.6 %collective-permute-start.9 = (bf16[2,128,512]{2,1,0:T(8,128)(2,1)S(1)}, bf16[2,128,512]{2,1,0:T(8,128)(2,1)S(1)}, u32[]{:S(2)}, u32[]{:S(2)}) collective-permute-start(bf16[2,128,512]{2,1,0:T(8,128)(2,1)S(1)} %select_convert_fusion), channel_id=1, source_target_pairs={{0,2},{1,3},{2,0},{3,1},{4,6},{5,7},{6,4},{7,5},{8,10},{9,11},{10,... | collective-permute-start | bytes 786440 | tf_op jit(solution)/shard_map/ppermute | solution.py:182
  49.9 9.1 %collective-permute-start.18 = (bf16[1,128,512]{2,1,0:T(8,128)(2,1)S(1)}, bf16[1,128,512]{2,1,0:T(8,128)(2,1)S(1)}, u32[]{:S(2)}, u32[]{:S(2)}) collective-permute-start(bf16[1,128,512]{2,1,0:T(8,128)(2,1)S(1)} %select_convert_fusion.1), channel_id=1, source_target_pairs={{0,4},{1,5},{2,6},{3,7},{4,0},{5,1},{6,2},{7,3},{8,12},{9,13},{10,... | collective-permute-start | bytes 393224 | tf_op jit(solution)/shard_map/ppermute | solution.py:182
  57.4 5.7 %collective-permute-start.10 = (bf16[2,64,512]{2,1,0:T(8,128)(2,1)S(1)}, bf16[2,64,512]{2,1,0:T(8,128)(2,1)S(1)}, u32[]{:S(2)}, u32[]{:S(2)}) collective-permute-start(bf16[2,64,512]{2,1,0:T(8,128)(2,1)S(1)} %select_convert_fusion.2), channel_id=1, source_target_pairs={{0,4},{1,5},{2,6},{3,7},{4,0},{5,1},{6,2},{7,3},{8,12},{9,13},{10,... | collective-permute-start | bytes 393224 | tf_op jit(solution)/shard_map/ppermute | solution.py:182
  59.1 6.6 %collective-permute-start.19 = (bf16[1,64,512]{2,1,0:T(8,128)(2,1)S(1)}, bf16[1,64,512]{2,1,0:T(8,128)(2,1)S(1)}, u32[]{:S(2)}, u32[]{:S(2)}) collective-permute-start(bf16[1,64,512]{2,1,0:T(8,128)(2,1)S(1)} %select_convert_fusion.3), channel_id=1, source_target_pairs={{0,8},{1,9},{2,10},{3,11},{4,12},{5,13},{6,14},{7,15},{8,0},{9,1},... | collective-permute-start | bytes 196616 | tf_op jit(solution)/shard_map/ppermute | solution.py:182
  63.2 7.7 %collective-permute-start.11 = (bf16[2,64,512]{2,1,0:T(8,128)(2,1)S(1)}, bf16[2,64,512]{2,1,0:T(8,128)(2,1)S(1)}, u32[]{:S(2)}, u32[]{:S(2)}) collective-permute-start(bf16[2,64,512]{2,1,0:T(8,128)(2,1)S(1)} %add_convert_fusion.1), channel_id=1, source_target_pairs={{0,8},{1,9},{2,10},{3,11},{4,12},{5,13},{6,14},{7,15},{8,0},{9,1},... | collective-permute-start | bytes 393224 | tf_op jit(solution)/shard_map/ppermute | solution.py:182
  65.8 19.8 %copy-start.1 = (f32[512,512]{1,0:T(8,128)S(1)}, f32[512,512]{1,0:T(8,128)}, u32[]{:S(2)}) copy-start(f32[512,512]{1,0:T(8,128)} %first_diag_ref.1) | copy-start | bytes 3145732
  65.8 19.8 %copy-start.2 = (f32[512,512]{1,0:T(8,128)S(1)}, f32[512,512]{1,0:T(8,128)}, u32[]{:S(2)}) copy-start(f32[512,512]{1,0:T(8,128)} %second_diag_ref.1) | copy-start | bytes 3145732
  65.8 5.3 %collective-permute-start.20 = (bf16[1,64,512]{2,1,0:T(8,128)(2,1)S(1)}, bf16[1,64,512]{2,1,0:T(8,128)(2,1)S(1)}, u32[]{:S(2)}, u32[]{:S(2)}) collective-permute-start(bf16[1,64,512]{2,1,0:T(8,128)(2,1)S(1)} %add_convert_fusion.3), channel_id=1, source_target_pairs={{0,2},{1,3},{2,0},{3,1},{4,6},{5,7},{6,4},{7,5},{8,10},{9,11},{10,... | collective-permute-start | bytes 196616 | tf_op jit(solution)/shard_map/ppermute | solution.py:182
  71.0 6.0 %collective-permute-start.12 = (bf16[2,64,512]{2,1,0:T(8,128)(2,1)S(1)}, bf16[2,64,512]{2,1,0:T(8,128)(2,1)S(1)}, u32[]{:S(2)}, u32[]{:S(2)}) collective-permute-start(bf16[2,64,512]{2,1,0:T(8,128)(2,1)S(1)} %add_convert_fusion), channel_id=1, source_target_pairs={{0,4},{1,5},{2,6},{3,7},{4,0},{5,1},{6,2},{7,3},{8,12},{9,13},{10,... | collective-permute-start | bytes 393224 | tf_op jit(solution)/shard_map/ppermute | solution.py:182
  71.1 6.0 %collective-permute-start.21 = (bf16[1,64,512]{2,1,0:T(8,128)(2,1)S(1)}, bf16[1,64,512]{2,1,0:T(8,128)(2,1)S(1)}, u32[]{:S(2)}, u32[]{:S(2)}) collective-permute-start(bf16[1,64,512]{2,1,0:T(8,128)(2,1)S(1)} %add_convert_fusion.2), channel_id=1, source_target_pairs={{0,8},{1,9},{2,10},{3,11},{4,12},{5,13},{6,14},{7,15},{8,0},{9,1},... | collective-permute-start | bytes 196616 | tf_op jit(solution)/shard_map/ppermute | solution.py:182
  77.0 6.4 %collective-permute-start.13 = (bf16[2,128,512]{2,1,0:T(8,128)(2,1)S(1)}, bf16[2,128,512]{2,1,0:T(8,128)(2,1)S(1)}, u32[]{:S(2)}, u32[]{:S(2)}) collective-permute-start(bf16[2,128,512]{2,1,0:T(8,128)(2,1)S(1)} %pad_maximum_fusion.2), channel_id=1, source_target_pairs={{0,2},{1,3},{2,0},{3,1},{4,6},{5,7},{6,4},{7,5},{8,10},{9,11},{10,... | collective-permute-start | bytes 786440 | tf_op jit(solution)/shard_map/ppermute | solution.py:182
  77.1 6.5 %collective-permute-start.22 = (bf16[1,128,512]{2,1,0:T(8,128)(2,1)S(1)}, bf16[1,128,512]{2,1,0:T(8,128)(2,1)S(1)}, u32[]{:S(2)}, u32[]{:S(2)}) collective-permute-start(bf16[1,128,512]{2,1,0:T(8,128)(2,1)S(1)} %pad_maximum_fusion.4), channel_id=1, source_target_pairs={{0,4},{1,5},{2,6},{3,7},{4,0},{5,1},{6,2},{7,3},{8,12},{9,13},{10,... | collective-permute-start | bytes 393224 | tf_op jit(solution)/shard_map/ppermute | solution.py:182
  83.6 2.0 %collective-permute-start.14 = (bf16[2,256,512]{2,1,0:T(8,128)(2,1)S(1)}, bf16[2,256,512]{2,1,0:T(8,128)(2,1)S(1)}, u32[]{:S(2)}, u32[]{:S(2)}) collective-permute-start(bf16[2,256,512]{2,1,0:T(8,128)(2,1)S(1)} %pad_maximum_fusion.1.mine_ref), channel_id=1, source_target_pairs={{0,1},{1,0},{2,3},{3,2},{4,5},{5,4},{6,7},{7,6},{8,9},{9,8},{10,11... | collective-permute-start | bytes 1572872 | tf_op jit(solution)/shard_map/ppermute | solution.py:182
  83.8 4.0 %collective-permute-start.23 = (bf16[1,256,512]{2,1,0:T(8,128)(2,1)S(1)}, bf16[1,256,512]{2,1,0:T(8,128)(2,1)S(1)}, u32[]{:S(2)}, u32[]{:S(2)}) collective-permute-start(bf16[1,256,512]{2,1,0:T(8,128)(2,1)S(1)} %pad_maximum_fusion.3.mine_ref), channel_id=1, source_target_pairs={{0,1},{1,0},{2,3},{3,2},{4,5},{5,4},{6,7},{7,6},{8,9},{9,8},{10,11... | collective-permute-start | bytes 786440 | tf_op jit(solution)/shard_map/ppermute | solution.py:182
